TPU v7x, 32 devices: a whole 2x2x4 slice. The times are simulated.
32 devices in a mesh: groups: 2 (over x), expert: 16 (over z, y, core).
Axes of the slice: x: 2, y: 2, z: 4, core: 2. Of those that a mesh axis runs over, the one named last changes fastest.
Arguments:
- layer_input: bfloat16 [4096, 3584], P(('groups', 'expert')), parts along dimension 0, may hold values from -6 to 6
- output_gradient: bfloat16 [4096, 3584], P(('groups', 'expert')), parts along dimension 0, may hold values from -6 to 6
- router_matrix: bfloat16 [3584, 16], replicated, may hold values from -0.09375 to 0.09375
- routed_expert_index: int32 [4096, 4], P(('groups', 'expert')), parts along dimension 0, may hold values from 0 to 15, all different within a row; in each aligned block of 128 rows (0 to 127, 128 to 255, ...) at most 48 rows name the same one
- gate_weight_frozen: bfloat16 [16, 3584, 1024], P('expert'), may hold values from -0.09375 to 0.09375
- up_weight_frozen: bfloat16 [16, 3584, 1024], P('expert'), may hold values from -0.09375 to 0.09375
- down_weight_frozen: bfloat16 [16, 1024, 3584], P('expert'), may hold values from -0.1875 to 0.1875
- gate_adapter_first: bfloat16 [32, 3584, 32], P(('groups', 'expert')), parts along dimension 0, may hold values from -0.09375 to 0.09375
- gate_adapter_second: bfloat16 [32, 32, 1024], P(('groups', 'expert')), parts along dimension 0, may hold values from -1 to 1
- up_adapter_first: bfloat16 [32, 3584, 32], P(('groups', 'expert')), parts along dimension 0, may hold values from -0.09375 to 0.09375
- up_adapter_second: bfloat16 [32, 32, 1024], P(('groups', 'expert')), parts along dimension 0, may hold values from -1 to 1
Outputs:
- in_grad: bfloat16 [4096, 3584], P(('groups', 'expert')), parts along dimension 0
- router_grad: float32 [7168, 16], P(('groups', 'expert')), parts along dimension 0
- grad_gate_a: float32 [32, 3584, 32], P(('groups', 'expert')), parts along dimension 0
- grad_gate_b: float32 [32, 32, 1024], P(('groups', 'expert')), parts along dimension 0
- grad_up_a: float32 [32, 3584, 32], P(('groups', 'expert')), parts along dimension 0
- grad_up_b: float32 [32, 32, 1024], P(('groups', 'expert')), parts along dimension 0
There are 2 independent parts, one for each index of `groups`. A program takes and returns all parts, laid end to end along the dimension named above; an argument that names none is the same for every part. Nothing has to cross between parts.
Inputs may be any that keep to these rules, and one draw needn't show every extreme that they name: `routed_expert_index`: within the 128 rows of one device no expert is named by more than 48 rows, and in every draw some expert is named by exactly 48 rows of some device; the 4 experts of a row differ.
All inputs are finite; a program needn't handle non-finite values.
Results may differ from a plain program's by a relative error of at most 0.0071.
Values may be sent and summed in bfloat16 or wider, within the bound.
No kernel may reach another device: no remote copies, remote signals or barrier semaphores. Data moves between devices by JAX's collectives and lax.ppermute only.
A program may use at most 192 MiB of HBM per device.

v0:
```python
import functools

import jax
import jax.numpy as jnp
from jax import lax
from jax.experimental import pallas as pl
from jax.experimental.pallas import tpu as pltpu
from jax.sharding import PartitionSpec as P

route_scale = 2.5
plane = 4
bf16 = jnp.bfloat16
f32 = jnp.float32
vmem_bytes = 56 * 1024 * 1024


def dot_nn(left, right):
    return jnp.dot(left, right, preferred_element_type=f32)


def dot_nt(left, right):
    return lax.dot_general(left, right, (((1,), (1,)), ((), ())), preferred_element_type=f32)


def dot_tn(left, right):
    return lax.dot_general(left, right, (((0,), (0,)), ((), ())), preferred_element_type=f32)


def after(array, *others):
    return lax.optimization_barrier((array, *others))[0]


def chunks(start, stop, step):
    return [(at, min(at + step, stop)) for at in range(start, stop, step)]


def whole_block(shape):
    return pl.BlockSpec(shape, lambda *_: (0,) * len(shape), pipeline_mode=pl.Buffered(1))


vmem = pl.BlockSpec(memory_space=pltpu.VMEM)
smem = pl.BlockSpec(memory_space=pltpu.SMEM)


def select_kernel(parts, meta_at, slots_held, cap, flag_ref, guide_ref, *refs):
    count = sum(len(p) for p in parts)
    ins, outs = refs[:count], refs[count:]
    tok = ins[0].shape[0]
    flag = flag_ref[0] == 1
    groups = []
    for part in parts:
        groups.append((part, ins[: len(part)]))
        ins = ins[len(part) :]

    def load(group, first, last):
        part, arrays = group
        values = [a[:, at + first : at + last] for (at, _), a in zip(part, arrays)]
        return values[0] if len(values) == 1 else jnp.where(flag, values[0], values[1])

    if slots_held:
        placed = guide_ref[...]
    else:
        meta = load(groups[0], *meta_at)
        named = dot_nt(guide_ref[...], meta)
        rank = lax.broadcasted_iota(jnp.int32, (cap, tok), 0).astype(f32) + 1.0
        placed = jnp.concatenate(
            [(named[p : p + 1, :] == rank).astype(bf16) for p in range(plane)], axis=0
        )
        outs[plane][...] = placed
    at = 0
    for group in groups:
        length = group[0][0][1]
        for first, last in chunks(0, length, 512):
            rows = dot_nn(placed, load(group, first, last)).astype(bf16)
            for p in range(plane):
                outs[p][:, at + first : at + last] = rows[p * cap : (p + 1) * cap]
        at += length


def select_rows(flag, guide, parts, arrays, meta_at, slots_held, cap):
    tok = arrays[0].shape[0]
    length = sum(p[0][1] for p in parts)
    shapes = [jax.ShapeDtypeStruct((cap, length), bf16)] * plane
    if not slots_held:
        shapes.append(jax.ShapeDtypeStruct((plane * cap, tok), bf16))
    return pl.pallas_call(
        functools.partial(select_kernel, parts, meta_at, slots_held, cap),
        out_shape=shapes,
        in_specs=[smem] + [vmem] * (1 + len(arrays)),
        out_specs=[vmem] * len(shapes),
        compiler_params=pltpu.CompilerParams(vmem_limit_bytes=vmem_bytes),
        cost_estimate=pl.CostEstimate(
            flops=2 * plane * cap * tok * length,
            bytes_accessed=2 * length * (tok + plane * cap),
            transcendentals=0,
        ),
    )(flag, guide, *arrays)


def sum_kernel(extra, cap, placed_ref, *refs):
    pieces, out = refs[:plane], refs[-1]
    for first, last in chunks(0, out.shape[1], 512):
        rows = jnp.concatenate([p[:, first:last] for p in pieces], axis=0)
        total = dot_tn(placed_ref[...], rows)
        for more in refs[plane : plane + extra]:
            total = total + more[:, first:last].astype(f32)
        out[:, first:last] = total.astype(bf16)


def sum_rows(placed, pieces, extra):
    cap, width = pieces[0].shape
    tok = placed.shape[1]
    return pl.pallas_call(
        functools.partial(sum_kernel, len(extra), cap),
        out_shape=jax.ShapeDtypeStruct((tok, width), bf16),
        in_specs=[vmem] * (1 + plane + len(extra)),
        out_specs=vmem,
        compiler_params=pltpu.CompilerParams(vmem_limit_bytes=vmem_bytes),
        cost_estimate=pl.CostEstimate(
            flops=2 * plane * cap * tok * width,
            bytes_accessed=2 * width * (2 * tok + plane * cap),
            transcendentals=0,
        ),
    )(placed, *pieces, *extra)


def expert_kernel(
    pieces, cap, width, rank, mine_ref, wg_ref, wu_ref, wd_ref, ag_ref, au_ref, bg_ref, bu_ref, *refs
):
    count = sum(len(p) for p in pieces)
    ins, refs = refs[:count], refs[count:]
    back_refs, refs = refs[: len(pieces)], refs[len(pieces) :]
    route_ref, ga_ref, gbg_ref, gbu_ref = refs[:4]
    xs, dys, weight, low, proj, both, acc = refs[4:]
    step = pl.program_id(0)
    tail = width + mine_ref.shape[1]

    @pl.when(step == 0)
    def _():
        left = ins
        for i, piece in enumerate(pieces):
            rows = slice(i * cap, (i + 1) * cap)
            x_ref, dy_ref = left[0], left[len(piece) - 1]
            left = left[len(piece) :]
            offset = tail if len(piece) == 1 else 0
            xs[rows, :] = x_ref[:, :width]
            dys[rows, :] = dy_ref[:, offset : offset + width]
            weight[rows, :] = jnp.sum(
                x_ref[:, width:tail].astype(f32) * mine_ref[...], axis=1, keepdims=True
            )
        both[:rank, :] = ag_ref[...]
        both[rank:, :] = au_ref[...]
        low[...] = dot_nt(xs[...], both[...]).astype(bf16)
        proj[...] = jnp.zeros_like(proj)
        acc[...] = jnp.zeros_like(acc)
        route_ref[...] = jnp.zeros_like(route_ref)

    bg, bu = bg_ref[...], bu_ref[...]
    low_gate, low_up = low[:, :rank], low[:, rank:]
    gate = dot_nn(xs[...], wg_ref[...]) + dot_nn(low_gate, bg)
    upval = dot_nn(xs[...], wu_ref[...]) + dot_nn(low_up, bu)
    back = dot_nt(dys[...], wd_ref[...])
    sigma = jax.nn.sigmoid(gate)
    act = gate * sigma
    route_ref[...] += jnp.sum(back * (act * upval), axis=1, keepdims=True)
    scaled = weight[...] * back
    d_gate = (scaled * upval * sigma * (1.0 + gate * (1.0 - sigma))).astype(bf16)
    d_up = (scaled * act).astype(bf16)
    gbg_ref[...] = dot_tn(low_gate, d_gate)
    gbu_ref[...] = dot_tn(low_up, d_up)
    proj[:, :rank] += dot_nt(d_gate, bg)
    proj[:, rank:] += dot_nt(d_up, bu)
    for first, last in chunks(0, width, 512):
        acc[:, first:last] += dot_nt(d_gate, wg_ref[first:last, :]) + dot_nt(
            d_up, wu_ref[first:last, :]
        )

    @pl.when(step == pl.num_programs(0) - 1)
    def _():
        proj_b = proj[...].astype(bf16)
        for first, last in chunks(0, width, 512):
            rows = (acc[:, first:last] + dot_nn(proj_b, both[:, first:last])).astype(bf16)
            for i, out in enumerate(back_refs):
                out[:, first:last] = rows[i * cap : (i + 1) * cap]
            ga_ref[:, first:last] = dot_tn(proj_b, xs[:, first:last])


def expert_rows(mine, mats, pieces):
    w_gate, w_up, w_down, a_gate, a_up, b_gate, b_up = mats
    width, hidden = w_gate.shape
    rank = a_gate.shape[0]
    cap = pieces[0][0].shape[0]
    rows = cap * len(pieces)
    tile = 256
    arrays = [a for piece in pieces for a in piece]
    return pl.pallas_call(
        functools.partial(expert_kernel, [(0,) * len(p) for p in pieces], cap, width, rank),
        grid=(hidden // tile,),
        in_specs=[
            whole_block(mine.shape),
            pl.BlockSpec((width, tile), lambda j: (0, j)),
            pl.BlockSpec((width, tile), lambda j: (0, j)),
            pl.BlockSpec((tile, width), lambda j: (j, 0)),
            whole_block(a_gate.shape),
            whole_block(a_up.shape),
            pl.BlockSpec((rank, tile), lambda j: (0, j)),
            pl.BlockSpec((rank, tile), lambda j: (0, j)),
        ]
        + [whole_block(a.shape) for a in arrays],
        out_shape=[jax.ShapeDtypeStruct((cap, width), bf16)] * len(pieces)
        + [
            jax.ShapeDtypeStruct((rows, 1), f32),
            jax.ShapeDtypeStruct((2 * rank, width), f32),
            jax.ShapeDtypeStruct((rank, hidden), f32),
            jax.ShapeDtypeStruct((rank, hidden), f32),
        ],
        out_specs=[whole_block((cap, width))] * len(pieces)
        + [
            whole_block((rows, 1)),
            whole_block((2 * rank, width)),
            pl.BlockSpec((rank, tile), lambda j: (0, j)),
            pl.BlockSpec((rank, tile), lambda j: (0, j)),
        ],
        scratch_shapes=[
            pltpu.VMEM((rows, width), bf16),
            pltpu.VMEM((rows, width), bf16),
            pltpu.VMEM((rows, 1), f32),
            pltpu.VMEM((rows, 2 * rank), bf16),
            pltpu.VMEM((rows, 2 * rank), f32),
            pltpu.VMEM((2 * rank, width), bf16),
            pltpu.VMEM((rows, width), f32),
        ],
        compiler_params=pltpu.CompilerParams(vmem_limit_bytes=vmem_bytes),
        cost_estimate=pl.CostEstimate(
            flops=2 * 5 * rows * width * hidden,
            bytes_accessed=2 * 3 * width * hidden + 6 * rows * width,
            transcendentals=rows * hidden,
        ),
    )(mine, w_gate, w_up, w_down, a_gate, a_up, b_gate, b_up, *arrays)


def solution(mesh):
    devices = mesh.shape["expert"]
    layers = devices // plane

    def along(pairs):
        return [(a * plane + q, b * plane + q) for a, b in pairs for q in range(plane)]

    def across(step):
        return [(i, i ^ step) for i in range(devices)]

    def send(array, pairs):
        return lax.ppermute(array, "expert", pairs)

    def spread(pieces):
        return [pieces[0]] + [send(pieces[p], across(p)) for p in range(1, plane)]

    def shards(
        layer_input,
        output_gradient,
        router_matrix,
        routed_expert_index,
        gate_weight_frozen,
        up_weight_frozen,
        down_weight_frozen,
        gate_adapter_first,
        gate_adapter_second,
        up_adapter_first,
        up_adapter_second,
    ):
        tok, width = layer_input.shape
        topk = routed_expert_index.shape[1]
        experts = router_matrix.shape[1]
        capacity = 3 * tok * topk // (2 * experts)
        cap = -(-capacity // 16) * 16
        me = lax.axis_index("expert")
        layer = me // plane
        place = me % plane
        mats = (
            gate_weight_frozen[0],
            up_weight_frozen[0],
            down_weight_frozen[0],
            gate_adapter_first[0].T,
            up_adapter_first[0].T,
            gate_adapter_second[0],
            up_adapter_second[0],
        )
        dy = output_gradient

        scores = jax.nn.sigmoid(dot_nn(layer_input, router_matrix))
        expert_ids = jnp.arange(experts, dtype=jnp.int32)
        mask = jnp.sum(
            (routed_expert_index[:, :, None] == expert_ids[None, None, :]).astype(f32), axis=1
        )
        picked = mask * scores
        total = jnp.sum(picked, axis=1, keepdims=True)
        combine = (route_scale * picked / total).astype(bf16)
        earlier = (jnp.arange(tok)[:, None] > jnp.arange(tok)[None, :]).astype(bf16)
        slot_dense = mask * (dot_nn(earlier, mask.astype(bf16)) + 1.0)
        meta_width = -(-2 * experts // 128) * 128
        meta = jnp.concatenate(
            [slot_dense.astype(bf16), combine, jnp.zeros((tok, meta_width - 2 * experts), bf16)],
            axis=1,
        )
        x_ext = jnp.concatenate([layer_input, meta], axis=1)
        own = jnp.concatenate([x_ext, dy], axis=1)
        ext = width + meta_width
        full = ext + width
        meta_at = (width, ext)

        here = layer * plane + (place ^ jnp.arange(plane, dtype=jnp.int32))
        guide = jnp.zeros((16, meta_width), bf16)
        guide = guide.at[:plane].set(
            (here[:, None] == jnp.arange(meta_width, dtype=jnp.int32)[None, :]).astype(bf16)
        )
        mine = (jnp.arange(meta_width) == experts + me).astype(f32)[None, :]
        take = functools.partial(select_rows, cap=cap)

        if layers == 4:
            mid = (layer == 1) | (layer == 2)
            flag = mid.astype(jnp.int32)[None]
            ends_in = along([(1, 0), (2, 3)])
            second = along([(0, 2), (3, 1), (1, 0), (2, 3)])
            dy_2 = send(dy, second)
            x_2 = send(x_ext, second)
            *sel_0, placed_0 = take(flag, guide, [[(0, full)]], [own], meta_at, False)
            got_0 = spread(sel_0)
            own_3 = after(own, x_2, dy_2)
            onward = jnp.where(mid, jnp.concatenate([x_2, dy_2], axis=1), own)
            block_2 = send(onward, across(plane))
            block_3 = send(own_3, along([(1, 2), (2, 1)]))
            *sel_1, placed_1 = take(
                flag, guide, [[(0, ext)], [(0, width)]], [x_2, dy_2], meta_at, False
            )
            sel_1 = lax.optimization_barrier((*sel_1, *got_0))[:plane]
            got_1 = spread(sel_1)
            x_5, dy_5, _, _ = lax.optimization_barrier((x_ext, dy, block_2, block_3))
            x_3 = send(x_5, along([(1, 3), (2, 0)]))
            dy_3 = send(dy_5, along([(1, 3), (2, 0)]))
            *sel_2, placed_2 = take(flag, guide, [[(0, full)]], [block_2], meta_at, False)
            sel_2 = lax.optimization_barrier((*sel_2, *got_1))[:plane]
            got_2 = spread(sel_2)
            early = lax.optimization_barrier((*got_0, *got_1, sel_2[0]))[: 2 * plane]
            done_01 = expert_rows(mine, mats, [(a,) for a in early])
            back_0 = spread(done_01[:plane])
            back_1 = spread(done_01[plane : 2 * plane])
            done_2 = expert_rows(mine, mats, [(a,) for a in got_2])
            *sel_3x, placed_3 = take(
                flag, guide, [[(0, ext), (0, ext)]], [block_3, x_3], meta_at, False
            )
            sel_3y = take(flag, placed_3, [[(ext, width), (0, width)]], [block_3, dy_3], None, True)
            got_3x = spread(sel_3x)
            got_3y = spread(sel_3y)
            done_3 = expert_rows(mine, mats, list(zip(got_3x, got_3y)))
            back_2 = spread(done_2[:plane])
            back_3 = spread(done_3[:plane])

            part_0 = sum_rows(placed_0, back_0, [])
            part_1 = sum_rows(placed_1, back_1, [])
            term_1 = send(part_1, along([(0, 1), (3, 2)]))
            part_2 = sum_rows(placed_2, back_2, [])
            term_2 = send(part_2, across(plane))
            joined = (part_1.astype(f32) + term_2.astype(f32)).astype(bf16)
            term_3 = send(joined, along([(1, 3), (2, 0)]))
            part_3 = sum_rows(placed_3, back_3, [])
            term_4 = send(part_3, along([(1, 2), (2, 1)]))
            term_5 = send(part_3, along([(0, 2), (3, 1)]))
            terms = [part_0, term_1, jnp.where(mid, jnp.zeros((), bf16), term_2), term_3, term_4, term_5]
            done = [done_01, done_2, done_3]
            counts = [2, 1, 1]
            sources = [
                layer,
                jnp.where(mid, layer ^ 2, layer ^ 1),
                jnp.where(mid, layer ^ 1, layer ^ 3),
                jnp.where(mid, layer ^ 3, layer ^ 2),
            ]
        else:
            flag = jnp.zeros((1,), jnp.int32)
            done, counts, sources, terms = [], [], [], []
            for g in range(layers):
                block = own if g == 0 else send(own, across(g * plane))
                *sel, placed = take(flag, guide, [[(0, full)]], [block], meta_at, False)
                result = expert_rows(mine, mats, [(a,) for a in spread(sel)])
                part = sum_rows(placed, spread(result[:plane]), [])
                terms.append(part if g == 0 else send(part, across(g * plane)))
                done.append(result)
                counts.append(1)
                sources.append(layer ^ g)

        route_all = jnp.concatenate(
            [d[c * plane].reshape(c * plane, cap) for d, c in zip(done, counts)], axis=0
        )
        origin = (
            jnp.stack(sources)[:, None] * plane
            + (place ^ jnp.arange(plane, dtype=jnp.int32))[None, :]
        ).reshape(-1)
        order = (origin[None, :] == jnp.arange(devices, dtype=jnp.int32)[:, None]).astype(bf16)
        route_sorted = dot_nn(order, route_all.astype(bf16)).astype(bf16)
        ret_route = lax.all_to_all(
            route_sorted, "expert", split_axis=0, concat_axis=0, tiled=True
        ).astype(f32)
        slots = jnp.arange(1, cap + 1, dtype=jnp.int32).astype(f32)
        hit = slot_dense[:, :, None] == slots[None, None, :]
        route_grad = jnp.sum(jnp.where(hit, ret_route[None, :, :], 0.0), axis=2)
        shared = jnp.sum(route_grad * picked, axis=1, keepdims=True) / (total * total)
        d_pick = route_scale * (route_grad / total - shared)
        d_logit = (mask * d_pick * scores * (1.0 - scores)).astype(bf16)

        router_part = dot_tn(d_logit, layer_input)
        share = width // devices
        router_part = router_part.reshape(experts, devices, share).transpose(1, 0, 2)
        router_got = lax.all_to_all(router_part, "expert", split_axis=0, concat_axis=0, tiled=True)
        router_grad = jnp.sum(router_got, axis=0).T

        in_grad = dot_nt(d_logit, router_matrix)
        for term in terms:
            in_grad = in_grad + term.astype(f32)
        in_grad = in_grad.astype(bf16)

        rank = gate_adapter_second.shape[1]
        grad_a = sum(d[c * plane + 1] for d, c in zip(done, counts))
        grad_gate_b = sum(d[c * plane + 2] for d, c in zip(done, counts))
        grad_up_b = sum(d[c * plane + 3] for d, c in zip(done, counts))
        return (
            in_grad,
            router_grad,
            grad_a[:rank].T[None],
            grad_gate_b[None],
            grad_a[rank:].T[None],
            grad_up_b[None],
        )

    rows = P(("groups", "expert"), None)
    stack = P(("groups", "expert"), None, None)
    frozen = P("expert", None, None)
    in_specs = (rows, rows, P(), rows, frozen, frozen, frozen, stack, stack, stack, stack)
    out_specs = (rows, rows, stack, stack, stack, stack)
    return jax.shard_map(shards, mesh=mesh, in_specs=in_specs, out_specs=out_specs, check_vma=False)
```

profile of v0, /device:TPU:15, one launch (start us, length us, event | category | flops | bytes accessed | tf_op | source)
XLA Modules:
  0.0 368.2 jit_solution(1752703081424047546)
XLA Ops:
  1.7 1.6 fusion.13
  4.8 2.3 collective-permute-start.4
  7.1 2.2 concatenate.20.refs_0_
  9.4 38.0 %collective-permute-done.4.refs_1_ = bf16[128,3584]{1,0:T(8,128)(2,1)} collective-permute-done((bf16[128,3584]{1,0:T(8,128)(2,1)}, bf16[128,3584]{1,0:T(8,128)(2,1)}, u32[]{:S(2)}, u32[]{:S(2)}) %collective-permute-start.4) | collective-permute-done | bytes 917536 | tf_op jit(solution)/shard_map/ppermute | solution.py:253
  47.4 3.2 collective-permute-start.12
  50.6 3.2 maximum_select_fusion
  54.5 4.1 %shard_map.154 = (bf16[48,7296]{1,0:T(8,128)(2,1)}, bf16[48,7296]{1,0:T(8,128)(2,1)}, bf16[48,7296]{1,0:T(8,128)(2,1)}, bf16[48,7296]{1,0:T(8,128)(2,1)}, bf16[192,128]{1,0:T(8,128)(2,1)}) custom-call(s32[1]{0:T(128)} %bitcast.13.flag_ref, bf16[16,128]{1,0:T(8,128)(2,1)} %pad_convert_fusion.guide_ref, bf16[128,7296]{1,0:T(8,128)(2,1)} %copy-done.1), custom_call_target="tpu_custom_call" | custom-call | flops 358612992 | bytes 4669440 | tf_op jit(solution)/shard_map/pallas_call | solution.py:86
  58.6 1.8 collective-permute-start
  62.0 4.0 %shard_map.155 = (bf16[48,7296]{1,0:T(8,128)(2,1)}, bf16[48,7296]{1,0:T(8,128)(2,1)}, bf16[48,7296]{1,0:T(8,128)(2,1)}, bf16[48,7296]{1,0:T(8,128)(2,1)}, bf16[192,128]{1,0:T(8,128)(2,1)}) custom-call(s32[1]{0:T(128)} %bitcast.13.flag_ref, bf16[16,128]{1,0:T(8,128)(2,1)} %pad_convert_fusion.guide_ref, bf16[128,3712]{1,0:T(8,128)(2,1)} %collective-permute-done.3.refs_0_, ...), custom_call_target="tpu_custom_call" | custom-call | flops 358612992 | bytes 4669440 | tf_op jit(solution)/shard_map/pallas_call | solution.py:86
  66.0 12.0 %collective-permute-done.1.refs_2_ = bf16[48,7296]{1,0:T(8,128)(2,1)} collective-permute-done((bf16[48,7296]{1,0:T(8,128)(2,1)}, bf16[48,7296]{1,0:T(8,128)(2,1)}, u32[]{:S(2)}, u32[]{:S(2)}) %collective-permute-start.1) | collective-permute-done | bytes 700448 | tf_op jit(solution)/shard_map/ppermute | solution.py:253
  78.0 15.4 %collective-permute-done.2.refs_3_ = bf16[48,7296]{1,0:T(8,128)(2,1)} collective-permute-done((bf16[48,7296]{1,0:T(8,128)(2,1)}, bf16[48,7296]{1,0:T(8,128)(2,1)}, u32[]{:S(2)}, u32[]{:S(2)}) %collective-permute-start.2) | collective-permute-done | bytes 700448 | tf_op jit(solution)/shard_map/ppermute | solution.py:253
  93.7 1.9 collective-permute-start.7
  96.2 3.6 collective-permute-start.13
  99.8 1.5 collective-permute-start.14
  101.3 4.1 %shard_map.156 = (bf16[48,7296]{1,0:T(8,128)(2,1)}, bf16[48,7296]{1,0:T(8,128)(2,1)}, bf16[48,7296]{1,0:T(8,128)(2,1)}, bf16[48,7296]{1,0:T(8,128)(2,1)}, bf16[192,128]{1,0:T(8,128)(2,1)}) custom-call(s32[1]{0:T(128)} %bitcast.13.flag_ref, bf16[16,128]{1,0:T(8,128)(2,1)} %pad_convert_fusion.guide_ref, bf16[128,7296]{1,0:T(8,128)(2,1)} %collective-permute-done.8.refs_0_), custom_call_target="tpu_custom_call" | custom-call | flops 358612992 | bytes 4669440 | tf_op jit(solution)/shard_map/pallas_call | solution.py:86
  105.4 5.1 %collective-permute-done.6.refs_6_ = bf16[48,7296]{1,0:T(8,128)(2,1)} collective-permute-done((bf16[48,7296]{1,0:T(8,128)(2,1)}, bf16[48,7296]{1,0:T(8,128)(2,1)}, u32[]{:S(2)}, u32[]{:S(2)}) %collective-permute-start.6) | collective-permute-done | bytes 700448 | tf_op jit(solution)/shard_map/ppermute | solution.py:253
  110.5 15.7 %collective-permute-done.7.refs_7_ = bf16[48,7296]{1,0:T(8,128)(2,1)} collective-permute-done((bf16[48,7296]{1,0:T(8,128)(2,1)}, bf16[48,7296]{1,0:T(8,128)(2,1)}, u32[]{:S(2)}, u32[]{:S(2)}) %collective-permute-start.7) | collective-permute-done | bytes 700448 | tf_op jit(solution)/shard_map/ppermute | solution.py:253
  126.4 1.9 collective-permute-start.11
  128.3 31.7 %shard_map.157 = (bf16[48,3584]{1,0:T(8,128)(2,1)}, bf16[48,3584]{1,0:T(8,128)(2,1)}, bf16[48,3584]{1,0:T(8,128)(2,1)}, bf16[48,3584]{1,0:T(8,128)(2,1)}, bf16[4...) custom-call(f32[1,128]{1,0:T(1,128)} %compare_convert_fusion.mine_re, ...), custom_call_target="tpu_custom_call" | custom-call | flops 14092861440 | bytes 30277632 | tf_op jit(solution)/shard_map/pallas_call | solution.py:196
  160.5 1.8 collective-permute-start.26
  162.6 21.8 %shard_map.158 = (bf16[48,3584]{1,0:T(8,128)(2,1)}, bf16[48,3584]{1,0:T(8,128)(2,1)}, bf16[48,3584]{1,0:T(8,128)(2,1)}, bf16[48,3584]{1,0:T(8,128)(2,1)}, f32[19...) custom-call(f32[1,128]{1,0:T(1,128)} %compare_convert_fusion.mine_ref, ...), custom_call_target="tpu_custom_call" | custom-call | flops 7046430720 | bytes 26148864 | tf_op jit(solution)/shard_map/pallas_call | solution.py:196
  184.5 3.5 shard_map.159
  188.0 3.4 shard_map.160
  191.4 1.6 collective-permute-start.23
  193.3 1.8 collective-permute-start.30
  195.4 6.7 %collective-permute-done.23.refs_3_ = bf16[48,3584]{1,0:T(8,128)(2,1)} collective-permute-done((bf16[48,3584]{1,0:T(8,128)(2,1)}, bf16[48,3584]{1,0:T(8,128)(2,1)}, u32[]{:S(2)}, u32[]{:S(2)}) %collective-permute-start.23) | collective-permute-done | bytes 344096 | tf_op jit(solution)/shard_map/ppermute | solution.py:253
  202.2 1.5 collective-permute-start.17
  203.7 5.4 %collective-permute-done.29.refs_2_ = bf16[48,3584]{1,0:T(8,128)(2,1)} collective-permute-done((bf16[48,3584]{1,0:T(8,128)(2,1)}, bf16[48,3584]{1,0:T(8,128)(2,1)}, u32[]{:S(2)}, u32[]{:S(2)}) %collective-permute-start.29) | collective-permute-done | bytes 344096 | tf_op jit(solution)/shard_map/ppermute | solution.py:253
  210.6 6.2 %collective-permute-done.30.refs_3_ = bf16[48,3584]{1,0:T(8,128)(2,1)} collective-permute-done((bf16[48,3584]{1,0:T(8,128)(2,1)}, bf16[48,3584]{1,0:T(8,128)(2,1)}, u32[]{:S(2)}, u32[]{:S(2)}) %collective-permute-start.30) | collective-permute-done | bytes 344096 | tf_op jit(solution)/shard_map/ppermute | solution.py:253
  216.8 1.6 collective-permute-start.19
  219.8 2.7 shard_map.163
  222.5 2.7 shard_map.162
  225.4 2.7 shard_map.164
  228.1 3.5 collective-permute-done.18.refs_5_
  232.8 14.0 %collective-permute-done.20.refs_7_ = bf16[48,3584]{1,0:T(8,128)(2,1)} collective-permute-done((bf16[48,3584]{1,0:T(8,128)(2,1)}, bf16[48,3584]{1,0:T(8,128)(2,1)}, u32[]{:S(2)}, u32[]{:S(2)}) %collective-permute-start.20) | collective-permute-done | bytes 344096 | tf_op jit(solution)/shard_map/ppermute | solution.py:253
  246.8 1.7 collective-permute-start.31
  248.5 21.6 %shard_map.161 = (bf16[48,3584]{1,0:T(8,128)(2,1)}, bf16[48,3584]{1,0:T(8,128)(2,1)}, bf16[48,3584]{1,0:T(8,128)(2,1)}, bf16[48,3584]{1,0:T(8,128)(2,1)}, f32[19...) custom-call(f32[1,128]{1,0:T(1,128)} %compare_convert_fusion.mine_ref, ...), custom_call_target="tpu_custom_call" | custom-call | flops 7046430720 | bytes 26148864 | tf_op jit(solution)/shard_map/pallas_call | solution.py:196
  270.9 1.5 collective-permute-start.34
  274.4 4.3 %all-to-all-start = ((bf16[16,1,48]{2,1,0:T(2,128)(2,1)}), bf16[16,1,48]{2,1,0:T(2,128)(2,1)S(1)}, u32[]{:S(2)}, u32[]{:S(2)}) async-start(bf16[16,1,48]{2,1,0:T(2,128)(2,1)} %copy.49), calls=%async_computation | async-start | bytes 16384 | tf_op jit(solution)/shard_map/all_to_all | solution.py:399
  278.8 1.6 add_add_fusion
  281.4 7.1 %all-to-all-done = bf16[16,1,48]{2,1,0:T(2,128)(2,1)S(1)} async-done(((bf16[16,1,48]{2,1,0:T(2,128)(2,1)}), bf16[16,1,48]{2,1,0:T(2,128)(2,1)S(1)}, u32[]{:S(2)}, u32[]{:S(2)}) %all-to-all-start) | async-done | bytes 1568 | tf_op jit(solution)/shard_map/all_to_all | solution.py:399
  289.8 2.7 shard_map.165
  293.7 2.1 collective-permute-start.36
  295.8 2.6 add_convert_fusion.1
  298.5 6.4 %collective-permute-start.32 = (bf16[128,3584]{1,0:T(8,128)(2,1)}, bf16[128,3584]{1,0:T(8,128)(2,1)}, u32[]{:S(2)}, u32[]{:S(2)}) collective-permute-start(bf16[128,3584]{1,0:T(8,128)(2,1)} %add_convert_fusion.1), channel_id=1, source_target_pairs={{4,12},{5,13},{6,14},{7,15},{8,0},{9,1},{10,2},{11,3},{20,28},{21,... | collective-permute-start | bytes 2752520 | tf_op jit(solution)/shard_map/ppermute | solution.py:253
  306.3 5.4 %all-to-all-start.1 = ((f32[16,16,224]{2,1,0:T(8,128)}), f32[16,16,224]{2,1,0:T(8,128)S(1)}, u32[]{:S(2)}, u32[]{:S(2)}) async-start(f32[16,16,224]{2,1,0:T(8,128)} %bitcast.40), calls=%async_computation.1 | async-start | bytes 524288 | tf_op jit(solution)/shard_map/all_to_all | solution.py:412
  312.8 51.0 %all-to-all-done.1 = f32[16,16,224]{2,1,0:T(8,128)S(1)} async-done(((f32[16,16,224]{2,1,0:T(8,128)}), f32[16,16,224]{2,1,0:T(8,128)S(1)}, u32[]{:S(2)}, u32[]{:S(2)}) %all-to-all-start.1) | async-done | bytes 229408 | tf_op jit(solution)/shard_map/all_to_all | solution.py:412
  364.5 3.7 %add_convert_fusion = bf16[128,3584]{1,0:T(8,128)(2,1)} fusion(bf16[128,3584]{1,0:T(8,128)(2,1)} %collective-permute-done.37, bf16[128,3584]{1,0:T(8,128)(2,1)} %collective-permute-done.36, bf16[128,3584]{1,0:T(8,128)(2,1)} %collective-permute-done.32, bf16[128,3584]{1,0:T(8,128)(2,1)} %collective-permute-done.27, f32[128,3584]{1,0:T(8,128)S(1)} %fusion.15, ...), kind=kLoop, calls=%fused_computation.1 | loop fusion | flops 6422528 | bytes 8257537 | tf_op jit(solution)/shard_map/convert_element_type | solution.py:418
  (139 shorter events, 21.1 us)
Async XLA Ops:
  4.7 42.8 %collective-permute-start.3 = (bf16[128,3712]{1,0:T(8,128)(2,1)}, bf16[128,3712]{1,0:T(8,128)(2,1)}, u32[]{:S(2)}, u32[]{:S(2)}) collective-permute-start(bf16[128,3712]{1,0:T(8,128)(2,1)} %concatenate.21), channel_id=1, source_target_pairs={{0,8},{1,9},{2,10},{3,11},{12,4},{13,5},{14,6},{15,7},{4,0},{5,1},... | collective-permute-start | bytes 2850824 | tf_op jit(solution)/shard_map/ppermute | solution.py:253
  4.8 42.6 %collective-permute-start.4 = (bf16[128,3584]{1,0:T(8,128)(2,1)}, bf16[128,3584]{1,0:T(8,128)(2,1)}, u32[]{:S(2)}, u32[]{:S(2)}) collective-permute-start(bf16[128,3584]{1,0:T(8,128)(2,1)} %param.14), channel_id=1, source_target_pairs={{0,8},{1,9},{2,10},{3,11},{12,4},{13,5},{14,6},{15,7},{4,0},{5,1},... | collective-permute-start | bytes 2752520 | tf_op jit(solution)/shard_map/ppermute | solution.py:253
  9.4 44.4 %copy-start.1 = (bf16[128,7296]{1,0:T(8,128)(2,1)}, bf16[128,7296]{1,0:T(8,128)(2,1)S(1)}, u32[]{:S(2)}) copy-start(bf16[128,7296]{1,0:T(8,128)(2,1)S(1)} %concatenate.20.refs_0_) | copy-start | bytes 5603332
  47.4 48.7 %collective-permute-start.12 = (bf16[128,7296]{1,0:T(8,128)(2,1)S(1)}, bf16[128,7296]{1,0:T(8,128)(2,1)}, u32[]{:S(2)}, u32[]{:S(2)}) collective-permute-start(bf16[128,7296]{1,0:T(8,128)(2,1)S(1)} %concatenate.20.refs_0_), channel_id=1, source_target_pairs={{4,8},{5,9},{6,10},{7,11},{8,4},{9,5},{10,6},{11,7},{20,24},{21,25... | collective-permute-start | bytes 5603336 | tf_op jit(solution)/shard_map/ppermute | solution.py:253
  53.8 42.4 %collective-permute-start.8 = (bf16[128,7296]{1,0:T(8,128)(2,1)}, bf16[128,7296]{1,0:T(8,128)(2,1)}, u32[]{:S(2)}, u32[]{:S(2)}) collective-permute-start(bf16[128,7296]{1,0:T(8,128)(2,1)} %maximum_select_fusion), channel_id=1, source_target_pairs={{0,4},{1,5},{2,6},{3,7},{4,0},{5,1},{6,2},{7,3},{8,12},{9,13},{10,... | collective-permute-start | bytes 5603336 | tf_op jit(solution)/shard_map/ppermute | solution.py:253
  58.6 7.5 %collective-permute-start = (bf16[48,7296]{1,0:T(8,128)(2,1)}, bf16[48,7296]{1,0:T(8,128)(2,1)}, u32[]{:S(2)}, u32[]{:S(2)}) collective-permute-start(bf16[48,7296]{1,0:T(8,128)(2,1)} %get-tuple-element.90), channel_id=1, source_target_pairs={{0,1},{1,0},{2,3},{3,2},{4,5},{5,4},{6,7},{7,6},{8,9},{9,8},{10,11... | collective-permute-start | bytes 2101256 | tf_op jit(solution)/shard_map/ppermute | solution.py:253
  60.4 17.6 %collective-permute-start.1 = (bf16[48,7296]{1,0:T(8,128)(2,1)}, bf16[48,7296]{1,0:T(8,128)(2,1)}, u32[]{:S(2)}, u32[]{:S(2)}) collective-permute-start(bf16[48,7296]{1,0:T(8,128)(2,1)} %get-tuple-element.91), channel_id=1, source_target_pairs={{0,2},{1,3},{2,0},{3,1},{4,6},{5,7},{6,4},{7,5},{8,10},{9,11},{10,... | collective-permute-start | bytes 2101256 | tf_op jit(solution)/shard_map/ppermute | solution.py:253
  60.6 32.8 %collective-permute-start.2 = (bf16[48,7296]{1,0:T(8,128)(2,1)}, bf16[48,7296]{1,0:T(8,128)(2,1)}, u32[]{:S(2)}, u32[]{:S(2)}) collective-permute-start(bf16[48,7296]{1,0:T(8,128)(2,1)} %get-tuple-element.92), channel_id=1, source_target_pairs={{0,3},{1,2},{2,1},{3,0},{4,7},{5,6},{6,5},{7,4},{8,11},{9,10},{10,... | collective-permute-start | bytes 2101256 | tf_op jit(solution)/shard_map/ppermute | solution.py:253
  93.4 11.9 %collective-permute-start.5 = (bf16[48,7296]{1,0:T(8,128)(2,1)}, bf16[48,7296]{1,0:T(8,128)(2,1)}, u32[]{:S(2)}, u32[]{:S(2)}) collective-permute-start(bf16[48,7296]{1,0:T(8,128)(2,1)} %get-tuple-element.98), channel_id=1, source_target_pairs={{0,1},{1,0},{2,3},{3,2},{4,5},{5,4},{6,7},{7,6},{8,9},{9,8},{10,11... | collective-permute-start | bytes 2101256 | tf_op jit(solution)/shard_map/ppermute | solution.py:253
  93.4 17.1 %collective-permute-start.6 = (bf16[48,7296]{1,0:T(8,128)(2,1)}, bf16[48,7296]{1,0:T(8,128)(2,1)}, u32[]{:S(2)}, u32[]{:S(2)}) collective-permute-start(bf16[48,7296]{1,0:T(8,128)(2,1)} %get-tuple-element.99), channel_id=1, source_target_pairs={{0,2},{1,3},{2,0},{3,1},{4,6},{5,7},{6,4},{7,5},{8,10},{9,11},{10,... | collective-permute-start | bytes 2101256 | tf_op jit(solution)/shard_map/ppermute | solution.py:253
  93.7 32.5 %collective-permute-start.7 = (bf16[48,7296]{1,0:T(8,128)(2,1)}, bf16[48,7296]{1,0:T(8,128)(2,1)}, u32[]{:S(2)}, u32[]{:S(2)}) collective-permute-start(bf16[48,7296]{1,0:T(8,128)(2,1)} %get-tuple-element.100), channel_id=1, source_target_pairs={{0,3},{1,2},{2,1},{3,0},{4,7},{5,6},{6,5},{7,4},{8,11},{9,10},{10,... | collective-permute-start | bytes 2101256 | tf_op jit(solution)/shard_map/ppermute | solution.py:253
  96.2 66.1 %collective-permute-start.13 = (bf16[128,3712]{1,0:T(8,128)(2,1)}, bf16[128,3712]{1,0:T(8,128)(2,1)S(1)}, u32[]{:S(2)}, u32[]{:S(2)}) collective-permute-start(bf16[128,3712]{1,0:T(8,128)(2,1)} %concatenate.21), channel_id=1, source_target_pairs={{4,12},{5,13},{6,14},{7,15},{8,0},{9,1},{10,2},{11,3},{20,28},{21,... | collective-permute-start | bytes 2850824 | tf_op jit(solution)/shard_map/ppermute | solution.py:253
  99.8 62.5 %collective-permute-start.14 = (bf16[128,3584]{1,0:T(8,128)(2,1)}, bf16[128,3584]{1,0:T(8,128)(2,1)S(1)}, u32[]{:S(2)}, u32[]{:S(2)}) collective-permute-start(bf16[128,3584]{1,0:T(8,128)(2,1)} %param.14), channel_id=1, source_target_pairs={{4,12},{5,13},{6,14},{7,15},{8,0},{9,1},{10,2},{11,3},{20,28},{21,... | collective-permute-start | bytes 2752520 | tf_op jit(solution)/shard_map/ppermute | solution.py:253
  126.2 33.9 %collective-permute-start.9 = (bf16[48,7296]{1,0:T(8,128)(2,1)}, bf16[48,7296]{1,0:T(8,128)(2,1)S(1)}, u32[]{:S(2)}, u32[]{:S(2)}) collective-permute-start(bf16[48,7296]{1,0:T(8,128)(2,1)} %get-tuple-element.115), channel_id=1, source_target_pairs={{0,1},{1,0},{2,3},{3,2},{4,5},{5,4},{6,7},{7,6},{8,9},{9,8},{10,11... | collective-permute-start | bytes 2101256 | tf_op jit(solution)/shard_map/ppermute | solution.py:253
  126.2 34.0 %collective-permute-start.10 = (bf16[48,7296]{1,0:T(8,128)(2,1)}, bf16[48,7296]{1,0:T(8,128)(2,1)S(1)}, u32[]{:S(2)}, u32[]{:S(2)}) collective-permute-start(bf16[48,7296]{1,0:T(8,128)(2,1)} %get-tuple-element.116), channel_id=1, source_target_pairs={{0,2},{1,3},{2,0},{3,1},{4,6},{5,7},{6,4},{7,5},{8,10},{9,11},{10,... | collective-permute-start | bytes 2101256 | tf_op jit(solution)/shard_map/ppermute | solution.py:253
  126.4 34.0 %collective-permute-start.11 = (bf16[48,7296]{1,0:T(8,128)(2,1)}, bf16[48,7296]{1,0:T(8,128)(2,1)S(1)}, u32[]{:S(2)}, u32[]{:S(2)}) collective-permute-start(bf16[48,7296]{1,0:T(8,128)(2,1)} %get-tuple-element.117), channel_id=1, source_target_pairs={{0,3},{1,2},{2,1},{3,0},{4,7},{5,6},{6,5},{7,4},{8,11},{9,10},{10,... | collective-permute-start | bytes 2101256 | tf_op jit(solution)/shard_map/ppermute | solution.py:253
  160.1 31.3 %collective-permute-start.24 = (bf16[48,3584]{1,0:T(8,128)(2,1)}, bf16[48,3584]{1,0:T(8,128)(2,1)S(1)}, u32[]{:S(2)}, u32[]{:S(2)}) collective-permute-start(bf16[48,3584]{1,0:T(8,128)(2,1)} %get-tuple-element.139), channel_id=1, source_target_pairs={{0,1},{1,0},{2,3},{3,2},{4,5},{5,4},{6,7},{7,6},{8,9},{9,8},{10,11... | collective-permute-start | bytes 1032200 | tf_op jit(solution)/shard_map/ppermute | solution.py:253
  160.2 32.7 %collective-permute-start.25 = (bf16[48,3584]{1,0:T(8,128)(2,1)}, bf16[48,3584]{1,0:T(8,128)(2,1)S(1)}, u32[]{:S(2)}, u32[]{:S(2)}) collective-permute-start(bf16[48,3584]{1,0:T(8,128)(2,1)} %get-tuple-element.140), channel_id=1, source_target_pairs={{0,2},{1,3},{2,0},{3,1},{4,6},{5,7},{6,4},{7,5},{8,10},{9,11},{10,... | collective-permute-start | bytes 1032200 | tf_op jit(solution)/shard_map/ppermute | solution.py:253
  160.5 32.5 %collective-permute-start.26 = (bf16[48,3584]{1,0:T(8,128)(2,1)}, bf16[48,3584]{1,0:T(8,128)(2,1)S(1)}, u32[]{:S(2)}, u32[]{:S(2)}) collective-permute-start(bf16[48,3584]{1,0:T(8,128)(2,1)} %get-tuple-element.141), channel_id=1, source_target_pairs={{0,3},{1,2},{2,1},{3,0},{4,7},{5,6},{6,5},{7,4},{8,11},{9,10},{10,... | collective-permute-start | bytes 1032200 | tf_op jit(solution)/shard_map/ppermute | solution.py:253
  162.3 31.0 %collective-permute-start.21 = (bf16[48,3584]{1,0:T(8,128)(2,1)}, bf16[48,3584]{1,0:T(8,128)(2,1)S(1)}, u32[]{:S(2)}, u32[]{:S(2)}) collective-permute-start(bf16[48,3584]{1,0:T(8,128)(2,1)} %get-tuple-element.134), channel_id=1, source_target_pairs={{0,1},{1,0},{2,3},{3,2},{4,5},{5,4},{6,7},{7,6},{8,9},{9,8},{10,11... | collective-permute-start | bytes 1032200 | tf_op jit(solution)/shard_map/ppermute | solution.py:253
  162.3 32.8 %collective-permute-start.22 = (bf16[48,3584]{1,0:T(8,128)(2,1)}, bf16[48,3584]{1,0:T(8,128)(2,1)S(1)}, u32[]{:S(2)}, u32[]{:S(2)}) collective-permute-start(bf16[48,3584]{1,0:T(8,128)(2,1)} %get-tuple-element.135), channel_id=1, source_target_pairs={{0,2},{1,3},{2,0},{3,1},{4,6},{5,7},{6,4},{7,5},{8,10},{9,11},{10,... | collective-permute-start | bytes 1032200 | tf_op jit(solution)/shard_map/ppermute | solution.py:253
  191.4 28.4 %copy-start.8 = (bf16[48,3584]{1,0:T(8,128)(2,1)}, bf16[48,3584]{1,0:T(8,128)(2,1)S(1)}, u32[]{:S(2)}) copy-start(bf16[48,3584]{1,0:T(8,128)(2,1)S(1)} %collective-permute-done.24.refs_1_) | copy-start | bytes 1032196
  191.4 10.7 %collective-permute-start.23 = (bf16[48,3584]{1,0:T(8,128)(2,1)}, bf16[48,3584]{1,0:T(8,128)(2,1)}, u32[]{:S(2)}, u32[]{:S(2)}) collective-permute-start(bf16[48,3584]{1,0:T(8,128)(2,1)} %get-tuple-element.136), channel_id=1, source_target_pairs={{0,3},{1,2},{2,1},{3,0},{4,7},{5,6},{6,5},{7,4},{8,11},{9,10},{10,... | collective-permute-start | bytes 1032200 | tf_op jit(solution)/shard_map/ppermute | solution.py:253
  192.9 26.8 %copy-start.9 = (bf16[48,3584]{1,0:T(8,128)(2,1)}, bf16[48,3584]{1,0:T(8,128)(2,1)S(1)}, u32[]{:S(2)}) copy-start(bf16[48,3584]{1,0:T(8,128)(2,1)S(1)} %collective-permute-done.25.refs_2_) | copy-start | bytes 1032196
  192.9 9.3 %collective-permute-start.28 = (bf16[48,3584]{1,0:T(8,128)(2,1)}, bf16[48,3584]{1,0:T(8,128)(2,1)S(1)}, u32[]{:S(2)}, u32[]{:S(2)}) collective-permute-start(bf16[48,3584]{1,0:T(8,128)(2,1)} %get-tuple-element.144), channel_id=1, source_target_pairs={{0,1},{1,0},{2,3},{3,2},{4,5},{5,4},{6,7},{7,6},{8,9},{9,8},{10,11... | collective-permute-start | bytes 1032200 | tf_op jit(solution)/shard_map/ppermute | solution.py:253
  192.9 26.8 %copy-start.10 = (bf16[48,3584]{1,0:T(8,128)(2,1)}, bf16[48,3584]{1,0:T(8,128)(2,1)S(1)}, u32[]{:S(2)}) copy-start(bf16[48,3584]{1,0:T(8,128)(2,1)S(1)} %collective-permute-done.26.refs_3_) | copy-start | bytes 1032196
  192.9 16.2 %collective-permute-start.29 = (bf16[48,3584]{1,0:T(8,128)(2,1)}, bf16[48,3584]{1,0:T(8,128)(2,1)}, u32[]{:S(2)}, u32[]{:S(2)}) collective-permute-start(bf16[48,3584]{1,0:T(8,128)(2,1)} %get-tuple-element.145), channel_id=1, source_target_pairs={{0,2},{1,3},{2,0},{3,1},{4,6},{5,7},{6,4},{7,5},{8,10},{9,11},{10,... | collective-permute-start | bytes 1032200 | tf_op jit(solution)/shard_map/ppermute | solution.py:253
  193.3 29.3 %copy-start.11 = (bf16[48,3584]{1,0:T(8,128)(2,1)}, bf16[48,3584]{1,0:T(8,128)(2,1)S(1)}, u32[]{:S(2)}) copy-start(bf16[48,3584]{1,0:T(8,128)(2,1)S(1)} %collective-permute-done.21.refs_1_) | copy-start | bytes 1032196
  193.3 23.5 %collective-permute-start.30 = (bf16[48,3584]{1,0:T(8,128)(2,1)}, bf16[48,3584]{1,0:T(8,128)(2,1)}, u32[]{:S(2)}, u32[]{:S(2)}) collective-permute-start(bf16[48,3584]{1,0:T(8,128)(2,1)} %get-tuple-element.146), channel_id=1, source_target_pairs={{0,3},{1,2},{2,1},{3,0},{4,7},{5,6},{6,5},{7,4},{8,11},{9,10},{10,... | collective-permute-start | bytes 1032200 | tf_op jit(solution)/shard_map/ppermute | solution.py:253
  195.1 27.4 %copy-start.12 = (bf16[48,3584]{1,0:T(8,128)(2,1)}, bf16[48,3584]{1,0:T(8,128)(2,1)S(1)}, u32[]{:S(2)}) copy-start(bf16[48,3584]{1,0:T(8,128)(2,1)S(1)} %collective-permute-done.22.refs_2_) | copy-start | bytes 1032196
  195.1 23.3 %collective-permute-start.16 = (bf16[48,3584]{1,0:T(8,128)(2,1)}, bf16[48,3584]{1,0:T(8,128)(2,1)}, u32[]{:S(2)}, u32[]{:S(2)}) collective-permute-start(bf16[48,3584]{1,0:T(8,128)(2,1)} %get-tuple-element.126), channel_id=1, source_target_pairs={{0,1},{1,0},{2,3},{3,2},{4,5},{5,4},{6,7},{7,6},{8,9},{9,8},{10,11... | collective-permute-start | bytes 1032200 | tf_op jit(solution)/shard_map/ppermute | solution.py:253
  202.1 46.4 %collective-permute-start.15 = (bf16[48,3712]{1,0:T(8,128)(2,1)}, bf16[48,3712]{1,0:T(8,128)(2,1)}, u32[]{:S(2)}, u32[]{:S(2)}) collective-permute-start(bf16[48,3712]{1,0:T(8,128)(2,1)} %get-tuple-element.125), channel_id=1, source_target_pairs={{0,1},{1,0},{2,3},{3,2},{4,5},{5,4},{6,7},{7,6},{8,9},{9,8},{10,11... | collective-permute-start | bytes 1069064 | tf_op jit(solution)/shard_map/ppermute | solution.py:253
  202.2 46.3 %collective-permute-start.17 = (bf16[48,3712]{1,0:T(8,128)(2,1)}, bf16[48,3712]{1,0:T(8,128)(2,1)}, u32[]{:S(2)}, u32[]{:S(2)}) collective-permute-start(bf16[48,3712]{1,0:T(8,128)(2,1)} %get-tuple-element.127), channel_id=1, source_target_pairs={{0,2},{1,3},{2,0},{3,1},{4,6},{5,7},{6,4},{7,5},{8,10},{9,11},{10,... | collective-permute-start | bytes 1069064 | tf_op jit(solution)/shard_map/ppermute | solution.py:253
  209.2 22.4 %collective-permute-start.18 = (bf16[48,3584]{1,0:T(8,128)(2,1)}, bf16[48,3584]{1,0:T(8,128)(2,1)}, u32[]{:S(2)}, u32[]{:S(2)}) collective-permute-start(bf16[48,3584]{1,0:T(8,128)(2,1)} %get-tuple-element.128), channel_id=1, source_target_pairs={{0,2},{1,3},{2,0},{3,1},{4,6},{5,7},{6,4},{7,5},{8,10},{9,11},{10,... | collective-permute-start | bytes 1032200 | tf_op jit(solution)/shard_map/ppermute | solution.py:253
  216.8 31.7 %collective-permute-start.19 = (bf16[48,3712]{1,0:T(8,128)(2,1)}, bf16[48,3712]{1,0:T(8,128)(2,1)}, u32[]{:S(2)}, u32[]{:S(2)}) collective-permute-start(bf16[48,3712]{1,0:T(8,128)(2,1)} %get-tuple-element.129), channel_id=1, source_target_pairs={{0,3},{1,2},{2,1},{3,0},{4,7},{5,6},{6,5},{7,4},{8,11},{9,10},{10,... | collective-permute-start | bytes 1069064 | tf_op jit(solution)/shard_map/ppermute | solution.py:253
  218.4 28.5 %collective-permute-start.20 = (bf16[48,3584]{1,0:T(8,128)(2,1)}, bf16[48,3584]{1,0:T(8,128)(2,1)}, u32[]{:S(2)}, u32[]{:S(2)}) collective-permute-start(bf16[48,3584]{1,0:T(8,128)(2,1)} %get-tuple-element.130), channel_id=1, source_target_pairs={{0,3},{1,2},{2,1},{3,0},{4,7},{5,6},{6,5},{7,4},{8,11},{9,10},{10,... | collective-permute-start | bytes 1032200 | tf_op jit(solution)/shard_map/ppermute | solution.py:253
  231.6 132.9 %collective-permute-start.27 = (bf16[128,3584]{1,0:T(8,128)(2,1)}, bf16[128,3584]{1,0:T(8,128)(2,1)}, u32[]{:S(2)}, u32[]{:S(2)}) collective-permute-start(bf16[128,3584]{1,0:T(8,128)(2,1)} %shard_map.163), channel_id=1, source_target_pairs={{0,4},{1,5},{2,6},{3,7},{12,8},{13,9},{14,10},{15,11},{16,20},{17,... | collective-permute-start | bytes 2752520 | tf_op jit(solution)/shard_map/ppermute | solution.py:253
  246.8 49.0 %collective-permute-start.31 = (bf16[128,3584]{1,0:T(8,128)(2,1)}, bf16[128,3584]{1,0:T(8,128)(2,1)S(1)}, u32[]{:S(2)}, u32[]{:S(2)}) collective-permute-start(bf16[128,3584]{1,0:T(8,128)(2,1)} %shard_map.164), channel_id=1, source_target_pairs={{0,4},{1,5},{2,6},{3,7},{4,0},{5,1},{6,2},{7,3},{8,12},{9,13},{10,... | collective-permute-start | bytes 2752520 | tf_op jit(solution)/shard_map/ppermute | solution.py:253
  248.5 30.3 %copy-start.6 = (f32[64,3584]{1,0:T(8,128)S(1)}, f32[64,3584]{1,0:T(8,128)}, u32[]{:S(2)}) copy-start(f32[64,3584]{1,0:T(8,128)} %get-tuple-element.151) | copy-start | bytes 2752516
  270.2 18.9 %collective-permute-start.33 = (bf16[48,3584]{1,0:T(8,128)(2,1)}, bf16[48,3584]{1,0:T(8,128)(2,1)S(1)}, u32[]{:S(2)}, u32[]{:S(2)}) collective-permute-start(bf16[48,3584]{1,0:T(8,128)(2,1)} %get-tuple-element.148), channel_id=1, source_target_pairs={{0,1},{1,0},{2,3},{3,2},{4,5},{5,4},{6,7},{7,6},{8,9},{9,8},{10,11... | collective-permute-start | bytes 1032200 | tf_op jit(solution)/shard_map/ppermute | solution.py:253
  270.9 18.1 %collective-permute-start.34 = (bf16[48,3584]{1,0:T(8,128)(2,1)}, bf16[48,3584]{1,0:T(8,128)(2,1)}, u32[]{:S(2)}, u32[]{:S(2)}) collective-permute-start(bf16[48,3584]{1,0:T(8,128)(2,1)} %get-tuple-element.149), channel_id=1, source_target_pairs={{0,2},{1,3},{2,0},{3,1},{4,6},{5,7},{6,4},{7,5},{8,10},{9,11},{10,... | collective-permute-start | bytes 1032200 | tf_op jit(solution)/shard_map/ppermute | solution.py:253
  272.4 16.7 %collective-permute-start.35 = (bf16[48,3584]{1,0:T(8,128)(2,1)}, bf16[48,3584]{1,0:T(8,128)(2,1)}, u32[]{:S(2)}, u32[]{:S(2)}) collective-permute-start(bf16[48,3584]{1,0:T(8,128)(2,1)} %get-tuple-element.150), channel_id=1, source_target_pairs={{0,3},{1,2},{2,1},{3,0},{4,7},{5,6},{6,5},{7,4},{8,11},{9,10},{10,... | collective-permute-start | bytes 1032200 | tf_op jit(solution)/shard_map/ppermute | solution.py:253
  274.4 14.0 %all-to-all-start = ((bf16[16,1,48]{2,1,0:T(2,128)(2,1)}), bf16[16,1,48]{2,1,0:T(2,128)(2,1)S(1)}, u32[]{:S(2)}, u32[]{:S(2)}) async-start(bf16[16,1,48]{2,1,0:T(2,128)(2,1)} %copy.49), calls=%async_computation | async-start | bytes 16384 | tf_op jit(solution)/shard_map/all_to_all | solution.py:399
  292.4 72.0 %collective-permute-start.37 = (bf16[128,3584]{1,0:T(8,128)(2,1)}, bf16[128,3584]{1,0:T(8,128)(2,1)}, u32[]{:S(2)}, u32[]{:S(2)}) collective-permute-start(bf16[128,3584]{1,0:T(8,128)(2,1)} %shard_map.165), channel_id=1, source_target_pairs={{0,8},{1,9},{2,10},{3,11},{12,4},{13,5},{14,6},{15,7},{16,24},{17,... | collective-permute-start | bytes 2752520 | tf_op jit(solution)/shard_map/ppermute | solution.py:253
  293.7 70.8 %collective-permute-start.36 = (bf16[128,3584]{1,0:T(8,128)(2,1)}, bf16[128,3584]{1,0:T(8,128)(2,1)}, u32[]{:S(2)}, u32[]{:S(2)}) collective-permute-start(bf16[128,3584]{1,0:T(8,128)(2,1)} %shard_map.165), channel_id=1, source_target_pairs={{4,8},{5,9},{6,10},{7,11},{8,4},{9,5},{10,6},{11,7},{20,24},{21,25... | collective-permute-start | bytes 2752520 | tf_op jit(solution)/shard_map/ppermute | solution.py:253
  298.5 66.0 %collective-permute-start.32 = (bf16[128,3584]{1,0:T(8,128)(2,1)}, bf16[128,3584]{1,0:T(8,128)(2,1)}, u32[]{:S(2)}, u32[]{:S(2)}) collective-permute-start(bf16[128,3584]{1,0:T(8,128)(2,1)} %add_convert_fusion.1), channel_id=1, source_target_pairs={{4,12},{5,13},{6,14},{7,15},{8,0},{9,1},{10,2},{11,3},{20,28},{21,... | collective-permute-start | bytes 2752520 | tf_op jit(solution)/shard_map/ppermute | solution.py:253
  306.3 58.2 %copy-start.3 = (bf16[128,3584]{1,0:T(8,128)(2,1)S(1)}, bf16[128,3584]{1,0:T(8,128)(2,1)}, u32[]{:S(2)}) copy-start(bf16[128,3584]{1,0:T(8,128)(2,1)} %shard_map.162) | copy-start | bytes 2752516
  306.3 57.6 %all-to-all-start.1 = ((f32[16,16,224]{2,1,0:T(8,128)}), f32[16,16,224]{2,1,0:T(8,128)S(1)}, u32[]{:S(2)}, u32[]{:S(2)}) async-start(f32[16,16,224]{2,1,0:T(8,128)} %bitcast.40), calls=%async_computation.1 | async-start | bytes 524288 | tf_op jit(solution)/shard_map/all_to_all | solution.py:412
  (17 other events, 173.2 us)
where the time goes:
time: 371 us; the launch traced here: 368 us
  waiting for transfers between devices  180 us (49%)
  Pallas kernels  105 us (28%)
  starting transfers between devices  54.5 us (15%)
  other arithmetic  17.3 us (5%)
  local copies, waits for them, and re-layouts  7.64 us (2%)
    ppermute x38, waiting for transfers between devices, send(): return lax.ppermute(array, 'expert', pairs)  122 us
    pallas_call x3, Pallas kernels, expert_rows(): pl.pallas_call(functools.partial(expert_kernel, [(0,) * len(p) for p in p...  75.2 us
    all_to_all x1, waiting for transfers between devices, shards(): lax.all_to_all(router_part, 'expert', split_axis=0, concat_axis=0, tiled=...  51 us
    ppermute x38, starting transfers between devices, send(): return lax.ppermute(array, 'expert', pairs)  44.7 us
    pallas_call x5, Pallas kernels, select_rows(): pl.pallas_call(functools.partial(select_kernel, parts, meta_at, slots_hel...  19 us
    pallas_call x4, Pallas kernels, sum_rows(): pl.pallas_call(functools.partial(sum_kernel, len(extra), cap), out_shape=...  10.8 us
  transfers between devices with their start and end apart: 40, of which 12 were waited for; matrix products, arithmetic and copies ran while one was open for 5% of the time, Pallas kernels for 29%

commit v1 on v0

--- a/solution.py
+++ b/solution.py
@@ -12,6 +12,7 @@
 bf16 = jnp.bfloat16
 f32 = jnp.float32
 vmem_bytes = 56 * 1024 * 1024
+light = pl.CostEstimate(flops=1024, bytes_accessed=1024, transcendentals=0)
 
 
 def dot_nn(left, right):
@@ -89,11 +90,7 @@
         in_specs=[smem] + [vmem] * (1 + len(arrays)),
         out_specs=[vmem] * len(shapes),
         compiler_params=pltpu.CompilerParams(vmem_limit_bytes=vmem_bytes),
-        cost_estimate=pl.CostEstimate(
-            flops=2 * plane * cap * tok * length,
-            bytes_accessed=2 * length * (tok + plane * cap),
-            transcendentals=0,
-        ),
+        cost_estimate=light,
     )(flag, guide, *arrays)
 
 
@@ -116,11 +113,7 @@
         in_specs=[vmem] * (1 + plane + len(extra)),
         out_specs=vmem,
         compiler_params=pltpu.CompilerParams(vmem_limit_bytes=vmem_bytes),
-        cost_estimate=pl.CostEstimate(
-            flops=2 * plane * cap * tok * width,
-            bytes_accessed=2 * width * (2 * tok + plane * cap),
-            transcendentals=0,
-        ),
+        cost_estimate=light,
     )(placed, *pieces, *extra)
 
 
@@ -231,11 +224,7 @@
             pltpu.VMEM((rows, width), f32),
         ],
         compiler_params=pltpu.CompilerParams(vmem_limit_bytes=vmem_bytes),
-        cost_estimate=pl.CostEstimate(
-            flops=2 * 5 * rows * width * hidden,
-            bytes_accessed=2 * 3 * width * hidden + 6 * rows * width,
-            transcendentals=rows * hidden,
-        ),
+        cost_estimate=light,
     )(mine, w_gate, w_up, w_down, a_gate, a_up, b_gate, b_up, *arrays)
 
 
@@ -302,11 +291,9 @@
             [slot_dense.astype(bf16), combine, jnp.zeros((tok, meta_width - 2 * experts), bf16)],
             axis=1,
         )
-        x_ext = jnp.concatenate([layer_input, meta], axis=1)
-        own = jnp.concatenate([x_ext, dy], axis=1)
-        ext = width + meta_width
-        full = ext + width
-        meta_at = (width, ext)
+        own = jnp.concatenate([layer_input, meta, dy], axis=1)
+        full = own.shape[1]
+        meta_at = (width, width + meta_width)
 
         here = layer * plane + (place ^ jnp.arange(plane, dtype=jnp.int32))
         guide = jnp.zeros((16, meta_width), bf16)
@@ -314,73 +301,71 @@
             (here[:, None] == jnp.arange(meta_width, dtype=jnp.int32)[None, :]).astype(bf16)
         )
         mine = (jnp.arange(meta_width) == experts + me).astype(f32)[None, :]
-        take = functools.partial(select_rows, cap=cap)
+
+        def take(flag, arrays):
+            *pieces, placed = select_rows(
+                flag, guide, [[(0, full)] * len(arrays)], arrays, meta_at, False, cap
+            )
+            return pieces, placed
+
+        def run(pieces):
+            return expert_rows(mine, mats, [(a,) for a in pieces])
 
         if layers == 4:
             mid = (layer == 1) | (layer == 2)
             flag = mid.astype(jnp.int32)[None]
-            ends_in = along([(1, 0), (2, 3)])
-            second = along([(0, 2), (3, 1), (1, 0), (2, 3)])
-            dy_2 = send(dy, second)
-            x_2 = send(x_ext, second)
-            *sel_0, placed_0 = take(flag, guide, [[(0, full)]], [own], meta_at, False)
-            got_0 = spread(sel_0)
-            own_3 = after(own, x_2, dy_2)
-            onward = jnp.where(mid, jnp.concatenate([x_2, dy_2], axis=1), own)
-            block_2 = send(onward, across(plane))
-            block_3 = send(own_3, along([(1, 2), (2, 1)]))
-            *sel_1, placed_1 = take(
-                flag, guide, [[(0, ext)], [(0, width)]], [x_2, dy_2], meta_at, False
-            )
-            sel_1 = lax.optimization_barrier((*sel_1, *got_0))[:plane]
+            join = lax.optimization_barrier
+            block_1 = send(own, along([(0, 2), (3, 1), (1, 0), (2, 3)]))
+            sel_0, placed_0 = take(flag, [own])
+            block_1, own, got_0 = join((block_1, own, spread(sel_0)))
+            block_2f = send(block_1, along([(1, 0), (2, 3)]))
+            block_2m = send(own, along([(1, 2), (2, 1)]))
+            sel_1, placed_1 = take(flag, [block_1])
             got_1 = spread(sel_1)
-            x_5, dy_5, _, _ = lax.optimization_barrier((x_ext, dy, block_2, block_3))
-            x_3 = send(x_5, along([(1, 3), (2, 0)]))
-            dy_3 = send(dy_5, along([(1, 3), (2, 0)]))
-            *sel_2, placed_2 = take(flag, guide, [[(0, full)]], [block_2], meta_at, False)
-            sel_2 = lax.optimization_barrier((*sel_2, *got_1))[:plane]
+            done_0 = run(got_0)
+            got_1, done_0, own = join((got_1, done_0, own))
+            block_2f, block_2m, own = join((block_2f, block_2m, own))
+            block_3 = send(own, along([(0, 1), (3, 2), (1, 3), (2, 0)]))
+            sel_2, placed_2 = take(flag, [block_2m, block_2f])
+            sel_2, back_0, got_1 = join((sel_2, spread(done_0[:plane]), got_1))
             got_2 = spread(sel_2)
-            early = lax.optimization_barrier((*got_0, *got_1, sel_2[0]))[: 2 * plane]
-            done_01 = expert_rows(mine, mats, [(a,) for a in early])
-            back_0 = spread(done_01[:plane])
-            back_1 = spread(done_01[plane : 2 * plane])
-            done_2 = expert_rows(mine, mats, [(a,) for a in got_2])
-            *sel_3x, placed_3 = take(
-                flag, guide, [[(0, ext), (0, ext)]], [block_3, x_3], meta_at, False
-            )
-            sel_3y = take(flag, placed_3, [[(ext, width), (0, width)]], [block_3, dy_3], None, True)
-            got_3x = spread(sel_3x)
-            got_3y = spread(sel_3y)
-            done_3 = expert_rows(mine, mats, list(zip(got_3x, got_3y)))
-            back_2 = spread(done_2[:plane])
-            back_3 = spread(done_3[:plane])
-
+            done_1 = run(got_1)
             part_0 = sum_rows(placed_0, back_0, [])
+            got_2, done_1, part_0 = join((got_2, done_1, part_0))
+            sel_3, placed_3 = take(flag, [block_3])
+            sel_3, back_1, got_2 = join((sel_3, spread(done_1[:plane]), got_2))
+            got_3 = spread(sel_3)
+            done_2 = run(got_2)
             part_1 = sum_rows(placed_1, back_1, [])
             term_1 = send(part_1, along([(0, 1), (3, 2)]))
+            got_3, done_2, part_1 = join((got_3, done_2, part_1))
+            back_2 = spread(done_2[:plane])
+            done_3 = run(got_3)
+            back_2, done_3 = join((back_2, done_3))
+            back_3 = spread(done_3[:plane])
             part_2 = sum_rows(placed_2, back_2, [])
-            term_2 = send(part_2, across(plane))
-            joined = (part_1.astype(f32) + term_2.astype(f32)).astype(bf16)
+            hop = send(part_2, along([(0, 1), (3, 2)]))
+            term_2 = send(part_2, along([(1, 2), (2, 1)]))
+            joined = (part_1.astype(f32) + hop.astype(f32)).astype(bf16)
             term_3 = send(joined, along([(1, 3), (2, 0)]))
             part_3 = sum_rows(placed_3, back_3, [])
-            term_4 = send(part_3, along([(1, 2), (2, 1)]))
-            term_5 = send(part_3, along([(0, 2), (3, 1)]))
-            terms = [part_0, term_1, jnp.where(mid, jnp.zeros((), bf16), term_2), term_3, term_4, term_5]
-            done = [done_01, done_2, done_3]
-            counts = [2, 1, 1]
+            term_4 = send(part_3, along([(1, 0), (2, 3), (3, 1), (0, 2)]))
+            terms = [part_0, term_1, term_2, term_3, term_4]
+            done = [done_0, done_1, done_2, done_3]
+            counts = [1, 1, 1, 1]
             sources = [
                 layer,
                 jnp.where(mid, layer ^ 2, layer ^ 1),
-                jnp.where(mid, layer ^ 1, layer ^ 3),
-                jnp.where(mid, layer ^ 3, layer ^ 2),
+                layer ^ 3,
+                jnp.where(mid, layer ^ 1, layer ^ 2),
             ]
         else:
             flag = jnp.zeros((1,), jnp.int32)
             done, counts, sources, terms = [], [], [], []
             for g in range(layers):
                 block = own if g == 0 else send(own, across(g * plane))
-                *sel, placed = take(flag, guide, [[(0, full)]], [block], meta_at, False)
-                result = expert_rows(mine, mats, [(a,) for a in spread(sel)])
+                sel, placed = take(flag, [block])
+                result = run(spread(sel))
                 part = sum_rows(placed, spread(result[:plane]), [])
                 terms.append(part if g == 0 else send(part, across(g * plane)))
                 done.append(result)

time: 371 us -> 321 us (0.87)
  waiting for transfers between devices: 180 us -> 125 us
  Pallas kernels: 105 us -> 114 us
  starting transfers between devices: 54.5 us -> 48.4 us
    ppermute x38 -> x33, waiting for transfers between devices: 122 us -> 88.7 us  [send(): return lax.ppermute(array, 'expert', pairs)]
    all_to_all x1, waiting for transfers between devices: 51 us -> 36.2 us  [shards(): lax.all_to_all(router_part, 'expert', split_axis=0, concat_axis=0, tiled=...]
    pallas_call x3 -> x4, Pallas kernels: 75.2 us -> 86.4 us  [expert_rows(): pl.pallas_call(functools.partial(expert_kernel, [(0,) * len(p) for p in p...]
    ppermute x38 -> x33, starting transfers between devices: 44.7 us -> 35.7 us  [send(): return lax.ppermute(array, 'expert', pairs)]
    all_to_all x1, waiting for transfers between devices: 7.12 us -> 0.01 us  [shards(): lax.all_to_all(route_sorted, 'expert', split_axis=0, concat_axis=0, tiled...]
    pallas_call x5 -> x4, Pallas kernels: 19 us -> 17 us  [select_rows(): pl.pallas_call(functools.partial(select_kernel, parts, meta_at, slots_hel...]
  transfers between devices with their start and end apart: 40 -> 35, of which waited for: 12 -> 14; matrix products, arithmetic and copies ran while one was open for 5% -> 5% of each run, Pallas kernels for 29% -> 36%
where the time goes in v1:
time: 321 us; the launch traced here: 318 us
  waiting for transfers between devices  125 us (39%)
  Pallas kernels  114 us (36%)
  starting transfers between devices  48.4 us (15%)
  other arithmetic  15.6 us (5%)
  local copies, waits for them, and re-layouts  10.2 us (3%)
  matrix products  3.69 us (1%)
    ppermute x33, waiting for transfers between devices, send(): return lax.ppermute(array, 'expert', pairs)  88.7 us
    pallas_call x4, Pallas kernels, expert_rows(): pl.pallas_call(functools.partial(expert_kernel, [(0,) * len(p) for p in p...  86.4 us
    all_to_all x1, waiting for transfers between devices, shards(): lax.all_to_all(router_part, 'expert', split_axis=0, concat_axis=0, tiled=...  36.2 us
    ppermute x33, starting transfers between devices, send(): return lax.ppermute(array, 'expert', pairs)  35.7 us
    pallas_call x4, Pallas kernels, select_rows(): pl.pallas_call(functools.partial(select_kernel, parts, meta_at, slots_hel...  17 us
    pallas_call x4, Pallas kernels, sum_rows(): pl.pallas_call(functools.partial(sum_kernel, len(extra), cap), out_shape=...  10.9 us
    all_to_all x1, starting transfers between devices, shards(): lax.all_to_all(route_sorted, 'expert', split_axis=0, concat_axis=0, tiled...  7.07 us
  transfers between devices with their start and end apart: 35, of which 14 were waited for; matrix products, arithmetic and copies ran while one was open for 5% of the time, Pallas kernels for 36%

profile of v1, /device:TPU:15, one launch (start us, length us, event | category | flops | bytes accessed | tf_op | source)
XLA Modules:
  0.0 318.2 jit_solution(8002681371259569032)
XLA Ops:
  2.3 2.2 fusion.15
  5.1 2.2 concatenate.13.refs_0_
  9.2 4.1 %shard_map.154 = (bf16[48,7296]{1,0:T(8,128)(2,1)}, bf16[48,7296]{1,0:T(8,128)(2,1)}, bf16[48,7296]{1,0:T(8,128)(2,1)}, bf16[48,7296]{1,0:T(8,128)(2,1)}, bf16[192,128]{1,0:T(8,128)(2,1)}) custom-call(s32[1]{0:T(128)} %bitcast.4.flag_ref, bf16[16,128]{1,0:T(8,128)(2,1)} %pad_convert_fusion.guide_ref, bf16[128,7296]{1,0:T(8,128)(2,1)} %copy-done.1), custom_call_target="tpu_custom_call" | custom-call | flops 1024 | bytes 1024 | tf_op jit(solution)/shard_map/pallas_call | solution.py:87
  14.3 1.4 collective-permute-start.3
  16.1 15.6 %collective-permute-done.2.refs_2_ = bf16[48,7296]{1,0:T(8,128)(2,1)S(1)} collective-permute-done((bf16[48,7296]{1,0:T(8,128)(2,1)}, bf16[48,7296]{1,0:T(8,128)(2,1)S(1)}, u32[]{:S(2)}, u32[]{:S(2)}) %collective-permute-start.2) | collective-permute-done | bytes 700448 | tf_op jit(solution)/shard_map/ppermute | solution.py:242
  31.7 15.4 %collective-permute-done.3.refs_3_ = bf16[48,7296]{1,0:T(8,128)(2,1)S(1)} collective-permute-done((bf16[48,7296]{1,0:T(8,128)(2,1)}, bf16[48,7296]{1,0:T(8,128)(2,1)S(1)}, u32[]{:S(2)}, u32[]{:S(2)}) %collective-permute-start.3) | collective-permute-done | bytes 700448 | tf_op jit(solution)/shard_map/ppermute | solution.py:242
  47.1 2.9 collective-permute-done.refs_0_
  50.0 1.4 collective-permute-start.7
  51.4 4.2 %collective-permute-start.8 = (bf16[128,7296]{1,0:T(8,128)(2,1)}, bf16[128,7296]{1,0:T(8,128)(2,1)}, u32[]{:S(2)}, u32[]{:S(2)}) collective-permute-start(bf16[128,7296]{1,0:T(8,128)(2,1)} %copy-done.1), channel_id=1, source_target_pairs={{4,8},{5,9},{6,10},{7,11},{8,4},{9,5},{10,6},{11,7},{20,24},{21,25... | collective-permute-start | bytes 5603336 | tf_op jit(solution)/shard_map/ppermute | solution.py:242
  55.7 4.1 %shard_map.155 = (bf16[48,7296]{1,0:T(8,128)(2,1)}, bf16[48,7296]{1,0:T(8,128)(2,1)}, bf16[48,7296]{1,0:T(8,128)(2,1)}, bf16[48,7296]{1,0:T(8,128)(2,1)}, bf16[192,128]{1,0:T(8,128)(2,1)}) custom-call(s32[1]{0:T(128)} %bitcast.4.flag_ref, bf16[16,128]{1,0:T(8,128)(2,1)} %pad_convert_fusion.guide_ref, bf16[128,7296]{1,0:T(8,128)(2,1)} %collective-permute-done.refs_0_), custom_call_target="tpu_custom_call" | custom-call | flops 1024 | bytes 1024 | tf_op jit(solution)/shard_map/pallas_call | solution.py:87
  59.8 2.1 collective-permute-start.4
  62.1 1.4 collective-permute-start.6
  64.1 21.6 %shard_map.156 = (bf16[48,3584]{1,0:T(8,128)(2,1)}, bf16[48,3584]{1,0:T(8,128)(2,1)}, bf16[48,3584]{1,0:T(8,128)(2,1)}, bf16[48,3584]{1,0:T(8,128)(2,1)}, f32[19...) custom-call(f32[1,128]{1,0:T(1,128)} %compare_convert_fusion.mine_ref, ...), custom_call_target="tpu_custom_call" | custom-call | flops 1024 | bytes 1024 | tf_op jit(solution)/shard_map/pallas_call | solution.py:189
  85.7 9.2 %collective-permute-done.6.refs_3_ = bf16[48,7296]{1,0:T(8,128)(2,1)} collective-permute-done((bf16[48,7296]{1,0:T(8,128)(2,1)}, bf16[48,7296]{1,0:T(8,128)(2,1)}, u32[]{:S(2)}, u32[]{:S(2)}) %collective-permute-start.6) | collective-permute-done | bytes 700448 | tf_op jit(solution)/shard_map/ppermute | solution.py:242
  96.2 2.0 collective-permute-start.9
  98.4 1.4 collective-permute-start.11
  99.8 4.7 %shard_map.157 = (bf16[48,7296]{1,0:T(8,128)(2,1)}, bf16[48,7296]{1,0:T(8,128)(2,1)}, bf16[48,7296]{1,0:T(8,128)(2,1)}, bf16[48,7296]{1,0:T(8,128)(2,1)}, bf16[192,128]{1,0:T(8,128)(2,1)}) custom-call(s32[1]{0:T(128)} %bitcast.4.flag_ref, bf16[16,128]{1,0:T(8,128)(2,1)} %pad_convert_fusion.guide_ref, bf16[128,7296]{1,0:T(8,128)(2,1)} %collective-permute-done.8.refs_0_, ...), custom_call_target="tpu_custom_call" | custom-call | flops 1024 | bytes 1024 | tf_op jit(solution)/shard_map/pallas_call | solution.py:87
  104.5 3.6 %collective-permute-done.10.refs_2_ = bf16[48,3584]{1,0:T(8,128)(2,1)S(1)} collective-permute-done((bf16[48,3584]{1,0:T(8,128)(2,1)}, bf16[48,3584]{1,0:T(8,128)(2,1)S(1)}, u32[]{:S(2)}, u32[]{:S(2)}) %collective-permute-start.10) | collective-permute-done | bytes 344096 | tf_op jit(solution)/shard_map/ppermute | solution.py:242
  108.1 7.8 %collective-permute-done.11.refs_3_ = bf16[48,3584]{1,0:T(8,128)(2,1)S(1)} collective-permute-done((bf16[48,3584]{1,0:T(8,128)(2,1)}, bf16[48,3584]{1,0:T(8,128)(2,1)S(1)}, u32[]{:S(2)}, u32[]{:S(2)}) %collective-permute-start.11) | collective-permute-done | bytes 344096 | tf_op jit(solution)/shard_map/ppermute | solution.py:242
  116.1 1.9 collective-permute-start.14
  118.0 21.6 %shard_map.158 = (bf16[48,3584]{1,0:T(8,128)(2,1)}, bf16[48,3584]{1,0:T(8,128)(2,1)}, bf16[48,3584]{1,0:T(8,128)(2,1)}, bf16[48,3584]{1,0:T(8,128)(2,1)}, f32[19...) custom-call(f32[1,128]{1,0:T(1,128)} %compare_convert_fusion.mine_ref, ...), custom_call_target="tpu_custom_call" | custom-call | flops 1024 | bytes 1024 | tf_op jit(solution)/shard_map/pallas_call | solution.py:189
  139.7 2.8 shard_map.159
  142.4 6.1 %collective-permute-done.14.refs_3_ = bf16[48,7296]{1,0:T(8,128)(2,1)S(1)} collective-permute-done((bf16[48,7296]{1,0:T(8,128)(2,1)}, bf16[48,7296]{1,0:T(8,128)(2,1)S(1)}, u32[]{:S(2)}, u32[]{:S(2)}) %collective-permute-start.14) | collective-permute-done | bytes 700448 | tf_op jit(solution)/shard_map/ppermute | solution.py:242
  148.8 1.8 collective-permute-start.18
  152.0 4.1 %shard_map.160 = (bf16[48,7296]{1,0:T(8,128)(2,1)}, bf16[48,7296]{1,0:T(8,128)(2,1)}, bf16[48,7296]{1,0:T(8,128)(2,1)}, bf16[48,7296]{1,0:T(8,128)(2,1)}, bf16[192,128]{1,0:T(8,128)(2,1)}) custom-call(s32[1]{0:T(128)} %bitcast.4.flag_ref, bf16[16,128]{1,0:T(8,128)(2,1)} %pad_convert_fusion.guide_ref, bf16[128,7296]{1,0:T(8,128)(2,1)} %copy-done.6), custom_call_target="tpu_custom_call" | custom-call | flops 1024 | bytes 1024 | tf_op jit(solution)/shard_map/pallas_call | solution.py:87
  156.1 1.8 collective-permute-done.17.refs_2_
  157.9 8.0 %collective-permute-done.18.refs_3_ = bf16[48,3584]{1,0:T(8,128)(2,1)} collective-permute-done((bf16[48,3584]{1,0:T(8,128)(2,1)S(1)}, bf16[48,3584]{1,0:T(8,128)(2,1)}, u32[]{:S(2)}, u32[]{:S(2)}) %collective-permute-start.18) | collective-permute-done | bytes 344096 | tf_op jit(solution)/shard_map/ppermute | solution.py:242
  166.1 1.9 collective-permute-start.21
  170.9 21.6 %shard_map.161 = (bf16[48,3584]{1,0:T(8,128)(2,1)}, bf16[48,3584]{1,0:T(8,128)(2,1)}, bf16[48,3584]{1,0:T(8,128)(2,1)}, bf16[48,3584]{1,0:T(8,128)(2,1)}, f32[19...) custom-call(f32[1,128]{1,0:T(1,128)} %compare_convert_fusion.mine_ref, ...), custom_call_target="tpu_custom_call" | custom-call | flops 1024 | bytes 1024 | tf_op jit(solution)/shard_map/pallas_call | solution.py:189
  192.6 2.8 shard_map.162
  195.4 3.2 %collective-permute-done.21.refs_3_ = bf16[48,7296]{1,0:T(8,128)(2,1)} collective-permute-done((bf16[48,7296]{1,0:T(8,128)(2,1)}, bf16[48,7296]{1,0:T(8,128)(2,1)}, u32[]{:S(2)}, u32[]{:S(2)}) %collective-permute-start.21) | collective-permute-done | bytes 700448 | tf_op jit(solution)/shard_map/ppermute | solution.py:242
  198.8 1.9 collective-permute-start.24
  201.2 1.6 collective-permute-start.25
  202.8 21.5 %shard_map.163 = (bf16[48,3584]{1,0:T(8,128)(2,1)}, bf16[48,3584]{1,0:T(8,128)(2,1)}, bf16[48,3584]{1,0:T(8,128)(2,1)}, bf16[48,3584]{1,0:T(8,128)(2,1)}, f32[19...) custom-call(f32[1,128]{1,0:T(1,128)} %compare_convert_fusion.mine_ref, ...), custom_call_target="tpu_custom_call" | custom-call | flops 1024 | bytes 1024 | tf_op jit(solution)/shard_map/pallas_call | solution.py:189
  225.7 1.6 add_add_fusion
  229.2 7.1 %all-to-all-start = ((bf16[16,1,48]{2,1,0:T(2,128)(2,1)}), bf16[16,1,48]{2,1,0:T(2,128)(2,1)S(1)}, u32[]{:S(2)}, u32[]{:S(2)}) async-start(bf16[16,1,48]{2,1,0:T(2,128)(2,1)} %copy.49), calls=%async_computation | async-start | bytes 16384 | tf_op jit(solution)/shard_map/all_to_all | solution.py:384
  236.9 1.5 collective-permute-start.31
  238.4 2.7 shard_map.164
  241.1 1.4 collective-permute-start.27
  242.5 1.7 add_bitcast_fusion
  244.8 3.1 collective-permute-start.26
  248.0 6.5 %collective-permute-done.31.refs_3_ = bf16[48,3584]{1,0:T(8,128)(2,1)} collective-permute-done((bf16[48,3584]{1,0:T(8,128)(2,1)}, bf16[48,3584]{1,0:T(8,128)(2,1)}, u32[]{:S(2)}, u32[]{:S(2)}) %collective-permute-start.31) | collective-permute-done | bytes 344096 | tf_op jit(solution)/shard_map/ppermute | solution.py:242
  254.4 2.7 shard_map.165
  257.1 8.2 %collective-permute-done.27 = bf16[128,3584]{1,0:T(8,128)(2,1)S(1)} collective-permute-done((bf16[128,3584]{1,0:T(8,128)(2,1)}, bf16[128,3584]{1,0:T(8,128)(2,1)S(1)}, u32[]{:S(2)}, u32[]{:S(2)}) %collective-permute-start.27) | collective-permute-done | bytes 917536 | tf_op jit(solution)/shard_map/ppermute | solution.py:242
  266.6 3.2 collective-permute-start.28
  271.1 5.6 %all-to-all-start.1 = ((f32[16,16,224]{2,1,0:T(8,128)}), f32[16,16,224]{2,1,0:T(8,128)S(1)}, u32[]{:S(2)}, u32[]{:S(2)}) async-start(f32[16,16,224]{2,1,0:T(8,128)} %bitcast.40), calls=%async_computation.1 | async-start | bytes 524288 | tf_op jit(solution)/shard_map/all_to_all | solution.py:397
  277.8 36.2 %all-to-all-done.1 = f32[16,16,224]{2,1,0:T(8,128)S(1)} async-done(((f32[16,16,224]{2,1,0:T(8,128)}), f32[16,16,224]{2,1,0:T(8,128)S(1)}, u32[]{:S(2)}, u32[]{:S(2)}) %all-to-all-start.1) | async-done | bytes 229408 | tf_op jit(solution)/shard_map/all_to_all | solution.py:397
  314.6 3.6 %add_convert_fusion = bf16[128,3584]{1,0:T(8,128)(2,1)} fusion(bf16[128,3584]{1,0:T(8,128)(2,1)} %collective-permute-done.32, bf16[128,3584]{1,0:T(8,128)(2,1)} %collective-permute-done.28, bf16[128,3584]{1,0:T(8,128)(2,1)} %collective-permute-done.26, bf16[128,3584]{1,0:T(8,128)(2,1)} %collective-permute-done.25, f32[128,3584]{1,0:T(8,128)S(1)} %fusion.17, ...), kind=kLoop, calls=%fused_computation | loop fusion | flops 5046272 | bytes 7340032 | tf_op jit(solution)/shard_map/convert_element_type | solution.py:403
  (155 shorter events, 21.9 us)
Async XLA Ops:
  7.4 42.6 %collective-permute-start = (bf16[128,7296]{1,0:T(8,128)(2,1)S(1)}, bf16[128,7296]{1,0:T(8,128)(2,1)}, u32[]{:S(2)}, u32[]{:S(2)}) collective-permute-start(bf16[128,7296]{1,0:T(8,128)(2,1)S(1)} %concatenate.13.refs_0_), channel_id=1, source_target_pairs={{0,8},{1,9},{2,10},{3,11},{12,4},{13,5},{14,6},{15,7},{4,0},{5,1},... | collective-permute-start | bytes 5603336 | tf_op jit(solution)/shard_map/ppermute | solution.py:242
  13.2 2.8 collective-permute-start.1
  14.1 17.6 %collective-permute-start.2 = (bf16[48,7296]{1,0:T(8,128)(2,1)}, bf16[48,7296]{1,0:T(8,128)(2,1)S(1)}, u32[]{:S(2)}, u32[]{:S(2)}) collective-permute-start(bf16[48,7296]{1,0:T(8,128)(2,1)} %get-tuple-element.156), channel_id=1, source_target_pairs={{0,2},{1,3},{2,0},{3,1},{4,6},{5,7},{6,4},{7,5},{8,10},{9,11},{10,... | collective-permute-start | bytes 2101256 | tf_op jit(solution)/shard_map/ppermute | solution.py:242
  14.3 32.8 %collective-permute-start.3 = (bf16[48,7296]{1,0:T(8,128)(2,1)}, bf16[48,7296]{1,0:T(8,128)(2,1)S(1)}, u32[]{:S(2)}, u32[]{:S(2)}) collective-permute-start(bf16[48,7296]{1,0:T(8,128)(2,1)} %get-tuple-element.157), channel_id=1, source_target_pairs={{0,3},{1,2},{2,1},{3,0},{4,7},{5,6},{6,5},{7,4},{8,11},{9,10},{10,... | collective-permute-start | bytes 2101256 | tf_op jit(solution)/shard_map/ppermute | solution.py:242
  16.1 34.0 %copy-start.13 = (bf16[48,7296]{1,0:T(8,128)(2,1)}, bf16[48,7296]{1,0:T(8,128)(2,1)S(1)}, u32[]{:S(2)}) copy-start(bf16[48,7296]{1,0:T(8,128)(2,1)S(1)} %collective-permute-done.1.refs_1_) | copy-start | bytes 2101252
  50.0 44.9 %collective-permute-start.7 = (bf16[128,7296]{1,0:T(8,128)(2,1)}, bf16[128,7296]{1,0:T(8,128)(2,1)S(1)}, u32[]{:S(2)}, u32[]{:S(2)}) collective-permute-start(bf16[128,7296]{1,0:T(8,128)(2,1)} %collective-permute-done.refs_0_), channel_id=1, source_target_pairs={{4,0},{5,1},{6,2},{7,3},{8,12},{9,13},{10,14},{11,15},{20,16},{21,... | collective-permute-start | bytes 5603336 | tf_op jit(solution)/shard_map/ppermute | solution.py:242
  51.4 44.7 %collective-permute-start.8 = (bf16[128,7296]{1,0:T(8,128)(2,1)}, bf16[128,7296]{1,0:T(8,128)(2,1)}, u32[]{:S(2)}, u32[]{:S(2)}) collective-permute-start(bf16[128,7296]{1,0:T(8,128)(2,1)} %copy-done.1), channel_id=1, source_target_pairs={{4,8},{5,9},{6,10},{7,11},{8,4},{9,5},{10,6},{11,7},{20,24},{21,25... | collective-permute-start | bytes 5603336 | tf_op jit(solution)/shard_map/ppermute | solution.py:242
  59.8 25.9 %collective-permute-start.4 = (bf16[48,7296]{1,0:T(8,128)(2,1)}, bf16[48,7296]{1,0:T(8,128)(2,1)}, u32[]{:S(2)}, u32[]{:S(2)}) collective-permute-start(bf16[48,7296]{1,0:T(8,128)(2,1)} %get-tuple-element.160), channel_id=1, source_target_pairs={{0,1},{1,0},{2,3},{3,2},{4,5},{5,4},{6,7},{7,6},{8,9},{9,8},{10,11... | collective-permute-start | bytes 2101256 | tf_op jit(solution)/shard_map/ppermute | solution.py:242
  61.9 23.8 %collective-permute-start.5 = (bf16[48,7296]{1,0:T(8,128)(2,1)}, bf16[48,7296]{1,0:T(8,128)(2,1)}, u32[]{:S(2)}, u32[]{:S(2)}) collective-permute-start(bf16[48,7296]{1,0:T(8,128)(2,1)} %get-tuple-element.161), channel_id=1, source_target_pairs={{0,2},{1,3},{2,0},{3,1},{4,6},{5,7},{6,4},{7,5},{8,10},{9,11},{10,... | collective-permute-start | bytes 2101256 | tf_op jit(solution)/shard_map/ppermute | solution.py:242
  62.1 32.8 %collective-permute-start.6 = (bf16[48,7296]{1,0:T(8,128)(2,1)}, bf16[48,7296]{1,0:T(8,128)(2,1)}, u32[]{:S(2)}, u32[]{:S(2)}) collective-permute-start(bf16[48,7296]{1,0:T(8,128)(2,1)} %get-tuple-element.162), channel_id=1, source_target_pairs={{0,3},{1,2},{2,1},{3,0},{4,7},{5,6},{6,5},{7,4},{8,11},{9,10},{10,... | collective-permute-start | bytes 2101256 | tf_op jit(solution)/shard_map/ppermute | solution.py:242
  64.0 32.1 %copy-start.2 = (bf16[128,7296]{1,0:T(8,128)(2,1)S(1)}, bf16[128,7296]{1,0:T(8,128)(2,1)}, u32[]{:S(2)}) copy-start(bf16[128,7296]{1,0:T(8,128)(2,1)} %copy-done.1) | copy-start | bytes 5603332
  96.2 54.5 %collective-permute-start.15 = (bf16[128,7296]{1,0:T(8,128)(2,1)S(1)}, bf16[128,7296]{1,0:T(8,128)(2,1)S(1)}, u32[]{:S(2)}, u32[]{:S(2)}) collective-permute-start(bf16[128,7296]{1,0:T(8,128)(2,1)S(1)} %copy-done.2), channel_id=1, source_target_pairs={{0,4},{1,5},{2,6},{3,7},{12,8},{13,9},{14,10},{15,11},{4,12},{5,13... | collective-permute-start | bytes 5603336 | tf_op jit(solution)/shard_map/ppermute | solution.py:242
  96.2 8.3 %collective-permute-start.9 = (bf16[48,3584]{1,0:T(8,128)(2,1)}, bf16[48,3584]{1,0:T(8,128)(2,1)S(1)}, u32[]{:S(2)}, u32[]{:S(2)}) collective-permute-start(bf16[48,3584]{1,0:T(8,128)(2,1)} %get-tuple-element.185), channel_id=1, source_target_pairs={{0,1},{1,0},{2,3},{3,2},{4,5},{5,4},{6,7},{7,6},{8,9},{9,8},{10,11... | collective-permute-start | bytes 1032200 | tf_op jit(solution)/shard_map/ppermute | solution.py:242
  98.2 9.9 %collective-permute-start.10 = (bf16[48,3584]{1,0:T(8,128)(2,1)}, bf16[48,3584]{1,0:T(8,128)(2,1)S(1)}, u32[]{:S(2)}, u32[]{:S(2)}) collective-permute-start(bf16[48,3584]{1,0:T(8,128)(2,1)} %get-tuple-element.186), channel_id=1, source_target_pairs={{0,2},{1,3},{2,0},{3,1},{4,6},{5,7},{6,4},{7,5},{8,10},{9,11},{10,... | collective-permute-start | bytes 1032200 | tf_op jit(solution)/shard_map/ppermute | solution.py:242
  98.4 17.4 %collective-permute-start.11 = (bf16[48,3584]{1,0:T(8,128)(2,1)}, bf16[48,3584]{1,0:T(8,128)(2,1)S(1)}, u32[]{:S(2)}, u32[]{:S(2)}) collective-permute-start(bf16[48,3584]{1,0:T(8,128)(2,1)} %get-tuple-element.187), channel_id=1, source_target_pairs={{0,3},{1,2},{2,1},{3,0},{4,7},{5,6},{6,5},{7,4},{8,11},{9,10},{10,... | collective-permute-start | bytes 1032200 | tf_op jit(solution)/shard_map/ppermute | solution.py:242
  104.5 35.1 %copy-start.19 = (bf16[48,3584]{1,0:T(8,128)(2,1)}, bf16[48,3584]{1,0:T(8,128)(2,1)S(1)}, u32[]{:S(2)}) copy-start(bf16[48,3584]{1,0:T(8,128)(2,1)S(1)} %collective-permute-done.9.refs_1_) | copy-start | bytes 1032196
  108.1 31.5 %copy-start.20 = (bf16[48,3584]{1,0:T(8,128)(2,1)}, bf16[48,3584]{1,0:T(8,128)(2,1)S(1)}, u32[]{:S(2)}) copy-start(bf16[48,3584]{1,0:T(8,128)(2,1)S(1)} %collective-permute-done.10.refs_2_) | copy-start | bytes 1032196
  115.9 23.8 %copy-start.21 = (bf16[48,3584]{1,0:T(8,128)(2,1)}, bf16[48,3584]{1,0:T(8,128)(2,1)S(1)}, u32[]{:S(2)}) copy-start(bf16[48,3584]{1,0:T(8,128)(2,1)S(1)} %collective-permute-done.11.refs_3_) | copy-start | bytes 1032196
  115.9 26.6 %collective-permute-start.12 = (bf16[48,7296]{1,0:T(8,128)(2,1)}, bf16[48,7296]{1,0:T(8,128)(2,1)S(1)}, u32[]{:S(2)}, u32[]{:S(2)}) collective-permute-start(bf16[48,7296]{1,0:T(8,128)(2,1)} %get-tuple-element.193), channel_id=1, source_target_pairs={{0,1},{1,0},{2,3},{3,2},{4,5},{5,4},{6,7},{7,6},{8,9},{9,8},{10,11... | collective-permute-start | bytes 2101256 | tf_op jit(solution)/shard_map/ppermute | solution.py:242
  115.9 26.6 %collective-permute-start.13 = (bf16[48,7296]{1,0:T(8,128)(2,1)}, bf16[48,7296]{1,0:T(8,128)(2,1)S(1)}, u32[]{:S(2)}, u32[]{:S(2)}) collective-permute-start(bf16[48,7296]{1,0:T(8,128)(2,1)} %get-tuple-element.194), channel_id=1, source_target_pairs={{0,2},{1,3},{2,0},{3,1},{4,6},{5,7},{6,4},{7,5},{8,10},{9,11},{10,... | collective-permute-start | bytes 2101256 | tf_op jit(solution)/shard_map/ppermute | solution.py:242
  116.1 32.4 %collective-permute-start.14 = (bf16[48,7296]{1,0:T(8,128)(2,1)}, bf16[48,7296]{1,0:T(8,128)(2,1)S(1)}, u32[]{:S(2)}, u32[]{:S(2)}) collective-permute-start(bf16[48,7296]{1,0:T(8,128)(2,1)} %get-tuple-element.195), channel_id=1, source_target_pairs={{0,3},{1,2},{2,1},{3,0},{4,7},{5,6},{6,5},{7,4},{8,11},{9,10},{10,... | collective-permute-start | bytes 2101256 | tf_op jit(solution)/shard_map/ppermute | solution.py:242
  142.4 28.5 %copy-start.10 = (bf16[48,7296]{1,0:T(8,128)(2,1)}, bf16[48,7296]{1,0:T(8,128)(2,1)S(1)}, u32[]{:S(2)}) copy-start(bf16[48,7296]{1,0:T(8,128)(2,1)S(1)} %collective-permute-done.12.refs_1_) | copy-start | bytes 2101252
  142.4 28.5 %copy-start.11 = (bf16[48,7296]{1,0:T(8,128)(2,1)}, bf16[48,7296]{1,0:T(8,128)(2,1)S(1)}, u32[]{:S(2)}) copy-start(bf16[48,7296]{1,0:T(8,128)(2,1)S(1)} %collective-permute-done.13.refs_2_) | copy-start | bytes 2101252
  148.5 7.6 %collective-permute-start.16 = (bf16[48,3584]{1,0:T(8,128)(2,1)S(1)}, bf16[48,3584]{1,0:T(8,128)(2,1)S(1)}, u32[]{:S(2)}, u32[]{:S(2)}) collective-permute-start(bf16[48,3584]{1,0:T(8,128)(2,1)S(1)} %copy-done.37), channel_id=1, source_target_pairs={{0,1},{1,0},{2,3},{3,2},{4,5},{5,4},{6,7},{7,6},{8,9},{9,8},{10,11... | collective-permute-start | bytes 1032200 | tf_op jit(solution)/shard_map/ppermute | solution.py:242
  148.5 9.4 %collective-permute-start.17 = (bf16[48,3584]{1,0:T(8,128)(2,1)S(1)}, bf16[48,3584]{1,0:T(8,128)(2,1)}, u32[]{:S(2)}, u32[]{:S(2)}) collective-permute-start(bf16[48,3584]{1,0:T(8,128)(2,1)S(1)} %copy-done.36), channel_id=1, source_target_pairs={{0,2},{1,3},{2,0},{3,1},{4,6},{5,7},{6,4},{7,5},{8,10},{9,11},{10,... | collective-permute-start | bytes 1032200 | tf_op jit(solution)/shard_map/ppermute | solution.py:242
  148.8 17.0 %collective-permute-start.18 = (bf16[48,3584]{1,0:T(8,128)(2,1)S(1)}, bf16[48,3584]{1,0:T(8,128)(2,1)}, u32[]{:S(2)}, u32[]{:S(2)}) collective-permute-start(bf16[48,3584]{1,0:T(8,128)(2,1)S(1)} %copy-done.35), channel_id=1, source_target_pairs={{0,3},{1,2},{2,1},{3,0},{4,7},{5,6},{6,5},{7,4},{8,11},{9,10},{10,... | collective-permute-start | bytes 1032200 | tf_op jit(solution)/shard_map/ppermute | solution.py:242
  156.1 36.5 %copy-start.17 = (bf16[48,3584]{1,0:T(8,128)(2,1)}, bf16[48,3584]{1,0:T(8,128)(2,1)S(1)}, u32[]{:S(2)}) copy-start(bf16[48,3584]{1,0:T(8,128)(2,1)S(1)} %collective-permute-done.16.refs_1_) | copy-start | bytes 1032196
  165.9 29.5 %collective-permute-start.19 = (bf16[48,7296]{1,0:T(8,128)(2,1)}, bf16[48,7296]{1,0:T(8,128)(2,1)}, u32[]{:S(2)}, u32[]{:S(2)}) collective-permute-start(bf16[48,7296]{1,0:T(8,128)(2,1)} %get-tuple-element.228), channel_id=1, source_target_pairs={{0,1},{1,0},{2,3},{3,2},{4,5},{5,4},{6,7},{7,6},{8,9},{9,8},{10,11... | collective-permute-start | bytes 2101256 | tf_op jit(solution)/shard_map/ppermute | solution.py:242
  165.9 29.5 %collective-permute-start.20 = (bf16[48,7296]{1,0:T(8,128)(2,1)}, bf16[48,7296]{1,0:T(8,128)(2,1)}, u32[]{:S(2)}, u32[]{:S(2)}) collective-permute-start(bf16[48,7296]{1,0:T(8,128)(2,1)} %get-tuple-element.229), channel_id=1, source_target_pairs={{0,2},{1,3},{2,0},{3,1},{4,6},{5,7},{6,4},{7,5},{8,10},{9,11},{10,... | collective-permute-start | bytes 2101256 | tf_op jit(solution)/shard_map/ppermute | solution.py:242
  166.1 32.5 %collective-permute-start.21 = (bf16[48,7296]{1,0:T(8,128)(2,1)}, bf16[48,7296]{1,0:T(8,128)(2,1)}, u32[]{:S(2)}, u32[]{:S(2)}) collective-permute-start(bf16[48,7296]{1,0:T(8,128)(2,1)} %get-tuple-element.230), channel_id=1, source_target_pairs={{0,3},{1,2},{2,1},{3,0},{4,7},{5,6},{6,5},{7,4},{8,11},{9,10},{10,... | collective-permute-start | bytes 2101256 | tf_op jit(solution)/shard_map/ppermute | solution.py:242
  198.6 26.0 %collective-permute-start.22 = (bf16[48,3584]{1,0:T(8,128)(2,1)}, bf16[48,3584]{1,0:T(8,128)(2,1)S(1)}, u32[]{:S(2)}, u32[]{:S(2)}) collective-permute-start(bf16[48,3584]{1,0:T(8,128)(2,1)} %get-tuple-element.250), channel_id=1, source_target_pairs={{0,1},{1,0},{2,3},{3,2},{4,5},{5,4},{6,7},{7,6},{8,9},{9,8},{10,11... | collective-permute-start | bytes 1032200 | tf_op jit(solution)/shard_map/ppermute | solution.py:242
  198.6 26.0 %collective-permute-start.23 = (bf16[48,3584]{1,0:T(8,128)(2,1)}, bf16[48,3584]{1,0:T(8,128)(2,1)}, u32[]{:S(2)}, u32[]{:S(2)}) collective-permute-start(bf16[48,3584]{1,0:T(8,128)(2,1)} %get-tuple-element.251), channel_id=1, source_target_pairs={{0,2},{1,3},{2,0},{3,1},{4,6},{5,7},{6,4},{7,5},{8,10},{9,11},{10,... | collective-permute-start | bytes 1032200 | tf_op jit(solution)/shard_map/ppermute | solution.py:242
  198.8 25.8 %collective-permute-start.24 = (bf16[48,3584]{1,0:T(8,128)(2,1)}, bf16[48,3584]{1,0:T(8,128)(2,1)}, u32[]{:S(2)}, u32[]{:S(2)}) collective-permute-start(bf16[48,3584]{1,0:T(8,128)(2,1)} %get-tuple-element.252), channel_id=1, source_target_pairs={{0,3},{1,2},{2,1},{3,0},{4,7},{5,6},{6,5},{7,4},{8,11},{9,10},{10,... | collective-permute-start | bytes 1032200 | tf_op jit(solution)/shard_map/ppermute | solution.py:242
  201.2 23.2 %copy-start.31 = (f32[192,1]{1,0:T(8,128)S(1)}, f32[192,1]{1,0:T(8,128)}, u32[]{:S(2)}) copy-start(f32[192,1]{1,0:T(8,128)} %get-tuple-element.248) | copy-start | bytes 2308
  201.2 24.5 %copy-start.8 = (f32[64,3584]{1,0:T(8,128)S(1)}, f32[64,3584]{1,0:T(8,128)}, u32[]{:S(2)}) copy-start(f32[64,3584]{1,0:T(8,128)} %get-tuple-element.278) | copy-start | bytes 2752516
  201.2 24.5 %copy-start.9 = (f32[64,3584]{1,0:T(8,128)S(1)}, f32[64,3584]{1,0:T(8,128)}, u32[]{:S(2)}) copy-start(f32[64,3584]{1,0:T(8,128)} %get-tuple-element.279) | copy-start | bytes 2752516
  201.2 113.4 %collective-permute-start.25 = (bf16[128,3584]{1,0:T(8,128)(2,1)}, bf16[128,3584]{1,0:T(8,128)(2,1)}, u32[]{:S(2)}, u32[]{:S(2)}) collective-permute-start(bf16[128,3584]{1,0:T(8,128)(2,1)} %shard_map.162), channel_id=1, source_target_pairs={{0,4},{1,5},{2,6},{3,7},{12,8},{13,9},{14,10},{15,11},{16,20},{17,... | collective-permute-start | bytes 2752520 | tf_op jit(solution)/shard_map/ppermute | solution.py:242
  229.2 15.1 %all-to-all-start = ((bf16[16,1,48]{2,1,0:T(2,128)(2,1)}), bf16[16,1,48]{2,1,0:T(2,128)(2,1)S(1)}, u32[]{:S(2)}, u32[]{:S(2)}) async-start(bf16[16,1,48]{2,1,0:T(2,128)(2,1)} %copy.49), calls=%async_computation | async-start | bytes 16384 | tf_op jit(solution)/shard_map/all_to_all | solution.py:384
  236.3 8.5 %collective-permute-start.29 = (bf16[48,3584]{1,0:T(8,128)(2,1)}, bf16[48,3584]{1,0:T(8,128)(2,1)S(1)}, u32[]{:S(2)}, u32[]{:S(2)}) collective-permute-start(bf16[48,3584]{1,0:T(8,128)(2,1)} %get-tuple-element.275), channel_id=1, source_target_pairs={{0,1},{1,0},{2,3},{3,2},{4,5},{5,4},{6,7},{7,6},{8,9},{9,8},{10,11... | collective-permute-start | bytes 1032200 | tf_op jit(solution)/shard_map/ppermute | solution.py:242
  236.6 11.3 %collective-permute-start.30 = (bf16[48,3584]{1,0:T(8,128)(2,1)}, bf16[48,3584]{1,0:T(8,128)(2,1)}, u32[]{:S(2)}, u32[]{:S(2)}) collective-permute-start(bf16[48,3584]{1,0:T(8,128)(2,1)} %get-tuple-element.276), channel_id=1, source_target_pairs={{0,2},{1,3},{2,0},{3,1},{4,6},{5,7},{6,4},{7,5},{8,10},{9,11},{10,... | collective-permute-start | bytes 1032200 | tf_op jit(solution)/shard_map/ppermute | solution.py:242
  236.9 17.5 %collective-permute-start.31 = (bf16[48,3584]{1,0:T(8,128)(2,1)}, bf16[48,3584]{1,0:T(8,128)(2,1)}, u32[]{:S(2)}, u32[]{:S(2)}) collective-permute-start(bf16[48,3584]{1,0:T(8,128)(2,1)} %get-tuple-element.277), channel_id=1, source_target_pairs={{0,3},{1,2},{2,1},{3,0},{4,7},{5,6},{6,5},{7,4},{8,11},{9,10},{10,... | collective-permute-start | bytes 1032200 | tf_op jit(solution)/shard_map/ppermute | solution.py:242
  241.1 24.2 %copy-start.4 = (bf16[128,3584]{1,0:T(8,128)(2,1)S(1)}, bf16[128,3584]{1,0:T(8,128)(2,1)}, u32[]{:S(2)}) copy-start(bf16[128,3584]{1,0:T(8,128)(2,1)} %shard_map.162) | copy-start | bytes 2752516
  241.1 24.2 %collective-permute-start.27 = (bf16[128,3584]{1,0:T(8,128)(2,1)}, bf16[128,3584]{1,0:T(8,128)(2,1)S(1)}, u32[]{:S(2)}, u32[]{:S(2)}) collective-permute-start(bf16[128,3584]{1,0:T(8,128)(2,1)} %shard_map.164), channel_id=1, source_target_pairs={{0,4},{1,5},{2,6},{3,7},{12,8},{13,9},{14,10},{15,11},{16,20},{17,... | collective-permute-start | bytes 2752520 | tf_op jit(solution)/shard_map/ppermute | solution.py:242
  244.8 69.8 %collective-permute-start.26 = (bf16[128,3584]{1,0:T(8,128)(2,1)}, bf16[128,3584]{1,0:T(8,128)(2,1)}, u32[]{:S(2)}, u32[]{:S(2)}) collective-permute-start(bf16[128,3584]{1,0:T(8,128)(2,1)} %shard_map.164), channel_id=1, source_target_pairs={{4,8},{5,9},{6,10},{7,11},{8,4},{9,5},{10,6},{11,7},{20,24},{21,25... | collective-permute-start | bytes 2752520 | tf_op jit(solution)/shard_map/ppermute | solution.py:242
  257.1 57.5 %collective-permute-start.32 = (bf16[128,3584]{1,0:T(8,128)(2,1)}, bf16[128,3584]{1,0:T(8,128)(2,1)}, u32[]{:S(2)}, u32[]{:S(2)}) collective-permute-start(bf16[128,3584]{1,0:T(8,128)(2,1)} %shard_map.165), channel_id=1, source_target_pairs={{4,0},{5,1},{6,2},{7,3},{8,12},{9,13},{10,14},{11,15},{12,4},{13,5... | collective-permute-start | bytes 2752520 | tf_op jit(solution)/shard_map/ppermute | solution.py:242
  266.6 48.0 %collective-permute-start.28 = (bf16[128,3584]{1,0:T(8,128)(2,1)}, bf16[128,3584]{1,0:T(8,128)(2,1)}, u32[]{:S(2)}, u32[]{:S(2)}) collective-permute-start(bf16[128,3584]{1,0:T(8,128)(2,1)} %add_convert_fusion.1), channel_id=1, source_target_pairs={{4,12},{5,13},{6,14},{7,15},{8,0},{9,1},{10,2},{11,3},{20,28},{21,... | collective-permute-start | bytes 2752520 | tf_op jit(solution)/shard_map/ppermute | solution.py:242
  271.1 43.5 %copy-start.3 = (bf16[128,3584]{1,0:T(8,128)(2,1)S(1)}, bf16[128,3584]{1,0:T(8,128)(2,1)}, u32[]{:S(2)}) copy-start(bf16[128,3584]{1,0:T(8,128)(2,1)} %shard_map.159) | copy-start | bytes 2752516
  271.1 42.9 %all-to-all-start.1 = ((f32[16,16,224]{2,1,0:T(8,128)}), f32[16,16,224]{2,1,0:T(8,128)S(1)}, u32[]{:S(2)}, u32[]{:S(2)}) async-start(f32[16,16,224]{2,1,0:T(8,128)} %bitcast.40), calls=%async_computation.1 | async-start | bytes 524288 | tf_op jit(solution)/shard_map/all_to_all | solution.py:397
  (25 other events, 213.6 us)

commit v2 on v1

--- a/solution.py
+++ b/solution.py
@@ -94,27 +94,53 @@
     )(flag, guide, *arrays)
 
 
-def sum_kernel(extra, cap, placed_ref, *refs):
-    pieces, out = refs[:plane], refs[-1]
-    for first, last in chunks(0, out.shape[1], 512):
+def sum_kernel(placed_ref, *refs):
+    pieces, outs = refs[:plane], refs[plane:]
+    for first, last in chunks(0, outs[0].shape[1], 512):
         rows = jnp.concatenate([p[:, first:last] for p in pieces], axis=0)
-        total = dot_tn(placed_ref[...], rows)
-        for more in refs[plane : plane + extra]:
-            total = total + more[:, first:last].astype(f32)
-        out[:, first:last] = total.astype(bf16)
-
-
-def sum_rows(placed, pieces, extra):
+        total = dot_tn(placed_ref[...], rows).astype(bf16)
+        at = 0
+        for out in outs:
+            out[:, first:last] = total[at : at + out.shape[0]]
+            at += out.shape[0]
+
+
+def sum_rows(placed, pieces, parts=1):
     cap, width = pieces[0].shape
     tok = placed.shape[1]
     return pl.pallas_call(
-        functools.partial(sum_kernel, len(extra), cap),
+        sum_kernel,
+        out_shape=[jax.ShapeDtypeStruct((tok // parts, width), bf16)] * parts,
+        in_specs=[vmem] * (1 + plane),
+        out_specs=[vmem] * parts,
+        compiler_params=pltpu.CompilerParams(vmem_limit_bytes=vmem_bytes),
+        cost_estimate=light,
+    )(placed, *pieces)
+
+
+def final_kernel(groups, logit_ref, router_ref, *refs):
+    out = refs[-1]
+    for first, last in chunks(0, out.shape[1], 512):
+        total = dot_nn(logit_ref[...], router_ref[:, first:last])
+        left = refs
+        for count in groups:
+            total = total + jnp.concatenate(
+                [r[:, first:last] for r in left[:count]], axis=0
+            ).astype(f32)
+            left = left[count:]
+        out[:, first:last] = total.astype(bf16)
+
+
+def final_sum(logit, router, terms):
+    tok, width = logit.shape[0], router.shape[1]
+    return pl.pallas_call(
+        functools.partial(final_kernel, [len(t) for t in terms]),
         out_shape=jax.ShapeDtypeStruct((tok, width), bf16),
-        in_specs=[vmem] * (1 + plane + len(extra)),
+        in_specs=[vmem] * (2 + sum(len(t) for t in terms)),
         out_specs=vmem,
         compiler_params=pltpu.CompilerParams(vmem_limit_bytes=vmem_bytes),
         cost_estimate=light,
-    )(placed, *pieces, *extra)
+    )(logit, router, *[a for t in terms for a in t])
 
 
 def expert_kernel(
@@ -324,34 +350,42 @@
             got_1 = spread(sel_1)
             done_0 = run(got_0)
             got_1, done_0, own = join((got_1, done_0, own))
-            block_2f, block_2m, own = join((block_2f, block_2m, own))
+            back_0 = spread(done_0[:plane])
+            block_2f, block_2m, own, back_0[1], back_0[2] = join(
+                (block_2f, block_2m, own, back_0[1], back_0[2])
+            )
             block_3 = send(own, along([(0, 1), (3, 2), (1, 3), (2, 0)]))
             sel_2, placed_2 = take(flag, [block_2m, block_2f])
-            sel_2, back_0, got_1 = join((sel_2, spread(done_0[:plane]), got_1))
+            sel_2, got_1 = join((sel_2, got_1))
             got_2 = spread(sel_2)
             done_1 = run(got_1)
-            part_0 = sum_rows(placed_0, back_0, [])
-            got_2, done_1, part_0 = join((got_2, done_1, part_0))
+            done_1, got_2[1], got_2[2] = join((done_1, got_2[1], got_2[2]))
+            back_1 = spread(done_1[:plane])
             sel_3, placed_3 = take(flag, [block_3])
-            sel_3, back_1, got_2 = join((sel_3, spread(done_1[:plane]), got_2))
+            part_0 = sum_rows(placed_0, back_0)
+            sel_3, back_1, got_2 = join((sel_3, back_1, got_2))
             got_3 = spread(sel_3)
             done_2 = run(got_2)
-            part_1 = sum_rows(placed_1, back_1, [])
-            term_1 = send(part_1, along([(0, 1), (3, 2)]))
-            got_3, done_2, part_1 = join((got_3, done_2, part_1))
+            done_2, got_3[1], got_3[2] = join((done_2, got_3[1], got_3[2]))
             back_2 = spread(done_2[:plane])
+            (part_1,) = sum_rows(placed_1, back_1)
+            term_1 = send(part_1, along([(0, 1), (3, 2), (1, 3), (2, 0)]))
+            got_3, back_2, part_1, part_0 = join((got_3, back_2, part_1, part_0))
+            part_2a, part_2b = sum_rows(placed_2, back_2, 2)
+            term_2a = send(part_2a, across(3 * plane))
             done_3 = run(got_3)
-            back_2, done_3 = join((back_2, done_3))
+            done_3, term_1, term_2a, part_2b = join((done_3, term_1, term_2a, part_2b))
             back_3 = spread(done_3[:plane])
-            part_2 = sum_rows(placed_2, back_2, [])
-            hop = send(part_2, along([(0, 1), (3, 2)]))
-            term_2 = send(part_2, along([(1, 2), (2, 1)]))
-            joined = (part_1.astype(f32) + hop.astype(f32)).astype(bf16)
-            term_3 = send(joined, along([(1, 3), (2, 0)]))
-            part_3 = sum_rows(placed_3, back_3, [])
-            term_4 = send(part_3, along([(1, 0), (2, 3), (3, 1), (0, 2)]))
-            terms = [part_0, term_1, term_2, term_3, term_4]
+            term_2b = send(part_2b, across(3 * plane))
+            aux = done_3[plane:]
+            back_3[1], back_3[2], aux = join((back_3[1], back_3[2], aux))
+            done_3 = [*done_3[:plane], *aux]
+            (part_3,) = sum_rows(placed_3, back_3)
             done = [done_0, done_1, done_2, done_3]
+            part_3, grads = join((part_3, [d[plane + 1 :] for d in done]))
+            done = [[*d[: plane + 1], *g] for d, g in zip(done, grads)]
+            term_3 = send(part_3, along([(1, 0), (2, 3), (3, 1), (0, 2)]))
+            terms = [part_0, [term_1], [term_2a, term_2b], [term_3]]
             counts = [1, 1, 1, 1]
             sources = [
                 layer,
@@ -366,8 +400,8 @@
                 block = own if g == 0 else send(own, across(g * plane))
                 sel, placed = take(flag, [block])
                 result = run(spread(sel))
-                part = sum_rows(placed, spread(result[:plane]), [])
-                terms.append(part if g == 0 else send(part, across(g * plane)))
+                (part,) = sum_rows(placed, spread(result[:plane]))
+                terms.append([part if g == 0 else send(part, across(g * plane))])
                 done.append(result)
                 counts.append(1)
                 sources.append(layer ^ g)
@@ -397,10 +431,7 @@
         router_got = lax.all_to_all(router_part, "expert", split_axis=0, concat_axis=0, tiled=True)
         router_grad = jnp.sum(router_got, axis=0).T
 
-        in_grad = dot_nt(d_logit, router_matrix)
-        for term in terms:
-            in_grad = in_grad + term.astype(f32)
-        in_grad = in_grad.astype(bf16)
+        in_grad = final_sum(d_logit, router_matrix.T, terms)
 
         rank = gate_adapter_second.shape[1]
         grad_a = sum(d[c * plane + 1] for d, c in zip(done, counts))

time: 321 us -> 309 us (0.963)
  starting transfers between devices: 48.4 us -> 37.7 us
  other arithmetic: 15.6 us -> 9.92 us
  Pallas kernels: 114 us -> 118 us
    all_to_all x1, waiting for transfers between devices: 36.2 us -> 17.2 us  [shards(): lax.all_to_all(router_part, 'expert', split_axis=0, concat_axis=0, tiled=...]
    ppermute x33 -> x32, waiting for transfers between devices: 88.7 us -> 107 us  [send(): return lax.ppermute(array, 'expert', pairs)]
    ppermute x33 -> x32, starting transfers between devices: 35.7 us -> 25.9 us  [send(): return lax.ppermute(array, 'expert', pairs)]
    convert_element_type x2 -> x0, other arithmetic: 4.79 us -> none  [the longest x1 3.58 us: shards(): in_grad = in_grad.astype(bf16)]
    pallas_call x4 -> x5, Pallas kernels: 10.9 us -> 14.5 us  [the longest x4 10.8 us: sum_rows(): pl.pallas_call(sum_kernel, out_shape=[jax.ShapeDtypeStruct((tok // parts,...]
    unnamed x76 -> x84, local copies, waits for them, and re-layouts: 3.23 us -> 6.57 us
  transfers between devices with their start and end apart: 35 -> 34, of which waited for: 14 -> 16; matrix products, arithmetic and copies ran while one was open for 5% -> 4% of each run, Pallas kernels for 36% -> 37%
where the time goes in v2:
time: 309 us; the launch traced here: 306 us
  waiting for transfers between devices  124 us (40%)
  Pallas kernels  118 us (38%)
  starting transfers between devices  37.7 us (12%)
  local copies, waits for them, and re-layouts  12.2 us (4%)
  other arithmetic  9.92 us (3%)
  matrix products  3.34 us (1%)
    ppermute x32, waiting for transfers between devices, send(): return lax.ppermute(array, 'expert', pairs)  107 us
    pallas_call x4, Pallas kernels, expert_rows(): pl.pallas_call(functools.partial(expert_kernel, [(0,) * len(p) for p in p...  86.3 us
    ppermute x32, starting transfers between devices, send(): return lax.ppermute(array, 'expert', pairs)  25.9 us
    all_to_all x1, waiting for transfers between devices, shards(): lax.all_to_all(router_part, 'expert', split_axis=0, concat_axis=0, tiled=...  17.2 us
    pallas_call x4, Pallas kernels, select_rows(): pl.pallas_call(functools.partial(select_kernel, parts, meta_at, slots_hel...  17.1 us
    pallas_call x4, Pallas kernels, sum_rows(): pl.pallas_call(sum_kernel, out_shape=[jax.ShapeDtypeStruct((tok // parts,...  10.8 us
    unnamed x84, local copies, waits for them, and re-layouts  6.57 us
  transfers between devices with their start and end apart: 34, of which 16 were waited for; matrix products, arithmetic and copies ran while one was open for 4% of the time, Pallas kernels for 37%

profile of v2, /device:TPU:15, one launch (start us, length us, event | category | flops | bytes accessed | tf_op | source)
XLA Modules:
  0.0 306.3 jit_solution(12767764088637407393)
XLA Ops:
  2.3 2.2 fusion.15
  4.6 2.2 concatenate.13.refs_0_
  8.6 4.1 %shard_map.154 = (bf16[48,7296]{1,0:T(8,128)(2,1)}, bf16[48,7296]{1,0:T(8,128)(2,1)}, bf16[48,7296]{1,0:T(8,128)(2,1)}, bf16[48,7296]{1,0:T(8,128)(2,1)}, bf16[192,128]{1,0:T(8,128)(2,1)}) custom-call(s32[1]{0:T(128)} %bitcast.4.flag_ref, bf16[16,128]{1,0:T(8,128)(2,1)} %pad_convert_fusion.guide_ref, bf16[128,7296]{1,0:T(8,128)(2,1)} %copy-done), custom_call_target="tpu_custom_call" | custom-call | flops 1024 | bytes 1024 | tf_op jit(solution)/shard_map/pallas_call | solution.py:87
  13.8 1.4 collective-permute-start.3
  15.5 15.6 %collective-permute-done.2.refs_2_ = bf16[48,7296]{1,0:T(8,128)(2,1)S(1)} collective-permute-done((bf16[48,7296]{1,0:T(8,128)(2,1)}, bf16[48,7296]{1,0:T(8,128)(2,1)S(1)}, u32[]{:S(2)}, u32[]{:S(2)}) %collective-permute-start.2) | collective-permute-done | bytes 700448 | tf_op jit(solution)/shard_map/ppermute | solution.py:268
  31.2 15.4 %collective-permute-done.3.refs_3_ = bf16[48,7296]{1,0:T(8,128)(2,1)S(1)} collective-permute-done((bf16[48,7296]{1,0:T(8,128)(2,1)}, bf16[48,7296]{1,0:T(8,128)(2,1)S(1)}, u32[]{:S(2)}, u32[]{:S(2)}) %collective-permute-start.3) | collective-permute-done | bytes 700448 | tf_op jit(solution)/shard_map/ppermute | solution.py:268
  46.6 2.9 collective-permute-done.refs_0_
  49.5 1.4 collective-permute-start.7
  50.9 4.2 %collective-permute-start.8 = (bf16[128,7296]{1,0:T(8,128)(2,1)}, bf16[128,7296]{1,0:T(8,128)(2,1)}, u32[]{:S(2)}, u32[]{:S(2)}) collective-permute-start(bf16[128,7296]{1,0:T(8,128)(2,1)} %copy-done), channel_id=1, source_target_pairs={{4,8},{5,9},{6,10},{7,11},{8,4},{9,5},{10,6},{11,7},{20,24},{21,25... | collective-permute-start | bytes 5603336 | tf_op jit(solution)/shard_map/ppermute | solution.py:268
  55.1 4.1 %shard_map.155 = (bf16[48,7296]{1,0:T(8,128)(2,1)}, bf16[48,7296]{1,0:T(8,128)(2,1)}, bf16[48,7296]{1,0:T(8,128)(2,1)}, bf16[48,7296]{1,0:T(8,128)(2,1)}, bf16[192,128]{1,0:T(8,128)(2,1)}) custom-call(s32[1]{0:T(128)} %bitcast.4.flag_ref, bf16[16,128]{1,0:T(8,128)(2,1)} %pad_convert_fusion.guide_ref, bf16[128,7296]{1,0:T(8,128)(2,1)} %collective-permute-done.refs_0_), custom_call_target="tpu_custom_call" | custom-call | flops 1024 | bytes 1024 | tf_op jit(solution)/shard_map/pallas_call | solution.py:87
  59.3 2.1 collective-permute-start.4
  61.6 1.4 collective-permute-start.6
  63.5 21.7 %shard_map.156 = (bf16[48,3584]{1,0:T(8,128)(2,1)}, bf16[48,3584]{1,0:T(8,128)(2,1)}, bf16[48,3584]{1,0:T(8,128)(2,1)}, bf16[48,3584]{1,0:T(8,128)(2,1)}, f32[19...) custom-call(f32[1,128]{1,0:T(1,128)} %compare_convert_fusion.mine_ref, ...), custom_call_target="tpu_custom_call" | custom-call | flops 1024 | bytes 1024 | tf_op jit(solution)/shard_map/pallas_call | solution.py:215
  85.2 9.2 %collective-permute-done.6.refs_3_ = bf16[48,7296]{1,0:T(8,128)(2,1)} collective-permute-done((bf16[48,7296]{1,0:T(8,128)(2,1)}, bf16[48,7296]{1,0:T(8,128)(2,1)}, u32[]{:S(2)}, u32[]{:S(2)}) %collective-permute-start.6) | collective-permute-done | bytes 700448 | tf_op jit(solution)/shard_map/ppermute | solution.py:268
  94.9 9.4 %collective-permute-done.10.refs_2_ = bf16[48,3584]{1,0:T(8,128)(2,1)S(1)} collective-permute-done((bf16[48,3584]{1,0:T(8,128)(2,1)}, bf16[48,3584]{1,0:T(8,128)(2,1)S(1)}, u32[]{:S(2)}, u32[]{:S(2)}) %collective-permute-start.10) | collective-permute-done | bytes 344096 | tf_op jit(solution)/shard_map/ppermute | solution.py:268
  105.4 1.0 copy-done.3
  106.4 4.7 %shard_map.157 = (bf16[48,7296]{1,0:T(8,128)(2,1)}, bf16[48,7296]{1,0:T(8,128)(2,1)}, bf16[48,7296]{1,0:T(8,128)(2,1)}, bf16[48,7296]{1,0:T(8,128)(2,1)}, bf16[192,128]{1,0:T(8,128)(2,1)}) custom-call(s32[1]{0:T(128)} %bitcast.4.flag_ref, bf16[16,128]{1,0:T(8,128)(2,1)} %pad_convert_fusion.guide_ref, bf16[128,7296]{1,0:T(8,128)(2,1)} %collective-permute-done.8.refs_0_, ...), custom_call_target="tpu_custom_call" | custom-call | flops 1024 | bytes 1024 | tf_op jit(solution)/shard_map/pallas_call | solution.py:87
  112.1 1.4 collective-permute-start.17
  113.5 21.5 %shard_map.158 = (bf16[48,3584]{1,0:T(8,128)(2,1)}, bf16[48,3584]{1,0:T(8,128)(2,1)}, bf16[48,3584]{1,0:T(8,128)(2,1)}, bf16[48,3584]{1,0:T(8,128)(2,1)}, f32[19...) custom-call(f32[1,128]{1,0:T(1,128)} %compare_convert_fusion.mine_ref, ...), custom_call_target="tpu_custom_call" | custom-call | flops 1024 | bytes 1024 | tf_op jit(solution)/shard_map/pallas_call | solution.py:215
  135.6 1.7 collective-permute-start.16
  137.3 9.6 %collective-permute-done.13.refs_0_ = bf16[128,7296]{1,0:T(8,128)(2,1)S(1)} collective-permute-done((bf16[128,7296]{1,0:T(8,128)(2,1)S(1)}, bf16[128,7296]{1,0:T(8,128)(2,1)S(1)}, u32[]{:S(2)}, u32[]{:S(2)}) %collective-permute-start.13) | collective-permute-done | bytes 1867808 | tf_op jit(solution)/shard_map/ppermute | solution.py:268
  146.9 1.3 copy-done.4
  148.1 4.1 %shard_map.159 = (bf16[48,7296]{1,0:T(8,128)(2,1)}, bf16[48,7296]{1,0:T(8,128)(2,1)}, bf16[48,7296]{1,0:T(8,128)(2,1)}, bf16[48,7296]{1,0:T(8,128)(2,1)}, bf16[192,128]{1,0:T(8,128)(2,1)}) custom-call(s32[1]{0:T(128)} %bitcast.4.flag_ref, bf16[16,128]{1,0:T(8,128)(2,1)} %pad_convert_fusion.guide_ref, bf16[128,7296]{1,0:T(8,128)(2,1)} %copy-done.4), custom_call_target="tpu_custom_call" | custom-call | flops 1024 | bytes 1024 | tf_op jit(solution)/shard_map/pallas_call | solution.py:87
  152.3 7.0 %collective-permute-done.16.refs_3_ = bf16[48,3584]{1,0:T(8,128)(2,1)S(1)} collective-permute-done((bf16[48,3584]{1,0:T(8,128)(2,1)}, bf16[48,3584]{1,0:T(8,128)(2,1)S(1)}, u32[]{:S(2)}, u32[]{:S(2)}) %collective-permute-start.16) | collective-permute-done | bytes 344096 | tf_op jit(solution)/shard_map/ppermute | solution.py:268
  160.5 1.6 collective-permute-start.20
  162.3 2.7 shard_map.161
  165.2 21.5 %shard_map.160 = (bf16[48,3584]{1,0:T(8,128)(2,1)}, bf16[48,3584]{1,0:T(8,128)(2,1)}, bf16[48,3584]{1,0:T(8,128)(2,1)}, bf16[48,3584]{1,0:T(8,128)(2,1)}, f32[19...) custom-call(f32[1,128]{1,0:T(1,128)} %compare_convert_fusion.mine_ref, ...), custom_call_target="tpu_custom_call" | custom-call | flops 1024 | bytes 1024 | tf_op jit(solution)/shard_map/pallas_call | solution.py:215
  187.6 1.3 collective-permute-start.22
  188.8 12.1 %collective-permute-done.24.refs_3_ = bf16[48,3584]{1,0:T(8,128)(2,1)S(1)} collective-permute-done((bf16[48,3584]{1,0:T(8,128)(2,1)}, bf16[48,3584]{1,0:T(8,128)(2,1)S(1)}, u32[]{:S(2)}, u32[]{:S(2)}) %collective-permute-start.24) | collective-permute-done | bytes 344096 | tf_op jit(solution)/shard_map/ppermute | solution.py:268
  201.7 2.7 shard_map.162.refs_0_
  204.4 2.9 collective-permute-done.22.refs_2_
  207.4 7.7 %collective-permute-done.23.refs_3_ = bf16[48,3584]{1,0:T(8,128)(2,1)S(1)} collective-permute-done((bf16[48,3584]{1,0:T(8,128)(2,1)}, bf16[48,3584]{1,0:T(8,128)(2,1)S(1)}, u32[]{:S(2)}, u32[]{:S(2)}) %collective-permute-start.23) | collective-permute-done | bytes 344096 | tf_op jit(solution)/shard_map/ppermute | solution.py:268
  215.8 2.7 shard_map.164
  218.9 21.6 %shard_map.163 = (bf16[48,3584]{1,0:T(8,128)(2,1)}, bf16[48,3584]{1,0:T(8,128)(2,1)}, bf16[48,3584]{1,0:T(8,128)(2,1)}, bf16[48,3584]{1,0:T(8,128)(2,1)}, f32[19...) custom-call(f32[1,128]{1,0:T(1,128)} %compare_convert_fusion.mine_ref, ...), custom_call_target="tpu_custom_call" | custom-call | flops 1024 | bytes 1024 | tf_op jit(solution)/shard_map/pallas_call | solution.py:215
  241.8 1.4 collective-permute-start.30
  243.8 1.1 collective-permute-start.29
  244.9 6.7 %collective-permute-done.28.refs_2_ = bf16[48,3584]{1,0:T(8,128)(2,1)} collective-permute-done((bf16[48,3584]{1,0:T(8,128)(2,1)}, bf16[48,3584]{1,0:T(8,128)(2,1)}, u32[]{:S(2)}, u32[]{:S(2)}) %collective-permute-start.28) | collective-permute-done | bytes 344096 | tf_op jit(solution)/shard_map/ppermute | solution.py:268
  251.5 7.7 %collective-permute-done.30.refs_3_ = bf16[48,3584]{1,0:T(8,128)(2,1)} collective-permute-done((bf16[48,3584]{1,0:T(8,128)(2,1)}, bf16[48,3584]{1,0:T(8,128)(2,1)}, u32[]{:S(2)}, u32[]{:S(2)}) %collective-permute-start.30) | collective-permute-done | bytes 344096 | tf_op jit(solution)/shard_map/ppermute | solution.py:268
  259.2 2.7 shard_map.165
  262.8 5.8 %all-to-all-start = ((bf16[16,1,48]{2,1,0:T(2,128)(2,1)}), bf16[16,1,48]{2,1,0:T(2,128)(2,1)S(1)}, u32[]{:S(2)}, u32[]{:S(2)}) async-start(bf16[16,1,48]{2,1,0:T(2,128)(2,1)} %copy.49), calls=%async_computation | async-start | bytes 16384 | tf_op jit(solution)/shard_map/all_to_all | solution.py:418
  268.6 2.2 add_add_fusion
  270.8 1.0 slice_bitcast_fusion
  273.4 0.9 copy.61
  274.3 6.1 %all-to-all-start.1 = ((f32[16,16,224]{2,1,0:T(8,128)}), f32[16,16,224]{2,1,0:T(8,128)S(1)}, u32[]{:S(2)}, u32[]{:S(2)}) async-start(f32[16,16,224]{2,1,0:T(8,128)} %bitcast.39), calls=%async_computation.1 | async-start | bytes 524288 | tf_op jit(solution)/shard_map/all_to_all | solution.py:431
  280.4 1.7 add_bitcast_fusion
  282.0 1.7 add_bitcast_fusion.1
  283.7 17.2 %all-to-all-done.1 = f32[16,16,224]{2,1,0:T(8,128)S(1)} async-done(((f32[16,16,224]{2,1,0:T(8,128)}), f32[16,16,224]{2,1,0:T(8,128)S(1)}, u32[]{:S(2)}, u32[]{:S(2)}) %all-to-all-start.1) | async-done | bytes 229408 | tf_op jit(solution)/shard_map/all_to_all | solution.py:431
  302.7 3.7 %shard_map.166 = bf16[128,3584]{1,0:T(8,128)(2,1)} custom-call(bf16[128,16]{1,0:T(8,128)(2,1)} %copy-done.28, bf16[16,3584]{1,0:T(8,128)(2,1)} %bitcast.68, bf16[128,3584]{1,0:T(8,128)(2,1)} %shard_map.162.refs_0_, bf16[128,3584]{1,0:T(8,128)(2,1)} %copy-done.5, bf16[64,3584]{1,0:T(8,128)(2,1)} %copy-done.17, bf16[64,3584]{1,0:T(8,128)(2,1)} %copy-done.18, ...), custom_call_target="tpu_custom_call" | custom-call | flops 1024 | bytes 1024 | tf_op jit(solution)/shard_map/pallas_call | solution.py:136
  (159 shorter events, 19.1 us)
Async XLA Ops:
  6.9 42.6 %collective-permute-start = (bf16[128,7296]{1,0:T(8,128)(2,1)S(1)}, bf16[128,7296]{1,0:T(8,128)(2,1)}, u32[]{:S(2)}, u32[]{:S(2)}) collective-permute-start(bf16[128,7296]{1,0:T(8,128)(2,1)S(1)} %concatenate.13.refs_0_), channel_id=1, source_target_pairs={{0,8},{1,9},{2,10},{3,11},{12,4},{13,5},{14,6},{15,7},{4,0},{5,1},... | collective-permute-start | bytes 5603336 | tf_op jit(solution)/shard_map/ppermute | solution.py:268
  12.7 2.8 collective-permute-start.1
  13.5 17.6 %collective-permute-start.2 = (bf16[48,7296]{1,0:T(8,128)(2,1)}, bf16[48,7296]{1,0:T(8,128)(2,1)S(1)}, u32[]{:S(2)}, u32[]{:S(2)}) collective-permute-start(bf16[48,7296]{1,0:T(8,128)(2,1)} %get-tuple-element.177), channel_id=1, source_target_pairs={{0,2},{1,3},{2,0},{3,1},{4,6},{5,7},{6,4},{7,5},{8,10},{9,11},{10,... | collective-permute-start | bytes 2101256 | tf_op jit(solution)/shard_map/ppermute | solution.py:268
  13.8 32.8 %collective-permute-start.3 = (bf16[48,7296]{1,0:T(8,128)(2,1)}, bf16[48,7296]{1,0:T(8,128)(2,1)S(1)}, u32[]{:S(2)}, u32[]{:S(2)}) collective-permute-start(bf16[48,7296]{1,0:T(8,128)(2,1)} %get-tuple-element.178), channel_id=1, source_target_pairs={{0,3},{1,2},{2,1},{3,0},{4,7},{5,6},{6,5},{7,4},{8,11},{9,10},{10,... | collective-permute-start | bytes 2101256 | tf_op jit(solution)/shard_map/ppermute | solution.py:268
  15.5 34.0 %copy-start.14 = (bf16[48,7296]{1,0:T(8,128)(2,1)}, bf16[48,7296]{1,0:T(8,128)(2,1)S(1)}, u32[]{:S(2)}) copy-start(bf16[48,7296]{1,0:T(8,128)(2,1)S(1)} %collective-permute-done.1.refs_1_) | copy-start | bytes 2101252
  31.2 18.3 %copy-start.15 = (bf16[48,7296]{1,0:T(8,128)(2,1)}, bf16[48,7296]{1,0:T(8,128)(2,1)S(1)}, u32[]{:S(2)}) copy-start(bf16[48,7296]{1,0:T(8,128)(2,1)S(1)} %collective-permute-done.2.refs_2_) | copy-start | bytes 2101252
  49.5 54.8 %collective-permute-start.7 = (bf16[128,7296]{1,0:T(8,128)(2,1)}, bf16[128,7296]{1,0:T(8,128)(2,1)S(1)}, u32[]{:S(2)}, u32[]{:S(2)}) collective-permute-start(bf16[128,7296]{1,0:T(8,128)(2,1)} %collective-permute-done.refs_0_), channel_id=1, source_target_pairs={{4,0},{5,1},{6,2},{7,3},{8,12},{9,13},{10,14},{11,15},{20,16},{21,... | collective-permute-start | bytes 5603336 | tf_op jit(solution)/shard_map/ppermute | solution.py:268
  50.9 54.2 %collective-permute-start.8 = (bf16[128,7296]{1,0:T(8,128)(2,1)}, bf16[128,7296]{1,0:T(8,128)(2,1)}, u32[]{:S(2)}, u32[]{:S(2)}) collective-permute-start(bf16[128,7296]{1,0:T(8,128)(2,1)} %copy-done), channel_id=1, source_target_pairs={{4,8},{5,9},{6,10},{7,11},{8,4},{9,5},{10,6},{11,7},{20,24},{21,25... | collective-permute-start | bytes 5603336 | tf_op jit(solution)/shard_map/ppermute | solution.py:268
  59.3 26.0 %collective-permute-start.4 = (bf16[48,7296]{1,0:T(8,128)(2,1)}, bf16[48,7296]{1,0:T(8,128)(2,1)S(1)}, u32[]{:S(2)}, u32[]{:S(2)}) collective-permute-start(bf16[48,7296]{1,0:T(8,128)(2,1)} %get-tuple-element.181), channel_id=1, source_target_pairs={{0,1},{1,0},{2,3},{3,2},{4,5},{5,4},{6,7},{7,6},{8,9},{9,8},{10,11... | collective-permute-start | bytes 2101256 | tf_op jit(solution)/shard_map/ppermute | solution.py:268
  61.4 23.9 %collective-permute-start.5 = (bf16[48,7296]{1,0:T(8,128)(2,1)}, bf16[48,7296]{1,0:T(8,128)(2,1)}, u32[]{:S(2)}, u32[]{:S(2)}) collective-permute-start(bf16[48,7296]{1,0:T(8,128)(2,1)} %get-tuple-element.182), channel_id=1, source_target_pairs={{0,2},{1,3},{2,0},{3,1},{4,6},{5,7},{6,4},{7,5},{8,10},{9,11},{10,... | collective-permute-start | bytes 2101256 | tf_op jit(solution)/shard_map/ppermute | solution.py:268
  61.6 32.8 %collective-permute-start.6 = (bf16[48,7296]{1,0:T(8,128)(2,1)}, bf16[48,7296]{1,0:T(8,128)(2,1)}, u32[]{:S(2)}, u32[]{:S(2)}) collective-permute-start(bf16[48,7296]{1,0:T(8,128)(2,1)} %get-tuple-element.183), channel_id=1, source_target_pairs={{0,3},{1,2},{2,1},{3,0},{4,7},{5,6},{6,5},{7,4},{8,11},{9,10},{10,... | collective-permute-start | bytes 2101256 | tf_op jit(solution)/shard_map/ppermute | solution.py:268
  63.5 41.6 %copy-start.1 = (bf16[128,7296]{1,0:T(8,128)(2,1)S(1)}, bf16[128,7296]{1,0:T(8,128)(2,1)}, u32[]{:S(2)}) copy-start(bf16[128,7296]{1,0:T(8,128)(2,1)} %copy-done) | copy-start | bytes 5603332
  85.2 28.3 %copy-start.13 = (bf16[48,7296]{1,0:T(8,128)(2,1)}, bf16[48,7296]{1,0:T(8,128)(2,1)S(1)}, u32[]{:S(2)}) copy-start(bf16[48,7296]{1,0:T(8,128)(2,1)S(1)} %collective-permute-done.4.refs_1_) | copy-start | bytes 2101252
  94.4 9.9 %collective-permute-start.10 = (bf16[48,3584]{1,0:T(8,128)(2,1)}, bf16[48,3584]{1,0:T(8,128)(2,1)S(1)}, u32[]{:S(2)}, u32[]{:S(2)}) collective-permute-start(bf16[48,3584]{1,0:T(8,128)(2,1)} %get-tuple-element.200), channel_id=1, source_target_pairs={{0,2},{1,3},{2,0},{3,1},{4,6},{5,7},{6,4},{7,5},{8,10},{9,11},{10,... | collective-permute-start | bytes 1032200 | tf_op jit(solution)/shard_map/ppermute | solution.py:268
  94.6 9.7 %collective-permute-start.9 = (bf16[48,3584]{1,0:T(8,128)(2,1)}, bf16[48,3584]{1,0:T(8,128)(2,1)S(1)}, u32[]{:S(2)}, u32[]{:S(2)}) collective-permute-start(bf16[48,3584]{1,0:T(8,128)(2,1)} %get-tuple-element.199), channel_id=1, source_target_pairs={{0,1},{1,0},{2,3},{3,2},{4,5},{5,4},{6,7},{7,6},{8,9},{9,8},{10,11... | collective-permute-start | bytes 1032200 | tf_op jit(solution)/shard_map/ppermute | solution.py:268
  105.2 41.7 %collective-permute-start.13 = (bf16[128,7296]{1,0:T(8,128)(2,1)S(1)}, bf16[128,7296]{1,0:T(8,128)(2,1)S(1)}, u32[]{:S(2)}, u32[]{:S(2)}) collective-permute-start(bf16[128,7296]{1,0:T(8,128)(2,1)S(1)} %copy-done.1), channel_id=1, source_target_pairs={{0,4},{1,5},{2,6},{3,7},{12,8},{13,9},{14,10},{15,11},{4,12},{5,13... | collective-permute-start | bytes 5603336 | tf_op jit(solution)/shard_map/ppermute | solution.py:268
  111.1 23.9 %collective-permute-start.11 = (bf16[48,7296]{1,0:T(8,128)(2,1)}, bf16[48,7296]{1,0:T(8,128)(2,1)S(1)}, u32[]{:S(2)}, u32[]{:S(2)}) collective-permute-start(bf16[48,7296]{1,0:T(8,128)(2,1)} %get-tuple-element.223), channel_id=1, source_target_pairs={{0,1},{1,0},{2,3},{3,2},{4,5},{5,4},{6,7},{7,6},{8,9},{9,8},{10,11... | collective-permute-start | bytes 2101256 | tf_op jit(solution)/shard_map/ppermute | solution.py:268
  111.9 23.2 %collective-permute-start.12 = (bf16[48,7296]{1,0:T(8,128)(2,1)}, bf16[48,7296]{1,0:T(8,128)(2,1)S(1)}, u32[]{:S(2)}, u32[]{:S(2)}) collective-permute-start(bf16[48,7296]{1,0:T(8,128)(2,1)} %get-tuple-element.224), channel_id=1, source_target_pairs={{0,2},{1,3},{2,0},{3,1},{4,6},{5,7},{6,4},{7,5},{8,10},{9,11},{10,... | collective-permute-start | bytes 2101256 | tf_op jit(solution)/shard_map/ppermute | solution.py:268
  112.1 40.1 %collective-permute-start.17 = (bf16[48,7296]{1,0:T(8,128)(2,1)}, bf16[48,7296]{1,0:T(8,128)(2,1)S(1)}, u32[]{:S(2)}, u32[]{:S(2)}) collective-permute-start(bf16[48,7296]{1,0:T(8,128)(2,1)} %get-tuple-element.238), channel_id=1, source_target_pairs={{0,3},{1,2},{2,1},{3,0},{4,7},{5,6},{6,5},{7,4},{8,11},{9,10},{10,... | collective-permute-start | bytes 2101256 | tf_op jit(solution)/shard_map/ppermute | solution.py:268
  135.1 30.1 %copy-start.10 = (bf16[48,7296]{1,0:T(8,128)(2,1)}, bf16[48,7296]{1,0:T(8,128)(2,1)S(1)}, u32[]{:S(2)}) copy-start(bf16[48,7296]{1,0:T(8,128)(2,1)S(1)} %collective-permute-done.11.refs_1_) | copy-start | bytes 2101252
  135.1 27.2 %copy-start.11 = (bf16[48,7296]{1,0:T(8,128)(2,1)}, bf16[48,7296]{1,0:T(8,128)(2,1)S(1)}, u32[]{:S(2)}) copy-start(bf16[48,7296]{1,0:T(8,128)(2,1)S(1)} %collective-permute-done.12.refs_2_) | copy-start | bytes 2101252
  135.1 17.2 %collective-permute-start.14 = (bf16[48,3584]{1,0:T(8,128)(2,1)}, bf16[48,3584]{1,0:T(8,128)(2,1)S(1)}, u32[]{:S(2)}, u32[]{:S(2)}) collective-permute-start(bf16[48,3584]{1,0:T(8,128)(2,1)} %get-tuple-element.232), channel_id=1, source_target_pairs={{0,1},{1,0},{2,3},{3,2},{4,5},{5,4},{6,7},{7,6},{8,9},{9,8},{10,11... | collective-permute-start | bytes 1032200 | tf_op jit(solution)/shard_map/ppermute | solution.py:268
  135.4 16.9 %collective-permute-start.15 = (bf16[48,3584]{1,0:T(8,128)(2,1)}, bf16[48,3584]{1,0:T(8,128)(2,1)S(1)}, u32[]{:S(2)}, u32[]{:S(2)}) collective-permute-start(bf16[48,3584]{1,0:T(8,128)(2,1)} %get-tuple-element.233), channel_id=1, source_target_pairs={{0,2},{1,3},{2,0},{3,1},{4,6},{5,7},{6,4},{7,5},{8,10},{9,11},{10,... | collective-permute-start | bytes 1032200 | tf_op jit(solution)/shard_map/ppermute | solution.py:268
  135.6 23.7 %collective-permute-start.16 = (bf16[48,3584]{1,0:T(8,128)(2,1)}, bf16[48,3584]{1,0:T(8,128)(2,1)S(1)}, u32[]{:S(2)}, u32[]{:S(2)}) collective-permute-start(bf16[48,3584]{1,0:T(8,128)(2,1)} %get-tuple-element.234), channel_id=1, source_target_pairs={{0,3},{1,2},{2,1},{3,0},{4,7},{5,6},{6,5},{7,4},{8,11},{9,10},{10,... | collective-permute-start | bytes 1032200 | tf_op jit(solution)/shard_map/ppermute | solution.py:268
  160.0 26.7 %collective-permute-start.18 = (bf16[48,7296]{1,0:T(8,128)(2,1)}, bf16[48,7296]{1,0:T(8,128)(2,1)S(1)}, u32[]{:S(2)}, u32[]{:S(2)}) collective-permute-start(bf16[48,7296]{1,0:T(8,128)(2,1)} %get-tuple-element.251), channel_id=1, source_target_pairs={{0,1},{1,0},{2,3},{3,2},{4,5},{5,4},{6,7},{7,6},{8,9},{9,8},{10,11... | collective-permute-start | bytes 2101256 | tf_op jit(solution)/shard_map/ppermute | solution.py:268
  160.3 26.4 %collective-permute-start.19 = (bf16[48,7296]{1,0:T(8,128)(2,1)}, bf16[48,7296]{1,0:T(8,128)(2,1)S(1)}, u32[]{:S(2)}, u32[]{:S(2)}) collective-permute-start(bf16[48,7296]{1,0:T(8,128)(2,1)} %get-tuple-element.252), channel_id=1, source_target_pairs={{0,2},{1,3},{2,0},{3,1},{4,6},{5,7},{6,4},{7,5},{8,10},{9,11},{10,... | collective-permute-start | bytes 2101256 | tf_op jit(solution)/shard_map/ppermute | solution.py:268
  160.5 43.9 %collective-permute-start.20 = (bf16[48,7296]{1,0:T(8,128)(2,1)}, bf16[48,7296]{1,0:T(8,128)(2,1)S(1)}, u32[]{:S(2)}, u32[]{:S(2)}) collective-permute-start(bf16[48,7296]{1,0:T(8,128)(2,1)} %get-tuple-element.257), channel_id=1, source_target_pairs={{0,3},{1,2},{2,1},{3,0},{4,7},{5,6},{6,5},{7,4},{8,11},{9,10},{10,... | collective-permute-start | bytes 2101256 | tf_op jit(solution)/shard_map/ppermute | solution.py:268
  162.1 38.8 %collective-permute-start.24 = (bf16[48,3584]{1,0:T(8,128)(2,1)}, bf16[48,3584]{1,0:T(8,128)(2,1)S(1)}, u32[]{:S(2)}, u32[]{:S(2)}) collective-permute-start(bf16[48,3584]{1,0:T(8,128)(2,1)} %get-tuple-element.271), channel_id=1, source_target_pairs={{0,3},{1,2},{2,1},{3,0},{4,7},{5,6},{6,5},{7,4},{8,11},{9,10},{10,... | collective-permute-start | bytes 1032200 | tf_op jit(solution)/shard_map/ppermute | solution.py:268
  165.0 75.6 %collective-permute-start.25 = (bf16[128,3584]{1,0:T(8,128)(2,1)}, bf16[128,3584]{1,0:T(8,128)(2,1)S(1)}, u32[]{:S(2)}, u32[]{:S(2)}) collective-permute-start(bf16[128,3584]{1,0:T(8,128)(2,1)} %shard_map.161), channel_id=1, source_target_pairs={{0,4},{1,5},{2,6},{3,7},{12,8},{13,9},{14,10},{15,11},{4,12},{5,13... | collective-permute-start | bytes 2752520 | tf_op jit(solution)/shard_map/ppermute | solution.py:268
  186.7 31.7 %copy-start.7 = (bf16[48,7296]{1,0:T(8,128)(2,1)}, bf16[48,7296]{1,0:T(8,128)(2,1)S(1)}, u32[]{:S(2)}) copy-start(bf16[48,7296]{1,0:T(8,128)(2,1)S(1)} %collective-permute-done.18.refs_1_) | copy-start | bytes 2101252
  186.7 31.7 %copy-start.8 = (bf16[48,7296]{1,0:T(8,128)(2,1)}, bf16[48,7296]{1,0:T(8,128)(2,1)S(1)}, u32[]{:S(2)}) copy-start(bf16[48,7296]{1,0:T(8,128)(2,1)S(1)} %collective-permute-done.19.refs_2_) | copy-start | bytes 2101252
  186.8 17.7 %collective-permute-start.21 = (bf16[48,3584]{1,0:T(8,128)(2,1)}, bf16[48,3584]{1,0:T(8,128)(2,1)S(1)}, u32[]{:S(2)}, u32[]{:S(2)}) collective-permute-start(bf16[48,3584]{1,0:T(8,128)(2,1)} %get-tuple-element.259), channel_id=1, source_target_pairs={{0,1},{1,0},{2,3},{3,2},{4,5},{5,4},{6,7},{7,6},{8,9},{9,8},{10,11... | collective-permute-start | bytes 1032200 | tf_op jit(solution)/shard_map/ppermute | solution.py:268
  187.6 19.8 %collective-permute-start.22 = (bf16[48,3584]{1,0:T(8,128)(2,1)}, bf16[48,3584]{1,0:T(8,128)(2,1)S(1)}, u32[]{:S(2)}, u32[]{:S(2)}) collective-permute-start(bf16[48,3584]{1,0:T(8,128)(2,1)} %get-tuple-element.260), channel_id=1, source_target_pairs={{0,2},{1,3},{2,0},{3,1},{4,6},{5,7},{6,4},{7,5},{8,10},{9,11},{10,... | collective-permute-start | bytes 1032200 | tf_op jit(solution)/shard_map/ppermute | solution.py:268
  200.9 14.1 %collective-permute-start.23 = (bf16[48,3584]{1,0:T(8,128)(2,1)}, bf16[48,3584]{1,0:T(8,128)(2,1)S(1)}, u32[]{:S(2)}, u32[]{:S(2)}) collective-permute-start(bf16[48,3584]{1,0:T(8,128)(2,1)} %get-tuple-element.261), channel_id=1, source_target_pairs={{0,3},{1,2},{2,1},{3,0},{4,7},{5,6},{6,5},{7,4},{8,11},{9,10},{10,... | collective-permute-start | bytes 1032200 | tf_op jit(solution)/shard_map/ppermute | solution.py:268
  218.5 22.2 %collective-permute-start.26 = (bf16[64,3584]{1,0:T(8,128)(2,1)}, bf16[64,3584]{1,0:T(8,128)(2,1)S(1)}, u32[]{:S(2)}, u32[]{:S(2)}) collective-permute-start(bf16[64,3584]{1,0:T(8,128)(2,1)} %get-tuple-element.289), channel_id=1, source_target_pairs={{0,12},{1,13},{2,14},{3,15},{4,8},{5,9},{6,10},{7,11},{8,4},{9,5},... | collective-permute-start | bytes 1376264 | tf_op jit(solution)/shard_map/ppermute | solution.py:268
  218.9 24.3 %copy-start.36 = (f32[192,1]{1,0:T(8,128)S(1)}, f32[192,1]{1,0:T(8,128)}, u32[]{:S(2)}) copy-start(f32[192,1]{1,0:T(8,128)} %get-tuple-element.197) | copy-start | bytes 2308
  218.9 24.5 %copy-start.37 = (f32[192,1]{1,0:T(8,128)S(1)}, f32[192,1]{1,0:T(8,128)}, u32[]{:S(2)}) copy-start(f32[192,1]{1,0:T(8,128)} %get-tuple-element.225) | copy-start | bytes 2308
  218.9 24.7 %copy-start.38 = (f32[192,1]{1,0:T(8,128)S(1)}, f32[192,1]{1,0:T(8,128)}, u32[]{:S(2)}) copy-start(f32[192,1]{1,0:T(8,128)} %get-tuple-element.253) | copy-start | bytes 2308
  240.5 21.4 %copy-start.39 = (f32[192,1]{1,0:T(8,128)S(1)}, f32[192,1]{1,0:T(8,128)}, u32[]{:S(2)}) copy-start(f32[192,1]{1,0:T(8,128)} %get-tuple-element.297) | copy-start | bytes 2308
  240.5 30.3 %copy-start.5 = (bf16[128,3584]{1,0:T(8,128)(2,1)}, bf16[128,3584]{1,0:T(8,128)(2,1)S(1)}, u32[]{:S(2)}) copy-start(bf16[128,3584]{1,0:T(8,128)(2,1)S(1)} %collective-permute-done.25.refs_1_) | copy-start | bytes 2752516
  240.7 30.1 %copy-start.17 = (bf16[64,3584]{1,0:T(8,128)(2,1)}, bf16[64,3584]{1,0:T(8,128)(2,1)S(1)}, u32[]{:S(2)}) copy-start(bf16[64,3584]{1,0:T(8,128)(2,1)S(1)} %collective-permute-done.26.refs_2_) | copy-start | bytes 1376260
  240.7 4.2 %collective-permute-start.27 = (bf16[48,3584]{1,0:T(8,128)(2,1)}, bf16[48,3584]{1,0:T(8,128)(2,1)}, u32[]{:S(2)}, u32[]{:S(2)}) collective-permute-start(bf16[48,3584]{1,0:T(8,128)(2,1)} %get-tuple-element.291), channel_id=1, source_target_pairs={{0,1},{1,0},{2,3},{3,2},{4,5},{5,4},{6,7},{7,6},{8,9},{9,8},{10,11... | collective-permute-start | bytes 1032200 | tf_op jit(solution)/shard_map/ppermute | solution.py:268
  241.5 10.0 %collective-permute-start.28 = (bf16[48,3584]{1,0:T(8,128)(2,1)}, bf16[48,3584]{1,0:T(8,128)(2,1)}, u32[]{:S(2)}, u32[]{:S(2)}) collective-permute-start(bf16[48,3584]{1,0:T(8,128)(2,1)} %get-tuple-element.292), channel_id=1, source_target_pairs={{0,2},{1,3},{2,0},{3,1},{4,6},{5,7},{6,4},{7,5},{8,10},{9,11},{10,... | collective-permute-start | bytes 1032200 | tf_op jit(solution)/shard_map/ppermute | solution.py:268
  241.8 17.4 %collective-permute-start.30 = (bf16[48,3584]{1,0:T(8,128)(2,1)}, bf16[48,3584]{1,0:T(8,128)(2,1)}, u32[]{:S(2)}, u32[]{:S(2)}) collective-permute-start(bf16[48,3584]{1,0:T(8,128)(2,1)} %get-tuple-element.306), channel_id=1, source_target_pairs={{0,3},{1,2},{2,1},{3,0},{4,7},{5,6},{6,5},{7,4},{8,11},{9,10},{10,... | collective-permute-start | bytes 1032200 | tf_op jit(solution)/shard_map/ppermute | solution.py:268
  243.8 57.7 %collective-permute-start.29 = (bf16[64,3584]{1,0:T(8,128)(2,1)}, bf16[64,3584]{1,0:T(8,128)(2,1)S(1)}, u32[]{:S(2)}, u32[]{:S(2)}) collective-permute-start(bf16[64,3584]{1,0:T(8,128)(2,1)} %get-tuple-element.301), channel_id=1, source_target_pairs={{0,12},{1,13},{2,14},{3,15},{4,8},{5,9},{6,10},{7,11},{8,4},{9,5},... | collective-permute-start | bytes 1376264 | tf_op jit(solution)/shard_map/ppermute | solution.py:268
  262.8 9.5 %all-to-all-start = ((bf16[16,1,48]{2,1,0:T(2,128)(2,1)}), bf16[16,1,48]{2,1,0:T(2,128)(2,1)S(1)}, u32[]{:S(2)}, u32[]{:S(2)}) async-start(bf16[16,1,48]{2,1,0:T(2,128)(2,1)} %copy.49), calls=%async_computation | async-start | bytes 16384 | tf_op jit(solution)/shard_map/all_to_all | solution.py:418
  271.8 29.7 %collective-permute-start.31 = (bf16[128,3584]{1,0:T(8,128)(2,1)}, bf16[128,3584]{1,0:T(8,128)(2,1)S(1)}, u32[]{:S(2)}, u32[]{:S(2)}) collective-permute-start(bf16[128,3584]{1,0:T(8,128)(2,1)} %shard_map.165), channel_id=1, source_target_pairs={{4,0},{5,1},{6,2},{7,3},{8,12},{9,13},{10,14},{11,15},{12,4},{13,5... | collective-permute-start | bytes 2752520 | tf_op jit(solution)/shard_map/ppermute | solution.py:268
  274.3 26.6 %all-to-all-start.1 = ((f32[16,16,224]{2,1,0:T(8,128)}), f32[16,16,224]{2,1,0:T(8,128)S(1)}, u32[]{:S(2)}, u32[]{:S(2)}) async-start(f32[16,16,224]{2,1,0:T(8,128)} %bitcast.39), calls=%async_computation.1 | async-start | bytes 524288 | tf_op jit(solution)/shard_map/all_to_all | solution.py:431
  (28 other events, 165.6 us)

commit v3 on v2

--- a/solution.py
+++ b/solution.py
@@ -144,28 +144,28 @@
 
 
 def expert_kernel(
-    pieces, cap, width, rank, mine_ref, wg_ref, wu_ref, wd_ref, ag_ref, au_ref, bg_ref, bu_ref, *refs
+    held, cap, width, rank, mine_ref, wg_ref, wu_ref, wd_ref, ag_ref, au_ref, bg_ref, bu_ref, *refs
 ):
-    count = sum(len(p) for p in pieces)
-    ins, refs = refs[:count], refs[count:]
-    back_refs, refs = refs[: len(pieces)], refs[len(pieces) :]
-    route_ref, ga_ref, gbg_ref, gbu_ref = refs[:4]
-    xs, dys, weight, low, proj, both, acc = refs[4:]
+    ins, refs = refs[:plane], refs[plane:]
+    carry, refs = refs[:held], refs[held:]
+    back_refs, refs = refs[:plane], refs[plane:]
+    route_ref, gag_ref, gau_ref, gbg_ref, gbu_ref = refs[:5]
+    xs, dys, weight, low, proj, both, acc = refs[5:]
+
+    def total(at, value, part=slice(None)):
+        return value + carry[at][:, part] if held else value
+
     step = pl.program_id(0)
     tail = width + mine_ref.shape[1]
 
     @pl.when(step == 0)
     def _():
-        left = ins
-        for i, piece in enumerate(pieces):
+        for i, ref in enumerate(ins):
             rows = slice(i * cap, (i + 1) * cap)
-            x_ref, dy_ref = left[0], left[len(piece) - 1]
-            left = left[len(piece) :]
-            offset = tail if len(piece) == 1 else 0
-            xs[rows, :] = x_ref[:, :width]
-            dys[rows, :] = dy_ref[:, offset : offset + width]
+            xs[rows, :] = ref[:, :width]
+            dys[rows, :] = ref[:, tail:]
             weight[rows, :] = jnp.sum(
-                x_ref[:, width:tail].astype(f32) * mine_ref[...], axis=1, keepdims=True
+                ref[:, width:tail].astype(f32) * mine_ref[...], axis=1, keepdims=True
             )
         both[:rank, :] = ag_ref[...]
         both[rank:, :] = au_ref[...]
@@ -185,8 +185,8 @@
     scaled = weight[...] * back
     d_gate = (scaled * upval * sigma * (1.0 + gate * (1.0 - sigma))).astype(bf16)
     d_up = (scaled * act).astype(bf16)
-    gbg_ref[...] = dot_tn(low_gate, d_gate)
-    gbu_ref[...] = dot_tn(low_up, d_up)
+    gbg_ref[...] = total(2, dot_tn(low_gate, d_gate))
+    gbu_ref[...] = total(3, dot_tn(low_up, d_up))
     proj[:, :rank] += dot_nt(d_gate, bg)
     proj[:, rank:] += dot_nt(d_up, bu)
     for first, last in chunks(0, width, 512):
@@ -201,19 +201,23 @@
             rows = (acc[:, first:last] + dot_nn(proj_b, both[:, first:last])).astype(bf16)
             for i, out in enumerate(back_refs):
                 out[:, first:last] = rows[i * cap : (i + 1) * cap]
-            ga_ref[:, first:last] = dot_tn(proj_b, xs[:, first:last])
-
-
-def expert_rows(mine, mats, pieces):
+            part = slice(first, last)
+            grad = dot_tn(proj_b, xs[:, part])
+            gag_ref[:, part] = total(0, grad[:rank], part)
+            gau_ref[:, part] = total(1, grad[rank:], part)
+
+
+def expert_rows(mine, mats, pieces, carry=()):
     w_gate, w_up, w_down, a_gate, a_up, b_gate, b_up = mats
     width, hidden = w_gate.shape
     rank = a_gate.shape[0]
-    cap = pieces[0][0].shape[0]
-    rows = cap * len(pieces)
+    cap = pieces[0].shape[0]
+    rows = cap * plane
     tile = 256
-    arrays = [a for piece in pieces for a in piece]
+    second = pl.BlockSpec((rank, tile), lambda j: (0, j))
+    grads = [whole_block((rank, width))] * 2 + [second] * 2
     return pl.pallas_call(
-        functools.partial(expert_kernel, [(0,) * len(p) for p in pieces], cap, width, rank),
+        functools.partial(expert_kernel, len(carry), cap, width, rank),
         grid=(hidden // tile,),
         in_specs=[
             whole_block(mine.shape),
@@ -222,24 +226,20 @@
             pl.BlockSpec((tile, width), lambda j: (j, 0)),
             whole_block(a_gate.shape),
             whole_block(a_up.shape),
-            pl.BlockSpec((rank, tile), lambda j: (0, j)),
-            pl.BlockSpec((rank, tile), lambda j: (0, j)),
+            second,
+            second,
         ]
-        + [whole_block(a.shape) for a in arrays],
-        out_shape=[jax.ShapeDtypeStruct((cap, width), bf16)] * len(pieces)
+        + [whole_block(a.shape) for a in pieces]
+        + (grads if carry else []),
+        out_shape=[jax.ShapeDtypeStruct((cap, width), bf16)] * plane
         + [
             jax.ShapeDtypeStruct((rows, 1), f32),
-            jax.ShapeDtypeStruct((2 * rank, width), f32),
+            jax.ShapeDtypeStruct((rank, width), f32),
+            jax.ShapeDtypeStruct((rank, width), f32),
             jax.ShapeDtypeStruct((rank, hidden), f32),
             jax.ShapeDtypeStruct((rank, hidden), f32),
         ],
-        out_specs=[whole_block((cap, width))] * len(pieces)
-        + [
-            whole_block((rows, 1)),
-            whole_block((2 * rank, width)),
-            pl.BlockSpec((rank, tile), lambda j: (0, j)),
-            pl.BlockSpec((rank, tile), lambda j: (0, j)),
-        ],
+        out_specs=[whole_block((cap, width))] * plane + [whole_block((rows, 1))] + grads,
         scratch_shapes=[
             pltpu.VMEM((rows, width), bf16),
             pltpu.VMEM((rows, width), bf16),
@@ -251,7 +251,7 @@
         ],
         compiler_params=pltpu.CompilerParams(vmem_limit_bytes=vmem_bytes),
         cost_estimate=light,
-    )(mine, w_gate, w_up, w_down, a_gate, a_up, b_gate, b_up, *arrays)
+    )(mine, w_gate, w_up, w_down, a_gate, a_up, b_gate, b_up, *pieces, *carry)
 
 
 def solution(mesh):
@@ -301,6 +301,7 @@
             up_adapter_second[0],
         )
         dy = output_gradient
+        join = lax.optimization_barrier
 
         scores = jax.nn.sigmoid(dot_nn(layer_input, router_matrix))
         expert_ids = jnp.arange(experts, dtype=jnp.int32)
@@ -334,13 +335,12 @@
             )
             return pieces, placed
 
-        def run(pieces):
-            return expert_rows(mine, mats, [(a,) for a in pieces])
+        def run(pieces, carry=()):
+            return expert_rows(mine, mats, pieces, carry)
 
         if layers == 4:
             mid = (layer == 1) | (layer == 2)
             flag = mid.astype(jnp.int32)[None]
-            join = lax.optimization_barrier
             block_1 = send(own, along([(0, 2), (3, 1), (1, 0), (2, 3)]))
             sel_0, placed_0 = take(flag, [own])
             block_1, own, got_0 = join((block_1, own, spread(sel_0)))
@@ -350,43 +350,37 @@
             got_1 = spread(sel_1)
             done_0 = run(got_0)
             got_1, done_0, own = join((got_1, done_0, own))
-            back_0 = spread(done_0[:plane])
-            block_2f, block_2m, own, back_0[1], back_0[2] = join(
-                (block_2f, block_2m, own, back_0[1], back_0[2])
-            )
+            block_2f, block_2m, own = join((block_2f, block_2m, own))
             block_3 = send(own, along([(0, 1), (3, 2), (1, 3), (2, 0)]))
             sel_2, placed_2 = take(flag, [block_2m, block_2f])
             sel_2, got_1 = join((sel_2, got_1))
             got_2 = spread(sel_2)
-            done_1 = run(got_1)
+            done_1 = run(got_1, done_0[plane + 1 :])
             done_1, got_2[1], got_2[2] = join((done_1, got_2[1], got_2[2]))
             back_1 = spread(done_1[:plane])
             sel_3, placed_3 = take(flag, [block_3])
-            part_0 = sum_rows(placed_0, back_0)
             sel_3, back_1, got_2 = join((sel_3, back_1, got_2))
             got_3 = spread(sel_3)
-            done_2 = run(got_2)
+            done_2 = run(got_2, done_1[plane + 1 :])
             done_2, got_3[1], got_3[2] = join((done_2, got_3[1], got_3[2]))
             back_2 = spread(done_2[:plane])
             (part_1,) = sum_rows(placed_1, back_1)
             term_1 = send(part_1, along([(0, 1), (3, 2), (1, 3), (2, 0)]))
-            got_3, back_2, part_1, part_0 = join((got_3, back_2, part_1, part_0))
+            got_3, back_2, part_1, done_0 = join((got_3, back_2, part_1, done_0))
+            back_0 = spread(done_0[:plane])
             part_2a, part_2b = sum_rows(placed_2, back_2, 2)
             term_2a = send(part_2a, across(3 * plane))
-            done_3 = run(got_3)
-            done_3, term_1, term_2a, part_2b = join((done_3, term_1, term_2a, part_2b))
+            done_3 = run(got_3, done_2[plane + 1 :])
+            done_3, term_1, term_2a, part_2b, back_0 = join(
+                (done_3, term_1, term_2a, part_2b, back_0)
+            )
             back_3 = spread(done_3[:plane])
             term_2b = send(part_2b, across(3 * plane))
             aux = done_3[plane:]
-            back_3[1], back_3[2], aux = join((back_3[1], back_3[2], aux))
+            back_3[1], back_3[2], aux, back_0 = join((back_3[1], back_3[2], aux, back_0))
             done_3 = [*done_3[:plane], *aux]
-            (part_3,) = sum_rows(placed_3, back_3)
+            (part_0,) = sum_rows(placed_0, back_0)
             done = [done_0, done_1, done_2, done_3]
-            part_3, grads = join((part_3, [d[plane + 1 :] for d in done]))
-            done = [[*d[: plane + 1], *g] for d, g in zip(done, grads)]
-            term_3 = send(part_3, along([(1, 0), (2, 3), (3, 1), (0, 2)]))
-            terms = [part_0, [term_1], [term_2a, term_2b], [term_3]]
-            counts = [1, 1, 1, 1]
             sources = [
                 layer,
                 jnp.where(mid, layer ^ 2, layer ^ 1),
@@ -395,19 +389,18 @@
             ]
         else:
             flag = jnp.zeros((1,), jnp.int32)
-            done, counts, sources, terms = [], [], [], []
+            done, sources, terms = [], [], []
             for g in range(layers):
                 block = own if g == 0 else send(own, across(g * plane))
                 sel, placed = take(flag, [block])
-                result = run(spread(sel))
+                result = run(spread(sel), done[-1][plane + 1 :] if done else ())
                 (part,) = sum_rows(placed, spread(result[:plane]))
                 terms.append([part if g == 0 else send(part, across(g * plane))])
                 done.append(result)
-                counts.append(1)
                 sources.append(layer ^ g)
 
         route_all = jnp.concatenate(
-            [d[c * plane].reshape(c * plane, cap) for d, c in zip(done, counts)], axis=0
+            [d[plane].reshape(plane, cap) for d in done], axis=0
         )
         origin = (
             jnp.stack(sources)[:, None] * plane
@@ -425,6 +418,12 @@
         d_pick = route_scale * (route_grad / total - shared)
         d_logit = (mask * d_pick * scores * (1.0 - scores)).astype(bf16)
 
+        if layers == 4:
+            (part_3,) = sum_rows(placed_3, back_3)
+            term_3 = send(part_3, along([(1, 0), (2, 3), (3, 1), (0, 2)]))
+            d_logit, part_3, part_0, term_2b = join((d_logit, part_3, part_0, term_2b))
+            terms = [[part_0], [term_1], [term_2a, term_2b], [term_3]]
+
         router_part = dot_tn(d_logit, layer_input)
         share = width // devices
         router_part = router_part.reshape(experts, devices, share).transpose(1, 0, 2)
@@ -433,16 +432,13 @@
 
         in_grad = final_sum(d_logit, router_matrix.T, terms)
 
-        rank = gate_adapter_second.shape[1]
-        grad_a = sum(d[c * plane + 1] for d, c in zip(done, counts))
-        grad_gate_b = sum(d[c * plane + 2] for d, c in zip(done, counts))
-        grad_up_b = sum(d[c * plane + 3] for d, c in zip(done, counts))
+        grad_gate_a, grad_up_a, grad_gate_b, grad_up_b = done[-1][plane + 1 :]
         return (
             in_grad,
             router_grad,
-            grad_a[:rank].T[None],
+            grad_gate_a.T[None],
             grad_gate_b[None],
-            grad_a[rank:].T[None],
+            grad_up_a.T[None],
             grad_up_b[None],
         )
 

time: 309 us -> 311 us (level)
  blocking collectives: 0 us -> 13.5 us
  waiting for transfers between devices: 124 us -> 112 us
  starting transfers between devices: 37.7 us -> 42.8 us
    all_to_all x1 -> x0, waiting for transfers between devices: 17.2 us -> none  [shards(): lax.all_to_all(router_part, 'expert', split_axis=0, concat_axis=0, tiled=...]
    all_to_all x0 -> x1, blocking collectives: none -> 13.5 us  [shards(): lax.all_to_all(router_part, 'expert', split_axis=0, concat_axis=0, tiled=...]
    ppermute x32, starting transfers between devices: 25.9 us -> 34.8 us  [send(): return lax.ppermute(array, 'expert', pairs)]
    all_to_all x1 -> x0, starting transfers between devices: 6.07 us -> none  [shards(): lax.all_to_all(router_part, 'expert', split_axis=0, concat_axis=0, tiled=...]
    ppermute x32, waiting for transfers between devices: 107 us -> 112 us  [send(): return lax.ppermute(array, 'expert', pairs)]
    broadcast_in_dim x2 -> x0, other arithmetic: 3.31 us -> none  [the longest x1 1.66 us: shards(): grad_up_b[None]]
    unnamed x84 -> x64, local copies, waits for them, and re-layouts: 6.57 us -> 5.17 us
  transfers between devices with their start and end apart: 34 -> 33, of which waited for: 16 -> 14; matrix products, arithmetic and copies ran while one was open for 4% -> 3% of each run, Pallas kernels for 37% -> 37%
where the time goes in v3:
time: 311 us; the launch traced here: 308 us
  Pallas kernels  119 us (38%)
  waiting for transfers between devices  112 us (36%)
  starting transfers between devices  42.8 us (14%)
  blocking collectives  13.5 us (4%)
  local copies, waits for them, and re-layouts  9.15 us (3%)
  other arithmetic  7.07 us (2%)
  matrix products  3.34 us (1%)
    ppermute x32, waiting for transfers between devices, send(): return lax.ppermute(array, 'expert', pairs)  112 us
    pallas_call x4, Pallas kernels, expert_rows(): pl.pallas_call(functools.partial(expert_kernel, len(carry), cap, width, r...  87.4 us
    ppermute x32, starting transfers between devices, send(): return lax.ppermute(array, 'expert', pairs)  34.8 us
    pallas_call x4, Pallas kernels, select_rows(): pl.pallas_call(functools.partial(select_kernel, parts, meta_at, slots_hel...  17 us
    all_to_all x1, blocking collectives, shards(): lax.all_to_all(router_part, 'expert', split_axis=0, concat_axis=0, tiled=...  13.5 us
    pallas_call x4, Pallas kernels, sum_rows(): pl.pallas_call(sum_kernel, out_shape=[jax.ShapeDtypeStruct((tok // parts,...  10.7 us
    all_to_all x1, starting transfers between devices, shards(): lax.all_to_all(route_sorted, 'expert', split_axis=0, concat_axis=0, tiled...  7.95 us
  transfers between devices with their start and end apart: 33, of which 14 were waited for; matrix products, arithmetic and copies ran while one was open for 3% of the time, Pallas kernels for 37%

profile of v3, /device:TPU:15, one launch (start us, length us, event | category | flops | bytes accessed | tf_op | source)
XLA Modules:
  0.0 307.5 jit_solution(17233543987294875270)
XLA Ops:
  2.3 2.2 fusion.15
  5.1 2.2 concatenate.13.refs_0_
  8.9 4.1 %shard_map.154 = (bf16[48,7296]{1,0:T(8,128)(2,1)}, bf16[48,7296]{1,0:T(8,128)(2,1)}, bf16[48,7296]{1,0:T(8,128)(2,1)}, bf16[48,7296]{1,0:T(8,128)(2,1)}, bf16[192,128]{1,0:T(8,128)(2,1)}) custom-call(s32[1]{0:T(128)} %bitcast.4.flag_ref, bf16[16,128]{1,0:T(8,128)(2,1)} %pad_convert_fusion.guide_ref, bf16[128,7296]{1,0:T(8,128)(2,1)} %copy-done), custom_call_target="tpu_custom_call" | custom-call | flops 1024 | bytes 1024 | tf_op jit(solution)/shard_map/pallas_call | solution.py:87
  14.1 1.4 collective-permute-start.3
  15.9 15.6 %collective-permute-done.2.refs_2_ = bf16[48,7296]{1,0:T(8,128)(2,1)S(1)} collective-permute-done((bf16[48,7296]{1,0:T(8,128)(2,1)}, bf16[48,7296]{1,0:T(8,128)(2,1)S(1)}, u32[]{:S(2)}, u32[]{:S(2)}) %collective-permute-start.2) | collective-permute-done | bytes 700448 | tf_op jit(solution)/shard_map/ppermute | solution.py:268
  31.6 15.4 %collective-permute-done.3.refs_3_ = bf16[48,7296]{1,0:T(8,128)(2,1)S(1)} collective-permute-done((bf16[48,7296]{1,0:T(8,128)(2,1)}, bf16[48,7296]{1,0:T(8,128)(2,1)S(1)}, u32[]{:S(2)}, u32[]{:S(2)}) %collective-permute-start.3) | collective-permute-done | bytes 700448 | tf_op jit(solution)/shard_map/ppermute | solution.py:268
  46.9 3.0 collective-permute-done.refs_0_
  50.0 1.4 collective-permute-start.4
  51.4 4.2 %collective-permute-start.5 = (bf16[128,7296]{1,0:T(8,128)(2,1)}, bf16[128,7296]{1,0:T(8,128)(2,1)}, u32[]{:S(2)}, u32[]{:S(2)}) collective-permute-start(bf16[128,7296]{1,0:T(8,128)(2,1)} %copy-done), channel_id=1, source_target_pairs={{4,8},{5,9},{6,10},{7,11},{8,4},{9,5},{10,6},{11,7},{20,24},{21,25... | collective-permute-start | bytes 5603336 | tf_op jit(solution)/shard_map/ppermute | solution.py:268
  55.6 4.1 %shard_map.155 = (bf16[48,7296]{1,0:T(8,128)(2,1)}, bf16[48,7296]{1,0:T(8,128)(2,1)}, bf16[48,7296]{1,0:T(8,128)(2,1)}, bf16[48,7296]{1,0:T(8,128)(2,1)}, bf16[192,128]{1,0:T(8,128)(2,1)}) custom-call(s32[1]{0:T(128)} %bitcast.4.flag_ref, bf16[16,128]{1,0:T(8,128)(2,1)} %pad_convert_fusion.guide_ref, bf16[128,7296]{1,0:T(8,128)(2,1)} %collective-permute-done.refs_0_), custom_call_target="tpu_custom_call" | custom-call | flops 1024 | bytes 1024 | tf_op jit(solution)/shard_map/pallas_call | solution.py:87
  59.7 2.1 collective-permute-start.6
  62.1 1.4 collective-permute-start.8
  64.1 21.6 %shard_map.156 = (bf16[48,3584]{1,0:T(8,128)(2,1)}, bf16[48,3584]{1,0:T(8,128)(2,1)}, bf16[48,3584]{1,0:T(8,128)(2,1)}, bf16[48,3584]{1,0:T(8,128)(2,1)}, f32[19...) custom-call(f32[1,128]{1,0:T(1,128)} %compare_convert_fusion.mine_ref, ...), custom_call_target="tpu_custom_call" | custom-call | flops 1024 | bytes 1024 | tf_op jit(solution)/shard_map/pallas_call | solution.py:219
  85.7 9.1 %collective-permute-done.8.refs_3_ = bf16[48,7296]{1,0:T(8,128)(2,1)} collective-permute-done((bf16[48,7296]{1,0:T(8,128)(2,1)}, bf16[48,7296]{1,0:T(8,128)(2,1)}, u32[]{:S(2)}, u32[]{:S(2)}) %collective-permute-start.8) | collective-permute-done | bytes 700448 | tf_op jit(solution)/shard_map/ppermute | solution.py:268
  95.1 1.0 copy-done.3
  96.2 4.6 %shard_map.158 = (bf16[48,7296]{1,0:T(8,128)(2,1)}, bf16[48,7296]{1,0:T(8,128)(2,1)}, bf16[48,7296]{1,0:T(8,128)(2,1)}, bf16[48,7296]{1,0:T(8,128)(2,1)}, bf16[192,128]{1,0:T(8,128)(2,1)}) custom-call(s32[1]{0:T(128)} %bitcast.4.flag_ref, bf16[16,128]{1,0:T(8,128)(2,1)} %pad_convert_fusion.guide_ref, bf16[128,7296]{1,0:T(8,128)(2,1)} %collective-permute-done.5.refs_0_, ...), custom_call_target="tpu_custom_call" | custom-call | flops 1024 | bytes 1024 | tf_op jit(solution)/shard_map/pallas_call | solution.py:87
  100.8 1.4 collective-permute-start.10
  102.5 1.4 collective-permute-start.15
  103.9 22.1 %shard_map.159 = (bf16[48,3584]{1,0:T(8,128)(2,1)}, bf16[48,3584]{1,0:T(8,128)(2,1)}, bf16[48,3584]{1,0:T(8,128)(2,1)}, bf16[48,3584]{1,0:T(8,128)(2,1)}, f32[19...) custom-call(f32[1,128]{1,0:T(1,128)} %compare_convert_fusion.mine_ref, ...), custom_call_target="tpu_custom_call" | custom-call | flops 1024 | bytes 1024 | tf_op jit(solution)/shard_map/pallas_call | solution.py:219
  126.5 1.7 collective-permute-start.14
  128.2 6.7 %collective-permute-done.9.refs_0_ = bf16[128,7296]{1,0:T(8,128)(2,1)S(1)} collective-permute-done((bf16[128,7296]{1,0:T(8,128)(2,1)S(1)}, bf16[128,7296]{1,0:T(8,128)(2,1)S(1)}, u32[]{:S(2)}, u32[]{:S(2)}) %collective-permute-start.9) | collective-permute-done | bytes 1867808 | tf_op jit(solution)/shard_map/ppermute | solution.py:268
  134.9 1.3 copy-done.4
  136.2 4.2 %shard_map.157 = (bf16[48,7296]{1,0:T(8,128)(2,1)}, bf16[48,7296]{1,0:T(8,128)(2,1)}, bf16[48,7296]{1,0:T(8,128)(2,1)}, bf16[48,7296]{1,0:T(8,128)(2,1)}, bf16[192,128]{1,0:T(8,128)(2,1)}) custom-call(s32[1]{0:T(128)} %bitcast.4.flag_ref, bf16[16,128]{1,0:T(8,128)(2,1)} %pad_convert_fusion.guide_ref, bf16[128,7296]{1,0:T(8,128)(2,1)} %copy-done.4), custom_call_target="tpu_custom_call" | custom-call | flops 1024 | bytes 1024 | tf_op jit(solution)/shard_map/pallas_call | solution.py:87
  140.4 1.8 collective-permute-done.13.refs_2_
  142.2 7.5 %collective-permute-done.14.refs_3_ = bf16[48,3584]{1,0:T(8,128)(2,1)S(1)} collective-permute-done((bf16[48,3584]{1,0:T(8,128)(2,1)}, bf16[48,3584]{1,0:T(8,128)(2,1)S(1)}, u32[]{:S(2)}, u32[]{:S(2)}) %collective-permute-start.14) | collective-permute-done | bytes 344096 | tf_op jit(solution)/shard_map/ppermute | solution.py:268
  150.9 1.6 collective-permute-start.18
  152.6 2.7 shard_map.161
  155.2 3.5 %collective-permute-start.22 = (bf16[128,3584]{1,0:T(8,128)(2,1)}, bf16[128,3584]{1,0:T(8,128)(2,1)S(1)}, u32[]{:S(2)}, u32[]{:S(2)}) collective-permute-start(bf16[128,3584]{1,0:T(8,128)(2,1)} %shard_map.161), channel_id=1, source_target_pairs={{0,4},{1,5},{2,6},{3,7},{12,8},{13,9},{14,10},{15,11},{4,12},{5,13... | collective-permute-start | bytes 2752520 | tf_op jit(solution)/shard_map/ppermute | solution.py:268
  158.8 21.8 %shard_map.160 = (bf16[48,3584]{1,0:T(8,128)(2,1)}, bf16[48,3584]{1,0:T(8,128)(2,1)}, bf16[48,3584]{1,0:T(8,128)(2,1)}, bf16[48,3584]{1,0:T(8,128)(2,1)}, f32[19...) custom-call(f32[1,128]{1,0:T(1,128)} %compare_convert_fusion.mine_ref, ...), custom_call_target="tpu_custom_call" | custom-call | flops 1024 | bytes 1024 | tf_op jit(solution)/shard_map/pallas_call | solution.py:219
  181.3 1.6 collective-permute-start.21
  183.5 7.2 %collective-permute-done.20.refs_2_ = bf16[48,3584]{1,0:T(8,128)(2,1)S(1)} collective-permute-done((bf16[48,3584]{1,0:T(8,128)(2,1)}, bf16[48,3584]{1,0:T(8,128)(2,1)S(1)}, u32[]{:S(2)}, u32[]{:S(2)}) %collective-permute-start.20) | collective-permute-done | bytes 344096 | tf_op jit(solution)/shard_map/ppermute | solution.py:268
  190.7 7.7 %collective-permute-done.21.refs_3_ = bf16[48,3584]{1,0:T(8,128)(2,1)S(1)} collective-permute-done((bf16[48,3584]{1,0:T(8,128)(2,1)}, bf16[48,3584]{1,0:T(8,128)(2,1)S(1)}, u32[]{:S(2)}, u32[]{:S(2)}) %collective-permute-start.21) | collective-permute-done | bytes 344096 | tf_op jit(solution)/shard_map/ppermute | solution.py:268
  199.1 2.6 shard_map.163
  201.8 1.8 collective-permute-start.23
  204.1 1.6 collective-permute-start.26
  205.9 21.9 %shard_map.162 = (bf16[48,3584]{1,0:T(8,128)(2,1)}, bf16[48,3584]{1,0:T(8,128)(2,1)}, bf16[48,3584]{1,0:T(8,128)(2,1)}, bf16[48,3584]{1,0:T(8,128)(2,1)}, f32[19...) custom-call(f32[1,128]{1,0:T(1,128)} %compare_convert_fusion.mine_ref, ...), custom_call_target="tpu_custom_call" | custom-call | flops 1024 | bytes 1024 | tf_op jit(solution)/shard_map/pallas_call | solution.py:219
  228.5 1.0 convert_reduce_fusion.1
  229.6 1.8 collective-permute-start.29
  232.5 4.9 %collective-permute-done.28.refs_2_ = bf16[48,3584]{1,0:T(8,128)(2,1)S(1)} collective-permute-done((bf16[48,3584]{1,0:T(8,128)(2,1)}, bf16[48,3584]{1,0:T(8,128)(2,1)S(1)}, u32[]{:S(2)}, u32[]{:S(2)}) %collective-permute-start.28) | collective-permute-done | bytes 344096 | tf_op jit(solution)/shard_map/ppermute | solution.py:268
  237.5 1.1 convert_reduce_fusion
  239.4 7.9 %all-to-all-start = ((bf16[16,1,48]{2,1,0:T(2,128)(2,1)}), bf16[16,1,48]{2,1,0:T(2,128)(2,1)S(1)}, u32[]{:S(2)}, u32[]{:S(2)}) async-start(bf16[16,1,48]{2,1,0:T(2,128)(2,1)} %copy.49), calls=%async_computation | async-start | bytes 16384 | tf_op jit(solution)/shard_map/all_to_all | solution.py:411
  247.4 1.2 collective-permute-start.30
  249.4 2.7 shard_map.164
  252.1 2.1 collective-permute-start.31
  254.2 2.7 shard_map.165.refs_0_
  257.5 31.6 %collective-permute-done.30.refs_3_ = bf16[64,3584]{1,0:T(8,128)(2,1)S(1)} collective-permute-done((bf16[64,3584]{1,0:T(8,128)(2,1)}, bf16[64,3584]{1,0:T(8,128)(2,1)S(1)}, u32[]{:S(2)}, u32[]{:S(2)}) %collective-permute-start.30) | collective-permute-done | bytes 458784 | tf_op jit(solution)/shard_map/ppermute | solution.py:268
  289.7 13.5 %all_to_all.14 = f32[16,16,224]{2,1,0:T(8,128)S(1)} all-to-all(f32[16,16,224]{2,1,0:T(8,128)S(1)} %bitcast.64), channel_id=1, replica_groups=mesh['groups'=2,'expert'=16] {'expert'}, dimensions={0} | all-to-all | bytes 458752 | tf_op jit(solution)/shard_map/all_to_all | solution.py:430
  303.8 3.7 %shard_map.166 = bf16[128,3584]{1,0:T(8,128)(2,1)} custom-call(bf16[128,16]{1,0:T(8,128)(2,1)} %copy-done.25, bf16[16,3584]{1,0:T(8,128)(2,1)} %bitcast.65, bf16[128,3584]{1,0:T(8,128)(2,1)} %shard_map.165.refs_0_, bf16[128,3584]{1,0:T(8,128)(2,1)} %copy-done.5, bf16[64,3584]{1,0:T(8,128)(2,1)} %collective-permute-done.23.refs_2_, ...), custom_call_target="tpu_custom_call" | custom-call | flops 1024 | bytes 1024 | tf_op jit(solution)/shard_map/pallas_call | solution.py:136
  (134 shorter events, 16.4 us)
Async XLA Ops:
  7.4 42.6 %collective-permute-start = (bf16[128,7296]{1,0:T(8,128)(2,1)S(1)}, bf16[128,7296]{1,0:T(8,128)(2,1)}, u32[]{:S(2)}, u32[]{:S(2)}) collective-permute-start(bf16[128,7296]{1,0:T(8,128)(2,1)S(1)} %concatenate.13.refs_0_), channel_id=1, source_target_pairs={{0,8},{1,9},{2,10},{3,11},{12,4},{13,5},{14,6},{15,7},{4,0},{5,1},... | collective-permute-start | bytes 5603336 | tf_op jit(solution)/shard_map/ppermute | solution.py:268
  13.0 2.9 collective-permute-start.1
  13.9 17.6 %collective-permute-start.2 = (bf16[48,7296]{1,0:T(8,128)(2,1)}, bf16[48,7296]{1,0:T(8,128)(2,1)S(1)}, u32[]{:S(2)}, u32[]{:S(2)}) collective-permute-start(bf16[48,7296]{1,0:T(8,128)(2,1)} %get-tuple-element.186), channel_id=1, source_target_pairs={{0,2},{1,3},{2,0},{3,1},{4,6},{5,7},{6,4},{7,5},{8,10},{9,11},{10,... | collective-permute-start | bytes 2101256 | tf_op jit(solution)/shard_map/ppermute | solution.py:268
  14.1 32.8 %collective-permute-start.3 = (bf16[48,7296]{1,0:T(8,128)(2,1)}, bf16[48,7296]{1,0:T(8,128)(2,1)S(1)}, u32[]{:S(2)}, u32[]{:S(2)}) collective-permute-start(bf16[48,7296]{1,0:T(8,128)(2,1)} %get-tuple-element.187), channel_id=1, source_target_pairs={{0,3},{1,2},{2,1},{3,0},{4,7},{5,6},{6,5},{7,4},{8,11},{9,10},{10,... | collective-permute-start | bytes 2101256 | tf_op jit(solution)/shard_map/ppermute | solution.py:268
  15.9 34.1 %copy-start.12 = (bf16[48,7296]{1,0:T(8,128)(2,1)}, bf16[48,7296]{1,0:T(8,128)(2,1)S(1)}, u32[]{:S(2)}) copy-start(bf16[48,7296]{1,0:T(8,128)(2,1)S(1)} %collective-permute-done.1.refs_1_) | copy-start | bytes 2101252
  31.5 18.4 %copy-start.13 = (bf16[48,7296]{1,0:T(8,128)(2,1)}, bf16[48,7296]{1,0:T(8,128)(2,1)S(1)}, u32[]{:S(2)}) copy-start(bf16[48,7296]{1,0:T(8,128)(2,1)S(1)} %collective-permute-done.2.refs_2_) | copy-start | bytes 2101252
  50.0 44.9 %collective-permute-start.4 = (bf16[128,7296]{1,0:T(8,128)(2,1)}, bf16[128,7296]{1,0:T(8,128)(2,1)S(1)}, u32[]{:S(2)}, u32[]{:S(2)}) collective-permute-start(bf16[128,7296]{1,0:T(8,128)(2,1)} %collective-permute-done.refs_0_), channel_id=1, source_target_pairs={{4,0},{5,1},{6,2},{7,3},{8,12},{9,13},{10,14},{11,15},{20,16},{21,... | collective-permute-start | bytes 5603336 | tf_op jit(solution)/shard_map/ppermute | solution.py:268
  51.4 43.7 %collective-permute-start.5 = (bf16[128,7296]{1,0:T(8,128)(2,1)}, bf16[128,7296]{1,0:T(8,128)(2,1)}, u32[]{:S(2)}, u32[]{:S(2)}) collective-permute-start(bf16[128,7296]{1,0:T(8,128)(2,1)} %copy-done), channel_id=1, source_target_pairs={{4,8},{5,9},{6,10},{7,11},{8,4},{9,5},{10,6},{11,7},{20,24},{21,25... | collective-permute-start | bytes 5603336 | tf_op jit(solution)/shard_map/ppermute | solution.py:268
  59.7 26.0 %collective-permute-start.6 = (bf16[48,7296]{1,0:T(8,128)(2,1)}, bf16[48,7296]{1,0:T(8,128)(2,1)S(1)}, u32[]{:S(2)}, u32[]{:S(2)}) collective-permute-start(bf16[48,7296]{1,0:T(8,128)(2,1)} %get-tuple-element.191), channel_id=1, source_target_pairs={{0,1},{1,0},{2,3},{3,2},{4,5},{5,4},{6,7},{7,6},{8,9},{9,8},{10,11... | collective-permute-start | bytes 2101256 | tf_op jit(solution)/shard_map/ppermute | solution.py:268
  61.8 23.9 %collective-permute-start.7 = (bf16[48,7296]{1,0:T(8,128)(2,1)}, bf16[48,7296]{1,0:T(8,128)(2,1)}, u32[]{:S(2)}, u32[]{:S(2)}) collective-permute-start(bf16[48,7296]{1,0:T(8,128)(2,1)} %get-tuple-element.192), channel_id=1, source_target_pairs={{0,2},{1,3},{2,0},{3,1},{4,6},{5,7},{6,4},{7,5},{8,10},{9,11},{10,... | collective-permute-start | bytes 2101256 | tf_op jit(solution)/shard_map/ppermute | solution.py:268
  62.1 32.8 %collective-permute-start.8 = (bf16[48,7296]{1,0:T(8,128)(2,1)}, bf16[48,7296]{1,0:T(8,128)(2,1)}, u32[]{:S(2)}, u32[]{:S(2)}) collective-permute-start(bf16[48,7296]{1,0:T(8,128)(2,1)} %get-tuple-element.193), channel_id=1, source_target_pairs={{0,3},{1,2},{2,1},{3,0},{4,7},{5,6},{6,5},{7,4},{8,11},{9,10},{10,... | collective-permute-start | bytes 2101256 | tf_op jit(solution)/shard_map/ppermute | solution.py:268
  64.1 31.1 %copy-start.1 = (bf16[128,7296]{1,0:T(8,128)(2,1)S(1)}, bf16[128,7296]{1,0:T(8,128)(2,1)}, u32[]{:S(2)}) copy-start(bf16[128,7296]{1,0:T(8,128)(2,1)} %copy-done) | copy-start | bytes 5603332
  85.7 18.2 %copy-start.11 = (bf16[48,7296]{1,0:T(8,128)(2,1)}, bf16[48,7296]{1,0:T(8,128)(2,1)S(1)}, u32[]{:S(2)}) copy-start(bf16[48,7296]{1,0:T(8,128)(2,1)S(1)} %collective-permute-done.6.refs_1_) | copy-start | bytes 2101252
  95.1 39.7 %collective-permute-start.9 = (bf16[128,7296]{1,0:T(8,128)(2,1)S(1)}, bf16[128,7296]{1,0:T(8,128)(2,1)S(1)}, u32[]{:S(2)}, u32[]{:S(2)}) collective-permute-start(bf16[128,7296]{1,0:T(8,128)(2,1)S(1)} %copy-done.1), channel_id=1, source_target_pairs={{0,4},{1,5},{2,6},{3,7},{12,8},{13,9},{14,10},{15,11},{4,12},{5,13... | collective-permute-start | bytes 5603336 | tf_op jit(solution)/shard_map/ppermute | solution.py:268
  100.8 25.1 %collective-permute-start.10 = (bf16[48,7296]{1,0:T(8,128)(2,1)}, bf16[48,7296]{1,0:T(8,128)(2,1)S(1)}, u32[]{:S(2)}, u32[]{:S(2)}) collective-permute-start(bf16[48,7296]{1,0:T(8,128)(2,1)} %get-tuple-element.240), channel_id=1, source_target_pairs={{0,1},{1,0},{2,3},{3,2},{4,5},{5,4},{6,7},{7,6},{8,9},{9,8},{10,11... | collective-permute-start | bytes 2101256 | tf_op jit(solution)/shard_map/ppermute | solution.py:268
  102.3 23.7 %collective-permute-start.11 = (bf16[48,7296]{1,0:T(8,128)(2,1)}, bf16[48,7296]{1,0:T(8,128)(2,1)S(1)}, u32[]{:S(2)}, u32[]{:S(2)}) collective-permute-start(bf16[48,7296]{1,0:T(8,128)(2,1)} %get-tuple-element.241), channel_id=1, source_target_pairs={{0,2},{1,3},{2,0},{3,1},{4,6},{5,7},{6,4},{7,5},{8,10},{9,11},{10,... | collective-permute-start | bytes 2101256 | tf_op jit(solution)/shard_map/ppermute | solution.py:268
  102.5 37.9 %collective-permute-start.15 = (bf16[48,7296]{1,0:T(8,128)(2,1)}, bf16[48,7296]{1,0:T(8,128)(2,1)S(1)}, u32[]{:S(2)}, u32[]{:S(2)}) collective-permute-start(bf16[48,7296]{1,0:T(8,128)(2,1)} %get-tuple-element.249), channel_id=1, source_target_pairs={{0,3},{1,2},{2,1},{3,0},{4,7},{5,6},{6,5},{7,4},{8,11},{9,10},{10,... | collective-permute-start | bytes 2101256 | tf_op jit(solution)/shard_map/ppermute | solution.py:268
  126.0 32.8 %copy-start.8 = (bf16[48,7296]{1,0:T(8,128)(2,1)}, bf16[48,7296]{1,0:T(8,128)(2,1)S(1)}, u32[]{:S(2)}) copy-start(bf16[48,7296]{1,0:T(8,128)(2,1)S(1)} %collective-permute-done.10.refs_1_) | copy-start | bytes 2101252
  126.0 26.6 %copy-start.9 = (bf16[48,7296]{1,0:T(8,128)(2,1)}, bf16[48,7296]{1,0:T(8,128)(2,1)S(1)}, u32[]{:S(2)}) copy-start(bf16[48,7296]{1,0:T(8,128)(2,1)S(1)} %collective-permute-done.11.refs_2_) | copy-start | bytes 2101252
  126.0 14.4 %collective-permute-start.12 = (bf16[48,3584]{1,0:T(8,128)(2,1)}, bf16[48,3584]{1,0:T(8,128)(2,1)S(1)}, u32[]{:S(2)}, u32[]{:S(2)}) collective-permute-start(bf16[48,3584]{1,0:T(8,128)(2,1)} %get-tuple-element.243), channel_id=1, source_target_pairs={{0,1},{1,0},{2,3},{3,2},{4,5},{5,4},{6,7},{7,6},{8,9},{9,8},{10,11... | collective-permute-start | bytes 1032200 | tf_op jit(solution)/shard_map/ppermute | solution.py:268
  126.3 15.9 %collective-permute-start.13 = (bf16[48,3584]{1,0:T(8,128)(2,1)}, bf16[48,3584]{1,0:T(8,128)(2,1)S(1)}, u32[]{:S(2)}, u32[]{:S(2)}) collective-permute-start(bf16[48,3584]{1,0:T(8,128)(2,1)} %get-tuple-element.244), channel_id=1, source_target_pairs={{0,2},{1,3},{2,0},{3,1},{4,6},{5,7},{6,4},{7,5},{8,10},{9,11},{10,... | collective-permute-start | bytes 1032200 | tf_op jit(solution)/shard_map/ppermute | solution.py:268
  126.5 23.1 %collective-permute-start.14 = (bf16[48,3584]{1,0:T(8,128)(2,1)}, bf16[48,3584]{1,0:T(8,128)(2,1)S(1)}, u32[]{:S(2)}, u32[]{:S(2)}) collective-permute-start(bf16[48,3584]{1,0:T(8,128)(2,1)} %get-tuple-element.245), channel_id=1, source_target_pairs={{0,3},{1,2},{2,1},{3,0},{4,7},{5,6},{6,5},{7,4},{8,11},{9,10},{10,... | collective-permute-start | bytes 1032200 | tf_op jit(solution)/shard_map/ppermute | solution.py:268
  150.4 30.2 %collective-permute-start.16 = (bf16[48,7296]{1,0:T(8,128)(2,1)}, bf16[48,7296]{1,0:T(8,128)(2,1)S(1)}, u32[]{:S(2)}, u32[]{:S(2)}) collective-permute-start(bf16[48,7296]{1,0:T(8,128)(2,1)} %get-tuple-element.268), channel_id=1, source_target_pairs={{0,1},{1,0},{2,3},{3,2},{4,5},{5,4},{6,7},{7,6},{8,9},{9,8},{10,11... | collective-permute-start | bytes 2101256 | tf_op jit(solution)/shard_map/ppermute | solution.py:268
  150.7 29.9 %collective-permute-start.17 = (bf16[48,7296]{1,0:T(8,128)(2,1)}, bf16[48,7296]{1,0:T(8,128)(2,1)S(1)}, u32[]{:S(2)}, u32[]{:S(2)}) collective-permute-start(bf16[48,7296]{1,0:T(8,128)(2,1)} %get-tuple-element.269), channel_id=1, source_target_pairs={{0,2},{1,3},{2,0},{3,1},{4,6},{5,7},{6,4},{7,5},{8,10},{9,11},{10,... | collective-permute-start | bytes 2101256 | tf_op jit(solution)/shard_map/ppermute | solution.py:268
  150.9 32.5 %collective-permute-start.18 = (bf16[48,7296]{1,0:T(8,128)(2,1)}, bf16[48,7296]{1,0:T(8,128)(2,1)}, u32[]{:S(2)}, u32[]{:S(2)}) collective-permute-start(bf16[48,7296]{1,0:T(8,128)(2,1)} %get-tuple-element.272), channel_id=1, source_target_pairs={{0,3},{1,2},{2,1},{3,0},{4,7},{5,6},{6,5},{7,4},{8,11},{9,10},{10,... | collective-permute-start | bytes 2101256 | tf_op jit(solution)/shard_map/ppermute | solution.py:268
  155.2 50.5 %copy-start.31 = (s32[4]{0:T(128)S(1)}, s32[4]{0:T(128)}, u32[]{:S(2)}) copy-start(s32[4]{0:T(128)} %get-tuple-element.355) | copy-start | bytes 52
  155.2 72.6 %collective-permute-start.22 = (bf16[128,3584]{1,0:T(8,128)(2,1)}, bf16[128,3584]{1,0:T(8,128)(2,1)S(1)}, u32[]{:S(2)}, u32[]{:S(2)}) collective-permute-start(bf16[128,3584]{1,0:T(8,128)(2,1)} %shard_map.161), channel_id=1, source_target_pairs={{0,4},{1,5},{2,6},{3,7},{12,8},{13,9},{14,10},{15,11},{4,12},{5,13... | collective-permute-start | bytes 2752520 | tf_op jit(solution)/shard_map/ppermute | solution.py:268
  180.6 25.3 %copy-start.6 = (bf16[48,7296]{1,0:T(8,128)(2,1)}, bf16[48,7296]{1,0:T(8,128)(2,1)S(1)}, u32[]{:S(2)}) copy-start(bf16[48,7296]{1,0:T(8,128)(2,1)S(1)} %collective-permute-done.16.refs_1_) | copy-start | bytes 2101252
  180.7 25.3 %copy-start.7 = (bf16[48,7296]{1,0:T(8,128)(2,1)}, bf16[48,7296]{1,0:T(8,128)(2,1)S(1)}, u32[]{:S(2)}) copy-start(bf16[48,7296]{1,0:T(8,128)(2,1)S(1)} %collective-permute-done.17.refs_2_) | copy-start | bytes 2101252
  180.7 2.8 collective-permute-start.19
  181.0 9.7 %collective-permute-start.20 = (bf16[48,3584]{1,0:T(8,128)(2,1)}, bf16[48,3584]{1,0:T(8,128)(2,1)S(1)}, u32[]{:S(2)}, u32[]{:S(2)}) collective-permute-start(bf16[48,3584]{1,0:T(8,128)(2,1)} %get-tuple-element.275), channel_id=1, source_target_pairs={{0,2},{1,3},{2,0},{3,1},{4,6},{5,7},{6,4},{7,5},{8,10},{9,11},{10,... | collective-permute-start | bytes 1032200 | tf_op jit(solution)/shard_map/ppermute | solution.py:268
  181.3 17.1 %collective-permute-start.21 = (bf16[48,3584]{1,0:T(8,128)(2,1)}, bf16[48,3584]{1,0:T(8,128)(2,1)S(1)}, u32[]{:S(2)}, u32[]{:S(2)}) collective-permute-start(bf16[48,3584]{1,0:T(8,128)(2,1)} %get-tuple-element.276), channel_id=1, source_target_pairs={{0,3},{1,2},{2,1},{3,0},{4,7},{5,6},{6,5},{7,4},{8,11},{9,10},{10,... | collective-permute-start | bytes 1032200 | tf_op jit(solution)/shard_map/ppermute | solution.py:268
  183.5 14.9 %copy-start.22 = (bf16[48,3584]{1,0:T(8,128)(2,1)}, bf16[48,3584]{1,0:T(8,128)(2,1)S(1)}, u32[]{:S(2)}) copy-start(bf16[48,3584]{1,0:T(8,128)(2,1)S(1)} %collective-permute-done.19.refs_1_) | copy-start | bytes 1032196
  201.8 26.1 %collective-permute-start.23 = (bf16[64,3584]{1,0:T(8,128)(2,1)}, bf16[64,3584]{1,0:T(8,128)(2,1)}, u32[]{:S(2)}, u32[]{:S(2)}) collective-permute-start(bf16[64,3584]{1,0:T(8,128)(2,1)} %get-tuple-element.312), channel_id=1, source_target_pairs={{0,12},{1,13},{2,14},{3,15},{4,8},{5,9},{6,10},{7,11},{8,4},{9,5},... | collective-permute-start | bytes 1376264 | tf_op jit(solution)/shard_map/ppermute | solution.py:268
  203.5 24.3 %collective-permute-start.24 = (bf16[48,3584]{1,0:T(8,128)(2,1)}, bf16[48,3584]{1,0:T(8,128)(2,1)}, u32[]{:S(2)}, u32[]{:S(2)}) collective-permute-start(bf16[48,3584]{1,0:T(8,128)(2,1)} %get-tuple-element.315), channel_id=1, source_target_pairs={{0,1},{1,0},{2,3},{3,2},{4,5},{5,4},{6,7},{7,6},{8,9},{9,8},{10,11... | collective-permute-start | bytes 1032200 | tf_op jit(solution)/shard_map/ppermute | solution.py:268
  203.9 24.0 %collective-permute-start.25 = (bf16[48,3584]{1,0:T(8,128)(2,1)}, bf16[48,3584]{1,0:T(8,128)(2,1)}, u32[]{:S(2)}, u32[]{:S(2)}) collective-permute-start(bf16[48,3584]{1,0:T(8,128)(2,1)} %get-tuple-element.316), channel_id=1, source_target_pairs={{0,2},{1,3},{2,0},{3,1},{4,6},{5,7},{6,4},{7,5},{8,10},{9,11},{10,... | collective-permute-start | bytes 1032200 | tf_op jit(solution)/shard_map/ppermute | solution.py:268
  204.1 23.8 %collective-permute-start.26 = (bf16[48,3584]{1,0:T(8,128)(2,1)}, bf16[48,3584]{1,0:T(8,128)(2,1)}, u32[]{:S(2)}, u32[]{:S(2)}) collective-permute-start(bf16[48,3584]{1,0:T(8,128)(2,1)} %get-tuple-element.317), channel_id=1, source_target_pairs={{0,3},{1,2},{2,1},{3,0},{4,7},{5,6},{6,5},{7,4},{8,11},{9,10},{10,... | collective-permute-start | bytes 1032200 | tf_op jit(solution)/shard_map/ppermute | solution.py:268
  205.9 22.3 %copy-start.29 = (f32[192,1]{1,0:T(8,128)S(1)}, f32[192,1]{1,0:T(8,128)}, u32[]{:S(2)}) copy-start(f32[192,1]{1,0:T(8,128)} %get-tuple-element.288) | copy-start | bytes 2308
  205.9 41.4 %copy-start.28 = (f32[128,16]{1,0:T(8,128)S(1)}, f32[128,16]{1,0:T(8,128)}, u32[]{:S(2)}) copy-start(f32[128,16]{1,0:T(8,128)} %get-tuple-element.353) | copy-start | bytes 24580
  227.9 29.0 %copy-start.5 = (bf16[128,3584]{1,0:T(8,128)(2,1)}, bf16[128,3584]{1,0:T(8,128)(2,1)S(1)}, u32[]{:S(2)}) copy-start(bf16[128,3584]{1,0:T(8,128)(2,1)S(1)} %collective-permute-done.22.refs_1_) | copy-start | bytes 2752516
  227.9 4.6 %collective-permute-start.27 = (bf16[48,3584]{1,0:T(8,128)(2,1)}, bf16[48,3584]{1,0:T(8,128)(2,1)S(1)}, u32[]{:S(2)}, u32[]{:S(2)}) collective-permute-start(bf16[48,3584]{1,0:T(8,128)(2,1)} %get-tuple-element.318), channel_id=1, source_target_pairs={{0,1},{1,0},{2,3},{3,2},{4,5},{5,4},{6,7},{7,6},{8,9},{9,8},{10,11... | collective-permute-start | bytes 1032200 | tf_op jit(solution)/shard_map/ppermute | solution.py:268
  228.0 9.4 %collective-permute-start.28 = (bf16[48,3584]{1,0:T(8,128)(2,1)}, bf16[48,3584]{1,0:T(8,128)(2,1)S(1)}, u32[]{:S(2)}, u32[]{:S(2)}) collective-permute-start(bf16[48,3584]{1,0:T(8,128)(2,1)} %get-tuple-element.319), channel_id=1, source_target_pairs={{0,2},{1,3},{2,0},{3,1},{4,6},{5,7},{6,4},{7,5},{8,10},{9,11},{10,... | collective-permute-start | bytes 1032200 | tf_op jit(solution)/shard_map/ppermute | solution.py:268
  229.6 19.1 %collective-permute-start.29 = (bf16[48,3584]{1,0:T(8,128)(2,1)}, bf16[48,3584]{1,0:T(8,128)(2,1)S(1)}, u32[]{:S(2)}, u32[]{:S(2)}) collective-permute-start(bf16[48,3584]{1,0:T(8,128)(2,1)} %get-tuple-element.334), channel_id=1, source_target_pairs={{0,3},{1,2},{2,1},{3,0},{4,7},{5,6},{6,5},{7,4},{8,11},{9,10},{10,... | collective-permute-start | bytes 1032200 | tf_op jit(solution)/shard_map/ppermute | solution.py:268
  232.5 16.1 %copy-start.16 = (bf16[48,3584]{1,0:T(8,128)(2,1)}, bf16[48,3584]{1,0:T(8,128)(2,1)S(1)}, u32[]{:S(2)}) copy-start(bf16[48,3584]{1,0:T(8,128)(2,1)S(1)} %collective-permute-done.27.refs_1_) | copy-start | bytes 1032196
  239.4 17.5 %all-to-all-start = ((bf16[16,1,48]{2,1,0:T(2,128)(2,1)}), bf16[16,1,48]{2,1,0:T(2,128)(2,1)S(1)}, u32[]{:S(2)}, u32[]{:S(2)}) async-start(bf16[16,1,48]{2,1,0:T(2,128)(2,1)} %copy.49), calls=%async_computation | async-start | bytes 16384 | tf_op jit(solution)/shard_map/all_to_all | solution.py:411
  247.4 41.7 %collective-permute-start.30 = (bf16[64,3584]{1,0:T(8,128)(2,1)}, bf16[64,3584]{1,0:T(8,128)(2,1)S(1)}, u32[]{:S(2)}, u32[]{:S(2)}) collective-permute-start(bf16[64,3584]{1,0:T(8,128)(2,1)} %get-tuple-element.340), channel_id=1, source_target_pairs={{0,12},{1,13},{2,14},{3,15},{4,8},{5,9},{6,10},{7,11},{8,4},{9,5},... | collective-permute-start | bytes 1376264 | tf_op jit(solution)/shard_map/ppermute | solution.py:268
  252.1 51.8 %collective-permute-start.31 = (bf16[128,3584]{1,0:T(8,128)(2,1)}, bf16[128,3584]{1,0:T(8,128)(2,1)}, u32[]{:S(2)}, u32[]{:S(2)}) collective-permute-start(bf16[128,3584]{1,0:T(8,128)(2,1)} %shard_map.164), channel_id=1, source_target_pairs={{4,0},{5,1},{6,2},{7,3},{8,12},{9,13},{10,14},{11,15},{12,4},{13,5... | collective-permute-start | bytes 2752520 | tf_op jit(solution)/shard_map/ppermute | solution.py:268
  257.4 46.4 %copy-start.25 = (bf16[128,16]{1,0:T(8,128)(2,1)}, bf16[128,16]{1,0:T(8,128)(2,1)S(1)}, u32[]{:S(2)}) copy-start(bf16[128,16]{1,0:T(8,128)(2,1)S(1)} %multiply_convert_fusion.logit_ref) | copy-start | bytes 12292
  (17 other events, 88.7 us)

commit v4 on v3

--- a/solution.py
+++ b/solution.py
@@ -350,10 +350,9 @@
             got_1 = spread(sel_1)
             done_0 = run(got_0)
             got_1, done_0, own = join((got_1, done_0, own))
-            block_2f, block_2m, own = join((block_2f, block_2m, own))
+            sel_2, placed_2 = take(flag, [block_2m, block_2f])
+            sel_2, got_1, own = join((sel_2, got_1, own))
             block_3 = send(own, along([(0, 1), (3, 2), (1, 3), (2, 0)]))
-            sel_2, placed_2 = take(flag, [block_2m, block_2f])
-            sel_2, got_1 = join((sel_2, got_1))
             got_2 = spread(sel_2)
             done_1 = run(got_1, done_0[plane + 1 :])
             done_1, got_2[1], got_2[2] = join((done_1, got_2[1], got_2[2]))
@@ -366,20 +365,17 @@
             back_2 = spread(done_2[:plane])
             (part_1,) = sum_rows(placed_1, back_1)
             term_1 = send(part_1, along([(0, 1), (3, 2), (1, 3), (2, 0)]))
-            got_3, back_2, part_1, done_0 = join((got_3, back_2, part_1, done_0))
-            back_0 = spread(done_0[:plane])
+            got_3, part_1 = join((got_3, part_1))
+            done_3 = run(got_3, done_2[plane + 1 :])
+            done_3, term_1, back_2, done_0 = join((done_3, term_1, back_2, done_0))
+            back_3 = spread(done_3[:plane])
             part_2a, part_2b = sum_rows(placed_2, back_2, 2)
             term_2a = send(part_2a, across(3 * plane))
-            done_3 = run(got_3, done_2[plane + 1 :])
-            done_3, term_1, term_2a, part_2b, back_0 = join(
-                (done_3, term_1, term_2a, part_2b, back_0)
+            aux = done_3[plane:]
+            back_3[1], back_3[2], aux, part_2b, done_0 = join(
+                (back_3[1], back_3[2], aux, part_2b, done_0)
             )
-            back_3 = spread(done_3[:plane])
-            term_2b = send(part_2b, across(3 * plane))
-            aux = done_3[plane:]
-            back_3[1], back_3[2], aux, back_0 = join((back_3[1], back_3[2], aux, back_0))
             done_3 = [*done_3[:plane], *aux]
-            (part_0,) = sum_rows(placed_0, back_0)
             done = [done_0, done_1, done_2, done_3]
             sources = [
                 layer,
@@ -410,7 +406,13 @@
         route_sorted = dot_nn(order, route_all.astype(bf16)).astype(bf16)
         ret_route = lax.all_to_all(
             route_sorted, "expert", split_axis=0, concat_axis=0, tiled=True
-        ).astype(f32)
+        )
+        if layers == 4:
+            ret_route, term_2a, part_2b, done_0 = join((ret_route, term_2a, part_2b, done_0))
+            term_2b = send(part_2b, across(3 * plane))
+            back_0 = spread(done_0[:plane])
+            (part_0,) = sum_rows(placed_0, back_0)
+        ret_route = ret_route.astype(f32)
         slots = jnp.arange(1, cap + 1, dtype=jnp.int32).astype(f32)
         hit = slot_dense[:, :, None] == slots[None, None, :]
         route_grad = jnp.sum(jnp.where(hit, ret_route[None, :, :], 0.0), axis=2)
@@ -421,7 +423,7 @@
         if layers == 4:
             (part_3,) = sum_rows(placed_3, back_3)
             term_3 = send(part_3, along([(1, 0), (2, 3), (3, 1), (0, 2)]))
-            d_logit, part_3, part_0, term_2b = join((d_logit, part_3, part_0, term_2b))
+            d_logit, part_3 = join((d_logit, part_3))
             terms = [[part_0], [term_1], [term_2a, term_2b], [term_3]]
 
         router_part = dot_tn(d_logit, layer_input)

time: 311 us -> 293 us (0.942)
  waiting for transfers between devices: 112 us -> 84.8 us
  starting transfers between devices: 42.8 us -> 64.3 us
  blocking collectives: 13.5 us -> 0 us
    ppermute x32, waiting for transfers between devices: 112 us -> 81.5 us  [send(): return lax.ppermute(array, 'expert', pairs)]
    ppermute x32, starting transfers between devices: 34.8 us -> 51 us  [send(): return lax.ppermute(array, 'expert', pairs)]
    all_to_all x1 -> x0, blocking collectives: 13.5 us -> none  [shards(): lax.all_to_all(router_part, 'expert', split_axis=0, concat_axis=0, tiled=...]
    all_to_all x0 -> x1, starting transfers between devices: none -> 6.08 us  [shards(): lax.all_to_all(router_part, 'expert', split_axis=0, concat_axis=0, tiled=...]
    all_to_all x1, waiting for transfers between devices: 0.01 us -> 3.31 us  [shards(): lax.all_to_all(route_sorted, 'expert', split_axis=0, concat_axis=0, tiled...]
    unnamed x64 -> x71, local copies, waits for them, and re-layouts: 5.17 us -> 6.5 us
  transfers between devices with their start and end apart: 33 -> 34, of which waited for: 14 -> 12; matrix products, arithmetic and copies ran while one was open for 3% -> 3% of each run, Pallas kernels for 37% -> 38%
where the time goes in v4:
time: 293 us; the launch traced here: 291 us
  Pallas kernels  119 us (41%)
  waiting for transfers between devices  84.8 us (29%)
  starting transfers between devices  64.3 us (22%)
  local copies, waits for them, and re-layouts  11.2 us (4%)
  other arithmetic  8.03 us (3%)
  matrix products  3.33 us (1%)
    pallas_call x4, Pallas kernels, expert_rows(): pl.pallas_call(functools.partial(expert_kernel, len(carry), cap, width, r...  87.3 us
    ppermute x32, waiting for transfers between devices, send(): return lax.ppermute(array, 'expert', pairs)  81.5 us
    ppermute x32, starting transfers between devices, send(): return lax.ppermute(array, 'expert', pairs)  51 us
    pallas_call x4, Pallas kernels, select_rows(): pl.pallas_call(functools.partial(select_kernel, parts, meta_at, slots_hel...  17 us
    pallas_call x4, Pallas kernels, sum_rows(): pl.pallas_call(sum_kernel, out_shape=[jax.ShapeDtypeStruct((tok // parts,...  10.7 us
    all_to_all x1, starting transfers between devices, shards(): lax.all_to_all(route_sorted, 'expert', split_axis=0, concat_axis=0, tiled...  7.2 us
    unnamed x71, local copies, waits for them, and re-layouts  6.5 us
    all_to_all x1, starting transfers between devices, shards(): lax.all_to_all(router_part, 'expert', split_axis=0, concat_axis=0, tiled=...  6.08 us
  transfers between devices with their start and end apart: 34, of which 12 were waited for; matrix products, arithmetic and copies ran while one was open for 3% of the time, Pallas kernels for 38%

profile of v4, /device:TPU:15, one launch (start us, length us, event | category | flops | bytes accessed | tf_op | source)
XLA Modules:
  0.0 291.4 jit_solution(14514751636819935984)
XLA Ops:
  2.3 2.2 fusion.15
  5.1 2.2 concatenate.13.refs_0_
  9.0 4.1 %shard_map.154 = (bf16[48,7296]{1,0:T(8,128)(2,1)}, bf16[48,7296]{1,0:T(8,128)(2,1)}, bf16[48,7296]{1,0:T(8,128)(2,1)}, bf16[48,7296]{1,0:T(8,128)(2,1)}, bf16[192,128]{1,0:T(8,128)(2,1)}) custom-call(s32[1]{0:T(128)} %bitcast.13.flag_ref, bf16[16,128]{1,0:T(8,128)(2,1)} %pad_convert_fusion.guide_ref, bf16[128,7296]{1,0:T(8,128)(2,1)} %copy-done), custom_call_target="tpu_custom_call" | custom-call | flops 1024 | bytes 1024 | tf_op jit(solution)/shard_map/pallas_call | solution.py:87
  14.3 1.4 collective-permute-start.3
  16.0 15.6 %collective-permute-done.2.refs_2_ = bf16[48,7296]{1,0:T(8,128)(2,1)S(1)} collective-permute-done((bf16[48,7296]{1,0:T(8,128)(2,1)}, bf16[48,7296]{1,0:T(8,128)(2,1)S(1)}, u32[]{:S(2)}, u32[]{:S(2)}) %collective-permute-start.2) | collective-permute-done | bytes 700448 | tf_op jit(solution)/shard_map/ppermute | solution.py:268
  31.7 15.4 %collective-permute-done.3.refs_3_ = bf16[48,7296]{1,0:T(8,128)(2,1)S(1)} collective-permute-done((bf16[48,7296]{1,0:T(8,128)(2,1)}, bf16[48,7296]{1,0:T(8,128)(2,1)S(1)}, u32[]{:S(2)}, u32[]{:S(2)}) %collective-permute-start.3) | collective-permute-done | bytes 700448 | tf_op jit(solution)/shard_map/ppermute | solution.py:268
  47.1 2.9 collective-permute-done.refs_0_
  50.0 3.2 %collective-permute-start.4 = (bf16[128,7296]{1,0:T(8,128)(2,1)}, bf16[128,7296]{1,0:T(8,128)(2,1)S(1)}, u32[]{:S(2)}, u32[]{:S(2)}) collective-permute-start(bf16[128,7296]{1,0:T(8,128)(2,1)} %copy-done), channel_id=1, source_target_pairs={{4,8},{5,9},{6,10},{7,11},{8,4},{9,5},{10,6},{11,7},{20,24},{21,25... | collective-permute-start | bytes 5603336 | tf_op jit(solution)/shard_map/ppermute | solution.py:268
  53.2 2.5 collective-permute-start.5
  55.7 4.1 %shard_map.156 = (bf16[48,7296]{1,0:T(8,128)(2,1)}, bf16[48,7296]{1,0:T(8,128)(2,1)}, bf16[48,7296]{1,0:T(8,128)(2,1)}, bf16[48,7296]{1,0:T(8,128)(2,1)}, bf16[192,128]{1,0:T(8,128)(2,1)}) custom-call(s32[1]{0:T(128)} %bitcast.13.flag_ref, bf16[16,128]{1,0:T(8,128)(2,1)} %pad_convert_fusion.guide_ref, bf16[128,7296]{1,0:T(8,128)(2,1)} %collective-permute-done.refs_0_), custom_call_target="tpu_custom_call" | custom-call | flops 1024 | bytes 1024 | tf_op jit(solution)/shard_map/pallas_call | solution.py:87
  59.8 1.8 collective-permute-start.6
  61.9 1.4 collective-permute-start.8
  63.9 21.5 %shard_map.157 = (bf16[48,3584]{1,0:T(8,128)(2,1)}, bf16[48,3584]{1,0:T(8,128)(2,1)}, bf16[48,3584]{1,0:T(8,128)(2,1)}, bf16[48,3584]{1,0:T(8,128)(2,1)}, f32[19...) custom-call(f32[1,128]{1,0:T(1,128)} %compare_convert_fusion.mine_ref, ...), custom_call_target="tpu_custom_call" | custom-call | flops 1024 | bytes 1024 | tf_op jit(solution)/shard_map/pallas_call | solution.py:219
  85.4 9.2 %collective-permute-done.8.refs_3_ = bf16[48,7296]{1,0:T(8,128)(2,1)} collective-permute-done((bf16[48,7296]{1,0:T(8,128)(2,1)}, bf16[48,7296]{1,0:T(8,128)(2,1)}, u32[]{:S(2)}, u32[]{:S(2)}) %collective-permute-start.8) | collective-permute-done | bytes 700448 | tf_op jit(solution)/shard_map/ppermute | solution.py:268
  94.6 1.3 copy-done.3
  95.9 4.7 %shard_map.155 = (bf16[48,7296]{1,0:T(8,128)(2,1)}, bf16[48,7296]{1,0:T(8,128)(2,1)}, bf16[48,7296]{1,0:T(8,128)(2,1)}, bf16[48,7296]{1,0:T(8,128)(2,1)}, bf16[192,128]{1,0:T(8,128)(2,1)}) custom-call(s32[1]{0:T(128)} %bitcast.13.flag_ref, bf16[16,128]{1,0:T(8,128)(2,1)} %pad_convert_fusion.guide_ref, bf16[128,7296]{1,0:T(8,128)(2,1)} %copy-done.3, ...), custom_call_target="tpu_custom_call" | custom-call | flops 1024 | bytes 1024 | tf_op jit(solution)/shard_map/pallas_call | solution.py:87
  100.5 2.2 collective-permute-start.10
  103.0 1.4 collective-permute-start.15
  104.4 21.9 %shard_map.159 = (bf16[48,3584]{1,0:T(8,128)(2,1)}, bf16[48,3584]{1,0:T(8,128)(2,1)}, bf16[48,3584]{1,0:T(8,128)(2,1)}, bf16[48,3584]{1,0:T(8,128)(2,1)}, f32[19...) custom-call(f32[1,128]{1,0:T(1,128)} %compare_convert_fusion.mine_ref, ...), custom_call_target="tpu_custom_call" | custom-call | flops 1024 | bytes 1024 | tf_op jit(solution)/shard_map/pallas_call | solution.py:219
  126.8 1.7 collective-permute-start.14
  128.5 13.6 %collective-permute-done.9.refs_0_ = bf16[128,7296]{1,0:T(8,128)(2,1)S(1)} collective-permute-done((bf16[128,7296]{1,0:T(8,128)(2,1)S(1)}, bf16[128,7296]{1,0:T(8,128)(2,1)S(1)}, u32[]{:S(2)}, u32[]{:S(2)}) %collective-permute-start.9) | collective-permute-done | bytes 1867808 | tf_op jit(solution)/shard_map/ppermute | solution.py:268
  142.1 1.3 copy-done.4
  143.5 4.1 %shard_map.158 = (bf16[48,7296]{1,0:T(8,128)(2,1)}, bf16[48,7296]{1,0:T(8,128)(2,1)}, bf16[48,7296]{1,0:T(8,128)(2,1)}, bf16[48,7296]{1,0:T(8,128)(2,1)}, bf16[192,128]{1,0:T(8,128)(2,1)}) custom-call(s32[1]{0:T(128)} %bitcast.13.flag_ref, bf16[16,128]{1,0:T(8,128)(2,1)} %pad_convert_fusion.guide_ref, bf16[128,7296]{1,0:T(8,128)(2,1)} %copy-done.4), custom_call_target="tpu_custom_call" | custom-call | flops 1024 | bytes 1024 | tf_op jit(solution)/shard_map/pallas_call | solution.py:87
  147.7 2.5 collective-permute-done.14.refs_3_
  150.9 2.7 shard_map.161
  153.6 1.2 collective-permute-start.19
  154.7 1.7 collective-permute-start.18
  156.4 22.1 %shard_map.160 = (bf16[48,3584]{1,0:T(8,128)(2,1)}, bf16[48,3584]{1,0:T(8,128)(2,1)}, bf16[48,3584]{1,0:T(8,128)(2,1)}, bf16[48,3584]{1,0:T(8,128)(2,1)}, f32[19...) custom-call(f32[1,128]{1,0:T(1,128)} %compare_convert_fusion.mine_ref, ...), custom_call_target="tpu_custom_call" | custom-call | flops 1024 | bytes 1024 | tf_op jit(solution)/shard_map/pallas_call | solution.py:219
  178.9 1.8 collective-permute-start.22
  180.8 3.0 %collective-permute-done.18.refs_3_ = bf16[48,7296]{1,0:T(8,128)(2,1)} collective-permute-done((bf16[48,7296]{1,0:T(8,128)(2,1)}, bf16[48,7296]{1,0:T(8,128)(2,1)}, u32[]{:S(2)}, u32[]{:S(2)}) %collective-permute-start.18) | collective-permute-done | bytes 700448 | tf_op jit(solution)/shard_map/ppermute | solution.py:268
  183.8 21.8 %shard_map.162 = (bf16[48,3584]{1,0:T(8,128)(2,1)}, bf16[48,3584]{1,0:T(8,128)(2,1)}, bf16[48,3584]{1,0:T(8,128)(2,1)}, bf16[48,3584]{1,0:T(8,128)(2,1)}, f32[19...) custom-call(f32[1,128]{1,0:T(1,128)} %compare_convert_fusion.mine_ref, ...), custom_call_target="tpu_custom_call" | custom-call | flops 1024 | bytes 1024 | tf_op jit(solution)/shard_map/pallas_call | solution.py:219
  207.1 2.7 shard_map.163
  209.8 1.3 collective-permute-start.25
  211.1 1.0 convert_reduce_fusion.1
  212.2 2.2 collective-permute-start.26
  214.4 1.4 collective-permute-done.24.refs_2_
  215.8 1.1 convert_reduce_fusion
  217.0 1.0 convert_reduce_fusion.3
  218.8 7.2 %all-to-all-start = ((bf16[16,1,48]{2,1,0:T(2,128)(2,1)}), bf16[16,1,48]{2,1,0:T(2,128)(2,1)S(1)}, u32[]{:S(2)}, u32[]{:S(2)}) async-start(bf16[16,1,48]{2,1,0:T(2,128)(2,1)} %copy.54), calls=%async_computation | async-start | bytes 16384 | tf_op jit(solution)/shard_map/all_to_all | solution.py:407
  226.9 2.7 shard_map.164
  229.9 3.3 %all-to-all-done = bf16[16,1,48]{2,1,0:T(2,128)(2,1)S(1)} async-done(((bf16[16,1,48]{2,1,0:T(2,128)(2,1)}), bf16[16,1,48]{2,1,0:T(2,128)(2,1)S(1)}, u32[]{:S(2)}, u32[]{:S(2)}) %all-to-all-start) | async-done | bytes 1568 | tf_op jit(solution)/shard_map/all_to_all | solution.py:407
  234.6 21.2 %collective-permute-start.30 = (bf16[64,3584]{1,0:T(8,128)(2,1)}, bf16[64,3584]{1,0:T(8,128)(2,1)S(1)}, u32[]{:S(2)}, u32[]{:S(2)}) collective-permute-start(bf16[64,3584]{1,0:T(8,128)(2,1)} %get-tuple-element.343), channel_id=1, source_target_pairs={{0,12},{1,13},{2,14},{3,15},{4,8},{5,9},{6,10},{7,11},{8,4},{9,5},... | collective-permute-start | bytes 1376264 | tf_op jit(solution)/shard_map/ppermute | solution.py:268
  257.2 6.1 %all-to-all-start.1 = ((f32[16,16,224]{2,1,0:T(8,128)}), f32[16,16,224]{2,1,0:T(8,128)S(1)}, u32[]{:S(2)}, u32[]{:S(2)}) async-start(f32[16,16,224]{2,1,0:T(8,128)} %bitcast.36), calls=%async_computation.1 | async-start | bytes 524288 | tf_op jit(solution)/shard_map/all_to_all | solution.py:432
  263.9 1.5 collective-permute-start.29
  265.4 9.1 %collective-permute-done.28.refs_2_ = bf16[48,3584]{1,0:T(8,128)(2,1)S(1)} collective-permute-done((bf16[48,3584]{1,0:T(8,128)(2,1)S(1)}, bf16[48,3584]{1,0:T(8,128)(2,1)S(1)}, u32[]{:S(2)}, u32[]{:S(2)}) %collective-permute-start.28) | collective-permute-done | bytes 344096 | tf_op jit(solution)/shard_map/ppermute | solution.py:268
  274.5 8.3 %collective-permute-done.29.refs_3_ = bf16[48,3584]{1,0:T(8,128)(2,1)S(1)} collective-permute-done((bf16[48,3584]{1,0:T(8,128)(2,1)S(1)}, bf16[48,3584]{1,0:T(8,128)(2,1)S(1)}, u32[]{:S(2)}, u32[]{:S(2)}) %collective-permute-start.29) | collective-permute-done | bytes 344096 | tf_op jit(solution)/shard_map/ppermute | solution.py:268
  283.6 2.7 shard_map.165.refs_0_
  287.8 3.7 %shard_map.166 = bf16[128,3584]{1,0:T(8,128)(2,1)} custom-call(bf16[128,16]{1,0:T(8,128)(2,1)} %copy-done.27, bf16[16,3584]{1,0:T(8,128)(2,1)} %bitcast.66, bf16[128,3584]{1,0:T(8,128)(2,1)} %shard_map.165.refs_0_, bf16[128,3584]{1,0:T(8,128)(2,1)} %copy-done.5, bf16[64,3584]{1,0:T(8,128)(2,1)} %copy-done.13, bf16[64,3584]{1,0:T(8,128)(2,1)} %copy-done.14, ...), custom_call_target="tpu_custom_call" | custom-call | flops 1024 | bytes 1024 | tf_op jit(solution)/shard_map/pallas_call | solution.py:136
  (142 shorter events, 17.3 us)
Async XLA Ops:
  7.3 42.6 %collective-permute-start = (bf16[128,7296]{1,0:T(8,128)(2,1)S(1)}, bf16[128,7296]{1,0:T(8,128)(2,1)}, u32[]{:S(2)}, u32[]{:S(2)}) collective-permute-start(bf16[128,7296]{1,0:T(8,128)(2,1)S(1)} %concatenate.13.refs_0_), channel_id=1, source_target_pairs={{0,8},{1,9},{2,10},{3,11},{12,4},{13,5},{14,6},{15,7},{4,0},{5,1},... | collective-permute-start | bytes 5603336 | tf_op jit(solution)/shard_map/ppermute | solution.py:268
  13.2 2.9 collective-permute-start.1
  14.0 17.6 %collective-permute-start.2 = (bf16[48,7296]{1,0:T(8,128)(2,1)}, bf16[48,7296]{1,0:T(8,128)(2,1)S(1)}, u32[]{:S(2)}, u32[]{:S(2)}) collective-permute-start(bf16[48,7296]{1,0:T(8,128)(2,1)} %get-tuple-element.185), channel_id=1, source_target_pairs={{0,2},{1,3},{2,0},{3,1},{4,6},{5,7},{6,4},{7,5},{8,10},{9,11},{10,... | collective-permute-start | bytes 2101256 | tf_op jit(solution)/shard_map/ppermute | solution.py:268
  14.3 32.8 %collective-permute-start.3 = (bf16[48,7296]{1,0:T(8,128)(2,1)}, bf16[48,7296]{1,0:T(8,128)(2,1)S(1)}, u32[]{:S(2)}, u32[]{:S(2)}) collective-permute-start(bf16[48,7296]{1,0:T(8,128)(2,1)} %get-tuple-element.186), channel_id=1, source_target_pairs={{0,3},{1,2},{2,1},{3,0},{4,7},{5,6},{6,5},{7,4},{8,11},{9,10},{10,... | collective-permute-start | bytes 2101256 | tf_op jit(solution)/shard_map/ppermute | solution.py:268
  16.0 33.9 %copy-start.10 = (bf16[48,7296]{1,0:T(8,128)(2,1)}, bf16[48,7296]{1,0:T(8,128)(2,1)S(1)}, u32[]{:S(2)}) copy-start(bf16[48,7296]{1,0:T(8,128)(2,1)S(1)} %collective-permute-done.1.refs_1_) | copy-start | bytes 2101252
  31.7 18.3 %copy-start.11 = (bf16[48,7296]{1,0:T(8,128)(2,1)}, bf16[48,7296]{1,0:T(8,128)(2,1)S(1)}, u32[]{:S(2)}) copy-start(bf16[48,7296]{1,0:T(8,128)(2,1)S(1)} %collective-permute-done.2.refs_2_) | copy-start | bytes 2101252
  50.0 44.6 %collective-permute-start.4 = (bf16[128,7296]{1,0:T(8,128)(2,1)}, bf16[128,7296]{1,0:T(8,128)(2,1)S(1)}, u32[]{:S(2)}, u32[]{:S(2)}) collective-permute-start(bf16[128,7296]{1,0:T(8,128)(2,1)} %copy-done), channel_id=1, source_target_pairs={{4,8},{5,9},{6,10},{7,11},{8,4},{9,5},{10,6},{11,7},{20,24},{21,25... | collective-permute-start | bytes 5603336 | tf_op jit(solution)/shard_map/ppermute | solution.py:268
  53.2 41.4 %collective-permute-start.5 = (bf16[128,7296]{1,0:T(8,128)(2,1)}, bf16[128,7296]{1,0:T(8,128)(2,1)}, u32[]{:S(2)}, u32[]{:S(2)}) collective-permute-start(bf16[128,7296]{1,0:T(8,128)(2,1)} %collective-permute-done.refs_0_), channel_id=1, source_target_pairs={{4,0},{5,1},{6,2},{7,3},{8,12},{9,13},{10,14},{11,15},{20,16},{21,... | collective-permute-start | bytes 5603336 | tf_op jit(solution)/shard_map/ppermute | solution.py:268
  59.8 25.6 %collective-permute-start.6 = (bf16[48,7296]{1,0:T(8,128)(2,1)}, bf16[48,7296]{1,0:T(8,128)(2,1)S(1)}, u32[]{:S(2)}, u32[]{:S(2)}) collective-permute-start(bf16[48,7296]{1,0:T(8,128)(2,1)} %get-tuple-element.194), channel_id=1, source_target_pairs={{0,1},{1,0},{2,3},{3,2},{4,5},{5,4},{6,7},{7,6},{8,9},{9,8},{10,11... | collective-permute-start | bytes 2101256 | tf_op jit(solution)/shard_map/ppermute | solution.py:268
  61.6 23.8 %collective-permute-start.7 = (bf16[48,7296]{1,0:T(8,128)(2,1)}, bf16[48,7296]{1,0:T(8,128)(2,1)}, u32[]{:S(2)}, u32[]{:S(2)}) collective-permute-start(bf16[48,7296]{1,0:T(8,128)(2,1)} %get-tuple-element.195), channel_id=1, source_target_pairs={{0,2},{1,3},{2,0},{3,1},{4,6},{5,7},{6,4},{7,5},{8,10},{9,11},{10,... | collective-permute-start | bytes 2101256 | tf_op jit(solution)/shard_map/ppermute | solution.py:268
  61.9 32.7 %collective-permute-start.8 = (bf16[48,7296]{1,0:T(8,128)(2,1)}, bf16[48,7296]{1,0:T(8,128)(2,1)}, u32[]{:S(2)}, u32[]{:S(2)}) collective-permute-start(bf16[48,7296]{1,0:T(8,128)(2,1)} %get-tuple-element.196), channel_id=1, source_target_pairs={{0,3},{1,2},{2,1},{3,0},{4,7},{5,6},{6,5},{7,4},{8,11},{9,10},{10,... | collective-permute-start | bytes 2101256 | tf_op jit(solution)/shard_map/ppermute | solution.py:268
  100.5 41.6 %collective-permute-start.9 = (bf16[128,7296]{1,0:T(8,128)(2,1)S(1)}, bf16[128,7296]{1,0:T(8,128)(2,1)S(1)}, u32[]{:S(2)}, u32[]{:S(2)}) collective-permute-start(bf16[128,7296]{1,0:T(8,128)(2,1)S(1)} %copy-done.1), channel_id=1, source_target_pairs={{0,4},{1,5},{2,6},{3,7},{12,8},{13,9},{14,10},{15,11},{4,12},{5,13... | collective-permute-start | bytes 5603336 | tf_op jit(solution)/shard_map/ppermute | solution.py:268
  100.5 25.8 %collective-permute-start.10 = (bf16[48,7296]{1,0:T(8,128)(2,1)}, bf16[48,7296]{1,0:T(8,128)(2,1)S(1)}, u32[]{:S(2)}, u32[]{:S(2)}) collective-permute-start(bf16[48,7296]{1,0:T(8,128)(2,1)} %get-tuple-element.237), channel_id=1, source_target_pairs={{0,1},{1,0},{2,3},{3,2},{4,5},{5,4},{6,7},{7,6},{8,9},{9,8},{10,11... | collective-permute-start | bytes 2101256 | tf_op jit(solution)/shard_map/ppermute | solution.py:268
  102.8 23.5 %collective-permute-start.11 = (bf16[48,7296]{1,0:T(8,128)(2,1)}, bf16[48,7296]{1,0:T(8,128)(2,1)S(1)}, u32[]{:S(2)}, u32[]{:S(2)}) collective-permute-start(bf16[48,7296]{1,0:T(8,128)(2,1)} %get-tuple-element.238), channel_id=1, source_target_pairs={{0,2},{1,3},{2,0},{3,1},{4,6},{5,7},{6,4},{7,5},{8,10},{9,11},{10,... | collective-permute-start | bytes 2101256 | tf_op jit(solution)/shard_map/ppermute | solution.py:268
  103.0 44.7 %collective-permute-start.15 = (bf16[48,7296]{1,0:T(8,128)(2,1)}, bf16[48,7296]{1,0:T(8,128)(2,1)S(1)}, u32[]{:S(2)}, u32[]{:S(2)}) collective-permute-start(bf16[48,7296]{1,0:T(8,128)(2,1)} %get-tuple-element.246), channel_id=1, source_target_pairs={{0,3},{1,2},{2,1},{3,0},{4,7},{5,6},{6,5},{7,4},{8,11},{9,10},{10,... | collective-permute-start | bytes 2101256 | tf_op jit(solution)/shard_map/ppermute | solution.py:268
  126.3 30.1 %copy-start.6 = (bf16[48,7296]{1,0:T(8,128)(2,1)}, bf16[48,7296]{1,0:T(8,128)(2,1)S(1)}, u32[]{:S(2)}) copy-start(bf16[48,7296]{1,0:T(8,128)(2,1)S(1)} %collective-permute-done.10.refs_1_) | copy-start | bytes 2101252
  126.3 30.1 %copy-start.7 = (bf16[48,7296]{1,0:T(8,128)(2,1)}, bf16[48,7296]{1,0:T(8,128)(2,1)S(1)}, u32[]{:S(2)}) copy-start(bf16[48,7296]{1,0:T(8,128)(2,1)S(1)} %collective-permute-done.11.refs_2_) | copy-start | bytes 2101252
  126.3 21.3 %collective-permute-start.12 = (bf16[48,3584]{1,0:T(8,128)(2,1)}, bf16[48,3584]{1,0:T(8,128)(2,1)S(1)}, u32[]{:S(2)}, u32[]{:S(2)}) collective-permute-start(bf16[48,3584]{1,0:T(8,128)(2,1)} %get-tuple-element.240), channel_id=1, source_target_pairs={{0,1},{1,0},{2,3},{3,2},{4,5},{5,4},{6,7},{7,6},{8,9},{9,8},{10,11... | collective-permute-start | bytes 1032200 | tf_op jit(solution)/shard_map/ppermute | solution.py:268
  126.6 21.1 %collective-permute-start.13 = (bf16[48,3584]{1,0:T(8,128)(2,1)}, bf16[48,3584]{1,0:T(8,128)(2,1)S(1)}, u32[]{:S(2)}, u32[]{:S(2)}) collective-permute-start(bf16[48,3584]{1,0:T(8,128)(2,1)} %get-tuple-element.241), channel_id=1, source_target_pairs={{0,2},{1,3},{2,0},{3,1},{4,6},{5,7},{6,4},{7,5},{8,10},{9,11},{10,... | collective-permute-start | bytes 1032200 | tf_op jit(solution)/shard_map/ppermute | solution.py:268
  126.8 23.3 %collective-permute-start.14 = (bf16[48,3584]{1,0:T(8,128)(2,1)}, bf16[48,3584]{1,0:T(8,128)(2,1)S(1)}, u32[]{:S(2)}, u32[]{:S(2)}) collective-permute-start(bf16[48,3584]{1,0:T(8,128)(2,1)} %get-tuple-element.242), channel_id=1, source_target_pairs={{0,3},{1,2},{2,1},{3,0},{4,7},{5,6},{6,5},{7,4},{8,11},{9,10},{10,... | collective-permute-start | bytes 1032200 | tf_op jit(solution)/shard_map/ppermute | solution.py:268
  150.1 28.3 %collective-permute-start.16 = (bf16[48,7296]{1,0:T(8,128)(2,1)}, bf16[48,7296]{1,0:T(8,128)(2,1)}, u32[]{:S(2)}, u32[]{:S(2)}) collective-permute-start(bf16[48,7296]{1,0:T(8,128)(2,1)} %get-tuple-element.265), channel_id=1, source_target_pairs={{0,1},{1,0},{2,3},{3,2},{4,5},{5,4},{6,7},{7,6},{8,9},{9,8},{10,11... | collective-permute-start | bytes 2101256 | tf_op jit(solution)/shard_map/ppermute | solution.py:268
  150.4 28.1 %collective-permute-start.17 = (bf16[48,7296]{1,0:T(8,128)(2,1)}, bf16[48,7296]{1,0:T(8,128)(2,1)}, u32[]{:S(2)}, u32[]{:S(2)}) collective-permute-start(bf16[48,7296]{1,0:T(8,128)(2,1)} %get-tuple-element.266), channel_id=1, source_target_pairs={{0,2},{1,3},{2,0},{3,1},{4,6},{5,7},{6,4},{7,5},{8,10},{9,11},{10,... | collective-permute-start | bytes 2101256 | tf_op jit(solution)/shard_map/ppermute | solution.py:268
  153.6 52.1 %collective-permute-start.19 = (bf16[128,3584]{1,0:T(8,128)(2,1)}, bf16[128,3584]{1,0:T(8,128)(2,1)S(1)}, u32[]{:S(2)}, u32[]{:S(2)}) collective-permute-start(bf16[128,3584]{1,0:T(8,128)(2,1)} %shard_map.161), channel_id=1, source_target_pairs={{0,4},{1,5},{2,6},{3,7},{12,8},{13,9},{14,10},{15,11},{4,12},{5,13... | collective-permute-start | bytes 2752520 | tf_op jit(solution)/shard_map/ppermute | solution.py:268
  154.7 29.1 %collective-permute-start.18 = (bf16[48,7296]{1,0:T(8,128)(2,1)}, bf16[48,7296]{1,0:T(8,128)(2,1)}, u32[]{:S(2)}, u32[]{:S(2)}) collective-permute-start(bf16[48,7296]{1,0:T(8,128)(2,1)} %get-tuple-element.269), channel_id=1, source_target_pairs={{0,3},{1,2},{2,1},{3,0},{4,7},{5,6},{6,5},{7,4},{8,11},{9,10},{10,... | collective-permute-start | bytes 2101256 | tf_op jit(solution)/shard_map/ppermute | solution.py:268
  178.5 27.2 %collective-permute-start.20 = (bf16[48,3584]{1,0:T(8,128)(2,1)}, bf16[48,3584]{1,0:T(8,128)(2,1)S(1)}, u32[]{:S(2)}, u32[]{:S(2)}) collective-permute-start(bf16[48,3584]{1,0:T(8,128)(2,1)} %get-tuple-element.293), channel_id=1, source_target_pairs={{0,1},{1,0},{2,3},{3,2},{4,5},{5,4},{6,7},{7,6},{8,9},{9,8},{10,11... | collective-permute-start | bytes 1032200 | tf_op jit(solution)/shard_map/ppermute | solution.py:268
  178.6 27.1 %collective-permute-start.21 = (bf16[48,3584]{1,0:T(8,128)(2,1)}, bf16[48,3584]{1,0:T(8,128)(2,1)S(1)}, u32[]{:S(2)}, u32[]{:S(2)}) collective-permute-start(bf16[48,3584]{1,0:T(8,128)(2,1)} %get-tuple-element.294), channel_id=1, source_target_pairs={{0,2},{1,3},{2,0},{3,1},{4,6},{5,7},{6,4},{7,5},{8,10},{9,11},{10,... | collective-permute-start | bytes 1032200 | tf_op jit(solution)/shard_map/ppermute | solution.py:268
  178.9 26.8 %collective-permute-start.22 = (bf16[48,3584]{1,0:T(8,128)(2,1)}, bf16[48,3584]{1,0:T(8,128)(2,1)S(1)}, u32[]{:S(2)}, u32[]{:S(2)}) collective-permute-start(bf16[48,3584]{1,0:T(8,128)(2,1)} %get-tuple-element.295), channel_id=1, source_target_pairs={{0,3},{1,2},{2,1},{3,0},{4,7},{5,6},{6,5},{7,4},{8,11},{9,10},{10,... | collective-permute-start | bytes 1032200 | tf_op jit(solution)/shard_map/ppermute | solution.py:268
  180.8 25.9 %copy-start.32 = (s32[4]{0:T(128)S(1)}, s32[4]{0:T(128)}, u32[]{:S(2)}) copy-start(s32[4]{0:T(128)} %get-tuple-element.353) | copy-start | bytes 52
  180.8 26.1 %copy-start.31 = (f32[192,1]{1,0:T(8,128)S(1)}, f32[192,1]{1,0:T(8,128)}, u32[]{:S(2)}) copy-start(f32[192,1]{1,0:T(8,128)} %get-tuple-element.320) | copy-start | bytes 2308
  205.7 20.4 %copy-start.30 = (f32[128,16]{1,0:T(8,128)S(1)}, f32[128,16]{1,0:T(8,128)}, u32[]{:S(2)}) copy-start(f32[128,16]{1,0:T(8,128)} %get-tuple-element.351) | copy-start | bytes 24580
  205.7 23.9 %copy-start.5 = (bf16[128,3584]{1,0:T(8,128)(2,1)}, bf16[128,3584]{1,0:T(8,128)(2,1)S(1)}, u32[]{:S(2)}) copy-start(bf16[128,3584]{1,0:T(8,128)(2,1)S(1)} %collective-permute-done.19.refs_1_) | copy-start | bytes 2752516
  206.5 7.9 %collective-permute-start.23 = (bf16[48,3584]{1,0:T(8,128)(2,1)}, bf16[48,3584]{1,0:T(8,128)(2,1)S(1)}, u32[]{:S(2)}, u32[]{:S(2)}) collective-permute-start(bf16[48,3584]{1,0:T(8,128)(2,1)} %get-tuple-element.301), channel_id=1, source_target_pairs={{0,1},{1,0},{2,3},{3,2},{4,5},{5,4},{6,7},{7,6},{8,9},{9,8},{10,11... | collective-permute-start | bytes 1032200 | tf_op jit(solution)/shard_map/ppermute | solution.py:268
  206.5 9.3 %collective-permute-start.24 = (bf16[48,3584]{1,0:T(8,128)(2,1)}, bf16[48,3584]{1,0:T(8,128)(2,1)S(1)}, u32[]{:S(2)}, u32[]{:S(2)}) collective-permute-start(bf16[48,3584]{1,0:T(8,128)(2,1)} %get-tuple-element.302), channel_id=1, source_target_pairs={{0,2},{1,3},{2,0},{3,1},{4,6},{5,7},{6,4},{7,5},{8,10},{9,11},{10,... | collective-permute-start | bytes 1032200 | tf_op jit(solution)/shard_map/ppermute | solution.py:268
  207.1 26.4 %copy-start.29 = (f32[128,16]{1,0:T(8,128)S(1)}, f32[128,16]{1,0:T(8,128)}, u32[]{:S(2)}) copy-start(f32[128,16]{1,0:T(8,128)} %copy-done.28) | copy-start | bytes 24580
  209.8 23.4 %collective-permute-start.25 = (bf16[64,3584]{1,0:T(8,128)(2,1)}, bf16[64,3584]{1,0:T(8,128)(2,1)S(1)}, u32[]{:S(2)}, u32[]{:S(2)}) collective-permute-start(bf16[64,3584]{1,0:T(8,128)(2,1)} %get-tuple-element.323), channel_id=1, source_target_pairs={{0,12},{1,13},{2,14},{3,15},{4,8},{5,9},{6,10},{7,11},{8,4},{9,5},... | collective-permute-start | bytes 1376264 | tf_op jit(solution)/shard_map/ppermute | solution.py:268
  212.2 13.9 %collective-permute-start.26 = (bf16[48,3584]{1,0:T(8,128)(2,1)}, bf16[48,3584]{1,0:T(8,128)(2,1)S(1)}, u32[]{:S(2)}, u32[]{:S(2)}) collective-permute-start(bf16[48,3584]{1,0:T(8,128)(2,1)} %get-tuple-element.334), channel_id=1, source_target_pairs={{0,3},{1,2},{2,1},{3,0},{4,7},{5,6},{6,5},{7,4},{8,11},{9,10},{10,... | collective-permute-start | bytes 1032200 | tf_op jit(solution)/shard_map/ppermute | solution.py:268
  218.8 14.4 %all-to-all-start = ((bf16[16,1,48]{2,1,0:T(2,128)(2,1)}), bf16[16,1,48]{2,1,0:T(2,128)(2,1)S(1)}, u32[]{:S(2)}, u32[]{:S(2)}) async-start(bf16[16,1,48]{2,1,0:T(2,128)(2,1)} %copy.54), calls=%async_computation | async-start | bytes 16384 | tf_op jit(solution)/shard_map/all_to_all | solution.py:407
  229.5 34.1 %copy-start.34 = (bf16[48,3584]{1,0:T(8,128)(2,1)S(1)}, bf16[48,3584]{1,0:T(8,128)(2,1)}, u32[]{:S(2)}) copy-start(bf16[48,3584]{1,0:T(8,128)(2,1)} %get-tuple-element.339) | copy-start | bytes 1032196
  229.5 34.3 %copy-start.33 = (bf16[48,3584]{1,0:T(8,128)(2,1)S(1)}, bf16[48,3584]{1,0:T(8,128)(2,1)}, u32[]{:S(2)}) copy-start(bf16[48,3584]{1,0:T(8,128)(2,1)} %get-tuple-element.340) | copy-start | bytes 1032196
  229.6 57.4 %collective-permute-start.31 = (bf16[128,3584]{1,0:T(8,128)(2,1)}, bf16[128,3584]{1,0:T(8,128)(2,1)}, u32[]{:S(2)}, u32[]{:S(2)}) collective-permute-start(bf16[128,3584]{1,0:T(8,128)(2,1)} %shard_map.164), channel_id=1, source_target_pairs={{4,0},{5,1},{6,2},{7,3},{8,12},{9,13},{10,14},{11,15},{12,4},{13,5... | collective-permute-start | bytes 2752520 | tf_op jit(solution)/shard_map/ppermute | solution.py:268
  233.2 53.1 %copy-start.13 = (bf16[64,3584]{1,0:T(8,128)(2,1)}, bf16[64,3584]{1,0:T(8,128)(2,1)S(1)}, u32[]{:S(2)}) copy-start(bf16[64,3584]{1,0:T(8,128)(2,1)S(1)} %collective-permute-done.25.refs_2_) | copy-start | bytes 1376260
  234.6 51.7 %copy-start.27 = (bf16[128,16]{1,0:T(8,128)(2,1)}, bf16[128,16]{1,0:T(8,128)(2,1)S(1)}, u32[]{:S(2)}) copy-start(bf16[128,16]{1,0:T(8,128)(2,1)S(1)} %multiply_convert_fusion.logit_ref) | copy-start | bytes 12292
  234.6 52.3 %collective-permute-start.30 = (bf16[64,3584]{1,0:T(8,128)(2,1)}, bf16[64,3584]{1,0:T(8,128)(2,1)S(1)}, u32[]{:S(2)}, u32[]{:S(2)}) collective-permute-start(bf16[64,3584]{1,0:T(8,128)(2,1)} %get-tuple-element.343), channel_id=1, source_target_pairs={{0,12},{1,13},{2,14},{3,15},{4,8},{5,9},{6,10},{7,11},{8,4},{9,5},... | collective-permute-start | bytes 1376264 | tf_op jit(solution)/shard_map/ppermute | solution.py:268
  257.2 29.2 %all-to-all-start.1 = ((f32[16,16,224]{2,1,0:T(8,128)}), f32[16,16,224]{2,1,0:T(8,128)S(1)}, u32[]{:S(2)}, u32[]{:S(2)}) async-start(f32[16,16,224]{2,1,0:T(8,128)} %bitcast.36), calls=%async_computation.1 | async-start | bytes 524288 | tf_op jit(solution)/shard_map/all_to_all | solution.py:432
  263.3 2.2 collective-permute-start.27
  263.6 10.9 %collective-permute-start.28 = (bf16[48,3584]{1,0:T(8,128)(2,1)S(1)}, bf16[48,3584]{1,0:T(8,128)(2,1)S(1)}, u32[]{:S(2)}, u32[]{:S(2)}) collective-permute-start(bf16[48,3584]{1,0:T(8,128)(2,1)S(1)} %copy-done.34), channel_id=1, source_target_pairs={{0,2},{1,3},{2,0},{3,1},{4,6},{5,7},{6,4},{7,5},{8,10},{9,11},{10,... | collective-permute-start | bytes 1032200 | tf_op jit(solution)/shard_map/ppermute | solution.py:268
  263.9 19.0 %collective-permute-start.29 = (bf16[48,3584]{1,0:T(8,128)(2,1)S(1)}, bf16[48,3584]{1,0:T(8,128)(2,1)S(1)}, u32[]{:S(2)}, u32[]{:S(2)}) collective-permute-start(bf16[48,3584]{1,0:T(8,128)(2,1)S(1)} %copy-done.33), channel_id=1, source_target_pairs={{0,3},{1,2},{2,1},{3,0},{4,7},{5,6},{6,5},{7,4},{8,11},{9,10},{10,... | collective-permute-start | bytes 1032200 | tf_op jit(solution)/shard_map/ppermute | solution.py:268
  265.4 17.5 %copy-start.21 = (bf16[48,3584]{1,0:T(8,128)(2,1)}, bf16[48,3584]{1,0:T(8,128)(2,1)S(1)}, u32[]{:S(2)}) copy-start(bf16[48,3584]{1,0:T(8,128)(2,1)S(1)} %collective-permute-done.27.refs_1_) | copy-start | bytes 1032196
  (21 other events, 90.6 us)

commit v5 on v4

--- a/solution.py
+++ b/solution.py
@@ -94,25 +94,35 @@
     )(flag, guide, *arrays)
 
 
-def sum_kernel(placed_ref, *refs):
+def sum_kernel(apart, placed_ref, *refs):
     pieces, outs = refs[:plane], refs[plane:]
-    for first, last in chunks(0, outs[0].shape[1], 512):
-        rows = jnp.concatenate([p[:, first:last] for p in pieces], axis=0)
-        total = dot_tn(placed_ref[...], rows).astype(bf16)
+    wide = pieces[0].shape[1]
+    rows, tags = (outs[:-1], outs[-1]) if apart else (outs, None)
+    stop = rows[0].shape[1]
+    for first, last in chunks(0, stop, 512) + chunks(stop, wide, 512):
+        joined = jnp.concatenate([p[:, first:last] for p in pieces], axis=0)
+        total = dot_tn(placed_ref[...], joined).astype(bf16)
+        if first >= stop:
+            tags[...] = total
+            continue
         at = 0
-        for out in outs:
+        for out in rows:
             out[:, first:last] = total[at : at + out.shape[0]]
             at += out.shape[0]
 
 
-def sum_rows(placed, pieces, parts=1):
-    cap, width = pieces[0].shape
+def sum_rows(placed, pieces, width, parts=1):
+    cap, wide = pieces[0].shape
     tok = placed.shape[1]
+    shapes = [jax.ShapeDtypeStruct((tok // parts, width), bf16)] * parts
+    apart = width < wide
+    if apart:
+        shapes.append(jax.ShapeDtypeStruct((tok, wide - width), bf16))
     return pl.pallas_call(
-        sum_kernel,
-        out_shape=[jax.ShapeDtypeStruct((tok // parts, width), bf16)] * parts,
+        functools.partial(sum_kernel, apart),
+        out_shape=shapes,
         in_specs=[vmem] * (1 + plane),
-        out_specs=[vmem] * parts,
+        out_specs=[vmem] * len(shapes),
         compiler_params=pltpu.CompilerParams(vmem_limit_bytes=vmem_bytes),
         cost_estimate=light,
     )(placed, *pieces)
@@ -149,8 +159,8 @@
     ins, refs = refs[:plane], refs[plane:]
     carry, refs = refs[:held], refs[held:]
     back_refs, refs = refs[:plane], refs[plane:]
-    route_ref, gag_ref, gau_ref, gbg_ref, gbu_ref = refs[:5]
-    xs, dys, weight, low, proj, both, acc = refs[5:]
+    gag_ref, gau_ref, gbg_ref, gbu_ref = refs[:4]
+    xs, dys, weight, route, low, proj, both, acc = refs[4:]
 
     def total(at, value, part=slice(None)):
         return value + carry[at][:, part] if held else value
@@ -172,7 +182,7 @@
         low[...] = dot_nt(xs[...], both[...]).astype(bf16)
         proj[...] = jnp.zeros_like(proj)
         acc[...] = jnp.zeros_like(acc)
-        route_ref[...] = jnp.zeros_like(route_ref)
+        route[...] = jnp.zeros_like(route)
 
     bg, bu = bg_ref[...], bu_ref[...]
     low_gate, low_up = low[:, :rank], low[:, rank:]
@@ -181,7 +191,7 @@
     back = dot_nt(dys[...], wd_ref[...])
     sigma = jax.nn.sigmoid(gate)
     act = gate * sigma
-    route_ref[...] += jnp.sum(back * (act * upval), axis=1, keepdims=True)
+    route[...] += jnp.sum(back * (act * upval), axis=1, keepdims=True)
     scaled = weight[...] * back
     d_gate = (scaled * upval * sigma * (1.0 + gate * (1.0 - sigma))).astype(bf16)
     d_up = (scaled * act).astype(bf16)
@@ -197,6 +207,9 @@
     @pl.when(step == pl.num_programs(0) - 1)
     def _():
         proj_b = proj[...].astype(bf16)
+        routes = (route[...] * mine_ref[...]).astype(bf16)
+        for i, out in enumerate(back_refs):
+            out[:, width:] = routes[i * cap : (i + 1) * cap]
         for first, last in chunks(0, width, 512):
             rows = (acc[:, first:last] + dot_nn(proj_b, both[:, first:last])).astype(bf16)
             for i, out in enumerate(back_refs):
@@ -213,7 +226,8 @@
     rank = a_gate.shape[0]
     cap = pieces[0].shape[0]
     rows = cap * plane
-    tile = 256
+    wide = width + mine.shape[1]
+    tile = 512
     second = pl.BlockSpec((rank, tile), lambda j: (0, j))
     grads = [whole_block((rank, width))] * 2 + [second] * 2
     return pl.pallas_call(
@@ -231,18 +245,18 @@
         ]
         + [whole_block(a.shape) for a in pieces]
         + (grads if carry else []),
-        out_shape=[jax.ShapeDtypeStruct((cap, width), bf16)] * plane
+        out_shape=[jax.ShapeDtypeStruct((cap, wide), bf16)] * plane
         + [
-            jax.ShapeDtypeStruct((rows, 1), f32),
             jax.ShapeDtypeStruct((rank, width), f32),
             jax.ShapeDtypeStruct((rank, width), f32),
             jax.ShapeDtypeStruct((rank, hidden), f32),
             jax.ShapeDtypeStruct((rank, hidden), f32),
         ],
-        out_specs=[whole_block((cap, width))] * plane + [whole_block((rows, 1))] + grads,
+        out_specs=[whole_block((cap, wide))] * plane + grads,
         scratch_shapes=[
             pltpu.VMEM((rows, width), bf16),
             pltpu.VMEM((rows, width), bf16),
+            pltpu.VMEM((rows, 1), f32),
             pltpu.VMEM((rows, 1), f32),
             pltpu.VMEM((rows, 2 * rank), bf16),
             pltpu.VMEM((rows, 2 * rank), f32),
@@ -320,6 +334,7 @@
         )
         own = jnp.concatenate([layer_input, meta, dy], axis=1)
         full = own.shape[1]
+        wide = width + meta_width
         meta_at = (width, width + meta_width)
 
         here = layer * plane + (place ^ jnp.arange(plane, dtype=jnp.int32))
@@ -350,81 +365,60 @@
             got_1 = spread(sel_1)
             done_0 = run(got_0)
             got_1, done_0, own = join((got_1, done_0, own))
+            back_0 = [done_0[0], send(done_0[1], across(1)), send(done_0[2], across(2))]
+            block_2f, block_2m, own, back_0[1] = join((block_2f, block_2m, own, back_0[1]))
             sel_2, placed_2 = take(flag, [block_2m, block_2f])
-            sel_2, got_1, own = join((sel_2, got_1, own))
+            sel_2, got_1, own, back_0[2] = join((sel_2, got_1, own, back_0[2]))
             block_3 = send(own, along([(0, 1), (3, 2), (1, 3), (2, 0)]))
             got_2 = spread(sel_2)
-            done_1 = run(got_1, done_0[plane + 1 :])
+            done_1 = run(got_1, done_0[plane:])
             done_1, got_2[1], got_2[2] = join((done_1, got_2[1], got_2[2]))
             back_1 = spread(done_1[:plane])
             sel_3, placed_3 = take(flag, [block_3])
             sel_3, back_1, got_2 = join((sel_3, back_1, got_2))
             got_3 = spread(sel_3)
-            done_2 = run(got_2, done_1[plane + 1 :])
-            done_2, got_3[1], got_3[2] = join((done_2, got_3[1], got_3[2]))
+            done_2 = run(got_2, done_1[plane:])
+            done_2, got_3[1], got_3[2], last_0 = join((done_2, got_3[1], got_3[2], done_0[3]))
             back_2 = spread(done_2[:plane])
-            (part_1,) = sum_rows(placed_1, back_1)
+            (part_1,) = sum_rows(placed_1, back_1, wide)
             term_1 = send(part_1, along([(0, 1), (3, 2), (1, 3), (2, 0)]))
-            got_3, part_1 = join((got_3, part_1))
-            done_3 = run(got_3, done_2[plane + 1 :])
-            done_3, term_1, back_2, done_0 = join((done_3, term_1, back_2, done_0))
+            got_3, part_1, back_2[1], last_0 = join((got_3, part_1, back_2[1], last_0))
+            back_0.append(send(last_0, across(3)))
+            done_3 = run(got_3, done_2[plane:])
+            done_3, term_1, back_2, back_0 = join((done_3, term_1, back_2, back_0))
             back_3 = spread(done_3[:plane])
-            part_2a, part_2b = sum_rows(placed_2, back_2, 2)
+            part_2a, part_2b, tag_2 = sum_rows(placed_2, back_2, width, 2)
+            tag_2 = send(tag_2, across(3 * plane))
             term_2a = send(part_2a, across(3 * plane))
-            aux = done_3[plane:]
-            back_3[1], back_3[2], aux, part_2b, done_0 = join(
-                (back_3[1], back_3[2], aux, part_2b, done_0)
+            back_3[1], back_3[2], part_2b, back_0, tag_2 = join(
+                (back_3[1], back_3[2], part_2b, back_0, tag_2)
             )
-            done_3 = [*done_3[:plane], *aux]
-            done = [done_0, done_1, done_2, done_3]
-            sources = [
-                layer,
-                jnp.where(mid, layer ^ 2, layer ^ 1),
-                layer ^ 3,
-                jnp.where(mid, layer ^ 1, layer ^ 2),
-            ]
+            part_0, tag_0 = sum_rows(placed_0, back_0, width)
+            part_3, tag_3 = sum_rows(placed_3, back_3, width)
+            swap_3 = along([(1, 0), (2, 3), (3, 1), (0, 2)])
+            tag_3 = send(tag_3, swap_3)
+            term_3 = send(part_3, swap_3)
+            tag_3, term_2a, part_2b = join((tag_3, term_2a, part_2b))
+            term_2b = send(part_2b, across(3 * plane))
+            tags = [tag_0, term_1[:, width:], tag_2, tag_3]
+            terms = [[part_0], [term_1], [term_2a, term_2b], [term_3]]
+            done = [done_3]
         else:
             flag = jnp.zeros((1,), jnp.int32)
-            done, sources, terms = [], [], []
+            done, tags, terms = [], [], []
             for g in range(layers):
                 block = own if g == 0 else send(own, across(g * plane))
                 sel, placed = take(flag, [block])
-                result = run(spread(sel), done[-1][plane + 1 :] if done else ())
-                (part,) = sum_rows(placed, spread(result[:plane]))
+                result = run(spread(sel), done[-1][plane:] if done else ())
+                (part,) = sum_rows(placed, spread(result[:plane]), wide)
                 terms.append([part if g == 0 else send(part, across(g * plane))])
                 done.append(result)
-                sources.append(layer ^ g)
-
-        route_all = jnp.concatenate(
-            [d[plane].reshape(plane, cap) for d in done], axis=0
-        )
-        origin = (
-            jnp.stack(sources)[:, None] * plane
-            + (place ^ jnp.arange(plane, dtype=jnp.int32))[None, :]
-        ).reshape(-1)
-        order = (origin[None, :] == jnp.arange(devices, dtype=jnp.int32)[:, None]).astype(bf16)
-        route_sorted = dot_nn(order, route_all.astype(bf16)).astype(bf16)
-        ret_route = lax.all_to_all(
-            route_sorted, "expert", split_axis=0, concat_axis=0, tiled=True
-        )
-        if layers == 4:
-            ret_route, term_2a, part_2b, done_0 = join((ret_route, term_2a, part_2b, done_0))
-            term_2b = send(part_2b, across(3 * plane))
-            back_0 = spread(done_0[:plane])
-            (part_0,) = sum_rows(placed_0, back_0)
-        ret_route = ret_route.astype(f32)
-        slots = jnp.arange(1, cap + 1, dtype=jnp.int32).astype(f32)
-        hit = slot_dense[:, :, None] == slots[None, None, :]
-        route_grad = jnp.sum(jnp.where(hit, ret_route[None, :, :], 0.0), axis=2)
+                tags.append(terms[-1][0][:, width:])
+
+        route_grad = sum(t[:, experts : 2 * experts].astype(f32) for t in tags)
         shared = jnp.sum(route_grad * picked, axis=1, keepdims=True) / (total * total)
         d_pick = route_scale * (route_grad / total - shared)
         d_logit = (mask * d_pick * scores * (1.0 - scores)).astype(bf16)
-
-        if layers == 4:
-            (part_3,) = sum_rows(placed_3, back_3)
-            term_3 = send(part_3, along([(1, 0), (2, 3), (3, 1), (0, 2)]))
-            d_logit, part_3 = join((d_logit, part_3))
-            terms = [[part_0], [term_1], [term_2a, term_2b], [term_3]]
 
         router_part = dot_tn(d_logit, layer_input)
         share = width // devices
@@ -434,7 +428,7 @@
 
         in_grad = final_sum(d_logit, router_matrix.T, terms)
 
-        grad_gate_a, grad_up_a, grad_gate_b, grad_up_b = done[-1][plane + 1 :]
+        grad_gate_a, grad_up_a, grad_gate_b, grad_up_b = done[-1][plane:]
         return (
             in_grad,
             router_grad,

time: 293 us -> 297 us (1.014)
  blocking collectives: 0 us -> 41.4 us
  starting transfers between devices: 64.3 us -> 29.3 us
  waiting for transfers between devices: 84.8 us -> 95.4 us
  Pallas kernels: 119 us -> 110 us
  other arithmetic: 8.03 us -> 4.89 us
    all_to_all x0 -> x1, blocking collectives: none -> 41.4 us  [shards(): lax.all_to_all(router_part, 'expert', split_axis=0, concat_axis=0, tiled=...]
    ppermute x32 -> x34, starting transfers between devices: 51 us -> 29.3 us  [send(): return lax.ppermute(array, 'expert', pairs)]
    ppermute x32 -> x34, waiting for transfers between devices: 81.5 us -> 95.4 us  [send(): return lax.ppermute(array, 'expert', pairs)]
    all_to_all x2 -> x0, starting transfers between devices: 13.3 us -> none  [the longest x1 7.2 us: shards(): lax.all_to_all(route_sorted, 'expert', split_axis=0, concat_axis=0, tiled...]
    pallas_call x4, Pallas kernels: 87.3 us -> 78.7 us  [expert_rows(): pl.pallas_call(functools.partial(expert_kernel, len(carry), cap, width, r...]
    all_to_all x2 -> x0, waiting for transfers between devices: 3.32 us -> none  [the longest x1 3.31 us: shards(): lax.all_to_all(route_sorted, 'expert', split_axis=0, concat_axis=0, tiled...]
    another operation x4 -> x0, other arithmetic: 3.18 us -> none
    unnamed x71 -> x72, local copies, waits for them, and re-layouts: 6.5 us -> 6.98 us
  transfers between devices with their start and end apart: 34 -> 34, of which waited for: 12 -> 12; matrix products, arithmetic and copies ran while one was open for 3% -> 2% of each run, Pallas kernels for 38% -> 35%
where the time goes in v5:
time: 297 us; the launch traced here: 295 us
  Pallas kernels  110 us (37%)
  waiting for transfers between devices  95.4 us (32%)
  blocking collectives  41.4 us (14%)
  starting transfers between devices  29.3 us (10%)
  local copies, waits for them, and re-layouts  9.68 us (3%)
  other arithmetic  4.89 us (2%)
    ppermute x34, waiting for transfers between devices, send(): return lax.ppermute(array, 'expert', pairs)  95.4 us
    pallas_call x4, Pallas kernels, expert_rows(): pl.pallas_call(functools.partial(expert_kernel, len(carry), cap, width, r...  78.7 us
    all_to_all x1, blocking collectives, shards(): lax.all_to_all(router_part, 'expert', split_axis=0, concat_axis=0, tiled=...  41.4 us
    ppermute x34, starting transfers between devices, send(): return lax.ppermute(array, 'expert', pairs)  29.3 us
    pallas_call x4, Pallas kernels, select_rows(): pl.pallas_call(functools.partial(select_kernel, parts, meta_at, slots_hel...  17 us
    pallas_call x4, Pallas kernels, sum_rows(): pl.pallas_call(functools.partial(sum_kernel, apart), out_shape=shapes, in...  10.9 us
    unnamed x72, local copies, waits for them, and re-layouts  6.98 us
  transfers between devices with their start and end apart: 34, of which 12 were waited for; matrix products, arithmetic and copies ran while one was open for 2% of the time, Pallas kernels for 35%

profile of v5, /device:TPU:15, one launch (start us, length us, event | category | flops | bytes accessed | tf_op | source)
XLA Modules:
  0.0 294.7 jit_solution(2497532812128511896)
XLA Ops:
  1.7 2.2 fusion.6
  4.5 2.2 concatenate.5.refs_0_
  7.0 0.8 pad_convert_fusion.guide_ref
  8.0 4.1 %shard_map.154 = (bf16[48,7296]{1,0:T(8,128)(2,1)}, bf16[48,7296]{1,0:T(8,128)(2,1)}, bf16[48,7296]{1,0:T(8,128)(2,1)}, bf16[48,7296]{1,0:T(8,128)(2,1)}, bf16[192,128]{1,0:T(8,128)(2,1)}) custom-call(s32[1]{0:T(128)} %bitcast.flag_ref, bf16[16,128]{1,0:T(8,128)(2,1)} %pad_convert_fusion.guide_ref, bf16[128,7296]{1,0:T(8,128)(2,1)} %copy-done), custom_call_target="tpu_custom_call" | custom-call | flops 1024 | bytes 1024 | tf_op jit(solution)/shard_map/pallas_call | solution.py:87
  13.0 1.4 collective-permute-start.3
  14.8 15.6 %collective-permute-done.2.refs_2_ = bf16[48,7296]{1,0:T(8,128)(2,1)S(1)} collective-permute-done((bf16[48,7296]{1,0:T(8,128)(2,1)}, bf16[48,7296]{1,0:T(8,128)(2,1)S(1)}, u32[]{:S(2)}, u32[]{:S(2)}) %collective-permute-start.2) | collective-permute-done | bytes 700448 | tf_op jit(solution)/shard_map/ppermute | solution.py:282
  30.4 15.4 %collective-permute-done.3.refs_3_ = bf16[48,7296]{1,0:T(8,128)(2,1)S(1)} collective-permute-done((bf16[48,7296]{1,0:T(8,128)(2,1)}, bf16[48,7296]{1,0:T(8,128)(2,1)S(1)}, u32[]{:S(2)}, u32[]{:S(2)}) %collective-permute-start.3) | collective-permute-done | bytes 700448 | tf_op jit(solution)/shard_map/ppermute | solution.py:282
  45.8 3.6 %collective-permute-done.refs_0_ = bf16[128,7296]{1,0:T(8,128)(2,1)} collective-permute-done((bf16[128,7296]{1,0:T(8,128)(2,1)S(1)}, bf16[128,7296]{1,0:T(8,128)(2,1)}, u32[]{:S(2)}, u32[]{:S(2)}) %collective-permute-start) | collective-permute-done | bytes 1867808 | tf_op jit(solution)/shard_map/ppermute | solution.py:282
  49.4 1.4 collective-permute-start.4
  50.8 4.2 %collective-permute-start.5 = (bf16[128,7296]{1,0:T(8,128)(2,1)}, bf16[128,7296]{1,0:T(8,128)(2,1)}, u32[]{:S(2)}, u32[]{:S(2)}) collective-permute-start(bf16[128,7296]{1,0:T(8,128)(2,1)} %copy-done), channel_id=1, source_target_pairs={{4,8},{5,9},{6,10},{7,11},{8,4},{9,5},{10,6},{11,7},{20,24},{21,25... | collective-permute-start | bytes 5603336 | tf_op jit(solution)/shard_map/ppermute | solution.py:282
  55.0 4.1 %shard_map.155 = (bf16[48,7296]{1,0:T(8,128)(2,1)}, bf16[48,7296]{1,0:T(8,128)(2,1)}, bf16[48,7296]{1,0:T(8,128)(2,1)}, bf16[48,7296]{1,0:T(8,128)(2,1)}, bf16[192,128]{1,0:T(8,128)(2,1)}) custom-call(s32[1]{0:T(128)} %bitcast.flag_ref, bf16[16,128]{1,0:T(8,128)(2,1)} %pad_convert_fusion.guide_ref, bf16[128,7296]{1,0:T(8,128)(2,1)} %collective-permute-done.refs_0_), custom_call_target="tpu_custom_call" | custom-call | flops 1024 | bytes 1024 | tf_op jit(solution)/shard_map/pallas_call | solution.py:87
  59.2 2.1 collective-permute-start.6
  61.5 1.4 collective-permute-start.8
  63.5 19.4 %shard_map.156 = (bf16[48,3712]{1,0:T(8,128)(2,1)}, bf16[48,3712]{1,0:T(8,128)(2,1)}, bf16[48,3712]{1,0:T(8,128)(2,1)}, bf16[48,3712]{1,0:T(8,128)(2,1)}, f32[32...) custom-call(f32[1,128]{1,0:T(1,128)} %compare_convert_fusion.mine_ref, ...), custom_call_target="tpu_custom_call" | custom-call | flops 1024 | bytes 1024 | tf_op jit(solution)/shard_map/pallas_call | solution.py:233
  82.9 11.4 %collective-permute-done.8.refs_3_ = bf16[48,7296]{1,0:T(8,128)(2,1)} collective-permute-done((bf16[48,7296]{1,0:T(8,128)(2,1)}, bf16[48,7296]{1,0:T(8,128)(2,1)}, u32[]{:S(2)}, u32[]{:S(2)}) %collective-permute-start.8) | collective-permute-done | bytes 700448 | tf_op jit(solution)/shard_map/ppermute | solution.py:282
  94.5 1.7 collective-permute-done.9.refs_1_
  96.2 1.3 copy-done.3
  97.5 4.7 %shard_map.157 = (bf16[48,7296]{1,0:T(8,128)(2,1)}, bf16[48,7296]{1,0:T(8,128)(2,1)}, bf16[48,7296]{1,0:T(8,128)(2,1)}, bf16[48,7296]{1,0:T(8,128)(2,1)}, bf16[192,128]{1,0:T(8,128)(2,1)}) custom-call(s32[1]{0:T(128)} %bitcast.flag_ref, bf16[16,128]{1,0:T(8,128)(2,1)} %pad_convert_fusion.guide_ref, bf16[128,7296]{1,0:T(8,128)(2,1)} %collective-permute-done.5.refs_0_, ...), custom_call_target="tpu_custom_call" | custom-call | flops 1024 | bytes 1024 | tf_op jit(solution)/shard_map/pallas_call | solution.py:87
  102.2 1.7 collective-permute-done.10.refs_2_
  103.9 0.8 copy-done.23
  104.7 1.4 collective-permute-start.12
  106.3 1.5 collective-permute-start.17
  107.8 19.8 %shard_map.159 = (bf16[48,3712]{1,0:T(8,128)(2,1)}, bf16[48,3712]{1,0:T(8,128)(2,1)}, bf16[48,3712]{1,0:T(8,128)(2,1)}, bf16[48,3712]{1,0:T(8,128)(2,1)}, f32[32...) custom-call(f32[1,128]{1,0:T(1,128)} %compare_convert_fusion.mine_ref, ...), custom_call_target="tpu_custom_call" | custom-call | flops 1024 | bytes 1024 | tf_op jit(solution)/shard_map/pallas_call | solution.py:233
  128.0 1.8 collective-permute-start.16
  129.8 15.7 %collective-permute-done.11.refs_0_ = bf16[128,7296]{1,0:T(8,128)(2,1)S(1)} collective-permute-done((bf16[128,7296]{1,0:T(8,128)(2,1)S(1)}, bf16[128,7296]{1,0:T(8,128)(2,1)S(1)}, u32[]{:S(2)}, u32[]{:S(2)}) %collective-permute-start.11) | collective-permute-done | bytes 1867808 | tf_op jit(solution)/shard_map/ppermute | solution.py:282
  145.5 1.3 copy-done.4
  146.9 4.1 %shard_map.158 = (bf16[48,7296]{1,0:T(8,128)(2,1)}, bf16[48,7296]{1,0:T(8,128)(2,1)}, bf16[48,7296]{1,0:T(8,128)(2,1)}, bf16[48,7296]{1,0:T(8,128)(2,1)}, bf16[192,128]{1,0:T(8,128)(2,1)}) custom-call(s32[1]{0:T(128)} %bitcast.flag_ref, bf16[16,128]{1,0:T(8,128)(2,1)} %pad_convert_fusion.guide_ref, bf16[128,7296]{1,0:T(8,128)(2,1)} %copy-done.4), custom_call_target="tpu_custom_call" | custom-call | flops 1024 | bytes 1024 | tf_op jit(solution)/shard_map/pallas_call | solution.py:87
  151.0 2.9 collective-permute-done.16.refs_3_
  154.4 1.7 collective-permute-start.20
  156.1 2.7 shard_map.161
  158.8 1.2 collective-permute-start.22
  160.0 19.8 %shard_map.160 = (bf16[48,3712]{1,0:T(8,128)(2,1)}, bf16[48,3712]{1,0:T(8,128)(2,1)}, bf16[48,3712]{1,0:T(8,128)(2,1)}, bf16[48,3712]{1,0:T(8,128)(2,1)}, f32[32...) custom-call(f32[1,128]{1,0:T(1,128)} %compare_convert_fusion.mine_ref, ...), custom_call_target="tpu_custom_call" | custom-call | flops 1024 | bytes 1024 | tf_op jit(solution)/shard_map/pallas_call | solution.py:233
  180.5 1.6 collective-permute-start.24
  182.1 5.4 %collective-permute-done.20.refs_3_ = bf16[48,7296]{1,0:T(8,128)(2,1)S(1)} collective-permute-done((bf16[48,7296]{1,0:T(8,128)(2,1)}, bf16[48,7296]{1,0:T(8,128)(2,1)S(1)}, u32[]{:S(2)}, u32[]{:S(2)}) %collective-permute-start.20) | collective-permute-done | bytes 700448 | tf_op jit(solution)/shard_map/ppermute | solution.py:282
  188.4 19.7 %shard_map.162 = (bf16[48,3712]{1,0:T(8,128)(2,1)}, bf16[48,3712]{1,0:T(8,128)(2,1)}, bf16[48,3712]{1,0:T(8,128)(2,1)}, bf16[48,3712]{1,0:T(8,128)(2,1)}, f32[32...) custom-call(f32[1,128]{1,0:T(1,128)} %compare_convert_fusion.mine_ref, ...), custom_call_target="tpu_custom_call" | custom-call | flops 1024 | bytes 1024 | tf_op jit(solution)/shard_map/pallas_call | solution.py:233
  208.2 1.5 collective-permute-done.25.refs_3_
  209.8 2.8 shard_map.163
  212.9 1.8 collective-permute-start.29
  214.8 1.4 collective-permute-start.28
  216.2 20.0 %collective-permute-done.28 = bf16[128,128]{1,0:T(8,128)(2,1)S(1)} collective-permute-done((bf16[128,128]{1,0:T(8,128)(2,1)}, bf16[128,128]{1,0:T(8,128)(2,1)S(1)}, u32[]{:S(2)}, u32[]{:S(2)}) %collective-permute-start.28) | collective-permute-done | bytes 32800 | tf_op jit(solution)/shard_map/ppermute | solution.py:282
  237.2 2.7 shard_map.165
  239.9 1.4 collective-permute-start.33
  241.3 2.7 shard_map.164
  244.0 1.0 multiply_reduce_fusion
  245.0 1.3 collective-permute-start.32
  246.3 0.9 multiply_convert_fusion.logit_ref
  247.9 41.4 %all_to_all.5 = f32[16,16,224]{2,1,0:T(8,128)S(1)} all-to-all(f32[16,16,224]{2,1,0:T(8,128)S(1)} %bitcast.57), channel_id=1, replica_groups=mesh['groups'=2,'expert'=16] {'expert'}, dimensions={0} | all-to-all | bytes 458752 | tf_op jit(solution)/shard_map/all_to_all | solution.py:426
  291.0 3.7 %shard_map.166 = bf16[128,3584]{1,0:T(8,128)(2,1)} custom-call(bf16[128,16]{1,0:T(8,128)(2,1)} %copy-done.31, bf16[16,3584]{1,0:T(8,128)(2,1)} %bitcast.58, bf16[128,3584]{1,0:T(8,128)(2,1)} %get-tuple-element.328.refs_0_, bf16[128,3712]{1,0:T(8,128)(2,1)} %copy-done.5, bf16[64,3584]{1,0:T(8,128)(2,1)} %copy-done.17, bf16[64,3584]{1,0:T(8,128)(2,1)} %copy-done.18, ...), custom_call_target="tpu_custom_call" | custom-call | flops 1024 | bytes 1024 | tf_op jit(solution)/shard_map/pallas_call | solution.py:146
  (124 shorter events, 10.6 us)
Async XLA Ops:
  6.7 42.6 %collective-permute-start = (bf16[128,7296]{1,0:T(8,128)(2,1)S(1)}, bf16[128,7296]{1,0:T(8,128)(2,1)}, u32[]{:S(2)}, u32[]{:S(2)}) collective-permute-start(bf16[128,7296]{1,0:T(8,128)(2,1)S(1)} %concatenate.5.refs_0_), channel_id=1, source_target_pairs={{0,8},{1,9},{2,10},{3,11},{12,4},{13,5},{14,6},{15,7},{4,0},{5,1},... | collective-permute-start | bytes 5603336 | tf_op jit(solution)/shard_map/ppermute | solution.py:282
  12.1 2.7 collective-permute-start.1
  12.8 17.6 %collective-permute-start.2 = (bf16[48,7296]{1,0:T(8,128)(2,1)}, bf16[48,7296]{1,0:T(8,128)(2,1)S(1)}, u32[]{:S(2)}, u32[]{:S(2)}) collective-permute-start(bf16[48,7296]{1,0:T(8,128)(2,1)} %get-tuple-element.180), channel_id=1, source_target_pairs={{0,2},{1,3},{2,0},{3,1},{4,6},{5,7},{6,4},{7,5},{8,10},{9,11},{10,... | collective-permute-start | bytes 2101256 | tf_op jit(solution)/shard_map/ppermute | solution.py:282
  13.0 32.8 %collective-permute-start.3 = (bf16[48,7296]{1,0:T(8,128)(2,1)}, bf16[48,7296]{1,0:T(8,128)(2,1)S(1)}, u32[]{:S(2)}, u32[]{:S(2)}) collective-permute-start(bf16[48,7296]{1,0:T(8,128)(2,1)} %get-tuple-element.181), channel_id=1, source_target_pairs={{0,3},{1,2},{2,1},{3,0},{4,7},{5,6},{6,5},{7,4},{8,11},{9,10},{10,... | collective-permute-start | bytes 2101256 | tf_op jit(solution)/shard_map/ppermute | solution.py:282
  14.8 34.6 %copy-start.14 = (bf16[48,7296]{1,0:T(8,128)(2,1)}, bf16[48,7296]{1,0:T(8,128)(2,1)S(1)}, u32[]{:S(2)}) copy-start(bf16[48,7296]{1,0:T(8,128)(2,1)S(1)} %collective-permute-done.1.refs_1_) | copy-start | bytes 2101252
  30.4 19.0 %copy-start.15 = (bf16[48,7296]{1,0:T(8,128)(2,1)}, bf16[48,7296]{1,0:T(8,128)(2,1)S(1)}, u32[]{:S(2)}) copy-start(bf16[48,7296]{1,0:T(8,128)(2,1)S(1)} %collective-permute-done.2.refs_2_) | copy-start | bytes 2101252
  49.4 46.8 %collective-permute-start.4 = (bf16[128,7296]{1,0:T(8,128)(2,1)}, bf16[128,7296]{1,0:T(8,128)(2,1)S(1)}, u32[]{:S(2)}, u32[]{:S(2)}) collective-permute-start(bf16[128,7296]{1,0:T(8,128)(2,1)} %collective-permute-done.refs_0_), channel_id=1, source_target_pairs={{4,0},{5,1},{6,2},{7,3},{8,12},{9,13},{10,14},{11,15},{20,16},{21,... | collective-permute-start | bytes 5603336 | tf_op jit(solution)/shard_map/ppermute | solution.py:282
  50.8 45.4 %collective-permute-start.5 = (bf16[128,7296]{1,0:T(8,128)(2,1)}, bf16[128,7296]{1,0:T(8,128)(2,1)}, u32[]{:S(2)}, u32[]{:S(2)}) collective-permute-start(bf16[128,7296]{1,0:T(8,128)(2,1)} %copy-done), channel_id=1, source_target_pairs={{4,8},{5,9},{6,10},{7,11},{8,4},{9,5},{10,6},{11,7},{20,24},{21,25... | collective-permute-start | bytes 5603336 | tf_op jit(solution)/shard_map/ppermute | solution.py:282
  59.2 23.7 %collective-permute-start.6 = (bf16[48,7296]{1,0:T(8,128)(2,1)}, bf16[48,7296]{1,0:T(8,128)(2,1)S(1)}, u32[]{:S(2)}, u32[]{:S(2)}) collective-permute-start(bf16[48,7296]{1,0:T(8,128)(2,1)} %get-tuple-element.185), channel_id=1, source_target_pairs={{0,1},{1,0},{2,3},{3,2},{4,5},{5,4},{6,7},{7,6},{8,9},{9,8},{10,11... | collective-permute-start | bytes 2101256 | tf_op jit(solution)/shard_map/ppermute | solution.py:282
  61.3 21.6 %collective-permute-start.7 = (bf16[48,7296]{1,0:T(8,128)(2,1)}, bf16[48,7296]{1,0:T(8,128)(2,1)}, u32[]{:S(2)}, u32[]{:S(2)}) collective-permute-start(bf16[48,7296]{1,0:T(8,128)(2,1)} %get-tuple-element.186), channel_id=1, source_target_pairs={{0,2},{1,3},{2,0},{3,1},{4,6},{5,7},{6,4},{7,5},{8,10},{9,11},{10,... | collective-permute-start | bytes 2101256 | tf_op jit(solution)/shard_map/ppermute | solution.py:282
  61.5 32.8 %collective-permute-start.8 = (bf16[48,7296]{1,0:T(8,128)(2,1)}, bf16[48,7296]{1,0:T(8,128)(2,1)}, u32[]{:S(2)}, u32[]{:S(2)}) collective-permute-start(bf16[48,7296]{1,0:T(8,128)(2,1)} %get-tuple-element.187), channel_id=1, source_target_pairs={{0,3},{1,2},{2,1},{3,0},{4,7},{5,6},{6,5},{7,4},{8,11},{9,10},{10,... | collective-permute-start | bytes 2101256 | tf_op jit(solution)/shard_map/ppermute | solution.py:282
  82.9 24.9 %copy-start.10 = (bf16[48,7296]{1,0:T(8,128)(2,1)}, bf16[48,7296]{1,0:T(8,128)(2,1)S(1)}, u32[]{:S(2)}) copy-start(bf16[48,7296]{1,0:T(8,128)(2,1)S(1)} %collective-permute-done.6.refs_1_) | copy-start | bytes 2101252
  94.3 10.4 %copy-start.1 = (bf16[128,7296]{1,0:T(8,128)(2,1)S(1)}, bf16[128,7296]{1,0:T(8,128)(2,1)}, u32[]{:S(2)}) copy-start(bf16[128,7296]{1,0:T(8,128)(2,1)} %copy-done) | copy-start | bytes 5603332
  94.3 1.9 collective-permute-start.9
  94.3 9.6 %collective-permute-start.10 = (bf16[48,3712]{1,0:T(8,128)(2,1)}, bf16[48,3712]{1,0:T(8,128)(2,1)S(1)}, u32[]{:S(2)}, u32[]{:S(2)}) collective-permute-start(bf16[48,3712]{1,0:T(8,128)(2,1)} %get-tuple-element.213), channel_id=1, source_target_pairs={{0,2},{1,3},{2,0},{3,1},{4,6},{5,7},{6,4},{7,5},{8,10},{9,11},{10,... | collective-permute-start | bytes 1069064 | tf_op jit(solution)/shard_map/ppermute | solution.py:282
  104.7 40.9 %collective-permute-start.11 = (bf16[128,7296]{1,0:T(8,128)(2,1)S(1)}, bf16[128,7296]{1,0:T(8,128)(2,1)S(1)}, u32[]{:S(2)}, u32[]{:S(2)}) collective-permute-start(bf16[128,7296]{1,0:T(8,128)(2,1)S(1)} %copy-done.1), channel_id=1, source_target_pairs={{0,4},{1,5},{2,6},{3,7},{12,8},{13,9},{14,10},{15,11},{4,12},{5,13... | collective-permute-start | bytes 5603336 | tf_op jit(solution)/shard_map/ppermute | solution.py:282
  104.7 22.8 %collective-permute-start.12 = (bf16[48,7296]{1,0:T(8,128)(2,1)}, bf16[48,7296]{1,0:T(8,128)(2,1)S(1)}, u32[]{:S(2)}, u32[]{:S(2)}) collective-permute-start(bf16[48,7296]{1,0:T(8,128)(2,1)} %get-tuple-element.235), channel_id=1, source_target_pairs={{0,1},{1,0},{2,3},{3,2},{4,5},{5,4},{6,7},{7,6},{8,9},{9,8},{10,11... | collective-permute-start | bytes 2101256 | tf_op jit(solution)/shard_map/ppermute | solution.py:282
  106.1 21.5 %collective-permute-start.13 = (bf16[48,7296]{1,0:T(8,128)(2,1)}, bf16[48,7296]{1,0:T(8,128)(2,1)S(1)}, u32[]{:S(2)}, u32[]{:S(2)}) collective-permute-start(bf16[48,7296]{1,0:T(8,128)(2,1)} %get-tuple-element.236), channel_id=1, source_target_pairs={{0,2},{1,3},{2,0},{3,1},{4,6},{5,7},{6,4},{7,5},{8,10},{9,11},{10,... | collective-permute-start | bytes 2101256 | tf_op jit(solution)/shard_map/ppermute | solution.py:282
  106.3 44.7 %collective-permute-start.17 = (bf16[48,7296]{1,0:T(8,128)(2,1)}, bf16[48,7296]{1,0:T(8,128)(2,1)S(1)}, u32[]{:S(2)}, u32[]{:S(2)}) collective-permute-start(bf16[48,7296]{1,0:T(8,128)(2,1)} %get-tuple-element.244), channel_id=1, source_target_pairs={{0,3},{1,2},{2,1},{3,0},{4,7},{5,6},{6,5},{7,4},{8,11},{9,10},{10,... | collective-permute-start | bytes 2101256 | tf_op jit(solution)/shard_map/ppermute | solution.py:282
  127.6 32.5 %copy-start.7 = (bf16[48,7296]{1,0:T(8,128)(2,1)}, bf16[48,7296]{1,0:T(8,128)(2,1)S(1)}, u32[]{:S(2)}) copy-start(bf16[48,7296]{1,0:T(8,128)(2,1)S(1)} %collective-permute-done.12.refs_1_) | copy-start | bytes 2101252
  127.6 32.5 %copy-start.8 = (bf16[48,7296]{1,0:T(8,128)(2,1)}, bf16[48,7296]{1,0:T(8,128)(2,1)S(1)}, u32[]{:S(2)}) copy-start(bf16[48,7296]{1,0:T(8,128)(2,1)S(1)} %collective-permute-done.13.refs_2_) | copy-start | bytes 2101252
  127.6 23.4 %collective-permute-start.14 = (bf16[48,3712]{1,0:T(8,128)(2,1)}, bf16[48,3712]{1,0:T(8,128)(2,1)S(1)}, u32[]{:S(2)}, u32[]{:S(2)}) collective-permute-start(bf16[48,3712]{1,0:T(8,128)(2,1)} %get-tuple-element.238), channel_id=1, source_target_pairs={{0,1},{1,0},{2,3},{3,2},{4,5},{5,4},{6,7},{7,6},{8,9},{9,8},{10,11... | collective-permute-start | bytes 1069064 | tf_op jit(solution)/shard_map/ppermute | solution.py:282
  127.8 23.2 %collective-permute-start.15 = (bf16[48,3712]{1,0:T(8,128)(2,1)}, bf16[48,3712]{1,0:T(8,128)(2,1)S(1)}, u32[]{:S(2)}, u32[]{:S(2)}) collective-permute-start(bf16[48,3712]{1,0:T(8,128)(2,1)} %get-tuple-element.239), channel_id=1, source_target_pairs={{0,2},{1,3},{2,0},{3,1},{4,6},{5,7},{6,4},{7,5},{8,10},{9,11},{10,... | collective-permute-start | bytes 1069064 | tf_op jit(solution)/shard_map/ppermute | solution.py:282
  128.0 25.9 %collective-permute-start.16 = (bf16[48,3712]{1,0:T(8,128)(2,1)}, bf16[48,3712]{1,0:T(8,128)(2,1)S(1)}, u32[]{:S(2)}, u32[]{:S(2)}) collective-permute-start(bf16[48,3712]{1,0:T(8,128)(2,1)} %get-tuple-element.240), channel_id=1, source_target_pairs={{0,3},{1,2},{2,1},{3,0},{4,7},{5,6},{6,5},{7,4},{8,11},{9,10},{10,... | collective-permute-start | bytes 1069064 | tf_op jit(solution)/shard_map/ppermute | solution.py:282
  154.0 25.9 %collective-permute-start.18 = (bf16[48,7296]{1,0:T(8,128)(2,1)}, bf16[48,7296]{1,0:T(8,128)(2,1)S(1)}, u32[]{:S(2)}, u32[]{:S(2)}) collective-permute-start(bf16[48,7296]{1,0:T(8,128)(2,1)} %get-tuple-element.262), channel_id=1, source_target_pairs={{0,1},{1,0},{2,3},{3,2},{4,5},{5,4},{6,7},{7,6},{8,9},{9,8},{10,11... | collective-permute-start | bytes 2101256 | tf_op jit(solution)/shard_map/ppermute | solution.py:282
  154.2 25.7 %collective-permute-start.19 = (bf16[48,7296]{1,0:T(8,128)(2,1)}, bf16[48,7296]{1,0:T(8,128)(2,1)S(1)}, u32[]{:S(2)}, u32[]{:S(2)}) collective-permute-start(bf16[48,7296]{1,0:T(8,128)(2,1)} %get-tuple-element.263), channel_id=1, source_target_pairs={{0,2},{1,3},{2,0},{3,1},{4,6},{5,7},{6,4},{7,5},{8,10},{9,11},{10,... | collective-permute-start | bytes 2101256 | tf_op jit(solution)/shard_map/ppermute | solution.py:282
  154.4 33.1 %collective-permute-start.20 = (bf16[48,7296]{1,0:T(8,128)(2,1)}, bf16[48,7296]{1,0:T(8,128)(2,1)S(1)}, u32[]{:S(2)}, u32[]{:S(2)}) collective-permute-start(bf16[48,7296]{1,0:T(8,128)(2,1)} %get-tuple-element.267), channel_id=1, source_target_pairs={{0,3},{1,2},{2,1},{3,0},{4,7},{5,6},{6,5},{7,4},{8,11},{9,10},{10,... | collective-permute-start | bytes 2101256 | tf_op jit(solution)/shard_map/ppermute | solution.py:282
  158.8 28.7 %copy-start.35 = (bf16[48,3712]{1,0:T(8,128)(2,1)S(1)}, bf16[48,3712]{1,0:T(8,128)(2,1)}, u32[]{:S(2)}) copy-start(bf16[48,3712]{1,0:T(8,128)(2,1)} %get-tuple-element.298) | copy-start | bytes 1069060
  158.8 49.3 %collective-permute-start.22 = (bf16[128,3712]{1,0:T(8,128)(2,1)}, bf16[128,3712]{1,0:T(8,128)(2,1)S(1)}, u32[]{:S(2)}, u32[]{:S(2)}) collective-permute-start(bf16[128,3712]{1,0:T(8,128)(2,1)} %shard_map.161), channel_id=1, source_target_pairs={{0,4},{1,5},{2,6},{3,7},{12,8},{13,9},{14,10},{15,11},{4,12},{5,13... | collective-permute-start | bytes 2850824 | tf_op jit(solution)/shard_map/ppermute | solution.py:282
  179.9 7.6 %collective-permute-start.21 = (bf16[48,3712]{1,0:T(8,128)(2,1)}, bf16[48,3712]{1,0:T(8,128)(2,1)S(1)}, u32[]{:S(2)}, u32[]{:S(2)}) collective-permute-start(bf16[48,3712]{1,0:T(8,128)(2,1)} %get-tuple-element.273), channel_id=1, source_target_pairs={{0,1},{1,0},{2,3},{3,2},{4,5},{5,4},{6,7},{7,6},{8,9},{9,8},{10,11... | collective-permute-start | bytes 1069064 | tf_op jit(solution)/shard_map/ppermute | solution.py:282
  180.3 27.9 %collective-permute-start.23 = (bf16[48,3712]{1,0:T(8,128)(2,1)}, bf16[48,3712]{1,0:T(8,128)(2,1)S(1)}, u32[]{:S(2)}, u32[]{:S(2)}) collective-permute-start(bf16[48,3712]{1,0:T(8,128)(2,1)} %get-tuple-element.293), channel_id=1, source_target_pairs={{0,2},{1,3},{2,0},{3,1},{4,6},{5,7},{6,4},{7,5},{8,10},{9,11},{10,... | collective-permute-start | bytes 1069064 | tf_op jit(solution)/shard_map/ppermute | solution.py:282
  180.5 27.7 %collective-permute-start.24 = (bf16[48,3712]{1,0:T(8,128)(2,1)}, bf16[48,3712]{1,0:T(8,128)(2,1)S(1)}, u32[]{:S(2)}, u32[]{:S(2)}) collective-permute-start(bf16[48,3712]{1,0:T(8,128)(2,1)} %get-tuple-element.294), channel_id=1, source_target_pairs={{0,3},{1,2},{2,1},{3,0},{4,7},{5,6},{6,5},{7,4},{8,11},{9,10},{10,... | collective-permute-start | bytes 1069064 | tf_op jit(solution)/shard_map/ppermute | solution.py:282
  187.6 20.6 %copy-start.25 = (bf16[48,3712]{1,0:T(8,128)(2,1)}, bf16[48,3712]{1,0:T(8,128)(2,1)S(1)}, u32[]{:S(2)}) copy-start(bf16[48,3712]{1,0:T(8,128)(2,1)S(1)} %collective-permute-done.21.refs_1_) | copy-start | bytes 1069060
  187.6 22.2 %collective-permute-start.25 = (bf16[48,3712]{1,0:T(8,128)(2,1)S(1)}, bf16[48,3712]{1,0:T(8,128)(2,1)S(1)}, u32[]{:S(2)}, u32[]{:S(2)}) collective-permute-start(bf16[48,3712]{1,0:T(8,128)(2,1)S(1)} %copy-done.35), channel_id=1, source_target_pairs={{0,3},{1,2},{2,1},{3,0},{4,7},{5,6},{6,5},{7,4},{8,11},{9,10},{10,... | collective-permute-start | bytes 1069064 | tf_op jit(solution)/shard_map/ppermute | solution.py:282
  208.2 38.2 %copy-start.5 = (bf16[128,3712]{1,0:T(8,128)(2,1)}, bf16[128,3712]{1,0:T(8,128)(2,1)S(1)}, u32[]{:S(2)}) copy-start(bf16[128,3712]{1,0:T(8,128)(2,1)S(1)} %collective-permute-done.22.refs_1_) | copy-start | bytes 2850820
  209.7 31.5 %copy-start.24 = (bf16[48,3712]{1,0:T(8,128)(2,1)}, bf16[48,3712]{1,0:T(8,128)(2,1)S(1)}, u32[]{:S(2)}) copy-start(bf16[48,3712]{1,0:T(8,128)(2,1)S(1)} %collective-permute-done.25.refs_3_) | copy-start | bytes 1069060
  209.8 34.2 %copy-start.33 = (f32[128,16]{1,0:T(8,128)S(1)}, f32[128,16]{1,0:T(8,128)}, u32[]{:S(2)}) copy-start(f32[128,16]{1,0:T(8,128)} %copy-done.32) | copy-start | bytes 24580
  212.6 33.8 %copy-start.34 = (f32[128,16]{1,0:T(8,128)S(1)}, f32[128,16]{1,0:T(8,128)}, u32[]{:S(2)}) copy-start(f32[128,16]{1,0:T(8,128)} %get-tuple-element.338) | copy-start | bytes 24580
  212.6 31.4 %collective-permute-start.31 = (bf16[64,3584]{1,0:T(8,128)(2,1)}, bf16[64,3584]{1,0:T(8,128)(2,1)S(1)}, u32[]{:S(2)}, u32[]{:S(2)}) collective-permute-start(bf16[64,3584]{1,0:T(8,128)(2,1)} %get-tuple-element.325), channel_id=1, source_target_pairs={{0,12},{1,13},{2,14},{3,15},{4,8},{5,9},{6,10},{7,11},{8,4},{9,5},... | collective-permute-start | bytes 1376264 | tf_op jit(solution)/shard_map/ppermute | solution.py:282
  212.6 23.6 %collective-permute-start.26 = (bf16[48,3712]{1,0:T(8,128)(2,1)}, bf16[48,3712]{1,0:T(8,128)(2,1)S(1)}, u32[]{:S(2)}, u32[]{:S(2)}) collective-permute-start(bf16[48,3712]{1,0:T(8,128)(2,1)} %get-tuple-element.299), channel_id=1, source_target_pairs={{0,1},{1,0},{2,3},{3,2},{4,5},{5,4},{6,7},{7,6},{8,9},{9,8},{10,11... | collective-permute-start | bytes 1069064 | tf_op jit(solution)/shard_map/ppermute | solution.py:282
  212.6 23.6 %collective-permute-start.27 = (bf16[48,3712]{1,0:T(8,128)(2,1)}, bf16[48,3712]{1,0:T(8,128)(2,1)S(1)}, u32[]{:S(2)}, u32[]{:S(2)}) collective-permute-start(bf16[48,3712]{1,0:T(8,128)(2,1)} %get-tuple-element.300), channel_id=1, source_target_pairs={{0,2},{1,3},{2,0},{3,1},{4,6},{5,7},{6,4},{7,5},{8,10},{9,11},{10,... | collective-permute-start | bytes 1069064 | tf_op jit(solution)/shard_map/ppermute | solution.py:282
  212.9 23.3 %collective-permute-start.29 = (bf16[48,3712]{1,0:T(8,128)(2,1)}, bf16[48,3712]{1,0:T(8,128)(2,1)S(1)}, u32[]{:S(2)}, u32[]{:S(2)}) collective-permute-start(bf16[48,3712]{1,0:T(8,128)(2,1)} %get-tuple-element.323), channel_id=1, source_target_pairs={{0,3},{1,2},{2,1},{3,0},{4,7},{5,6},{6,5},{7,4},{8,11},{9,10},{10,... | collective-permute-start | bytes 1069064 | tf_op jit(solution)/shard_map/ppermute | solution.py:282
  214.8 21.5 %collective-permute-start.28 = (bf16[128,128]{1,0:T(8,128)(2,1)}, bf16[128,128]{1,0:T(8,128)(2,1)S(1)}, u32[]{:S(2)}, u32[]{:S(2)}) collective-permute-start(bf16[128,128]{1,0:T(8,128)(2,1)} %get-tuple-element.311), channel_id=1, source_target_pairs={{0,12},{1,13},{2,14},{3,15},{4,8},{5,9},{6,10},{7,11},{8,4},{9,5},... | collective-permute-start | bytes 98312 | tf_op jit(solution)/shard_map/ppermute | solution.py:282
  239.9 4.1 %collective-permute-start.30 = (bf16[128,128]{1,0:T(8,128)(2,1)}, bf16[128,128]{1,0:T(8,128)(2,1)S(1)}, u32[]{:S(2)}, u32[]{:S(2)}) collective-permute-start(bf16[128,128]{1,0:T(8,128)(2,1)} %get-tuple-element.324), channel_id=1, source_target_pairs={{4,0},{5,1},{6,2},{7,3},{8,12},{9,13},{10,14},{11,15},{12,4},{13,5... | collective-permute-start | bytes 98312 | tf_op jit(solution)/shard_map/ppermute | solution.py:282
  239.9 50.0 %collective-permute-start.33 = (bf16[128,3584]{1,0:T(8,128)(2,1)}, bf16[128,3584]{1,0:T(8,128)(2,1)S(1)}, u32[]{:S(2)}, u32[]{:S(2)}) collective-permute-start(bf16[128,3584]{1,0:T(8,128)(2,1)} %get-tuple-element.331), channel_id=1, source_target_pairs={{4,0},{5,1},{6,2},{7,3},{8,12},{9,13},{10,14},{11,15},{12,4},{13,5... | collective-permute-start | bytes 2752520 | tf_op jit(solution)/shard_map/ppermute | solution.py:282
  244.0 45.9 %copy-start.17 = (bf16[64,3584]{1,0:T(8,128)(2,1)}, bf16[64,3584]{1,0:T(8,128)(2,1)S(1)}, u32[]{:S(2)}) copy-start(bf16[64,3584]{1,0:T(8,128)(2,1)S(1)} %collective-permute-done.31.refs_2_) | copy-start | bytes 1376260
  245.0 44.9 %collective-permute-start.32 = (bf16[64,3584]{1,0:T(8,128)(2,1)}, bf16[64,3584]{1,0:T(8,128)(2,1)S(1)}, u32[]{:S(2)}, u32[]{:S(2)}) collective-permute-start(bf16[64,3584]{1,0:T(8,128)(2,1)} %get-tuple-element.330), channel_id=1, source_target_pairs={{0,12},{1,13},{2,14},{3,15},{4,8},{5,9},{6,10},{7,11},{8,4},{9,5},... | collective-permute-start | bytes 1376264 | tf_op jit(solution)/shard_map/ppermute | solution.py:282
  247.3 42.7 %copy-start.31 = (bf16[128,16]{1,0:T(8,128)(2,1)}, bf16[128,16]{1,0:T(8,128)(2,1)S(1)}, u32[]{:S(2)}) copy-start(bf16[128,16]{1,0:T(8,128)(2,1)S(1)} %multiply_convert_fusion.logit_ref) | copy-start | bytes 12292
  (22 other events, 67.2 us)

commit v6 on v5

--- a/solution.py
+++ b/solution.py
@@ -43,114 +43,105 @@
 smem = pl.BlockSpec(memory_space=pltpu.SMEM)
 
 
-def select_kernel(parts, meta_at, slots_held, cap, flag_ref, guide_ref, *refs):
-    count = sum(len(p) for p in parts)
-    ins, outs = refs[:count], refs[count:]
-    tok = ins[0].shape[0]
+def select_kernel(count, cap, flag_ref, guide_ref, *refs):
+    metas, blocks, outs = refs[:count], refs[count : 2 * count], refs[2 * count :]
+    placed_ref = outs[plane]
+    tok, step = blocks[0].shape
     flag = flag_ref[0] == 1
-    groups = []
-    for part in parts:
-        groups.append((part, ins[: len(part)]))
-        ins = ins[len(part) :]
-
-    def load(group, first, last):
-        part, arrays = group
-        values = [a[:, at + first : at + last] for (at, _), a in zip(part, arrays)]
-        return values[0] if len(values) == 1 else jnp.where(flag, values[0], values[1])
-
-    if slots_held:
-        placed = guide_ref[...]
-    else:
-        meta = load(groups[0], *meta_at)
-        named = dot_nt(guide_ref[...], meta)
+
+    def pick(arrays, part):
+        values = [a[:, part] for a in arrays]
+        return values[0] if count == 1 else jnp.where(flag, values[0], values[1])
+
+    @pl.when(pl.program_id(0) == 0)
+    def _():
+        named = dot_nt(guide_ref[...], pick(metas, slice(None)))
         rank = lax.broadcasted_iota(jnp.int32, (cap, tok), 0).astype(f32) + 1.0
-        placed = jnp.concatenate(
-            [(named[p : p + 1, :] == rank).astype(bf16) for p in range(plane)], axis=0
-        )
-        outs[plane][...] = placed
-    at = 0
-    for group in groups:
-        length = group[0][0][1]
-        for first, last in chunks(0, length, 512):
-            rows = dot_nn(placed, load(group, first, last)).astype(bf16)
-            for p in range(plane):
-                outs[p][:, at + first : at + last] = rows[p * cap : (p + 1) * cap]
-        at += length
-
-
-def select_rows(flag, guide, parts, arrays, meta_at, slots_held, cap):
-    tok = arrays[0].shape[0]
-    length = sum(p[0][1] for p in parts)
-    shapes = [jax.ShapeDtypeStruct((cap, length), bf16)] * plane
-    if not slots_held:
-        shapes.append(jax.ShapeDtypeStruct((plane * cap, tok), bf16))
+        for p in range(plane):
+            hit = (named[p : p + 1, :] == rank).astype(bf16)
+            placed_ref[p * cap : (p + 1) * cap, :] = hit
+
+    for first, last in chunks(0, step, 512):
+        rows = dot_nn(placed_ref[...], pick(blocks, slice(first, last))).astype(bf16)
+        for p in range(plane):
+            outs[p][:, first:last] = rows[p * cap : (p + 1) * cap]
+
+
+def select_rows(flag, guide, arrays, width, cap):
+    tok, full = arrays[0].shape
+    meta = guide.shape[1]
+    step = full // 3 if full % 384 == 0 else full
+    column = pl.BlockSpec((tok, step), lambda j: (0, j))
     return pl.pallas_call(
-        functools.partial(select_kernel, parts, meta_at, slots_held, cap),
-        out_shape=shapes,
-        in_specs=[smem] + [vmem] * (1 + len(arrays)),
-        out_specs=[vmem] * len(shapes),
+        functools.partial(select_kernel, len(arrays), cap),
+        grid=(full // step,),
+        out_shape=[jax.ShapeDtypeStruct((cap, full), bf16)] * plane
+        + [jax.ShapeDtypeStruct((plane * cap, tok), bf16)],
+        in_specs=[smem, whole_block(guide.shape)]
+        + [pl.BlockSpec((tok, meta), lambda j: (0, width // meta))] * len(arrays)
+        + [column] * len(arrays),
+        out_specs=[pl.BlockSpec((cap, step), lambda j: (0, j))] * plane
+        + [whole_block((plane * cap, tok))],
         compiler_params=pltpu.CompilerParams(vmem_limit_bytes=vmem_bytes),
         cost_estimate=light,
-    )(flag, guide, *arrays)
-
-
-def sum_kernel(apart, placed_ref, *refs):
-    pieces, outs = refs[:plane], refs[plane:]
-    wide = pieces[0].shape[1]
-    rows, tags = (outs[:-1], outs[-1]) if apart else (outs, None)
-    stop = rows[0].shape[1]
-    for first, last in chunks(0, stop, 512) + chunks(stop, wide, 512):
-        joined = jnp.concatenate([p[:, first:last] for p in pieces], axis=0)
-        total = dot_tn(placed_ref[...], joined).astype(bf16)
-        if first >= stop:
-            tags[...] = total
-            continue
-        at = 0
-        for out in rows:
-            out[:, first:last] = total[at : at + out.shape[0]]
-            at += out.shape[0]
-
-
-def sum_rows(placed, pieces, width, parts=1):
+    )(flag, guide, *arrays, *arrays)
+
+
+def sum_kernel(placed_ref, *refs):
+    tags, pieces, (out, tag) = refs[:plane], refs[plane : 2 * plane], refs[2 * plane :]
+
+    def total(arrays):
+        return dot_tn(placed_ref[...], jnp.concatenate([a[...] for a in arrays], axis=0))
+
+    @pl.when(pl.program_id(0) == 0)
+    def _():
+        tag[...] = total(tags).astype(bf16)
+
+    out[...] = total(pieces).astype(bf16)
+
+
+def sum_rows(placed, pieces, width):
     cap, wide = pieces[0].shape
     tok = placed.shape[1]
-    shapes = [jax.ShapeDtypeStruct((tok // parts, width), bf16)] * parts
-    apart = width < wide
-    if apart:
-        shapes.append(jax.ShapeDtypeStruct((tok, wide - width), bf16))
+    meta = wide - width
+    step = width // 4 if width % 512 == 0 else width
     return pl.pallas_call(
-        functools.partial(sum_kernel, apart),
-        out_shape=shapes,
-        in_specs=[vmem] * (1 + plane),
-        out_specs=[vmem] * len(shapes),
+        sum_kernel,
+        grid=(width // step,),
+        out_shape=[
+            jax.ShapeDtypeStruct((tok, width), bf16),
+            jax.ShapeDtypeStruct((tok, meta), bf16),
+        ],
+        in_specs=[whole_block(placed.shape)]
+        + [pl.BlockSpec((cap, meta), lambda j: (0, width // meta))] * plane
+        + [pl.BlockSpec((cap, step), lambda j: (0, j))] * plane,
+        out_specs=[pl.BlockSpec((tok, step), lambda j: (0, j)), whole_block((tok, meta))],
         compiler_params=pltpu.CompilerParams(vmem_limit_bytes=vmem_bytes),
         cost_estimate=light,
-    )(placed, *pieces)
-
-
-def final_kernel(groups, logit_ref, router_ref, *refs):
-    out = refs[-1]
-    for first, last in chunks(0, out.shape[1], 512):
-        total = dot_nn(logit_ref[...], router_ref[:, first:last])
-        left = refs
-        for count in groups:
-            total = total + jnp.concatenate(
-                [r[:, first:last] for r in left[:count]], axis=0
-            ).astype(f32)
-            left = left[count:]
-        out[:, first:last] = total.astype(bf16)
+    )(placed, *pieces, *pieces)
+
+
+def final_kernel(logit_ref, router_ref, *refs):
+    total = dot_nn(logit_ref[...], router_ref[...])
+    for term in refs[:-1]:
+        total = total + term[...].astype(f32)
+    refs[-1][...] = total.astype(bf16)
 
 
 def final_sum(logit, router, terms):
-    tok, width = logit.shape[0], router.shape[1]
+    tok, width = terms[0].shape
+    step = width // 4 if width % 512 == 0 else width
+    column = pl.BlockSpec((tok, step), lambda j: (0, j))
     return pl.pallas_call(
-        functools.partial(final_kernel, [len(t) for t in terms]),
+        final_kernel,
+        grid=(width // step,),
         out_shape=jax.ShapeDtypeStruct((tok, width), bf16),
-        in_specs=[vmem] * (2 + sum(len(t) for t in terms)),
-        out_specs=vmem,
+        in_specs=[whole_block(logit.shape), pl.BlockSpec((router.shape[0], step), lambda j: (0, j))]
+        + [column] * len(terms),
+        out_specs=column,
         compiler_params=pltpu.CompilerParams(vmem_limit_bytes=vmem_bytes),
         cost_estimate=light,
-    )(logit, router, *[a for t in terms for a in t])
+    )(logit, router, *terms)
 
 
 def expert_kernel(
@@ -334,8 +325,6 @@
         )
         own = jnp.concatenate([layer_input, meta, dy], axis=1)
         full = own.shape[1]
-        wide = width + meta_width
-        meta_at = (width, width + meta_width)
 
         here = layer * plane + (place ^ jnp.arange(plane, dtype=jnp.int32))
         guide = jnp.zeros((16, meta_width), bf16)
@@ -345,9 +334,7 @@
         mine = (jnp.arange(meta_width) == experts + me).astype(f32)[None, :]
 
         def take(flag, arrays):
-            *pieces, placed = select_rows(
-                flag, guide, [[(0, full)] * len(arrays)], arrays, meta_at, False, cap
-            )
+            *pieces, placed = select_rows(flag, guide, arrays, width, cap)
             return pieces, placed
 
         def run(pieces, carry=()):
@@ -380,28 +367,25 @@
             done_2 = run(got_2, done_1[plane:])
             done_2, got_3[1], got_3[2], last_0 = join((done_2, got_3[1], got_3[2], done_0[3]))
             back_2 = spread(done_2[:plane])
-            (part_1,) = sum_rows(placed_1, back_1, wide)
-            term_1 = send(part_1, along([(0, 1), (3, 2), (1, 3), (2, 0)]))
+            part_1, tag_1 = sum_rows(placed_1, back_1, width)
+            swap_1 = along([(0, 1), (3, 2), (1, 3), (2, 0)])
+            tag_1, term_1 = send(tag_1, swap_1), send(part_1, swap_1)
             got_3, part_1, back_2[1], last_0 = join((got_3, part_1, back_2[1], last_0))
             back_0.append(send(last_0, across(3)))
             done_3 = run(got_3, done_2[plane:])
-            done_3, term_1, back_2, back_0 = join((done_3, term_1, back_2, back_0))
+            done_3, term_1, tag_1, back_2, back_0 = join((done_3, term_1, tag_1, back_2, back_0))
             back_3 = spread(done_3[:plane])
-            part_2a, part_2b, tag_2 = sum_rows(placed_2, back_2, width, 2)
-            tag_2 = send(tag_2, across(3 * plane))
-            term_2a = send(part_2a, across(3 * plane))
-            back_3[1], back_3[2], part_2b, back_0, tag_2 = join(
-                (back_3[1], back_3[2], part_2b, back_0, tag_2)
-            )
+            part_2, tag_2 = sum_rows(placed_2, back_2, width)
+            tag_2, term_2 = send(tag_2, across(3 * plane)), send(part_2, across(3 * plane))
+            back_3[1], back_3[2], back_0 = join((back_3[1], back_3[2], back_0))
             part_0, tag_0 = sum_rows(placed_0, back_0, width)
             part_3, tag_3 = sum_rows(placed_3, back_3, width)
             swap_3 = along([(1, 0), (2, 3), (3, 1), (0, 2)])
             tag_3 = send(tag_3, swap_3)
             term_3 = send(part_3, swap_3)
-            tag_3, term_2a, part_2b = join((tag_3, term_2a, part_2b))
-            term_2b = send(part_2b, across(3 * plane))
-            tags = [tag_0, term_1[:, width:], tag_2, tag_3]
-            terms = [[part_0], [term_1], [term_2a, term_2b], [term_3]]
+            tag_3, tag_2, term_2, part_0 = join((tag_3, tag_2, term_2, part_0))
+            tags = [tag_0, tag_1, tag_2, tag_3]
+            terms = [part_0, term_1, term_2, term_3]
             done = [done_3]
         else:
             flag = jnp.zeros((1,), jnp.int32)
@@ -410,10 +394,10 @@
                 block = own if g == 0 else send(own, across(g * plane))
                 sel, placed = take(flag, [block])
                 result = run(spread(sel), done[-1][plane:] if done else ())
-                (part,) = sum_rows(placed, spread(result[:plane]), wide)
-                terms.append([part if g == 0 else send(part, across(g * plane))])
+                part, tag = sum_rows(placed, spread(result[:plane]), width)
+                terms.append(part if g == 0 else send(part, across(g * plane)))
+                tags.append(tag if g == 0 else send(tag, across(g * plane)))
                 done.append(result)
-                tags.append(terms[-1][0][:, width:])
 
         route_grad = sum(t[:, experts : 2 * experts].astype(f32) for t in tags)
         shared = jnp.sum(route_grad * picked, axis=1, keepdims=True) / (total * total)

time: 297 us -> 300 us (1.010)
  blocking collectives: 41.4 us -> 0 us
  waiting for transfers between devices: 95.4 us -> 125 us
  Pallas kernels: 110 us -> 119 us
  starting transfers between devices: 29.3 us -> 35.8 us
    all_to_all x1 -> x0, blocking collectives: 41.4 us -> none  [shards(): lax.all_to_all(router_part, 'expert', split_axis=0, concat_axis=0, tiled=...]
    ppermute x34, waiting for transfers between devices: 95.4 us -> 121 us  [send(): return lax.ppermute(array, 'expert', pairs)]
    pallas_call x9, Pallas kernels: 31.6 us -> 40 us  [the longest x4 18.6 us: select_rows(): pl.pallas_call(functools.partial(select_kernel, len(arrays), cap), grid=(...]
    all_to_all x0 -> x1, starting transfers between devices: none -> 6.19 us  [shards(): lax.all_to_all(router_part, 'expert', split_axis=0, concat_axis=0, tiled=...]
    all_to_all x0 -> x1, waiting for transfers between devices: none -> 3.47 us  [shards(): lax.all_to_all(router_part, 'expert', split_axis=0, concat_axis=0, tiled=...]
    unnamed x72 -> x76, local copies, waits for them, and re-layouts: 6.98 us -> 4.11 us
  transfers between devices with their start and end apart: 34 -> 35, of which waited for: 12 -> 15; matrix products, arithmetic and copies ran while one was open for 2% -> 2% of each run, Pallas kernels for 35% -> 39%
where the time goes in v6:
time: 300 us; the launch traced here: 295 us
  waiting for transfers between devices  125 us (42%)
  Pallas kernels  119 us (40%)
  starting transfers between devices  35.8 us (12%)
  local copies, waits for them, and re-layouts  7.51 us (3%)
  other arithmetic  4.92 us (2%)
    ppermute x34, waiting for transfers between devices, send(): return lax.ppermute(array, 'expert', pairs)  121 us
    pallas_call x4, Pallas kernels, expert_rows(): pl.pallas_call(functools.partial(expert_kernel, len(carry), cap, width, r...  78.7 us
    ppermute x34, starting transfers between devices, send(): return lax.ppermute(array, 'expert', pairs)  29.6 us
    pallas_call x4, Pallas kernels, select_rows(): pl.pallas_call(functools.partial(select_kernel, len(arrays), cap), grid=(...  18.6 us
    pallas_call x4, Pallas kernels, sum_rows(): pl.pallas_call(sum_kernel, grid=(width // step,), out_shape=[jax.ShapeDty...  16.9 us
    all_to_all x1, starting transfers between devices, shards(): lax.all_to_all(router_part, 'expert', split_axis=0, concat_axis=0, tiled=...  6.19 us
  transfers between devices with their start and end apart: 35, of which 15 were waited for; matrix products, arithmetic and copies ran while one was open for 2% of the time, Pallas kernels for 39%

profile of v6, /device:TPU:15, one launch (start us, length us, event | category | flops | bytes accessed | tf_op | source)
XLA Modules:
  0.0 295.3 jit_solution(9762010571702985564)
XLA Ops:
  1.7 2.2 fusion.6
  4.5 2.2 concatenate.5.refs_0_.refs_1_
  8.0 4.5 %shard_map.154 = (bf16[48,7296]{1,0:T(8,128)(2,1)}, bf16[48,7296]{1,0:T(8,128)(2,1)}, bf16[48,7296]{1,0:T(8,128)(2,1)}, bf16[48,7296]{1,0:T(8,128)(2,1)}, bf16[192,128]{1,0:T(8,128)(2,1)}) custom-call(s32[1]{0:T(128)} %bitcast.flag_ref, bf16[16,128]{1,0:T(8,128)(2,1)} %pad_convert_fusion.guide_ref, bf16[128,7296]{1,0:T(8,128)(2,1)} %copy-done, ...), custom_call_target="tpu_custom_call" | custom-call | flops 1024 | bytes 1024 | tf_op jit(solution)/shard_map/pallas_call | solution.py:75
  13.3 1.5 collective-permute-start.3
  15.1 15.6 %collective-permute-done.2.refs_2_ = bf16[48,7296]{1,0:T(8,128)(2,1)S(1)} collective-permute-done((bf16[48,7296]{1,0:T(8,128)(2,1)}, bf16[48,7296]{1,0:T(8,128)(2,1)S(1)}, u32[]{:S(2)}, u32[]{:S(2)}) %collective-permute-start.2) | collective-permute-done | bytes 700448 | tf_op jit(solution)/shard_map/ppermute | solution.py:273
  30.7 15.5 %collective-permute-done.3.refs_3_ = bf16[48,7296]{1,0:T(8,128)(2,1)S(1)} collective-permute-done((bf16[48,7296]{1,0:T(8,128)(2,1)}, bf16[48,7296]{1,0:T(8,128)(2,1)S(1)}, u32[]{:S(2)}, u32[]{:S(2)}) %collective-permute-start.3) | collective-permute-done | bytes 700448 | tf_op jit(solution)/shard_map/ppermute | solution.py:273
  46.2 3.2 %collective-permute-done.refs_0_.refs_1_ = bf16[128,7296]{1,0:T(8,128)(2,1)} collective-permute-done((bf16[128,7296]{1,0:T(8,128)(2,1)S(1)}, bf16[128,7296]{1,0:T(8,128)(2,1)}, u32[]{:S(2)}, u32[]{:S(2)}) %collective-permute-start) | collective-permute-done | bytes 1867808 | tf_op jit(solution)/shard_map/ppermute | solution.py:273
  49.4 1.4 collective-permute-start.4
  50.8 4.2 %collective-permute-start.5 = (bf16[128,7296]{1,0:T(8,128)(2,1)}, bf16[128,7296]{1,0:T(8,128)(2,1)}, u32[]{:S(2)}, u32[]{:S(2)}) collective-permute-start(bf16[128,7296]{1,0:T(8,128)(2,1)} %copy-done), channel_id=1, source_target_pairs={{4,8},{5,9},{6,10},{7,11},{8,4},{9,5},{10,6},{11,7},{20,24},{21,25... | collective-permute-start | bytes 5603336 | tf_op jit(solution)/shard_map/ppermute | solution.py:273
  55.0 4.5 %shard_map.155 = (bf16[48,7296]{1,0:T(8,128)(2,1)}, bf16[48,7296]{1,0:T(8,128)(2,1)}, bf16[48,7296]{1,0:T(8,128)(2,1)}, bf16[48,7296]{1,0:T(8,128)(2,1)}, bf16[192,128]{1,0:T(8,128)(2,1)}) custom-call(s32[1]{0:T(128)} %bitcast.flag_ref, bf16[16,128]{1,0:T(8,128)(2,1)} %pad_convert_fusion.guide_ref, bf16[128,7296]{1,0:T(8,128)(2,1)} %collective-permute-done.refs_0_.refs_1_, ...), custom_call_target="tpu_custom_call" | custom-call | flops 1024 | bytes 1024 | tf_op jit(solution)/shard_map/pallas_call | solution.py:75
  59.6 2.1 collective-permute-start.6
  61.9 1.5 collective-permute-start.8
  64.0 19.4 %shard_map.156 = (bf16[48,3712]{1,0:T(8,128)(2,1)}, bf16[48,3712]{1,0:T(8,128)(2,1)}, bf16[48,3712]{1,0:T(8,128)(2,1)}, bf16[48,3712]{1,0:T(8,128)(2,1)}, f32[32...) custom-call(f32[1,128]{1,0:T(1,128)} %compare_convert_fusion.mine_ref, ...), custom_call_target="tpu_custom_call" | custom-call | flops 1024 | bytes 1024 | tf_op jit(solution)/shard_map/pallas_call | solution.py:224
  83.4 11.3 %collective-permute-done.8.refs_3_ = bf16[48,7296]{1,0:T(8,128)(2,1)} collective-permute-done((bf16[48,7296]{1,0:T(8,128)(2,1)}, bf16[48,7296]{1,0:T(8,128)(2,1)}, u32[]{:S(2)}, u32[]{:S(2)}) %collective-permute-start.8) | collective-permute-done | bytes 700448 | tf_op jit(solution)/shard_map/ppermute | solution.py:273
  94.9 1.6 collective-permute-done.9.refs_1_.refs_5_
  96.6 1.3 copy-done.2
  97.9 5.1 %shard_map.157 = (bf16[48,7296]{1,0:T(8,128)(2,1)}, bf16[48,7296]{1,0:T(8,128)(2,1)}, bf16[48,7296]{1,0:T(8,128)(2,1)}, bf16[48,7296]{1,0:T(8,128)(2,1)}, bf16[192,128]{1,0:T(8,128)(2,1)}) custom-call(s32[1]{0:T(128)} %bitcast.flag_ref, bf16[16,128]{1,0:T(8,128)(2,1)} %pad_convert_fusion.guide_ref, bf16[128,7296]{1,0:T(8,128)(2,1)} %collective-permute-done.5.refs_0_.refs_2_, ...), custom_call_target="tpu_custom_call" | custom-call | flops 1024 | bytes 1024 | tf_op jit(solution)/shard_map/pallas_call | solution.py:75
  102.9 1.4 collective-permute-done.10.refs_2_.refs_6_
  104.3 1.4 collective-permute-start.12
  106.0 1.5 collective-permute-start.17
  107.5 19.8 %shard_map.159 = (bf16[48,3712]{1,0:T(8,128)(2,1)}, bf16[48,3712]{1,0:T(8,128)(2,1)}, bf16[48,3712]{1,0:T(8,128)(2,1)}, bf16[48,3712]{1,0:T(8,128)(2,1)}, f32[32...) custom-call(f32[1,128]{1,0:T(1,128)} %compare_convert_fusion.mine_ref, ...), custom_call_target="tpu_custom_call" | custom-call | flops 1024 | bytes 1024 | tf_op jit(solution)/shard_map/pallas_call | solution.py:224
  127.8 1.8 collective-permute-start.16
  129.6 15.6 %collective-permute-done.11.refs_0_.refs_1_ = bf16[128,7296]{1,0:T(8,128)(2,1)S(1)} collective-permute-done((bf16[128,7296]{1,0:T(8,128)(2,1)S(1)}, bf16[128,7296]{1,0:T(8,128)(2,1)S(1)}, u32[]{:S(2)}, u32[]{:S(2)}) %collective-permute-start.11) | collective-permute-done | bytes 1867808 | tf_op jit(solution)/shard_map/ppermute | solution.py:273
  145.2 1.3 copy-done.3
  146.5 4.6 %shard_map.158 = (bf16[48,7296]{1,0:T(8,128)(2,1)}, bf16[48,7296]{1,0:T(8,128)(2,1)}, bf16[48,7296]{1,0:T(8,128)(2,1)}, bf16[48,7296]{1,0:T(8,128)(2,1)}, bf16[192,128]{1,0:T(8,128)(2,1)}) custom-call(s32[1]{0:T(128)} %bitcast.flag_ref, bf16[16,128]{1,0:T(8,128)(2,1)} %pad_convert_fusion.guide_ref, bf16[128,7296]{1,0:T(8,128)(2,1)} %copy-done.3, ...), custom_call_target="tpu_custom_call" | custom-call | flops 1024 | bytes 1024 | tf_op jit(solution)/shard_map/pallas_call | solution.py:75
  151.1 2.5 collective-permute-done.16.refs_3_.refs_7_
  154.1 1.7 collective-permute-start.20
  155.8 4.2 %shard_map.161 = (bf16[128,3584]{1,0:T(8,128)(2,1)}, bf16[128,128]{1,0:T(8,128)(2,1)}) custom-call(bf16[192,128]{1,0:T(8,128)(2,1)} %get-tuple-element.269.placed_ref, bf16[48,3712]{1,0:T(8,128)(2,1)} %get-tuple-element.270.refs_0_.refs_4_, bf16[48,3712]{1,0:T(8,128)(2,1)} %copy-done.11, bf16[48,3712]{1,0:T(8,128)(2,1)} %copy-done.12, ...), custom_call_target="tpu_custom_call" | custom-call | flops 1024 | bytes 1024 | tf_op jit(solution)/shard_map/pallas_call | solution.py:108
  160.0 1.2 collective-permute-start.22
  161.2 19.8 %shard_map.160 = (bf16[48,3712]{1,0:T(8,128)(2,1)}, bf16[48,3712]{1,0:T(8,128)(2,1)}, bf16[48,3712]{1,0:T(8,128)(2,1)}, bf16[48,3712]{1,0:T(8,128)(2,1)}, f32[32...) custom-call(f32[1,128]{1,0:T(1,128)} %compare_convert_fusion.mine_ref, ...), custom_call_target="tpu_custom_call" | custom-call | flops 1024 | bytes 1024 | tf_op jit(solution)/shard_map/pallas_call | solution.py:224
  181.6 1.6 collective-permute-start.25
  183.2 4.0 %collective-permute-done.20.refs_3_ = bf16[48,7296]{1,0:T(8,128)(2,1)S(1)} collective-permute-done((bf16[48,7296]{1,0:T(8,128)(2,1)}, bf16[48,7296]{1,0:T(8,128)(2,1)S(1)}, u32[]{:S(2)}, u32[]{:S(2)}) %collective-permute-start.20) | collective-permute-done | bytes 700448 | tf_op jit(solution)/shard_map/ppermute | solution.py:273
  187.4 1.4 collective-permute-start.23
  188.7 19.8 %shard_map.162 = (bf16[48,3712]{1,0:T(8,128)(2,1)}, bf16[48,3712]{1,0:T(8,128)(2,1)}, bf16[48,3712]{1,0:T(8,128)(2,1)}, bf16[48,3712]{1,0:T(8,128)(2,1)}, f32[32...) custom-call(f32[1,128]{1,0:T(1,128)} %compare_convert_fusion.mine_ref, ...), custom_call_target="tpu_custom_call" | custom-call | flops 1024 | bytes 1024 | tf_op jit(solution)/shard_map/pallas_call | solution.py:224
  209.5 4.3 %shard_map.165 = (bf16[128,3584]{1,0:T(8,128)(2,1)}, bf16[128,128]{1,0:T(8,128)(2,1)}) custom-call(bf16[192,128]{1,0:T(8,128)(2,1)} %get-tuple-element.320.placed_ref, bf16[48,3712]{1,0:T(8,128)(2,1)} %get-tuple-element.321.refs_0_.refs_4_, bf16[48,3712]{1,0:T(8,128)(2,1)} %copy-done.8, bf16[48,3712]{1,0:T(8,128)(2,1)} %copy-done.9, ...), custom_call_target="tpu_custom_call" | custom-call | flops 1024 | bytes 1024 | tf_op jit(solution)/shard_map/pallas_call | solution.py:108
  213.8 1.7 collective-permute-start.32
  215.5 0.9 collective-permute-start.27
  216.4 1.2 collective-permute-start.28
  218.1 8.2 %collective-permute-done.28.refs_2_.refs_6_ = bf16[48,3712]{1,0:T(8,128)(2,1)S(1)} collective-permute-done((bf16[48,3712]{1,0:T(8,128)(2,1)S(1)}, bf16[48,3712]{1,0:T(8,128)(2,1)S(1)}, u32[]{:S(2)}, u32[]{:S(2)}) %collective-permute-start.28) | collective-permute-done | bytes 356384 | tf_op jit(solution)/shard_map/ppermute | solution.py:273
  226.2 8.1 %collective-permute-done.29.refs_3_.refs_7_ = bf16[48,3712]{1,0:T(8,128)(2,1)S(1)} collective-permute-done((bf16[48,3712]{1,0:T(8,128)(2,1)S(1)}, bf16[48,3712]{1,0:T(8,128)(2,1)S(1)}, u32[]{:S(2)}, u32[]{:S(2)}) %collective-permute-start.29) | collective-permute-done | bytes 356384 | tf_op jit(solution)/shard_map/ppermute | solution.py:273
  235.1 4.2 %shard_map.164 = (bf16[128,3584]{1,0:T(8,128)(2,1)}, bf16[128,128]{1,0:T(8,128)(2,1)}) custom-call(bf16[192,128]{1,0:T(8,128)(2,1)} %get-tuple-element.314.placed_ref, bf16[48,3712]{1,0:T(8,128)(2,1)} %get-tuple-element.315.refs_0_.refs_4_, bf16[48,3712]{1,0:T(8,128)(2,1)} %copy-done.14, bf16[48,3712]{1,0:T(8,128)(2,1)} %copy-done.15, ...), custom_call_target="tpu_custom_call" | custom-call | flops 1024 | bytes 1024 | tf_op jit(solution)/shard_map/pallas_call | solution.py:108
  240.0 4.2 %shard_map.163 = (bf16[128,3584]{1,0:T(8,128)(2,1)}, bf16[128,128]{1,0:T(8,128)(2,1)}) custom-call(bf16[192,128]{1,0:T(8,128)(2,1)} %get-tuple-element.178.placed_ref, bf16[48,3712]{1,0:T(8,128)(2,1)} %get-tuple-element.308.refs_0_.refs_4_, bf16[48,3712]{1,0:T(8,128)(2,1)} %copy-done.5, bf16[48,3712]{1,0:T(8,128)(2,1)} %copy-done.6, ...), custom_call_target="tpu_custom_call" | custom-call | flops 1024 | bytes 1024 | tf_op jit(solution)/shard_map/pallas_call | solution.py:108
  244.2 33.0 %collective-permute-done.31 = bf16[128,128]{1,0:T(8,128)(2,1)S(1)} collective-permute-done((bf16[128,128]{1,0:T(8,128)(2,1)}, bf16[128,128]{1,0:T(8,128)(2,1)S(1)}, u32[]{:S(2)}, u32[]{:S(2)}) %collective-permute-start.31) | collective-permute-done | bytes 32800 | tf_op jit(solution)/shard_map/ppermute | solution.py:273
  277.3 1.0 multiply_reduce_fusion
  278.3 0.9 multiply_convert_fusion.logit_ref
  280.5 6.2 %all-to-all-start = ((f32[16,16,224]{2,1,0:T(8,128)}), f32[16,16,224]{2,1,0:T(8,128)S(1)}, u32[]{:S(2)}, u32[]{:S(2)}) async-start(f32[16,16,224]{2,1,0:T(8,128)} %bitcast.28), calls=%async_computation | async-start | bytes 524288 | tf_op jit(solution)/shard_map/all_to_all | solution.py:410
  286.7 4.5 %shard_map.166 = bf16[128,3584]{1,0:T(8,128)(2,1)} custom-call(bf16[128,16]{1,0:T(8,128)(2,1)} %copy-done.29, bf16[16,3584]{1,0:T(8,128)(2,1)} %bitcast.57, bf16[128,3584]{1,0:T(8,128)(2,1)} %get-tuple-element.330.refs_0_, bf16[128,3584]{1,0:T(8,128)(2,1)} %copy-done.17, bf16[128,3584]{1,0:T(8,128)(2,1)} %copy-done.18, ...), custom_call_target="tpu_custom_call" | custom-call | flops 1024 | bytes 1024 | tf_op jit(solution)/shard_map/pallas_call | solution.py:135
  291.2 3.5 %all-to-all-done = f32[16,16,224]{2,1,0:T(8,128)S(1)} async-done(((f32[16,16,224]{2,1,0:T(8,128)}), f32[16,16,224]{2,1,0:T(8,128)S(1)}, u32[]{:S(2)}, u32[]{:S(2)}) %all-to-all-start) | async-done | bytes 229408 | tf_op jit(solution)/shard_map/all_to_all | solution.py:410
  (129 shorter events, 11.9 us)
Async XLA Ops:
  6.7 42.6 %collective-permute-start = (bf16[128,7296]{1,0:T(8,128)(2,1)S(1)}, bf16[128,7296]{1,0:T(8,128)(2,1)}, u32[]{:S(2)}, u32[]{:S(2)}) collective-permute-start(bf16[128,7296]{1,0:T(8,128)(2,1)S(1)} %concatenate.5.refs_0_.refs_1_), channel_id=1, source_target_pairs={{0,8},{1,9},{2,10},{3,11},{12,4},{13,5},{14,6},{15,7},{4,0},{5,1},... | collective-permute-start | bytes 5603336 | tf_op jit(solution)/shard_map/ppermute | solution.py:273
  12.5 2.7 collective-permute-start.1
  13.1 17.6 %collective-permute-start.2 = (bf16[48,7296]{1,0:T(8,128)(2,1)}, bf16[48,7296]{1,0:T(8,128)(2,1)S(1)}, u32[]{:S(2)}, u32[]{:S(2)}) collective-permute-start(bf16[48,7296]{1,0:T(8,128)(2,1)} %get-tuple-element.181), channel_id=1, source_target_pairs={{0,2},{1,3},{2,0},{3,1},{4,6},{5,7},{6,4},{7,5},{8,10},{9,11},{10,... | collective-permute-start | bytes 2101256 | tf_op jit(solution)/shard_map/ppermute | solution.py:273
  13.3 32.8 %collective-permute-start.3 = (bf16[48,7296]{1,0:T(8,128)(2,1)}, bf16[48,7296]{1,0:T(8,128)(2,1)S(1)}, u32[]{:S(2)}, u32[]{:S(2)}) collective-permute-start(bf16[48,7296]{1,0:T(8,128)(2,1)} %get-tuple-element.182), channel_id=1, source_target_pairs={{0,3},{1,2},{2,1},{3,0},{4,7},{5,6},{6,5},{7,4},{8,11},{9,10},{10,... | collective-permute-start | bytes 2101256 | tf_op jit(solution)/shard_map/ppermute | solution.py:273
  15.1 34.2 %copy-start.26 = (bf16[48,7296]{1,0:T(8,128)(2,1)}, bf16[48,7296]{1,0:T(8,128)(2,1)S(1)}, u32[]{:S(2)}) copy-start(bf16[48,7296]{1,0:T(8,128)(2,1)S(1)} %collective-permute-done.1.refs_1_) | copy-start | bytes 2101252
  49.4 47.2 %collective-permute-start.4 = (bf16[128,7296]{1,0:T(8,128)(2,1)}, bf16[128,7296]{1,0:T(8,128)(2,1)S(1)}, u32[]{:S(2)}, u32[]{:S(2)}) collective-permute-start(bf16[128,7296]{1,0:T(8,128)(2,1)} %collective-permute-done.refs_0_.refs_1_), channel_id=1, source_target_pairs={{4,0},{5,1},{6,2},{7,3},{8,12},{9,13},{10,14},{11,15},{20,16},{21,... | collective-permute-start | bytes 5603336 | tf_op jit(solution)/shard_map/ppermute | solution.py:273
  50.8 45.8 %collective-permute-start.5 = (bf16[128,7296]{1,0:T(8,128)(2,1)}, bf16[128,7296]{1,0:T(8,128)(2,1)}, u32[]{:S(2)}, u32[]{:S(2)}) collective-permute-start(bf16[128,7296]{1,0:T(8,128)(2,1)} %copy-done), channel_id=1, source_target_pairs={{4,8},{5,9},{6,10},{7,11},{8,4},{9,5},{10,6},{11,7},{20,24},{21,25... | collective-permute-start | bytes 5603336 | tf_op jit(solution)/shard_map/ppermute | solution.py:273
  59.6 23.8 %collective-permute-start.6 = (bf16[48,7296]{1,0:T(8,128)(2,1)}, bf16[48,7296]{1,0:T(8,128)(2,1)S(1)}, u32[]{:S(2)}, u32[]{:S(2)}) collective-permute-start(bf16[48,7296]{1,0:T(8,128)(2,1)} %get-tuple-element.186), channel_id=1, source_target_pairs={{0,1},{1,0},{2,3},{3,2},{4,5},{5,4},{6,7},{7,6},{8,9},{9,8},{10,11... | collective-permute-start | bytes 2101256 | tf_op jit(solution)/shard_map/ppermute | solution.py:273
  61.7 21.7 %collective-permute-start.7 = (bf16[48,7296]{1,0:T(8,128)(2,1)}, bf16[48,7296]{1,0:T(8,128)(2,1)}, u32[]{:S(2)}, u32[]{:S(2)}) collective-permute-start(bf16[48,7296]{1,0:T(8,128)(2,1)} %get-tuple-element.187), channel_id=1, source_target_pairs={{0,2},{1,3},{2,0},{3,1},{4,6},{5,7},{6,4},{7,5},{8,10},{9,11},{10,... | collective-permute-start | bytes 2101256 | tf_op jit(solution)/shard_map/ppermute | solution.py:273
  61.9 32.8 %collective-permute-start.8 = (bf16[48,7296]{1,0:T(8,128)(2,1)}, bf16[48,7296]{1,0:T(8,128)(2,1)}, u32[]{:S(2)}, u32[]{:S(2)}) collective-permute-start(bf16[48,7296]{1,0:T(8,128)(2,1)} %get-tuple-element.188), channel_id=1, source_target_pairs={{0,3},{1,2},{2,1},{3,0},{4,7},{5,6},{6,5},{7,4},{8,11},{9,10},{10,... | collective-permute-start | bytes 2101256 | tf_op jit(solution)/shard_map/ppermute | solution.py:273
  83.3 21.0 %copy-start.22 = (bf16[48,7296]{1,0:T(8,128)(2,1)}, bf16[48,7296]{1,0:T(8,128)(2,1)S(1)}, u32[]{:S(2)}) copy-start(bf16[48,7296]{1,0:T(8,128)(2,1)S(1)} %collective-permute-done.6.refs_1_) | copy-start | bytes 2101252
  94.7 1.9 collective-permute-start.9
  94.7 9.6 %collective-permute-start.10 = (bf16[48,3712]{1,0:T(8,128)(2,1)}, bf16[48,3712]{1,0:T(8,128)(2,1)S(1)}, u32[]{:S(2)}, u32[]{:S(2)}) collective-permute-start(bf16[48,3712]{1,0:T(8,128)(2,1)} %get-tuple-element.214), channel_id=1, source_target_pairs={{0,2},{1,3},{2,0},{3,1},{4,6},{5,7},{6,4},{7,5},{8,10},{9,11},{10,... | collective-permute-start | bytes 1069064 | tf_op jit(solution)/shard_map/ppermute | solution.py:273
  96.6 30.7 %copy-start.5 = (bf16[48,3712]{1,0:T(8,128)(2,1)}, bf16[48,3712]{1,0:T(8,128)(2,1)S(1)}, u32[]{:S(2)}) copy-start(bf16[48,3712]{1,0:T(8,128)(2,1)S(1)} %collective-permute-done.9.refs_1_.refs_5_) | copy-start | bytes 1069060
  104.3 23.0 %copy-start.6 = (bf16[48,3712]{1,0:T(8,128)(2,1)}, bf16[48,3712]{1,0:T(8,128)(2,1)S(1)}, u32[]{:S(2)}) copy-start(bf16[48,3712]{1,0:T(8,128)(2,1)S(1)} %collective-permute-done.10.refs_2_.refs_6_) | copy-start | bytes 1069060
  104.3 40.8 %collective-permute-start.11 = (bf16[128,7296]{1,0:T(8,128)(2,1)S(1)}, bf16[128,7296]{1,0:T(8,128)(2,1)S(1)}, u32[]{:S(2)}, u32[]{:S(2)}) collective-permute-start(bf16[128,7296]{1,0:T(8,128)(2,1)S(1)} %copy-done.1), channel_id=1, source_target_pairs={{0,4},{1,5},{2,6},{3,7},{12,8},{13,9},{14,10},{15,11},{4,12},{5,13... | collective-permute-start | bytes 5603336 | tf_op jit(solution)/shard_map/ppermute | solution.py:273
  104.3 23.0 %collective-permute-start.12 = (bf16[48,7296]{1,0:T(8,128)(2,1)}, bf16[48,7296]{1,0:T(8,128)(2,1)S(1)}, u32[]{:S(2)}, u32[]{:S(2)}) collective-permute-start(bf16[48,7296]{1,0:T(8,128)(2,1)} %get-tuple-element.236), channel_id=1, source_target_pairs={{0,1},{1,0},{2,3},{3,2},{4,5},{5,4},{6,7},{7,6},{8,9},{9,8},{10,11... | collective-permute-start | bytes 2101256 | tf_op jit(solution)/shard_map/ppermute | solution.py:273
  105.7 21.6 %collective-permute-start.13 = (bf16[48,7296]{1,0:T(8,128)(2,1)}, bf16[48,7296]{1,0:T(8,128)(2,1)S(1)}, u32[]{:S(2)}, u32[]{:S(2)}) collective-permute-start(bf16[48,7296]{1,0:T(8,128)(2,1)} %get-tuple-element.237), channel_id=1, source_target_pairs={{0,2},{1,3},{2,0},{3,1},{4,6},{5,7},{6,4},{7,5},{8,10},{9,11},{10,... | collective-permute-start | bytes 2101256 | tf_op jit(solution)/shard_map/ppermute | solution.py:273
  106.0 45.1 %collective-permute-start.17 = (bf16[48,7296]{1,0:T(8,128)(2,1)}, bf16[48,7296]{1,0:T(8,128)(2,1)S(1)}, u32[]{:S(2)}, u32[]{:S(2)}) collective-permute-start(bf16[48,7296]{1,0:T(8,128)(2,1)} %get-tuple-element.245), channel_id=1, source_target_pairs={{0,3},{1,2},{2,1},{3,0},{4,7},{5,6},{6,5},{7,4},{8,11},{9,10},{10,... | collective-permute-start | bytes 2101256 | tf_op jit(solution)/shard_map/ppermute | solution.py:273
  127.3 33.9 %copy-start.19 = (bf16[48,7296]{1,0:T(8,128)(2,1)}, bf16[48,7296]{1,0:T(8,128)(2,1)S(1)}, u32[]{:S(2)}) copy-start(bf16[48,7296]{1,0:T(8,128)(2,1)S(1)} %collective-permute-done.12.refs_1_) | copy-start | bytes 2101252
  127.3 33.9 %copy-start.20 = (bf16[48,7296]{1,0:T(8,128)(2,1)}, bf16[48,7296]{1,0:T(8,128)(2,1)S(1)}, u32[]{:S(2)}) copy-start(bf16[48,7296]{1,0:T(8,128)(2,1)S(1)} %collective-permute-done.13.refs_2_) | copy-start | bytes 2101252
  127.3 23.8 %collective-permute-start.14 = (bf16[48,3712]{1,0:T(8,128)(2,1)}, bf16[48,3712]{1,0:T(8,128)(2,1)S(1)}, u32[]{:S(2)}, u32[]{:S(2)}) collective-permute-start(bf16[48,3712]{1,0:T(8,128)(2,1)} %get-tuple-element.239), channel_id=1, source_target_pairs={{0,1},{1,0},{2,3},{3,2},{4,5},{5,4},{6,7},{7,6},{8,9},{9,8},{10,11... | collective-permute-start | bytes 1069064 | tf_op jit(solution)/shard_map/ppermute | solution.py:273
  127.5 23.6 %collective-permute-start.15 = (bf16[48,3712]{1,0:T(8,128)(2,1)}, bf16[48,3712]{1,0:T(8,128)(2,1)S(1)}, u32[]{:S(2)}, u32[]{:S(2)}) collective-permute-start(bf16[48,3712]{1,0:T(8,128)(2,1)} %get-tuple-element.240), channel_id=1, source_target_pairs={{0,2},{1,3},{2,0},{3,1},{4,6},{5,7},{6,4},{7,5},{8,10},{9,11},{10,... | collective-permute-start | bytes 1069064 | tf_op jit(solution)/shard_map/ppermute | solution.py:273
  127.8 25.9 %collective-permute-start.16 = (bf16[48,3712]{1,0:T(8,128)(2,1)}, bf16[48,3712]{1,0:T(8,128)(2,1)S(1)}, u32[]{:S(2)}, u32[]{:S(2)}) collective-permute-start(bf16[48,3712]{1,0:T(8,128)(2,1)} %get-tuple-element.241), channel_id=1, source_target_pairs={{0,3},{1,2},{2,1},{3,0},{4,7},{5,6},{6,5},{7,4},{8,11},{9,10},{10,... | collective-permute-start | bytes 1069064 | tf_op jit(solution)/shard_map/ppermute | solution.py:273
  153.7 27.3 %collective-permute-start.18 = (bf16[48,7296]{1,0:T(8,128)(2,1)}, bf16[48,7296]{1,0:T(8,128)(2,1)S(1)}, u32[]{:S(2)}, u32[]{:S(2)}) collective-permute-start(bf16[48,7296]{1,0:T(8,128)(2,1)} %get-tuple-element.263), channel_id=1, source_target_pairs={{0,1},{1,0},{2,3},{3,2},{4,5},{5,4},{6,7},{7,6},{8,9},{9,8},{10,11... | collective-permute-start | bytes 2101256 | tf_op jit(solution)/shard_map/ppermute | solution.py:273
  153.9 27.1 %collective-permute-start.19 = (bf16[48,7296]{1,0:T(8,128)(2,1)}, bf16[48,7296]{1,0:T(8,128)(2,1)S(1)}, u32[]{:S(2)}, u32[]{:S(2)}) collective-permute-start(bf16[48,7296]{1,0:T(8,128)(2,1)} %get-tuple-element.264), channel_id=1, source_target_pairs={{0,2},{1,3},{2,0},{3,1},{4,6},{5,7},{6,4},{7,5},{8,10},{9,11},{10,... | collective-permute-start | bytes 2101256 | tf_op jit(solution)/shard_map/ppermute | solution.py:273
  154.1 33.1 %collective-permute-start.20 = (bf16[48,7296]{1,0:T(8,128)(2,1)}, bf16[48,7296]{1,0:T(8,128)(2,1)S(1)}, u32[]{:S(2)}, u32[]{:S(2)}) collective-permute-start(bf16[48,7296]{1,0:T(8,128)(2,1)} %get-tuple-element.268), channel_id=1, source_target_pairs={{0,3},{1,2},{2,1},{3,0},{4,7},{5,6},{6,5},{7,4},{8,11},{9,10},{10,... | collective-permute-start | bytes 2101256 | tf_op jit(solution)/shard_map/ppermute | solution.py:273
  160.0 27.2 %copy-start.33 = (bf16[48,3712]{1,0:T(8,128)(2,1)S(1)}, bf16[48,3712]{1,0:T(8,128)(2,1)}, u32[]{:S(2)}) copy-start(bf16[48,3712]{1,0:T(8,128)(2,1)} %get-tuple-element.301) | copy-start | bytes 1069060
  160.0 27.3 %copy-start.37 = (bf16[128,128]{1,0:T(8,128)(2,1)S(1)}, bf16[128,128]{1,0:T(8,128)(2,1)}, u32[]{:S(2)}) copy-start(bf16[128,128]{1,0:T(8,128)(2,1)} %get-tuple-element.293) | copy-start | bytes 98308
  160.0 48.5 %collective-permute-start.22 = (bf16[128,3584]{1,0:T(8,128)(2,1)}, bf16[128,3584]{1,0:T(8,128)(2,1)S(1)}, u32[]{:S(2)}, u32[]{:S(2)}) collective-permute-start(bf16[128,3584]{1,0:T(8,128)(2,1)} %get-tuple-element.274), channel_id=1, source_target_pairs={{0,4},{1,5},{2,6},{3,7},{12,8},{13,9},{14,10},{15,11},{4,12},{5,13... | collective-permute-start | bytes 2752520 | tf_op jit(solution)/shard_map/ppermute | solution.py:273
  181.0 6.2 %collective-permute-start.21 = (bf16[48,3712]{1,0:T(8,128)(2,1)}, bf16[48,3712]{1,0:T(8,128)(2,1)S(1)}, u32[]{:S(2)}, u32[]{:S(2)}) collective-permute-start(bf16[48,3712]{1,0:T(8,128)(2,1)} %get-tuple-element.275), channel_id=1, source_target_pairs={{0,1},{1,0},{2,3},{3,2},{4,5},{5,4},{6,7},{7,6},{8,9},{9,8},{10,11... | collective-permute-start | bytes 1069064 | tf_op jit(solution)/shard_map/ppermute | solution.py:273
  181.4 27.2 %collective-permute-start.24 = (bf16[48,3712]{1,0:T(8,128)(2,1)}, bf16[48,3712]{1,0:T(8,128)(2,1)S(1)}, u32[]{:S(2)}, u32[]{:S(2)}) collective-permute-start(bf16[48,3712]{1,0:T(8,128)(2,1)} %get-tuple-element.296), channel_id=1, source_target_pairs={{0,2},{1,3},{2,0},{3,1},{4,6},{5,7},{6,4},{7,5},{8,10},{9,11},{10,... | collective-permute-start | bytes 1069064 | tf_op jit(solution)/shard_map/ppermute | solution.py:273
  181.6 26.9 %collective-permute-start.25 = (bf16[48,3712]{1,0:T(8,128)(2,1)}, bf16[48,3712]{1,0:T(8,128)(2,1)S(1)}, u32[]{:S(2)}, u32[]{:S(2)}) collective-permute-start(bf16[48,3712]{1,0:T(8,128)(2,1)} %get-tuple-element.297), channel_id=1, source_target_pairs={{0,3},{1,2},{2,1},{3,0},{4,7},{5,6},{6,5},{7,4},{8,11},{9,10},{10,... | collective-permute-start | bytes 1069064 | tf_op jit(solution)/shard_map/ppermute | solution.py:273
  187.3 21.2 %copy-start.8 = (bf16[48,3712]{1,0:T(8,128)(2,1)}, bf16[48,3712]{1,0:T(8,128)(2,1)S(1)}, u32[]{:S(2)}) copy-start(bf16[48,3712]{1,0:T(8,128)(2,1)S(1)} %collective-permute-done.21.refs_1_.refs_5_) | copy-start | bytes 1069060
  187.3 22.2 %collective-permute-start.26 = (bf16[48,3712]{1,0:T(8,128)(2,1)S(1)}, bf16[48,3712]{1,0:T(8,128)(2,1)S(1)}, u32[]{:S(2)}, u32[]{:S(2)}) collective-permute-start(bf16[48,3712]{1,0:T(8,128)(2,1)S(1)} %copy-done.33), channel_id=1, source_target_pairs={{0,3},{1,2},{2,1},{3,0},{4,7},{5,6},{6,5},{7,4},{8,11},{9,10},{10,... | collective-permute-start | bytes 1069064 | tf_op jit(solution)/shard_map/ppermute | solution.py:273
  187.4 21.2 %collective-permute-start.23 = (bf16[128,128]{1,0:T(8,128)(2,1)S(1)}, bf16[128,128]{1,0:T(8,128)(2,1)S(1)}, u32[]{:S(2)}, u32[]{:S(2)}) collective-permute-start(bf16[128,128]{1,0:T(8,128)(2,1)S(1)} %copy-done.37), channel_id=1, source_target_pairs={{0,4},{1,5},{2,6},{3,7},{12,8},{13,9},{14,10},{15,11},{4,12},{5,13... | collective-permute-start | bytes 98312 | tf_op jit(solution)/shard_map/ppermute | solution.py:273
  208.6 72.0 %copy-start.17 = (bf16[128,3584]{1,0:T(8,128)(2,1)}, bf16[128,3584]{1,0:T(8,128)(2,1)S(1)}, u32[]{:S(2)}) copy-start(bf16[128,3584]{1,0:T(8,128)(2,1)S(1)} %collective-permute-done.22.refs_1_) | copy-start | bytes 2752516
  209.5 29.8 %copy-start.7 = (bf16[48,3712]{1,0:T(8,128)(2,1)}, bf16[48,3712]{1,0:T(8,128)(2,1)S(1)}, u32[]{:S(2)}) copy-start(bf16[48,3712]{1,0:T(8,128)(2,1)S(1)} %collective-permute-done.26.refs_3_.refs_7_) | copy-start | bytes 1069060
  213.8 63.4 %collective-permute-start.32 = (bf16[128,3584]{1,0:T(8,128)(2,1)}, bf16[128,3584]{1,0:T(8,128)(2,1)S(1)}, u32[]{:S(2)}, u32[]{:S(2)}) collective-permute-start(bf16[128,3584]{1,0:T(8,128)(2,1)} %get-tuple-element.326), channel_id=1, source_target_pairs={{0,12},{1,13},{2,14},{3,15},{4,8},{5,9},{6,10},{7,11},{8,4},{9,5},... | collective-permute-start | bytes 2752520 | tf_op jit(solution)/shard_map/ppermute | solution.py:273
  215.5 2.6 collective-permute-start.27
  216.4 9.9 %collective-permute-start.28 = (bf16[48,3712]{1,0:T(8,128)(2,1)S(1)}, bf16[48,3712]{1,0:T(8,128)(2,1)S(1)}, u32[]{:S(2)}, u32[]{:S(2)}) collective-permute-start(bf16[48,3712]{1,0:T(8,128)(2,1)S(1)} %copy-done.35), channel_id=1, source_target_pairs={{0,2},{1,3},{2,0},{3,1},{4,6},{5,7},{6,4},{7,5},{8,10},{9,11},{10,... | collective-permute-start | bytes 1069064 | tf_op jit(solution)/shard_map/ppermute | solution.py:273
  217.6 16.7 %collective-permute-start.29 = (bf16[48,3712]{1,0:T(8,128)(2,1)S(1)}, bf16[48,3712]{1,0:T(8,128)(2,1)S(1)}, u32[]{:S(2)}, u32[]{:S(2)}) collective-permute-start(bf16[48,3712]{1,0:T(8,128)(2,1)S(1)} %copy-done.34), channel_id=1, source_target_pairs={{0,3},{1,2},{2,1},{3,0},{4,7},{5,6},{6,5},{7,4},{8,11},{9,10},{10,... | collective-permute-start | bytes 1069064 | tf_op jit(solution)/shard_map/ppermute | solution.py:273
  218.1 59.2 %collective-permute-start.31 = (bf16[128,128]{1,0:T(8,128)(2,1)}, bf16[128,128]{1,0:T(8,128)(2,1)S(1)}, u32[]{:S(2)}, u32[]{:S(2)}) collective-permute-start(bf16[128,128]{1,0:T(8,128)(2,1)} %get-tuple-element.325), channel_id=1, source_target_pairs={{0,12},{1,13},{2,14},{3,15},{4,8},{5,9},{6,10},{7,11},{8,4},{9,5},... | collective-permute-start | bytes 98312 | tf_op jit(solution)/shard_map/ppermute | solution.py:273
  239.2 38.0 %copy-start.31 = (f32[128,16]{1,0:T(8,128)S(1)}, f32[128,16]{1,0:T(8,128)}, u32[]{:S(2)}) copy-start(f32[128,16]{1,0:T(8,128)} %copy-done.30) | copy-start | bytes 24580
  239.2 39.0 %copy-start.32 = (f32[128,16]{1,0:T(8,128)S(1)}, f32[128,16]{1,0:T(8,128)}, u32[]{:S(2)}) copy-start(f32[128,16]{1,0:T(8,128)} %get-tuple-element.340) | copy-start | bytes 24580
  239.2 38.0 %collective-permute-start.30 = (bf16[128,128]{1,0:T(8,128)(2,1)}, bf16[128,128]{1,0:T(8,128)(2,1)S(1)}, u32[]{:S(2)}, u32[]{:S(2)}) collective-permute-start(bf16[128,128]{1,0:T(8,128)(2,1)} %get-tuple-element.319), channel_id=1, source_target_pairs={{4,0},{5,1},{6,2},{7,3},{8,12},{9,13},{10,14},{11,15},{12,4},{13,5... | collective-permute-start | bytes 98312 | tf_op jit(solution)/shard_map/ppermute | solution.py:273
  239.5 47.3 %collective-permute-start.33 = (bf16[128,3584]{1,0:T(8,128)(2,1)}, bf16[128,3584]{1,0:T(8,128)(2,1)}, u32[]{:S(2)}, u32[]{:S(2)}) collective-permute-start(bf16[128,3584]{1,0:T(8,128)(2,1)} %get-tuple-element.333), channel_id=1, source_target_pairs={{4,0},{5,1},{6,2},{7,3},{8,12},{9,13},{10,14},{11,15},{12,4},{13,5... | collective-permute-start | bytes 2752520 | tf_op jit(solution)/shard_map/ppermute | solution.py:273
  280.5 14.1 %all-to-all-start = ((f32[16,16,224]{2,1,0:T(8,128)}), f32[16,16,224]{2,1,0:T(8,128)S(1)}, u32[]{:S(2)}, u32[]{:S(2)}) async-start(f32[16,16,224]{2,1,0:T(8,128)} %bitcast.28), calls=%async_computation | async-start | bytes 524288 | tf_op jit(solution)/shard_map/all_to_all | solution.py:410
  (25 other events, 138.9 us)

commit v7 on v5

--- a/solution.py
+++ b/solution.py
@@ -111,10 +111,10 @@
             at += out.shape[0]
 
 
-def sum_rows(placed, pieces, width, parts=1):
+def sum_rows(placed, pieces, width, lengths=None):
     cap, wide = pieces[0].shape
     tok = placed.shape[1]
-    shapes = [jax.ShapeDtypeStruct((tok // parts, width), bf16)] * parts
+    shapes = [jax.ShapeDtypeStruct((length, width), bf16) for length in lengths or (tok,)]
     apart = width < wide
     if apart:
         shapes.append(jax.ShapeDtypeStruct((tok, wide - width), bf16))
@@ -382,24 +382,23 @@
             back_2 = spread(done_2[:plane])
             (part_1,) = sum_rows(placed_1, back_1, wide)
             term_1 = send(part_1, along([(0, 1), (3, 2), (1, 3), (2, 0)]))
-            got_3, part_1, back_2[1], last_0 = join((got_3, part_1, back_2[1], last_0))
+            got_3, part_1, back_2, last_0 = join((got_3, part_1, back_2, last_0))
+            part_2a, part_2b, tag_2 = sum_rows(placed_2, back_2, width, (tok * 5 // 8, tok * 3 // 8))
+            tag_2 = send(tag_2, across(3 * plane))
+            term_2a = send(part_2a, across(3 * plane))
             back_0.append(send(last_0, across(3)))
             done_3 = run(got_3, done_2[plane:])
-            done_3, term_1, back_2, back_0 = join((done_3, term_1, back_2, back_0))
+            done_3, term_1, term_2a, tag_2, part_2b, back_0 = join(
+                (done_3, term_1, term_2a, tag_2, part_2b, back_0)
+            )
             back_3 = spread(done_3[:plane])
-            part_2a, part_2b, tag_2 = sum_rows(placed_2, back_2, width, 2)
-            tag_2 = send(tag_2, across(3 * plane))
-            term_2a = send(part_2a, across(3 * plane))
-            back_3[1], back_3[2], part_2b, back_0, tag_2 = join(
-                (back_3[1], back_3[2], part_2b, back_0, tag_2)
-            )
+            term_2b = send(part_2b, across(3 * plane))
+            back_3, back_0, term_2b = join((back_3, back_0, term_2b))
             part_0, tag_0 = sum_rows(placed_0, back_0, width)
             part_3, tag_3 = sum_rows(placed_3, back_3, width)
             swap_3 = along([(1, 0), (2, 3), (3, 1), (0, 2)])
             tag_3 = send(tag_3, swap_3)
             term_3 = send(part_3, swap_3)
-            tag_3, term_2a, part_2b = join((tag_3, term_2a, part_2b))
-            term_2b = send(part_2b, across(3 * plane))
             tags = [tag_0, term_1[:, width:], tag_2, tag_3]
             terms = [[part_0], [term_1], [term_2a, term_2b], [term_3]]
             done = [done_3]

time: 297 us -> 294 us (0.990)
  blocking collectives: 41.4 us -> 23.3 us
  waiting for transfers between devices: 95.4 us -> 112 us
    all_to_all x1, blocking collectives: 41.4 us -> 23.3 us  [shards(): lax.all_to_all(router_part, 'expert', split_axis=0, concat_axis=0, tiled=...]
    ppermute x34, waiting for transfers between devices: 95.4 us -> 112 us  [send(): return lax.ppermute(array, 'expert', pairs)]
    unnamed x72 -> x74, local copies, waits for them, and re-layouts: 6.98 us -> 6.49 us
  transfers between devices with their start and end apart: 34 -> 34, of which waited for: 12 -> 15; matrix products, arithmetic and copies ran while one was open for 2% -> 2% of each run, Pallas kernels for 35% -> 36%
where the time goes in v7:
time: 294 us; the launch traced here: 291 us
  waiting for transfers between devices  112 us (38%)
  Pallas kernels  110 us (37%)
  starting transfers between devices  28.5 us (10%)
  blocking collectives  23.3 us (8%)
  local copies, waits for them, and re-layouts  9.18 us (3%)
  other arithmetic  4.78 us (2%)
    ppermute x34, waiting for transfers between devices, send(): return lax.ppermute(array, 'expert', pairs)  112 us
    pallas_call x4, Pallas kernels, expert_rows(): pl.pallas_call(functools.partial(expert_kernel, len(carry), cap, width, r...  78.7 us
    ppermute x34, starting transfers between devices, send(): return lax.ppermute(array, 'expert', pairs)  28.5 us
    all_to_all x1, blocking collectives, shards(): lax.all_to_all(router_part, 'expert', split_axis=0, concat_axis=0, tiled=...  23.3 us
    pallas_call x4, Pallas kernels, select_rows(): pl.pallas_call(functools.partial(select_kernel, parts, meta_at, slots_hel...  16.9 us
    pallas_call x4, Pallas kernels, sum_rows(): pl.pallas_call(functools.partial(sum_kernel, apart), out_shape=shapes, in...  10.9 us
    unnamed x74, local copies, waits for them, and re-layouts  6.49 us
  transfers between devices with their start and end apart: 34, of which 15 were waited for; matrix products, arithmetic and copies ran while one was open for 2% of the time, Pallas kernels for 36%

profile of v7, /device:TPU:15, one launch (start us, length us, event | category | flops | bytes accessed | tf_op | source)
XLA Modules:
  0.0 291.3 jit_solution(10525990653955808009)
XLA Ops:
  1.7 2.2 fusion.6
  4.5 2.2 concatenate.5.refs_0_
  8.0 4.1 %shard_map.154 = (bf16[48,7296]{1,0:T(8,128)(2,1)}, bf16[48,7296]{1,0:T(8,128)(2,1)}, bf16[48,7296]{1,0:T(8,128)(2,1)}, bf16[48,7296]{1,0:T(8,128)(2,1)}, bf16[192,128]{1,0:T(8,128)(2,1)}) custom-call(s32[1]{0:T(128)} %bitcast.flag_ref, bf16[16,128]{1,0:T(8,128)(2,1)} %pad_convert_fusion.guide_ref, bf16[128,7296]{1,0:T(8,128)(2,1)} %copy-done), custom_call_target="tpu_custom_call" | custom-call | flops 1024 | bytes 1024 | tf_op jit(solution)/shard_map/pallas_call | solution.py:87
  12.9 1.4 collective-permute-start.3
  14.7 15.6 %collective-permute-done.2.refs_2_ = bf16[48,7296]{1,0:T(8,128)(2,1)S(1)} collective-permute-done((bf16[48,7296]{1,0:T(8,128)(2,1)}, bf16[48,7296]{1,0:T(8,128)(2,1)S(1)}, u32[]{:S(2)}, u32[]{:S(2)}) %collective-permute-start.2) | collective-permute-done | bytes 700448 | tf_op jit(solution)/shard_map/ppermute | solution.py:282
  30.4 15.4 %collective-permute-done.3.refs_3_ = bf16[48,7296]{1,0:T(8,128)(2,1)S(1)} collective-permute-done((bf16[48,7296]{1,0:T(8,128)(2,1)}, bf16[48,7296]{1,0:T(8,128)(2,1)S(1)}, u32[]{:S(2)}, u32[]{:S(2)}) %collective-permute-start.3) | collective-permute-done | bytes 700448 | tf_op jit(solution)/shard_map/ppermute | solution.py:282
  45.8 3.6 %collective-permute-done.refs_0_ = bf16[128,7296]{1,0:T(8,128)(2,1)} collective-permute-done((bf16[128,7296]{1,0:T(8,128)(2,1)S(1)}, bf16[128,7296]{1,0:T(8,128)(2,1)}, u32[]{:S(2)}, u32[]{:S(2)}) %collective-permute-start) | collective-permute-done | bytes 1867808 | tf_op jit(solution)/shard_map/ppermute | solution.py:282
  49.4 1.4 collective-permute-start.4
  50.8 4.2 %collective-permute-start.5 = (bf16[128,7296]{1,0:T(8,128)(2,1)}, bf16[128,7296]{1,0:T(8,128)(2,1)}, u32[]{:S(2)}, u32[]{:S(2)}) collective-permute-start(bf16[128,7296]{1,0:T(8,128)(2,1)} %copy-done), channel_id=1, source_target_pairs={{4,8},{5,9},{6,10},{7,11},{8,4},{9,5},{10,6},{11,7},{20,24},{21,25... | collective-permute-start | bytes 5603336 | tf_op jit(solution)/shard_map/ppermute | solution.py:282
  55.0 4.1 %shard_map.155 = (bf16[48,7296]{1,0:T(8,128)(2,1)}, bf16[48,7296]{1,0:T(8,128)(2,1)}, bf16[48,7296]{1,0:T(8,128)(2,1)}, bf16[48,7296]{1,0:T(8,128)(2,1)}, bf16[192,128]{1,0:T(8,128)(2,1)}) custom-call(s32[1]{0:T(128)} %bitcast.flag_ref, bf16[16,128]{1,0:T(8,128)(2,1)} %pad_convert_fusion.guide_ref, bf16[128,7296]{1,0:T(8,128)(2,1)} %collective-permute-done.refs_0_), custom_call_target="tpu_custom_call" | custom-call | flops 1024 | bytes 1024 | tf_op jit(solution)/shard_map/pallas_call | solution.py:87
  59.1 2.1 collective-permute-start.6
  61.4 1.4 collective-permute-start.8
  63.4 19.4 %shard_map.156 = (bf16[48,3712]{1,0:T(8,128)(2,1)}, bf16[48,3712]{1,0:T(8,128)(2,1)}, bf16[48,3712]{1,0:T(8,128)(2,1)}, bf16[48,3712]{1,0:T(8,128)(2,1)}, f32[32...) custom-call(f32[1,128]{1,0:T(1,128)} %compare_convert_fusion.mine_ref, ...), custom_call_target="tpu_custom_call" | custom-call | flops 1024 | bytes 1024 | tf_op jit(solution)/shard_map/pallas_call | solution.py:233
  82.8 11.5 %collective-permute-done.8.refs_3_ = bf16[48,7296]{1,0:T(8,128)(2,1)} collective-permute-done((bf16[48,7296]{1,0:T(8,128)(2,1)}, bf16[48,7296]{1,0:T(8,128)(2,1)}, u32[]{:S(2)}, u32[]{:S(2)}) %collective-permute-start.8) | collective-permute-done | bytes 700448 | tf_op jit(solution)/shard_map/ppermute | solution.py:282
  94.5 1.6 collective-permute-done.9.refs_1_
  96.2 1.3 copy-done.3
  97.4 4.6 %shard_map.157 = (bf16[48,7296]{1,0:T(8,128)(2,1)}, bf16[48,7296]{1,0:T(8,128)(2,1)}, bf16[48,7296]{1,0:T(8,128)(2,1)}, bf16[48,7296]{1,0:T(8,128)(2,1)}, bf16[192,128]{1,0:T(8,128)(2,1)}) custom-call(s32[1]{0:T(128)} %bitcast.flag_ref, bf16[16,128]{1,0:T(8,128)(2,1)} %pad_convert_fusion.guide_ref, bf16[128,7296]{1,0:T(8,128)(2,1)} %collective-permute-done.5.refs_0_, ...), custom_call_target="tpu_custom_call" | custom-call | flops 1024 | bytes 1024 | tf_op jit(solution)/shard_map/pallas_call | solution.py:87
  102.1 1.8 collective-permute-done.10.refs_2_
  104.7 1.4 collective-permute-start.12
  106.3 1.5 collective-permute-start.17
  107.7 19.8 %shard_map.159 = (bf16[48,3712]{1,0:T(8,128)(2,1)}, bf16[48,3712]{1,0:T(8,128)(2,1)}, bf16[48,3712]{1,0:T(8,128)(2,1)}, bf16[48,3712]{1,0:T(8,128)(2,1)}, f32[32...) custom-call(f32[1,128]{1,0:T(1,128)} %compare_convert_fusion.mine_ref, ...), custom_call_target="tpu_custom_call" | custom-call | flops 1024 | bytes 1024 | tf_op jit(solution)/shard_map/pallas_call | solution.py:233
  128.0 1.8 collective-permute-start.16
  129.8 15.7 %collective-permute-done.11.refs_0_ = bf16[128,7296]{1,0:T(8,128)(2,1)S(1)} collective-permute-done((bf16[128,7296]{1,0:T(8,128)(2,1)S(1)}, bf16[128,7296]{1,0:T(8,128)(2,1)S(1)}, u32[]{:S(2)}, u32[]{:S(2)}) %collective-permute-start.11) | collective-permute-done | bytes 1867808 | tf_op jit(solution)/shard_map/ppermute | solution.py:282
  145.5 1.3 copy-done.4
  146.8 4.1 %shard_map.158 = (bf16[48,7296]{1,0:T(8,128)(2,1)}, bf16[48,7296]{1,0:T(8,128)(2,1)}, bf16[48,7296]{1,0:T(8,128)(2,1)}, bf16[48,7296]{1,0:T(8,128)(2,1)}, bf16[192,128]{1,0:T(8,128)(2,1)}) custom-call(s32[1]{0:T(128)} %bitcast.flag_ref, bf16[16,128]{1,0:T(8,128)(2,1)} %pad_convert_fusion.guide_ref, bf16[128,7296]{1,0:T(8,128)(2,1)} %copy-done.4), custom_call_target="tpu_custom_call" | custom-call | flops 1024 | bytes 1024 | tf_op jit(solution)/shard_map/pallas_call | solution.py:87
  151.0 3.0 %collective-permute-done.16.refs_3_ = bf16[48,3712]{1,0:T(8,128)(2,1)S(1)} collective-permute-done((bf16[48,3712]{1,0:T(8,128)(2,1)}, bf16[48,3712]{1,0:T(8,128)(2,1)S(1)}, u32[]{:S(2)}, u32[]{:S(2)}) %collective-permute-start.16) | collective-permute-done | bytes 356384 | tf_op jit(solution)/shard_map/ppermute | solution.py:282
  154.4 1.7 collective-permute-start.20
  156.1 2.7 shard_map.161
  158.8 1.2 collective-permute-start.24
  160.0 19.8 %shard_map.160 = (bf16[48,3712]{1,0:T(8,128)(2,1)}, bf16[48,3712]{1,0:T(8,128)(2,1)}, bf16[48,3712]{1,0:T(8,128)(2,1)}, bf16[48,3712]{1,0:T(8,128)(2,1)}, f32[32...) custom-call(f32[1,128]{1,0:T(1,128)} %compare_convert_fusion.mine_ref, ...), custom_call_target="tpu_custom_call" | custom-call | flops 1024 | bytes 1024 | tf_op jit(solution)/shard_map/pallas_call | solution.py:233
  180.4 1.6 collective-permute-start.23
  182.0 5.5 %collective-permute-done.20.refs_3_ = bf16[48,7296]{1,0:T(8,128)(2,1)S(1)} collective-permute-done((bf16[48,7296]{1,0:T(8,128)(2,1)}, bf16[48,7296]{1,0:T(8,128)(2,1)S(1)}, u32[]{:S(2)}, u32[]{:S(2)}) %collective-permute-start.20) | collective-permute-done | bytes 700448 | tf_op jit(solution)/shard_map/ppermute | solution.py:282
  187.5 6.5 %collective-permute-done.22.refs_2_ = bf16[48,3712]{1,0:T(8,128)(2,1)S(1)} collective-permute-done((bf16[48,3712]{1,0:T(8,128)(2,1)}, bf16[48,3712]{1,0:T(8,128)(2,1)S(1)}, u32[]{:S(2)}, u32[]{:S(2)}) %collective-permute-start.22) | collective-permute-done | bytes 356384 | tf_op jit(solution)/shard_map/ppermute | solution.py:282
  194.1 8.0 %collective-permute-done.23.refs_3_ = bf16[48,3712]{1,0:T(8,128)(2,1)S(1)} collective-permute-done((bf16[48,3712]{1,0:T(8,128)(2,1)}, bf16[48,3712]{1,0:T(8,128)(2,1)S(1)}, u32[]{:S(2)}, u32[]{:S(2)}) %collective-permute-start.23) | collective-permute-done | bytes 356384 | tf_op jit(solution)/shard_map/ppermute | solution.py:282
  202.8 2.7 shard_map.163
  205.7 1.7 collective-permute-start.26
  207.4 19.7 %shard_map.162 = (bf16[48,3712]{1,0:T(8,128)(2,1)}, bf16[48,3712]{1,0:T(8,128)(2,1)}, bf16[48,3712]{1,0:T(8,128)(2,1)}, bf16[48,3712]{1,0:T(8,128)(2,1)}, f32[32...) custom-call(f32[1,128]{1,0:T(1,128)} %compare_convert_fusion.mine_ref, ...), custom_call_target="tpu_custom_call" | custom-call | flops 1024 | bytes 1024 | tf_op jit(solution)/shard_map/pallas_call | solution.py:233
  227.2 6.9 %collective-permute-done.26 = bf16[128,128]{1,0:T(8,128)(2,1)S(1)} collective-permute-done((bf16[128,128]{1,0:T(8,128)(2,1)}, bf16[128,128]{1,0:T(8,128)(2,1)S(1)}, u32[]{:S(2)}, u32[]{:S(2)}) %collective-permute-start.26) | collective-permute-done | bytes 32800 | tf_op jit(solution)/shard_map/ppermute | solution.py:282
  235.2 1.5 collective-permute-start.30
  236.7 14.5 %collective-permute-done.31.refs_3_ = bf16[48,3584]{1,0:T(8,128)(2,1)S(1)} collective-permute-done((bf16[48,3584]{1,0:T(8,128)(2,1)S(1)}, bf16[48,3584]{1,0:T(8,128)(2,1)S(1)}, u32[]{:S(2)}, u32[]{:S(2)}) %collective-permute-start.31) | collective-permute-done | bytes 344096 | tf_op jit(solution)/shard_map/ppermute | solution.py:282
  251.2 1.7 collective-permute-done.30.refs_3_
  253.6 2.7 shard_map.165
  256.3 1.2 collective-permute-start.33
  257.5 2.8 shard_map.164
  260.2 0.9 multiply_reduce_fusion
  262.8 23.3 %all_to_all.5 = f32[16,16,224]{2,1,0:T(8,128)S(1)} all-to-all(f32[16,16,224]{2,1,0:T(8,128)S(1)} %bitcast.57), channel_id=1, replica_groups=mesh['groups'=2,'expert'=16] {'expert'}, dimensions={0} | all-to-all | bytes 458752 | tf_op jit(solution)/shard_map/all_to_all | solution.py:425
  286.7 0.9 copy-done.6
  287.6 3.7 %shard_map.166 = bf16[128,3584]{1,0:T(8,128)(2,1)} custom-call(bf16[128,16]{1,0:T(8,128)(2,1)} %copy-done.31, bf16[16,3584]{1,0:T(8,128)(2,1)} %bitcast.58, bf16[128,3584]{1,0:T(8,128)(2,1)} %get-tuple-element.328.refs_0_, bf16[128,3712]{1,0:T(8,128)(2,1)} %copy-done.5, bf16[80,3584]{1,0:T(8,128)(2,1)} %copy-done.17, bf16[48,3584]{1,0:T(8,128)(2,1)} %copy-done.30, ...), custom_call_target="tpu_custom_call" | custom-call | flops 1024 | bytes 1024 | tf_op jit(solution)/shard_map/pallas_call | solution.py:146
  (126 shorter events, 12.6 us)
Async XLA Ops:
  6.7 42.6 %collective-permute-start = (bf16[128,7296]{1,0:T(8,128)(2,1)S(1)}, bf16[128,7296]{1,0:T(8,128)(2,1)}, u32[]{:S(2)}, u32[]{:S(2)}) collective-permute-start(bf16[128,7296]{1,0:T(8,128)(2,1)S(1)} %concatenate.5.refs_0_), channel_id=1, source_target_pairs={{0,8},{1,9},{2,10},{3,11},{12,4},{13,5},{14,6},{15,7},{4,0},{5,1},... | collective-permute-start | bytes 5603336 | tf_op jit(solution)/shard_map/ppermute | solution.py:282
  12.0 2.7 collective-permute-start.1
  12.7 17.6 %collective-permute-start.2 = (bf16[48,7296]{1,0:T(8,128)(2,1)}, bf16[48,7296]{1,0:T(8,128)(2,1)S(1)}, u32[]{:S(2)}, u32[]{:S(2)}) collective-permute-start(bf16[48,7296]{1,0:T(8,128)(2,1)} %get-tuple-element.180), channel_id=1, source_target_pairs={{0,2},{1,3},{2,0},{3,1},{4,6},{5,7},{6,4},{7,5},{8,10},{9,11},{10,... | collective-permute-start | bytes 2101256 | tf_op jit(solution)/shard_map/ppermute | solution.py:282
  12.9 32.8 %collective-permute-start.3 = (bf16[48,7296]{1,0:T(8,128)(2,1)}, bf16[48,7296]{1,0:T(8,128)(2,1)S(1)}, u32[]{:S(2)}, u32[]{:S(2)}) collective-permute-start(bf16[48,7296]{1,0:T(8,128)(2,1)} %get-tuple-element.181), channel_id=1, source_target_pairs={{0,3},{1,2},{2,1},{3,0},{4,7},{5,6},{6,5},{7,4},{8,11},{9,10},{10,... | collective-permute-start | bytes 2101256 | tf_op jit(solution)/shard_map/ppermute | solution.py:282
  14.7 34.7 %copy-start.14 = (bf16[48,7296]{1,0:T(8,128)(2,1)}, bf16[48,7296]{1,0:T(8,128)(2,1)S(1)}, u32[]{:S(2)}) copy-start(bf16[48,7296]{1,0:T(8,128)(2,1)S(1)} %collective-permute-done.1.refs_1_) | copy-start | bytes 2101252
  49.4 46.8 %collective-permute-start.4 = (bf16[128,7296]{1,0:T(8,128)(2,1)}, bf16[128,7296]{1,0:T(8,128)(2,1)S(1)}, u32[]{:S(2)}, u32[]{:S(2)}) collective-permute-start(bf16[128,7296]{1,0:T(8,128)(2,1)} %collective-permute-done.refs_0_), channel_id=1, source_target_pairs={{4,0},{5,1},{6,2},{7,3},{8,12},{9,13},{10,14},{11,15},{20,16},{21,... | collective-permute-start | bytes 5603336 | tf_op jit(solution)/shard_map/ppermute | solution.py:282
  50.8 45.4 %collective-permute-start.5 = (bf16[128,7296]{1,0:T(8,128)(2,1)}, bf16[128,7296]{1,0:T(8,128)(2,1)}, u32[]{:S(2)}, u32[]{:S(2)}) collective-permute-start(bf16[128,7296]{1,0:T(8,128)(2,1)} %copy-done), channel_id=1, source_target_pairs={{4,8},{5,9},{6,10},{7,11},{8,4},{9,5},{10,6},{11,7},{20,24},{21,25... | collective-permute-start | bytes 5603336 | tf_op jit(solution)/shard_map/ppermute | solution.py:282
  59.1 23.6 %collective-permute-start.6 = (bf16[48,7296]{1,0:T(8,128)(2,1)}, bf16[48,7296]{1,0:T(8,128)(2,1)S(1)}, u32[]{:S(2)}, u32[]{:S(2)}) collective-permute-start(bf16[48,7296]{1,0:T(8,128)(2,1)} %get-tuple-element.185), channel_id=1, source_target_pairs={{0,1},{1,0},{2,3},{3,2},{4,5},{5,4},{6,7},{7,6},{8,9},{9,8},{10,11... | collective-permute-start | bytes 2101256 | tf_op jit(solution)/shard_map/ppermute | solution.py:282
  61.2 21.6 %collective-permute-start.7 = (bf16[48,7296]{1,0:T(8,128)(2,1)}, bf16[48,7296]{1,0:T(8,128)(2,1)}, u32[]{:S(2)}, u32[]{:S(2)}) collective-permute-start(bf16[48,7296]{1,0:T(8,128)(2,1)} %get-tuple-element.186), channel_id=1, source_target_pairs={{0,2},{1,3},{2,0},{3,1},{4,6},{5,7},{6,4},{7,5},{8,10},{9,11},{10,... | collective-permute-start | bytes 2101256 | tf_op jit(solution)/shard_map/ppermute | solution.py:282
  61.4 32.8 %collective-permute-start.8 = (bf16[48,7296]{1,0:T(8,128)(2,1)}, bf16[48,7296]{1,0:T(8,128)(2,1)}, u32[]{:S(2)}, u32[]{:S(2)}) collective-permute-start(bf16[48,7296]{1,0:T(8,128)(2,1)} %get-tuple-element.187), channel_id=1, source_target_pairs={{0,3},{1,2},{2,1},{3,0},{4,7},{5,6},{6,5},{7,4},{8,11},{9,10},{10,... | collective-permute-start | bytes 2101256 | tf_op jit(solution)/shard_map/ppermute | solution.py:282
  82.8 23.2 %copy-start.13 = (bf16[48,7296]{1,0:T(8,128)(2,1)}, bf16[48,7296]{1,0:T(8,128)(2,1)S(1)}, u32[]{:S(2)}) copy-start(bf16[48,7296]{1,0:T(8,128)(2,1)S(1)} %collective-permute-done.6.refs_1_) | copy-start | bytes 2101252
  94.3 1.9 collective-permute-start.9
  94.3 9.6 %collective-permute-start.10 = (bf16[48,3712]{1,0:T(8,128)(2,1)}, bf16[48,3712]{1,0:T(8,128)(2,1)S(1)}, u32[]{:S(2)}, u32[]{:S(2)}) collective-permute-start(bf16[48,3712]{1,0:T(8,128)(2,1)} %get-tuple-element.213), channel_id=1, source_target_pairs={{0,2},{1,3},{2,0},{3,1},{4,6},{5,7},{6,4},{7,5},{8,10},{9,11},{10,... | collective-permute-start | bytes 1069064 | tf_op jit(solution)/shard_map/ppermute | solution.py:282
  104.7 40.9 %collective-permute-start.11 = (bf16[128,7296]{1,0:T(8,128)(2,1)S(1)}, bf16[128,7296]{1,0:T(8,128)(2,1)S(1)}, u32[]{:S(2)}, u32[]{:S(2)}) collective-permute-start(bf16[128,7296]{1,0:T(8,128)(2,1)S(1)} %copy-done.1), channel_id=1, source_target_pairs={{0,4},{1,5},{2,6},{3,7},{12,8},{13,9},{14,10},{15,11},{4,12},{5,13... | collective-permute-start | bytes 5603336 | tf_op jit(solution)/shard_map/ppermute | solution.py:282
  104.7 22.9 %collective-permute-start.12 = (bf16[48,7296]{1,0:T(8,128)(2,1)}, bf16[48,7296]{1,0:T(8,128)(2,1)S(1)}, u32[]{:S(2)}, u32[]{:S(2)}) collective-permute-start(bf16[48,7296]{1,0:T(8,128)(2,1)} %get-tuple-element.235), channel_id=1, source_target_pairs={{0,1},{1,0},{2,3},{3,2},{4,5},{5,4},{6,7},{7,6},{8,9},{9,8},{10,11... | collective-permute-start | bytes 2101256 | tf_op jit(solution)/shard_map/ppermute | solution.py:282
  106.0 21.5 %collective-permute-start.13 = (bf16[48,7296]{1,0:T(8,128)(2,1)}, bf16[48,7296]{1,0:T(8,128)(2,1)S(1)}, u32[]{:S(2)}, u32[]{:S(2)}) collective-permute-start(bf16[48,7296]{1,0:T(8,128)(2,1)} %get-tuple-element.236), channel_id=1, source_target_pairs={{0,2},{1,3},{2,0},{3,1},{4,6},{5,7},{6,4},{7,5},{8,10},{9,11},{10,... | collective-permute-start | bytes 2101256 | tf_op jit(solution)/shard_map/ppermute | solution.py:282
  106.3 44.7 %collective-permute-start.17 = (bf16[48,7296]{1,0:T(8,128)(2,1)}, bf16[48,7296]{1,0:T(8,128)(2,1)S(1)}, u32[]{:S(2)}, u32[]{:S(2)}) collective-permute-start(bf16[48,7296]{1,0:T(8,128)(2,1)} %get-tuple-element.244), channel_id=1, source_target_pairs={{0,3},{1,2},{2,1},{3,0},{4,7},{5,6},{6,5},{7,4},{8,11},{9,10},{10,... | collective-permute-start | bytes 2101256 | tf_op jit(solution)/shard_map/ppermute | solution.py:282
  127.5 32.5 %copy-start.7 = (bf16[48,7296]{1,0:T(8,128)(2,1)}, bf16[48,7296]{1,0:T(8,128)(2,1)S(1)}, u32[]{:S(2)}) copy-start(bf16[48,7296]{1,0:T(8,128)(2,1)S(1)} %collective-permute-done.12.refs_1_) | copy-start | bytes 2101252
  127.5 32.5 %copy-start.9 = (bf16[48,7296]{1,0:T(8,128)(2,1)}, bf16[48,7296]{1,0:T(8,128)(2,1)S(1)}, u32[]{:S(2)}) copy-start(bf16[48,7296]{1,0:T(8,128)(2,1)S(1)} %collective-permute-done.13.refs_2_) | copy-start | bytes 2101252
  127.6 23.4 %collective-permute-start.14 = (bf16[48,3712]{1,0:T(8,128)(2,1)}, bf16[48,3712]{1,0:T(8,128)(2,1)S(1)}, u32[]{:S(2)}, u32[]{:S(2)}) collective-permute-start(bf16[48,3712]{1,0:T(8,128)(2,1)} %get-tuple-element.238), channel_id=1, source_target_pairs={{0,1},{1,0},{2,3},{3,2},{4,5},{5,4},{6,7},{7,6},{8,9},{9,8},{10,11... | collective-permute-start | bytes 1069064 | tf_op jit(solution)/shard_map/ppermute | solution.py:282
  127.8 23.2 %collective-permute-start.15 = (bf16[48,3712]{1,0:T(8,128)(2,1)}, bf16[48,3712]{1,0:T(8,128)(2,1)S(1)}, u32[]{:S(2)}, u32[]{:S(2)}) collective-permute-start(bf16[48,3712]{1,0:T(8,128)(2,1)} %get-tuple-element.239), channel_id=1, source_target_pairs={{0,2},{1,3},{2,0},{3,1},{4,6},{5,7},{6,4},{7,5},{8,10},{9,11},{10,... | collective-permute-start | bytes 1069064 | tf_op jit(solution)/shard_map/ppermute | solution.py:282
  128.0 25.9 %collective-permute-start.16 = (bf16[48,3712]{1,0:T(8,128)(2,1)}, bf16[48,3712]{1,0:T(8,128)(2,1)S(1)}, u32[]{:S(2)}, u32[]{:S(2)}) collective-permute-start(bf16[48,3712]{1,0:T(8,128)(2,1)} %get-tuple-element.240), channel_id=1, source_target_pairs={{0,3},{1,2},{2,1},{3,0},{4,7},{5,6},{6,5},{7,4},{8,11},{9,10},{10,... | collective-permute-start | bytes 1069064 | tf_op jit(solution)/shard_map/ppermute | solution.py:282
  153.9 25.9 %collective-permute-start.18 = (bf16[48,7296]{1,0:T(8,128)(2,1)}, bf16[48,7296]{1,0:T(8,128)(2,1)S(1)}, u32[]{:S(2)}, u32[]{:S(2)}) collective-permute-start(bf16[48,7296]{1,0:T(8,128)(2,1)} %get-tuple-element.262), channel_id=1, source_target_pairs={{0,1},{1,0},{2,3},{3,2},{4,5},{5,4},{6,7},{7,6},{8,9},{9,8},{10,11... | collective-permute-start | bytes 2101256 | tf_op jit(solution)/shard_map/ppermute | solution.py:282
  154.2 25.6 %collective-permute-start.19 = (bf16[48,7296]{1,0:T(8,128)(2,1)}, bf16[48,7296]{1,0:T(8,128)(2,1)S(1)}, u32[]{:S(2)}, u32[]{:S(2)}) collective-permute-start(bf16[48,7296]{1,0:T(8,128)(2,1)} %get-tuple-element.263), channel_id=1, source_target_pairs={{0,2},{1,3},{2,0},{3,1},{4,6},{5,7},{6,4},{7,5},{8,10},{9,11},{10,... | collective-permute-start | bytes 2101256 | tf_op jit(solution)/shard_map/ppermute | solution.py:282
  154.4 33.1 %collective-permute-start.20 = (bf16[48,7296]{1,0:T(8,128)(2,1)}, bf16[48,7296]{1,0:T(8,128)(2,1)S(1)}, u32[]{:S(2)}, u32[]{:S(2)}) collective-permute-start(bf16[48,7296]{1,0:T(8,128)(2,1)} %get-tuple-element.267), channel_id=1, source_target_pairs={{0,3},{1,2},{2,1},{3,0},{4,7},{5,6},{6,5},{7,4},{8,11},{9,10},{10,... | collective-permute-start | bytes 2101256 | tf_op jit(solution)/shard_map/ppermute | solution.py:282
  158.8 46.7 %copy-start.35 = (bf16[48,3712]{1,0:T(8,128)(2,1)S(1)}, bf16[48,3712]{1,0:T(8,128)(2,1)}, u32[]{:S(2)}) copy-start(bf16[48,3712]{1,0:T(8,128)(2,1)} %get-tuple-element.305) | copy-start | bytes 1069060
  158.8 68.4 %collective-permute-start.24 = (bf16[128,3712]{1,0:T(8,128)(2,1)}, bf16[128,3712]{1,0:T(8,128)(2,1)S(1)}, u32[]{:S(2)}, u32[]{:S(2)}) collective-permute-start(bf16[128,3712]{1,0:T(8,128)(2,1)} %shard_map.161), channel_id=1, source_target_pairs={{0,4},{1,5},{2,6},{3,7},{12,8},{13,9},{14,10},{15,11},{4,12},{5,13... | collective-permute-start | bytes 2850824 | tf_op jit(solution)/shard_map/ppermute | solution.py:282
  179.8 27.6 %copy-start.8 = (bf16[48,7296]{1,0:T(8,128)(2,1)}, bf16[48,7296]{1,0:T(8,128)(2,1)S(1)}, u32[]{:S(2)}) copy-start(bf16[48,7296]{1,0:T(8,128)(2,1)S(1)} %collective-permute-done.18.refs_1_) | copy-start | bytes 2101252
  179.8 27.6 %copy-start.10 = (bf16[48,7296]{1,0:T(8,128)(2,1)}, bf16[48,7296]{1,0:T(8,128)(2,1)S(1)}, u32[]{:S(2)}) copy-start(bf16[48,7296]{1,0:T(8,128)(2,1)S(1)} %collective-permute-done.19.refs_2_) | copy-start | bytes 2101252
  179.8 7.7 %collective-permute-start.21 = (bf16[48,3712]{1,0:T(8,128)(2,1)}, bf16[48,3712]{1,0:T(8,128)(2,1)S(1)}, u32[]{:S(2)}, u32[]{:S(2)}) collective-permute-start(bf16[48,3712]{1,0:T(8,128)(2,1)} %get-tuple-element.274), channel_id=1, source_target_pairs={{0,1},{1,0},{2,3},{3,2},{4,5},{5,4},{6,7},{7,6},{8,9},{9,8},{10,11... | collective-permute-start | bytes 1069064 | tf_op jit(solution)/shard_map/ppermute | solution.py:282
  180.2 13.9 %collective-permute-start.22 = (bf16[48,3712]{1,0:T(8,128)(2,1)}, bf16[48,3712]{1,0:T(8,128)(2,1)S(1)}, u32[]{:S(2)}, u32[]{:S(2)}) collective-permute-start(bf16[48,3712]{1,0:T(8,128)(2,1)} %get-tuple-element.275), channel_id=1, source_target_pairs={{0,2},{1,3},{2,0},{3,1},{4,6},{5,7},{6,4},{7,5},{8,10},{9,11},{10,... | collective-permute-start | bytes 1069064 | tf_op jit(solution)/shard_map/ppermute | solution.py:282
  180.4 21.7 %collective-permute-start.23 = (bf16[48,3712]{1,0:T(8,128)(2,1)}, bf16[48,3712]{1,0:T(8,128)(2,1)S(1)}, u32[]{:S(2)}, u32[]{:S(2)}) collective-permute-start(bf16[48,3712]{1,0:T(8,128)(2,1)} %get-tuple-element.276), channel_id=1, source_target_pairs={{0,3},{1,2},{2,1},{3,0},{4,7},{5,6},{6,5},{7,4},{8,11},{9,10},{10,... | collective-permute-start | bytes 1069064 | tf_op jit(solution)/shard_map/ppermute | solution.py:282
  205.6 28.5 %collective-permute-start.25 = (bf16[80,3584]{1,0:T(8,128)(2,1)}, bf16[80,3584]{1,0:T(8,128)(2,1)S(1)}, u32[]{:S(2)}, u32[]{:S(2)}) collective-permute-start(bf16[80,3584]{1,0:T(8,128)(2,1)} %get-tuple-element.299), channel_id=1, source_target_pairs={{0,12},{1,13},{2,14},{3,15},{4,8},{5,9},{6,10},{7,11},{8,4},{9,5},... | collective-permute-start | bytes 1720328 | tf_op jit(solution)/shard_map/ppermute | solution.py:282
  205.6 28.5 %collective-permute-start.27 = (bf16[48,3712]{1,0:T(8,128)(2,1)S(1)}, bf16[48,3712]{1,0:T(8,128)(2,1)S(1)}, u32[]{:S(2)}, u32[]{:S(2)}) collective-permute-start(bf16[48,3712]{1,0:T(8,128)(2,1)S(1)} %copy-done.35), channel_id=1, source_target_pairs={{0,3},{1,2},{2,1},{3,0},{4,7},{5,6},{6,5},{7,4},{8,11},{9,10},{10,... | collective-permute-start | bytes 1069064 | tf_op jit(solution)/shard_map/ppermute | solution.py:282
  205.7 30.9 %copy-start.36 = (bf16[48,3584]{1,0:T(8,128)(2,1)S(1)}, bf16[48,3584]{1,0:T(8,128)(2,1)}, u32[]{:S(2)}) copy-start(bf16[48,3584]{1,0:T(8,128)(2,1)} %get-tuple-element.314) | copy-start | bytes 1032196
  205.7 28.4 %collective-permute-start.26 = (bf16[128,128]{1,0:T(8,128)(2,1)}, bf16[128,128]{1,0:T(8,128)(2,1)S(1)}, u32[]{:S(2)}, u32[]{:S(2)}) collective-permute-start(bf16[128,128]{1,0:T(8,128)(2,1)} %get-tuple-element.300), channel_id=1, source_target_pairs={{0,12},{1,13},{2,14},{3,15},{4,8},{5,9},{6,10},{7,11},{8,4},{9,5},... | collective-permute-start | bytes 98312 | tf_op jit(solution)/shard_map/ppermute | solution.py:282
  227.2 33.1 %copy-start.33 = (f32[128,16]{1,0:T(8,128)S(1)}, f32[128,16]{1,0:T(8,128)}, u32[]{:S(2)}) copy-start(f32[128,16]{1,0:T(8,128)} %copy-done.32) | copy-start | bytes 24580
  227.2 34.0 %copy-start.34 = (f32[128,16]{1,0:T(8,128)S(1)}, f32[128,16]{1,0:T(8,128)}, u32[]{:S(2)}) copy-start(f32[128,16]{1,0:T(8,128)} %get-tuple-element.338) | copy-start | bytes 24580
  227.2 35.2 %copy-start.5 = (bf16[128,3712]{1,0:T(8,128)(2,1)}, bf16[128,3712]{1,0:T(8,128)(2,1)S(1)}, u32[]{:S(2)}) copy-start(bf16[128,3712]{1,0:T(8,128)(2,1)S(1)} %collective-permute-done.24.refs_1_) | copy-start | bytes 2850820
  234.1 23.4 %copy-start.23 = (bf16[48,3712]{1,0:T(8,128)(2,1)}, bf16[48,3712]{1,0:T(8,128)(2,1)S(1)}, u32[]{:S(2)}) copy-start(bf16[48,3712]{1,0:T(8,128)(2,1)S(1)} %collective-permute-done.27.refs_3_) | copy-start | bytes 1069060
  234.1 17.1 %collective-permute-start.28 = (bf16[48,3712]{1,0:T(8,128)(2,1)}, bf16[48,3712]{1,0:T(8,128)(2,1)S(1)}, u32[]{:S(2)}, u32[]{:S(2)}) collective-permute-start(bf16[48,3712]{1,0:T(8,128)(2,1)} %get-tuple-element.307), channel_id=1, source_target_pairs={{0,1},{1,0},{2,3},{3,2},{4,5},{5,4},{6,7},{7,6},{8,9},{9,8},{10,11... | collective-permute-start | bytes 1069064 | tf_op jit(solution)/shard_map/ppermute | solution.py:282
  234.9 16.2 %collective-permute-start.29 = (bf16[48,3712]{1,0:T(8,128)(2,1)}, bf16[48,3712]{1,0:T(8,128)(2,1)S(1)}, u32[]{:S(2)}, u32[]{:S(2)}) collective-permute-start(bf16[48,3712]{1,0:T(8,128)(2,1)} %get-tuple-element.308), channel_id=1, source_target_pairs={{0,2},{1,3},{2,0},{3,1},{4,6},{5,7},{6,4},{7,5},{8,10},{9,11},{10,... | collective-permute-start | bytes 1069064 | tf_op jit(solution)/shard_map/ppermute | solution.py:282
  235.2 17.7 %collective-permute-start.30 = (bf16[48,3712]{1,0:T(8,128)(2,1)}, bf16[48,3712]{1,0:T(8,128)(2,1)S(1)}, u32[]{:S(2)}, u32[]{:S(2)}) collective-permute-start(bf16[48,3712]{1,0:T(8,128)(2,1)} %get-tuple-element.309), channel_id=1, source_target_pairs={{0,3},{1,2},{2,1},{3,0},{4,7},{5,6},{6,5},{7,4},{8,11},{9,10},{10,... | collective-permute-start | bytes 1069064 | tf_op jit(solution)/shard_map/ppermute | solution.py:282
  236.7 14.5 %collective-permute-start.31 = (bf16[48,3584]{1,0:T(8,128)(2,1)S(1)}, bf16[48,3584]{1,0:T(8,128)(2,1)S(1)}, u32[]{:S(2)}, u32[]{:S(2)}) collective-permute-start(bf16[48,3584]{1,0:T(8,128)(2,1)S(1)} %copy-done.36), channel_id=1, source_target_pairs={{0,12},{1,13},{2,14},{3,15},{4,8},{5,9},{6,10},{7,11},{8,4},{9,5},... | collective-permute-start | bytes 1032200 | tf_op jit(solution)/shard_map/ppermute | solution.py:282
  251.2 35.5 %copy-start.30 = (bf16[48,3584]{1,0:T(8,128)(2,1)}, bf16[48,3584]{1,0:T(8,128)(2,1)S(1)}, u32[]{:S(2)}) copy-start(bf16[48,3584]{1,0:T(8,128)(2,1)S(1)} %collective-permute-done.31.refs_3_) | copy-start | bytes 1032196
  256.3 4.0 %collective-permute-start.32 = (bf16[128,128]{1,0:T(8,128)(2,1)}, bf16[128,128]{1,0:T(8,128)(2,1)S(1)}, u32[]{:S(2)}, u32[]{:S(2)}) collective-permute-start(bf16[128,128]{1,0:T(8,128)(2,1)} %get-tuple-element.327), channel_id=1, source_target_pairs={{4,0},{5,1},{6,2},{7,3},{8,12},{9,13},{10,14},{11,15},{12,4},{13,5... | collective-permute-start | bytes 98312 | tf_op jit(solution)/shard_map/ppermute | solution.py:282
  256.3 30.4 %collective-permute-start.33 = (bf16[128,3584]{1,0:T(8,128)(2,1)}, bf16[128,3584]{1,0:T(8,128)(2,1)S(1)}, u32[]{:S(2)}, u32[]{:S(2)}) collective-permute-start(bf16[128,3584]{1,0:T(8,128)(2,1)} %get-tuple-element.331), channel_id=1, source_target_pairs={{4,0},{5,1},{6,2},{7,3},{8,12},{9,13},{10,14},{11,15},{12,4},{13,5... | collective-permute-start | bytes 2752520 | tf_op jit(solution)/shard_map/ppermute | solution.py:282
  262.1 24.5 %copy-start.31 = (bf16[128,16]{1,0:T(8,128)(2,1)}, bf16[128,16]{1,0:T(8,128)(2,1)S(1)}, u32[]{:S(2)}) copy-start(bf16[128,16]{1,0:T(8,128)(2,1)S(1)} %multiply_convert_fusion.logit_ref) | copy-start | bytes 12292
  (23 other events, 143.3 us)

commit v8 on v7

--- a/solution.py
+++ b/solution.py
@@ -365,10 +365,8 @@
             got_1 = spread(sel_1)
             done_0 = run(got_0)
             got_1, done_0, own = join((got_1, done_0, own))
-            back_0 = [done_0[0], send(done_0[1], across(1)), send(done_0[2], across(2))]
-            block_2f, block_2m, own, back_0[1] = join((block_2f, block_2m, own, back_0[1]))
             sel_2, placed_2 = take(flag, [block_2m, block_2f])
-            sel_2, got_1, own, back_0[2] = join((sel_2, got_1, own, back_0[2]))
+            sel_2, got_1, own = join((sel_2, got_1, own))
             block_3 = send(own, along([(0, 1), (3, 2), (1, 3), (2, 0)]))
             got_2 = spread(sel_2)
             done_1 = run(got_1, done_0[plane:])
@@ -378,18 +376,18 @@
             sel_3, back_1, got_2 = join((sel_3, back_1, got_2))
             got_3 = spread(sel_3)
             done_2 = run(got_2, done_1[plane:])
-            done_2, got_3[1], got_3[2], last_0 = join((done_2, got_3[1], got_3[2], done_0[3]))
+            done_2, got_3[1], got_3[2], done_0 = join((done_2, got_3[1], got_3[2], done_0))
             back_2 = spread(done_2[:plane])
             (part_1,) = sum_rows(placed_1, back_1, wide)
             term_1 = send(part_1, along([(0, 1), (3, 2), (1, 3), (2, 0)]))
-            got_3, part_1, back_2, last_0 = join((got_3, part_1, back_2, last_0))
+            got_3, part_1, back_2, done_0 = join((got_3, part_1, back_2, done_0))
             part_2a, part_2b, tag_2 = sum_rows(placed_2, back_2, width, (tok * 5 // 8, tok * 3 // 8))
             tag_2 = send(tag_2, across(3 * plane))
             term_2a = send(part_2a, across(3 * plane))
-            back_0.append(send(last_0, across(3)))
+            back_0 = spread(done_0[:plane])
             done_3 = run(got_3, done_2[plane:])
-            done_3, term_1, term_2a, tag_2, part_2b, back_0 = join(
-                (done_3, term_1, term_2a, tag_2, part_2b, back_0)
+            done_3, term_1, term_2a, part_2b, back_0 = join(
+                (done_3, term_1, term_2a, part_2b, back_0)
             )
             back_3 = spread(done_3[:plane])
             term_2b = send(part_2b, across(3 * plane))

time: 294 us -> 289 us (0.983)
  waiting for transfers between devices: 112 us -> 104 us
  starting transfers between devices: 28.5 us -> 32.8 us
    ppermute x34, waiting for transfers between devices: 112 us -> 104 us  [send(): return lax.ppermute(array, 'expert', pairs)]
    ppermute x34, starting transfers between devices: 28.5 us -> 32.8 us  [send(): return lax.ppermute(array, 'expert', pairs)]
    unnamed x74 -> x78, local copies, waits for them, and re-layouts: 6.49 us -> 5.72 us
  transfers between devices with their start and end apart: 34 -> 34, of which waited for: 15 -> 13; matrix products, arithmetic and copies ran while one was open for 2% -> 2% of each run, Pallas kernels for 36% -> 36%
where the time goes in v8:
time: 289 us; the launch traced here: 286 us
  Pallas kernels  110 us (38%)
  waiting for transfers between devices  104 us (36%)
  starting transfers between devices  32.8 us (11%)
  blocking collectives  22.3 us (8%)
  local copies, waits for them, and re-layouts  8.42 us (3%)
  other arithmetic  4.77 us (2%)
    ppermute x34, waiting for transfers between devices, send(): return lax.ppermute(array, 'expert', pairs)  104 us
    pallas_call x4, Pallas kernels, expert_rows(): pl.pallas_call(functools.partial(expert_kernel, len(carry), cap, width, r...  78.7 us
    ppermute x34, starting transfers between devices, send(): return lax.ppermute(array, 'expert', pairs)  32.8 us
    all_to_all x1, blocking collectives, shards(): lax.all_to_all(router_part, 'expert', split_axis=0, concat_axis=0, tiled=...  22.3 us
    pallas_call x4, Pallas kernels, select_rows(): pl.pallas_call(functools.partial(select_kernel, parts, meta_at, slots_hel...  17 us
    pallas_call x4, Pallas kernels, sum_rows(): pl.pallas_call(functools.partial(sum_kernel, apart), out_shape=shapes, in...  10.9 us
  transfers between devices with their start and end apart: 34, of which 13 were waited for; matrix products, arithmetic and copies ran while one was open for 2% of the time, Pallas kernels for 36%

profile of v8, /device:TPU:15, one launch (start us, length us, event | category | flops | bytes accessed | tf_op | source)
XLA Modules:
  0.0 286.3 jit_solution(7269972131165027348)
XLA Ops:
  1.7 2.2 fusion.6
  4.5 2.2 concatenate.5.refs_0_
  8.0 4.1 %shard_map.154 = (bf16[48,7296]{1,0:T(8,128)(2,1)}, bf16[48,7296]{1,0:T(8,128)(2,1)}, bf16[48,7296]{1,0:T(8,128)(2,1)}, bf16[48,7296]{1,0:T(8,128)(2,1)}, bf16[192,128]{1,0:T(8,128)(2,1)}) custom-call(s32[1]{0:T(128)} %bitcast.flag_ref, bf16[16,128]{1,0:T(8,128)(2,1)} %pad_convert_fusion.guide_ref, bf16[128,7296]{1,0:T(8,128)(2,1)} %copy-done), custom_call_target="tpu_custom_call" | custom-call | flops 1024 | bytes 1024 | tf_op jit(solution)/shard_map/pallas_call | solution.py:87
  13.0 1.4 collective-permute-start.3
  14.8 15.6 %collective-permute-done.2.refs_2_ = bf16[48,7296]{1,0:T(8,128)(2,1)S(1)} collective-permute-done((bf16[48,7296]{1,0:T(8,128)(2,1)}, bf16[48,7296]{1,0:T(8,128)(2,1)S(1)}, u32[]{:S(2)}, u32[]{:S(2)}) %collective-permute-start.2) | collective-permute-done | bytes 700448 | tf_op jit(solution)/shard_map/ppermute | solution.py:282
  30.5 15.4 %collective-permute-done.3.refs_3_ = bf16[48,7296]{1,0:T(8,128)(2,1)S(1)} collective-permute-done((bf16[48,7296]{1,0:T(8,128)(2,1)}, bf16[48,7296]{1,0:T(8,128)(2,1)S(1)}, u32[]{:S(2)}, u32[]{:S(2)}) %collective-permute-start.3) | collective-permute-done | bytes 700448 | tf_op jit(solution)/shard_map/ppermute | solution.py:282
  45.9 3.5 %collective-permute-done.refs_0_ = bf16[128,7296]{1,0:T(8,128)(2,1)} collective-permute-done((bf16[128,7296]{1,0:T(8,128)(2,1)S(1)}, bf16[128,7296]{1,0:T(8,128)(2,1)}, u32[]{:S(2)}, u32[]{:S(2)}) %collective-permute-start) | collective-permute-done | bytes 1867808 | tf_op jit(solution)/shard_map/ppermute | solution.py:282
  49.4 3.2 %collective-permute-start.4 = (bf16[128,7296]{1,0:T(8,128)(2,1)}, bf16[128,7296]{1,0:T(8,128)(2,1)S(1)}, u32[]{:S(2)}, u32[]{:S(2)}) collective-permute-start(bf16[128,7296]{1,0:T(8,128)(2,1)} %copy-done), channel_id=1, source_target_pairs={{4,8},{5,9},{6,10},{7,11},{8,4},{9,5},{10,6},{11,7},{20,24},{21,25... | collective-permute-start | bytes 5603336 | tf_op jit(solution)/shard_map/ppermute | solution.py:282
  52.6 2.6 collective-permute-start.5
  55.2 4.1 %shard_map.156 = (bf16[48,7296]{1,0:T(8,128)(2,1)}, bf16[48,7296]{1,0:T(8,128)(2,1)}, bf16[48,7296]{1,0:T(8,128)(2,1)}, bf16[48,7296]{1,0:T(8,128)(2,1)}, bf16[192,128]{1,0:T(8,128)(2,1)}) custom-call(s32[1]{0:T(128)} %bitcast.flag_ref, bf16[16,128]{1,0:T(8,128)(2,1)} %pad_convert_fusion.guide_ref, bf16[128,7296]{1,0:T(8,128)(2,1)} %collective-permute-done.refs_0_), custom_call_target="tpu_custom_call" | custom-call | flops 1024 | bytes 1024 | tf_op jit(solution)/shard_map/pallas_call | solution.py:87
  59.4 1.8 collective-permute-start.6
  61.4 1.4 collective-permute-start.8
  63.3 19.4 %shard_map.157 = (bf16[48,3712]{1,0:T(8,128)(2,1)}, bf16[48,3712]{1,0:T(8,128)(2,1)}, bf16[48,3712]{1,0:T(8,128)(2,1)}, bf16[48,3712]{1,0:T(8,128)(2,1)}, f32[32...) custom-call(f32[1,128]{1,0:T(1,128)} %compare_convert_fusion.mine_ref, ...), custom_call_target="tpu_custom_call" | custom-call | flops 1024 | bytes 1024 | tf_op jit(solution)/shard_map/pallas_call | solution.py:233
  82.7 11.4 %collective-permute-done.8.refs_3_ = bf16[48,7296]{1,0:T(8,128)(2,1)} collective-permute-done((bf16[48,7296]{1,0:T(8,128)(2,1)}, bf16[48,7296]{1,0:T(8,128)(2,1)}, u32[]{:S(2)}, u32[]{:S(2)}) %collective-permute-start.8) | collective-permute-done | bytes 700448 | tf_op jit(solution)/shard_map/ppermute | solution.py:282
  94.1 1.3 copy-done.3
  95.4 4.7 %shard_map.155 = (bf16[48,7296]{1,0:T(8,128)(2,1)}, bf16[48,7296]{1,0:T(8,128)(2,1)}, bf16[48,7296]{1,0:T(8,128)(2,1)}, bf16[48,7296]{1,0:T(8,128)(2,1)}, bf16[192,128]{1,0:T(8,128)(2,1)}) custom-call(s32[1]{0:T(128)} %bitcast.flag_ref, bf16[16,128]{1,0:T(8,128)(2,1)} %pad_convert_fusion.guide_ref, bf16[128,7296]{1,0:T(8,128)(2,1)} %copy-done.3, ...), custom_call_target="tpu_custom_call" | custom-call | flops 1024 | bytes 1024 | tf_op jit(solution)/shard_map/pallas_call | solution.py:87
  100.1 2.1 collective-permute-start.10
  102.4 1.4 collective-permute-start.15
  103.8 19.8 %shard_map.159 = (bf16[48,3712]{1,0:T(8,128)(2,1)}, bf16[48,3712]{1,0:T(8,128)(2,1)}, bf16[48,3712]{1,0:T(8,128)(2,1)}, bf16[48,3712]{1,0:T(8,128)(2,1)}, f32[32...) custom-call(f32[1,128]{1,0:T(1,128)} %compare_convert_fusion.mine_ref, ...), custom_call_target="tpu_custom_call" | custom-call | flops 1024 | bytes 1024 | tf_op jit(solution)/shard_map/pallas_call | solution.py:233
  124.1 1.7 collective-permute-start.14
  125.8 16.1 %collective-permute-done.9.refs_0_ = bf16[128,7296]{1,0:T(8,128)(2,1)S(1)} collective-permute-done((bf16[128,7296]{1,0:T(8,128)(2,1)S(1)}, bf16[128,7296]{1,0:T(8,128)(2,1)S(1)}, u32[]{:S(2)}, u32[]{:S(2)}) %collective-permute-start.9) | collective-permute-done | bytes 1867808 | tf_op jit(solution)/shard_map/ppermute | solution.py:282
  141.9 1.3 copy-done.4
  143.2 4.1 %shard_map.158 = (bf16[48,7296]{1,0:T(8,128)(2,1)}, bf16[48,7296]{1,0:T(8,128)(2,1)}, bf16[48,7296]{1,0:T(8,128)(2,1)}, bf16[48,7296]{1,0:T(8,128)(2,1)}, bf16[192,128]{1,0:T(8,128)(2,1)}) custom-call(s32[1]{0:T(128)} %bitcast.flag_ref, bf16[16,128]{1,0:T(8,128)(2,1)} %pad_convert_fusion.guide_ref, bf16[128,7296]{1,0:T(8,128)(2,1)} %copy-done.4), custom_call_target="tpu_custom_call" | custom-call | flops 1024 | bytes 1024 | tf_op jit(solution)/shard_map/pallas_call | solution.py:87
  147.3 2.8 collective-permute-done.14.refs_3_
  150.6 1.6 collective-permute-start.18
  152.2 2.8 shard_map.161
  155.0 1.2 collective-permute-start.22
  156.2 19.8 %shard_map.160 = (bf16[48,3712]{1,0:T(8,128)(2,1)}, bf16[48,3712]{1,0:T(8,128)(2,1)}, bf16[48,3712]{1,0:T(8,128)(2,1)}, bf16[48,3712]{1,0:T(8,128)(2,1)}, f32[32...) custom-call(f32[1,128]{1,0:T(1,128)} %compare_convert_fusion.mine_ref, ...), custom_call_target="tpu_custom_call" | custom-call | flops 1024 | bytes 1024 | tf_op jit(solution)/shard_map/pallas_call | solution.py:233
  176.6 1.6 collective-permute-start.21
  178.2 5.5 %collective-permute-done.18.refs_3_ = bf16[48,7296]{1,0:T(8,128)(2,1)S(1)} collective-permute-done((bf16[48,7296]{1,0:T(8,128)(2,1)}, bf16[48,7296]{1,0:T(8,128)(2,1)S(1)}, u32[]{:S(2)}, u32[]{:S(2)}) %collective-permute-start.18) | collective-permute-done | bytes 700448 | tf_op jit(solution)/shard_map/ppermute | solution.py:282
  183.7 6.7 %collective-permute-done.20.refs_2_ = bf16[48,3712]{1,0:T(8,128)(2,1)S(1)} collective-permute-done((bf16[48,3712]{1,0:T(8,128)(2,1)}, bf16[48,3712]{1,0:T(8,128)(2,1)S(1)}, u32[]{:S(2)}, u32[]{:S(2)}) %collective-permute-start.20) | collective-permute-done | bytes 356384 | tf_op jit(solution)/shard_map/ppermute | solution.py:282
  190.4 8.0 %collective-permute-done.21.refs_3_ = bf16[48,3712]{1,0:T(8,128)(2,1)S(1)} collective-permute-done((bf16[48,3712]{1,0:T(8,128)(2,1)}, bf16[48,3712]{1,0:T(8,128)(2,1)S(1)}, u32[]{:S(2)}, u32[]{:S(2)}) %collective-permute-start.21) | collective-permute-done | bytes 356384 | tf_op jit(solution)/shard_map/ppermute | solution.py:282
  199.1 2.7 shard_map.163
  201.8 1.3 collective-permute-start.23
  203.6 1.6 collective-permute-start.26
  205.2 19.8 %shard_map.162 = (bf16[48,3712]{1,0:T(8,128)(2,1)}, bf16[48,3712]{1,0:T(8,128)(2,1)}, bf16[48,3712]{1,0:T(8,128)(2,1)}, bf16[48,3712]{1,0:T(8,128)(2,1)}, f32[32...) custom-call(f32[1,128]{1,0:T(1,128)} %compare_convert_fusion.mine_ref, ...), custom_call_target="tpu_custom_call" | custom-call | flops 1024 | bytes 1024 | tf_op jit(solution)/shard_map/pallas_call | solution.py:233
  225.1 3.7 %collective-permute-done.23.refs_2_ = bf16[80,3584]{1,0:T(8,128)(2,1)S(1)} collective-permute-done((bf16[80,3584]{1,0:T(8,128)(2,1)}, bf16[80,3584]{1,0:T(8,128)(2,1)S(1)}, u32[]{:S(2)}, u32[]{:S(2)}) %collective-permute-start.23) | collective-permute-done | bytes 573472 | tf_op jit(solution)/shard_map/ppermute | solution.py:282
  229.9 1.4 collective-permute-start.29
  231.3 1.3 collective-permute-start.30
  232.8 14.3 %collective-permute-done.30.refs_3_ = bf16[48,3584]{1,0:T(8,128)(2,1)S(1)} collective-permute-done((bf16[48,3584]{1,0:T(8,128)(2,1)S(1)}, bf16[48,3584]{1,0:T(8,128)(2,1)S(1)}, u32[]{:S(2)}, u32[]{:S(2)}) %collective-permute-start.30) | collective-permute-done | bytes 344096 | tf_op jit(solution)/shard_map/ppermute | solution.py:282
  248.6 2.7 shard_map.165
  251.3 2.2 collective-permute-start.33
  253.5 2.7 shard_map.164
  256.2 0.9 multiply_reduce_fusion
  257.2 0.9 multiply_convert_fusion.logit_ref
  258.7 22.3 %all_to_all.5 = f32[16,16,224]{2,1,0:T(8,128)S(1)} all-to-all(f32[16,16,224]{2,1,0:T(8,128)S(1)} %bitcast.57), channel_id=1, replica_groups=mesh['groups'=2,'expert'=16] {'expert'}, dimensions={0} | all-to-all | bytes 458752 | tf_op jit(solution)/shard_map/all_to_all | solution.py:423
  281.7 0.9 copy-done.6
  282.6 3.7 %shard_map.166 = bf16[128,3584]{1,0:T(8,128)(2,1)} custom-call(bf16[128,16]{1,0:T(8,128)(2,1)} %copy-done.31, bf16[16,3584]{1,0:T(8,128)(2,1)} %bitcast.58, bf16[128,3584]{1,0:T(8,128)(2,1)} %get-tuple-element.328.refs_0_, bf16[128,3712]{1,0:T(8,128)(2,1)} %copy-done.5, bf16[80,3584]{1,0:T(8,128)(2,1)} %copy-done.17, bf16[48,3584]{1,0:T(8,128)(2,1)} %copy-done.30, ...), custom_call_target="tpu_custom_call" | custom-call | flops 1024 | bytes 1024 | tf_op jit(solution)/shard_map/pallas_call | solution.py:146
  (130 shorter events, 12.2 us)
Async XLA Ops:
  6.7 42.6 %collective-permute-start = (bf16[128,7296]{1,0:T(8,128)(2,1)S(1)}, bf16[128,7296]{1,0:T(8,128)(2,1)}, u32[]{:S(2)}, u32[]{:S(2)}) collective-permute-start(bf16[128,7296]{1,0:T(8,128)(2,1)S(1)} %concatenate.5.refs_0_), channel_id=1, source_target_pairs={{0,8},{1,9},{2,10},{3,11},{12,4},{13,5},{14,6},{15,7},{4,0},{5,1},... | collective-permute-start | bytes 5603336 | tf_op jit(solution)/shard_map/ppermute | solution.py:282
  12.1 2.7 collective-permute-start.1
  12.8 17.6 %collective-permute-start.2 = (bf16[48,7296]{1,0:T(8,128)(2,1)}, bf16[48,7296]{1,0:T(8,128)(2,1)S(1)}, u32[]{:S(2)}, u32[]{:S(2)}) collective-permute-start(bf16[48,7296]{1,0:T(8,128)(2,1)} %get-tuple-element.180), channel_id=1, source_target_pairs={{0,2},{1,3},{2,0},{3,1},{4,6},{5,7},{6,4},{7,5},{8,10},{9,11},{10,... | collective-permute-start | bytes 2101256 | tf_op jit(solution)/shard_map/ppermute | solution.py:282
  13.0 32.8 %collective-permute-start.3 = (bf16[48,7296]{1,0:T(8,128)(2,1)}, bf16[48,7296]{1,0:T(8,128)(2,1)S(1)}, u32[]{:S(2)}, u32[]{:S(2)}) collective-permute-start(bf16[48,7296]{1,0:T(8,128)(2,1)} %get-tuple-element.181), channel_id=1, source_target_pairs={{0,3},{1,2},{2,1},{3,0},{4,7},{5,6},{6,5},{7,4},{8,11},{9,10},{10,... | collective-permute-start | bytes 2101256 | tf_op jit(solution)/shard_map/ppermute | solution.py:282
  14.8 34.6 %copy-start.14 = (bf16[48,7296]{1,0:T(8,128)(2,1)}, bf16[48,7296]{1,0:T(8,128)(2,1)S(1)}, u32[]{:S(2)}) copy-start(bf16[48,7296]{1,0:T(8,128)(2,1)S(1)} %collective-permute-done.1.refs_1_) | copy-start | bytes 2101252
  49.4 44.7 %collective-permute-start.4 = (bf16[128,7296]{1,0:T(8,128)(2,1)}, bf16[128,7296]{1,0:T(8,128)(2,1)S(1)}, u32[]{:S(2)}, u32[]{:S(2)}) collective-permute-start(bf16[128,7296]{1,0:T(8,128)(2,1)} %copy-done), channel_id=1, source_target_pairs={{4,8},{5,9},{6,10},{7,11},{8,4},{9,5},{10,6},{11,7},{20,24},{21,25... | collective-permute-start | bytes 5603336 | tf_op jit(solution)/shard_map/ppermute | solution.py:282
  52.6 41.5 %collective-permute-start.5 = (bf16[128,7296]{1,0:T(8,128)(2,1)}, bf16[128,7296]{1,0:T(8,128)(2,1)}, u32[]{:S(2)}, u32[]{:S(2)}) collective-permute-start(bf16[128,7296]{1,0:T(8,128)(2,1)} %collective-permute-done.refs_0_), channel_id=1, source_target_pairs={{4,0},{5,1},{6,2},{7,3},{8,12},{9,13},{10,14},{11,15},{20,16},{21,... | collective-permute-start | bytes 5603336 | tf_op jit(solution)/shard_map/ppermute | solution.py:282
  59.4 23.4 %collective-permute-start.6 = (bf16[48,7296]{1,0:T(8,128)(2,1)}, bf16[48,7296]{1,0:T(8,128)(2,1)S(1)}, u32[]{:S(2)}, u32[]{:S(2)}) collective-permute-start(bf16[48,7296]{1,0:T(8,128)(2,1)} %get-tuple-element.189), channel_id=1, source_target_pairs={{0,1},{1,0},{2,3},{3,2},{4,5},{5,4},{6,7},{7,6},{8,9},{9,8},{10,11... | collective-permute-start | bytes 2101256 | tf_op jit(solution)/shard_map/ppermute | solution.py:282
  61.2 21.5 %collective-permute-start.7 = (bf16[48,7296]{1,0:T(8,128)(2,1)}, bf16[48,7296]{1,0:T(8,128)(2,1)}, u32[]{:S(2)}, u32[]{:S(2)}) collective-permute-start(bf16[48,7296]{1,0:T(8,128)(2,1)} %get-tuple-element.190), channel_id=1, source_target_pairs={{0,2},{1,3},{2,0},{3,1},{4,6},{5,7},{6,4},{7,5},{8,10},{9,11},{10,... | collective-permute-start | bytes 2101256 | tf_op jit(solution)/shard_map/ppermute | solution.py:282
  61.4 32.7 %collective-permute-start.8 = (bf16[48,7296]{1,0:T(8,128)(2,1)}, bf16[48,7296]{1,0:T(8,128)(2,1)}, u32[]{:S(2)}, u32[]{:S(2)}) collective-permute-start(bf16[48,7296]{1,0:T(8,128)(2,1)} %get-tuple-element.191), channel_id=1, source_target_pairs={{0,3},{1,2},{2,1},{3,0},{4,7},{5,6},{6,5},{7,4},{8,11},{9,10},{10,... | collective-permute-start | bytes 2101256 | tf_op jit(solution)/shard_map/ppermute | solution.py:282
  100.1 41.8 %collective-permute-start.9 = (bf16[128,7296]{1,0:T(8,128)(2,1)S(1)}, bf16[128,7296]{1,0:T(8,128)(2,1)S(1)}, u32[]{:S(2)}, u32[]{:S(2)}) collective-permute-start(bf16[128,7296]{1,0:T(8,128)(2,1)S(1)} %copy-done.1), channel_id=1, source_target_pairs={{0,4},{1,5},{2,6},{3,7},{12,8},{13,9},{14,10},{15,11},{4,12},{5,13... | collective-permute-start | bytes 5603336 | tf_op jit(solution)/shard_map/ppermute | solution.py:282
  100.1 23.5 %collective-permute-start.10 = (bf16[48,7296]{1,0:T(8,128)(2,1)}, bf16[48,7296]{1,0:T(8,128)(2,1)S(1)}, u32[]{:S(2)}, u32[]{:S(2)}) collective-permute-start(bf16[48,7296]{1,0:T(8,128)(2,1)} %get-tuple-element.230), channel_id=1, source_target_pairs={{0,1},{1,0},{2,3},{3,2},{4,5},{5,4},{6,7},{7,6},{8,9},{9,8},{10,11... | collective-permute-start | bytes 2101256 | tf_op jit(solution)/shard_map/ppermute | solution.py:282
  102.2 21.4 %collective-permute-start.11 = (bf16[48,7296]{1,0:T(8,128)(2,1)}, bf16[48,7296]{1,0:T(8,128)(2,1)S(1)}, u32[]{:S(2)}, u32[]{:S(2)}) collective-permute-start(bf16[48,7296]{1,0:T(8,128)(2,1)} %get-tuple-element.231), channel_id=1, source_target_pairs={{0,2},{1,3},{2,0},{3,1},{4,6},{5,7},{6,4},{7,5},{8,10},{9,11},{10,... | collective-permute-start | bytes 2101256 | tf_op jit(solution)/shard_map/ppermute | solution.py:282
  102.4 44.9 %collective-permute-start.15 = (bf16[48,7296]{1,0:T(8,128)(2,1)}, bf16[48,7296]{1,0:T(8,128)(2,1)S(1)}, u32[]{:S(2)}, u32[]{:S(2)}) collective-permute-start(bf16[48,7296]{1,0:T(8,128)(2,1)} %get-tuple-element.239), channel_id=1, source_target_pairs={{0,3},{1,2},{2,1},{3,0},{4,7},{5,6},{6,5},{7,4},{8,11},{9,10},{10,... | collective-permute-start | bytes 2101256 | tf_op jit(solution)/shard_map/ppermute | solution.py:282
  123.6 32.6 %copy-start.8 = (bf16[48,7296]{1,0:T(8,128)(2,1)}, bf16[48,7296]{1,0:T(8,128)(2,1)S(1)}, u32[]{:S(2)}) copy-start(bf16[48,7296]{1,0:T(8,128)(2,1)S(1)} %collective-permute-done.10.refs_1_) | copy-start | bytes 2101252
  123.6 32.6 %copy-start.10 = (bf16[48,7296]{1,0:T(8,128)(2,1)}, bf16[48,7296]{1,0:T(8,128)(2,1)S(1)}, u32[]{:S(2)}) copy-start(bf16[48,7296]{1,0:T(8,128)(2,1)S(1)} %collective-permute-done.11.refs_2_) | copy-start | bytes 2101252
  123.6 23.6 %collective-permute-start.12 = (bf16[48,3712]{1,0:T(8,128)(2,1)}, bf16[48,3712]{1,0:T(8,128)(2,1)S(1)}, u32[]{:S(2)}, u32[]{:S(2)}) collective-permute-start(bf16[48,3712]{1,0:T(8,128)(2,1)} %get-tuple-element.233), channel_id=1, source_target_pairs={{0,1},{1,0},{2,3},{3,2},{4,5},{5,4},{6,7},{7,6},{8,9},{9,8},{10,11... | collective-permute-start | bytes 1069064 | tf_op jit(solution)/shard_map/ppermute | solution.py:282
  123.9 23.4 %collective-permute-start.13 = (bf16[48,3712]{1,0:T(8,128)(2,1)}, bf16[48,3712]{1,0:T(8,128)(2,1)S(1)}, u32[]{:S(2)}, u32[]{:S(2)}) collective-permute-start(bf16[48,3712]{1,0:T(8,128)(2,1)} %get-tuple-element.234), channel_id=1, source_target_pairs={{0,2},{1,3},{2,0},{3,1},{4,6},{5,7},{6,4},{7,5},{8,10},{9,11},{10,... | collective-permute-start | bytes 1069064 | tf_op jit(solution)/shard_map/ppermute | solution.py:282
  124.1 25.9 %collective-permute-start.14 = (bf16[48,3712]{1,0:T(8,128)(2,1)}, bf16[48,3712]{1,0:T(8,128)(2,1)S(1)}, u32[]{:S(2)}, u32[]{:S(2)}) collective-permute-start(bf16[48,3712]{1,0:T(8,128)(2,1)} %get-tuple-element.235), channel_id=1, source_target_pairs={{0,3},{1,2},{2,1},{3,0},{4,7},{5,6},{6,5},{7,4},{8,11},{9,10},{10,... | collective-permute-start | bytes 1069064 | tf_op jit(solution)/shard_map/ppermute | solution.py:282
  150.1 25.9 %collective-permute-start.16 = (bf16[48,7296]{1,0:T(8,128)(2,1)}, bf16[48,7296]{1,0:T(8,128)(2,1)S(1)}, u32[]{:S(2)}, u32[]{:S(2)}) collective-permute-start(bf16[48,7296]{1,0:T(8,128)(2,1)} %get-tuple-element.257), channel_id=1, source_target_pairs={{0,1},{1,0},{2,3},{3,2},{4,5},{5,4},{6,7},{7,6},{8,9},{9,8},{10,11... | collective-permute-start | bytes 2101256 | tf_op jit(solution)/shard_map/ppermute | solution.py:282
  150.4 25.6 %collective-permute-start.17 = (bf16[48,7296]{1,0:T(8,128)(2,1)}, bf16[48,7296]{1,0:T(8,128)(2,1)S(1)}, u32[]{:S(2)}, u32[]{:S(2)}) collective-permute-start(bf16[48,7296]{1,0:T(8,128)(2,1)} %get-tuple-element.258), channel_id=1, source_target_pairs={{0,2},{1,3},{2,0},{3,1},{4,6},{5,7},{6,4},{7,5},{8,10},{9,11},{10,... | collective-permute-start | bytes 2101256 | tf_op jit(solution)/shard_map/ppermute | solution.py:282
  150.6 33.0 %collective-permute-start.18 = (bf16[48,7296]{1,0:T(8,128)(2,1)}, bf16[48,7296]{1,0:T(8,128)(2,1)S(1)}, u32[]{:S(2)}, u32[]{:S(2)}) collective-permute-start(bf16[48,7296]{1,0:T(8,128)(2,1)} %get-tuple-element.265), channel_id=1, source_target_pairs={{0,3},{1,2},{2,1},{3,0},{4,7},{5,6},{6,5},{7,4},{8,11},{9,10},{10,... | collective-permute-start | bytes 2101256 | tf_op jit(solution)/shard_map/ppermute | solution.py:282
  155.0 48.4 %copy-start.36 = (bf16[48,3712]{1,0:T(8,128)(2,1)S(1)}, bf16[48,3712]{1,0:T(8,128)(2,1)}, u32[]{:S(2)}) copy-start(bf16[48,3712]{1,0:T(8,128)(2,1)} %get-tuple-element.304) | copy-start | bytes 1069060
  155.0 48.6 %copy-start.35 = (bf16[48,3712]{1,0:T(8,128)(2,1)S(1)}, bf16[48,3712]{1,0:T(8,128)(2,1)}, u32[]{:S(2)}) copy-start(bf16[48,3712]{1,0:T(8,128)(2,1)} %get-tuple-element.305) | copy-start | bytes 1069060
  155.0 70.0 %collective-permute-start.22 = (bf16[128,3712]{1,0:T(8,128)(2,1)}, bf16[128,3712]{1,0:T(8,128)(2,1)S(1)}, u32[]{:S(2)}, u32[]{:S(2)}) collective-permute-start(bf16[128,3712]{1,0:T(8,128)(2,1)} %shard_map.161), channel_id=1, source_target_pairs={{0,4},{1,5},{2,6},{3,7},{12,8},{13,9},{14,10},{15,11},{4,12},{5,13... | collective-permute-start | bytes 2850824 | tf_op jit(solution)/shard_map/ppermute | solution.py:282
  176.0 29.3 %copy-start.7 = (bf16[48,7296]{1,0:T(8,128)(2,1)}, bf16[48,7296]{1,0:T(8,128)(2,1)S(1)}, u32[]{:S(2)}) copy-start(bf16[48,7296]{1,0:T(8,128)(2,1)S(1)} %collective-permute-done.16.refs_1_) | copy-start | bytes 2101252
  176.0 29.2 %copy-start.9 = (bf16[48,7296]{1,0:T(8,128)(2,1)}, bf16[48,7296]{1,0:T(8,128)(2,1)S(1)}, u32[]{:S(2)}) copy-start(bf16[48,7296]{1,0:T(8,128)(2,1)S(1)} %collective-permute-done.17.refs_2_) | copy-start | bytes 2101252
  176.0 7.7 %collective-permute-start.19 = (bf16[48,3712]{1,0:T(8,128)(2,1)}, bf16[48,3712]{1,0:T(8,128)(2,1)S(1)}, u32[]{:S(2)}, u32[]{:S(2)}) collective-permute-start(bf16[48,3712]{1,0:T(8,128)(2,1)} %get-tuple-element.272), channel_id=1, source_target_pairs={{0,1},{1,0},{2,3},{3,2},{4,5},{5,4},{6,7},{7,6},{8,9},{9,8},{10,11... | collective-permute-start | bytes 1069064 | tf_op jit(solution)/shard_map/ppermute | solution.py:282
  176.4 14.0 %collective-permute-start.20 = (bf16[48,3712]{1,0:T(8,128)(2,1)}, bf16[48,3712]{1,0:T(8,128)(2,1)S(1)}, u32[]{:S(2)}, u32[]{:S(2)}) collective-permute-start(bf16[48,3712]{1,0:T(8,128)(2,1)} %get-tuple-element.273), channel_id=1, source_target_pairs={{0,2},{1,3},{2,0},{3,1},{4,6},{5,7},{6,4},{7,5},{8,10},{9,11},{10,... | collective-permute-start | bytes 1069064 | tf_op jit(solution)/shard_map/ppermute | solution.py:282
  176.6 21.7 %collective-permute-start.21 = (bf16[48,3712]{1,0:T(8,128)(2,1)}, bf16[48,3712]{1,0:T(8,128)(2,1)S(1)}, u32[]{:S(2)}, u32[]{:S(2)}) collective-permute-start(bf16[48,3712]{1,0:T(8,128)(2,1)} %get-tuple-element.274), channel_id=1, source_target_pairs={{0,3},{1,2},{2,1},{3,0},{4,7},{5,6},{6,5},{7,4},{8,11},{9,10},{10,... | collective-permute-start | bytes 1069064 | tf_op jit(solution)/shard_map/ppermute | solution.py:282
  201.8 29.5 %copy-start.37 = (bf16[48,3584]{1,0:T(8,128)(2,1)S(1)}, bf16[48,3584]{1,0:T(8,128)(2,1)}, u32[]{:S(2)}) copy-start(bf16[48,3584]{1,0:T(8,128)(2,1)} %get-tuple-element.314) | copy-start | bytes 1032196
  201.8 30.8 %copy-start.38 = (bf16[128,128]{1,0:T(8,128)(2,1)S(1)}, bf16[128,128]{1,0:T(8,128)(2,1)}, u32[]{:S(2)}) copy-start(bf16[128,128]{1,0:T(8,128)(2,1)} %get-tuple-element.321) | copy-start | bytes 98308
  201.8 27.0 %collective-permute-start.23 = (bf16[80,3584]{1,0:T(8,128)(2,1)}, bf16[80,3584]{1,0:T(8,128)(2,1)S(1)}, u32[]{:S(2)}, u32[]{:S(2)}) collective-permute-start(bf16[80,3584]{1,0:T(8,128)(2,1)} %get-tuple-element.300), channel_id=1, source_target_pairs={{0,12},{1,13},{2,14},{3,15},{4,8},{5,9},{6,10},{7,11},{8,4},{9,5},... | collective-permute-start | bytes 1720328 | tf_op jit(solution)/shard_map/ppermute | solution.py:282
  203.1 22.0 %collective-permute-start.24 = (bf16[48,3712]{1,0:T(8,128)(2,1)}, bf16[48,3712]{1,0:T(8,128)(2,1)S(1)}, u32[]{:S(2)}, u32[]{:S(2)}) collective-permute-start(bf16[48,3712]{1,0:T(8,128)(2,1)} %get-tuple-element.303), channel_id=1, source_target_pairs={{0,1},{1,0},{2,3},{3,2},{4,5},{5,4},{6,7},{7,6},{8,9},{9,8},{10,11... | collective-permute-start | bytes 1069064 | tf_op jit(solution)/shard_map/ppermute | solution.py:282
  203.4 21.6 %collective-permute-start.25 = (bf16[48,3712]{1,0:T(8,128)(2,1)S(1)}, bf16[48,3712]{1,0:T(8,128)(2,1)S(1)}, u32[]{:S(2)}, u32[]{:S(2)}) collective-permute-start(bf16[48,3712]{1,0:T(8,128)(2,1)S(1)} %copy-done.36), channel_id=1, source_target_pairs={{0,2},{1,3},{2,0},{3,1},{4,6},{5,7},{6,4},{7,5},{8,10},{9,11},{10,... | collective-permute-start | bytes 1069064 | tf_op jit(solution)/shard_map/ppermute | solution.py:282
  203.6 21.4 %collective-permute-start.26 = (bf16[48,3712]{1,0:T(8,128)(2,1)S(1)}, bf16[48,3712]{1,0:T(8,128)(2,1)S(1)}, u32[]{:S(2)}, u32[]{:S(2)}) collective-permute-start(bf16[48,3712]{1,0:T(8,128)(2,1)S(1)} %copy-done.35), channel_id=1, source_target_pairs={{0,3},{1,2},{2,1},{3,0},{4,7},{5,6},{6,5},{7,4},{8,11},{9,10},{10,... | collective-permute-start | bytes 1069064 | tf_op jit(solution)/shard_map/ppermute | solution.py:282
  225.0 31.2 %copy-start.33 = (f32[128,16]{1,0:T(8,128)S(1)}, f32[128,16]{1,0:T(8,128)}, u32[]{:S(2)}) copy-start(f32[128,16]{1,0:T(8,128)} %copy-done.32) | copy-start | bytes 24580
  225.0 32.2 %copy-start.34 = (f32[128,16]{1,0:T(8,128)S(1)}, f32[128,16]{1,0:T(8,128)}, u32[]{:S(2)}) copy-start(f32[128,16]{1,0:T(8,128)} %get-tuple-element.338) | copy-start | bytes 24580
  225.0 33.3 %copy-start.5 = (bf16[128,3712]{1,0:T(8,128)(2,1)}, bf16[128,3712]{1,0:T(8,128)(2,1)S(1)}, u32[]{:S(2)}) copy-start(bf16[128,3712]{1,0:T(8,128)(2,1)S(1)} %collective-permute-done.22.refs_1_) | copy-start | bytes 2850820
  225.0 28.4 %copy-start.21 = (bf16[48,3712]{1,0:T(8,128)(2,1)}, bf16[48,3712]{1,0:T(8,128)(2,1)S(1)}, u32[]{:S(2)}) copy-start(bf16[48,3712]{1,0:T(8,128)(2,1)S(1)} %collective-permute-done.24.refs_1_) | copy-start | bytes 1069060
  228.8 18.3 %collective-permute-start.27 = (bf16[48,3712]{1,0:T(8,128)(2,1)}, bf16[48,3712]{1,0:T(8,128)(2,1)S(1)}, u32[]{:S(2)}, u32[]{:S(2)}) collective-permute-start(bf16[48,3712]{1,0:T(8,128)(2,1)} %get-tuple-element.307), channel_id=1, source_target_pairs={{0,1},{1,0},{2,3},{3,2},{4,5},{5,4},{6,7},{7,6},{8,9},{9,8},{10,11... | collective-permute-start | bytes 1069064 | tf_op jit(solution)/shard_map/ppermute | solution.py:282
  229.7 17.4 %collective-permute-start.28 = (bf16[48,3712]{1,0:T(8,128)(2,1)}, bf16[48,3712]{1,0:T(8,128)(2,1)S(1)}, u32[]{:S(2)}, u32[]{:S(2)}) collective-permute-start(bf16[48,3712]{1,0:T(8,128)(2,1)} %get-tuple-element.308), channel_id=1, source_target_pairs={{0,2},{1,3},{2,0},{3,1},{4,6},{5,7},{6,4},{7,5},{8,10},{9,11},{10,... | collective-permute-start | bytes 1069064 | tf_op jit(solution)/shard_map/ppermute | solution.py:282
  229.9 17.9 %collective-permute-start.29 = (bf16[48,3712]{1,0:T(8,128)(2,1)}, bf16[48,3712]{1,0:T(8,128)(2,1)S(1)}, u32[]{:S(2)}, u32[]{:S(2)}) collective-permute-start(bf16[48,3712]{1,0:T(8,128)(2,1)} %get-tuple-element.309), channel_id=1, source_target_pairs={{0,3},{1,2},{2,1},{3,0},{4,7},{5,6},{6,5},{7,4},{8,11},{9,10},{10,... | collective-permute-start | bytes 1069064 | tf_op jit(solution)/shard_map/ppermute | solution.py:282
  231.3 15.8 %collective-permute-start.30 = (bf16[48,3584]{1,0:T(8,128)(2,1)S(1)}, bf16[48,3584]{1,0:T(8,128)(2,1)S(1)}, u32[]{:S(2)}, u32[]{:S(2)}) collective-permute-start(bf16[48,3584]{1,0:T(8,128)(2,1)S(1)} %copy-done.37), channel_id=1, source_target_pairs={{0,12},{1,13},{2,14},{3,15},{4,8},{5,9},{6,10},{7,11},{8,4},{9,5},... | collective-permute-start | bytes 1032200 | tf_op jit(solution)/shard_map/ppermute | solution.py:282
  232.6 23.6 %collective-permute-start.31 = (bf16[128,128]{1,0:T(8,128)(2,1)S(1)}, bf16[128,128]{1,0:T(8,128)(2,1)S(1)}, u32[]{:S(2)}, u32[]{:S(2)}) collective-permute-start(bf16[128,128]{1,0:T(8,128)(2,1)S(1)} %copy-done.38), channel_id=1, source_target_pairs={{0,12},{1,13},{2,14},{3,15},{4,8},{5,9},{6,10},{7,11},{8,4},{9,5},... | collective-permute-start | bytes 98312 | tf_op jit(solution)/shard_map/ppermute | solution.py:282
  247.1 34.6 %copy-start.30 = (bf16[48,3584]{1,0:T(8,128)(2,1)}, bf16[48,3584]{1,0:T(8,128)(2,1)S(1)}, u32[]{:S(2)}) copy-start(bf16[48,3584]{1,0:T(8,128)(2,1)S(1)} %collective-permute-done.30.refs_3_) | copy-start | bytes 1032196
  251.3 4.9 %collective-permute-start.32 = (bf16[128,128]{1,0:T(8,128)(2,1)}, bf16[128,128]{1,0:T(8,128)(2,1)S(1)}, u32[]{:S(2)}, u32[]{:S(2)}) collective-permute-start(bf16[128,128]{1,0:T(8,128)(2,1)} %get-tuple-element.327), channel_id=1, source_target_pairs={{4,0},{5,1},{6,2},{7,3},{8,12},{9,13},{10,14},{11,15},{12,4},{13,5... | collective-permute-start | bytes 98312 | tf_op jit(solution)/shard_map/ppermute | solution.py:282
  251.3 30.4 %collective-permute-start.33 = (bf16[128,3584]{1,0:T(8,128)(2,1)}, bf16[128,3584]{1,0:T(8,128)(2,1)S(1)}, u32[]{:S(2)}, u32[]{:S(2)}) collective-permute-start(bf16[128,3584]{1,0:T(8,128)(2,1)} %get-tuple-element.331), channel_id=1, source_target_pairs={{4,0},{5,1},{6,2},{7,3},{8,12},{9,13},{10,14},{11,15},{12,4},{13,5... | collective-permute-start | bytes 2752520 | tf_op jit(solution)/shard_map/ppermute | solution.py:282
  (25 other events, 231.6 us)

commit v9 on v8

--- a/solution.py
+++ b/solution.py
@@ -159,8 +159,8 @@
     ins, refs = refs[:plane], refs[plane:]
     carry, refs = refs[:held], refs[held:]
     back_refs, refs = refs[:plane], refs[plane:]
-    gag_ref, gau_ref, gbg_ref, gbu_ref = refs[:4]
-    xs, dys, weight, route, low, proj, both, acc = refs[4:]
+    gag_ref, gau_ref, gbg_ref, gbu_ref, tag_ref = refs[:5]
+    xs, dys, weight, route, low, proj, both, acc = refs[5:]
 
     def total(at, value, part=slice(None)):
         return value + carry[at][:, part] if held else value
@@ -208,6 +208,7 @@
     def _():
         proj_b = proj[...].astype(bf16)
         routes = (route[...] * mine_ref[...]).astype(bf16)
+        tag_ref[...] = routes
         for i, out in enumerate(back_refs):
             out[:, width:] = routes[i * cap : (i + 1) * cap]
         for first, last in chunks(0, width, 512):
@@ -251,8 +252,11 @@
             jax.ShapeDtypeStruct((rank, width), f32),
             jax.ShapeDtypeStruct((rank, hidden), f32),
             jax.ShapeDtypeStruct((rank, hidden), f32),
+            jax.ShapeDtypeStruct((rows, wide - width), bf16),
         ],
-        out_specs=[whole_block((cap, wide))] * plane + grads,
+        out_specs=[whole_block((cap, wide))] * plane
+        + grads
+        + [whole_block((rows, wide - width))],
         scratch_shapes=[
             pltpu.VMEM((rows, width), bf16),
             pltpu.VMEM((rows, width), bf16),
@@ -369,33 +373,36 @@
             sel_2, got_1, own = join((sel_2, got_1, own))
             block_3 = send(own, along([(0, 1), (3, 2), (1, 3), (2, 0)]))
             got_2 = spread(sel_2)
-            done_1 = run(got_1, done_0[plane:])
+            done_1 = run(got_1, done_0[plane:-1])
             done_1, got_2[1], got_2[2] = join((done_1, got_2[1], got_2[2]))
             back_1 = spread(done_1[:plane])
             sel_3, placed_3 = take(flag, [block_3])
             sel_3, back_1, got_2 = join((sel_3, back_1, got_2))
             got_3 = spread(sel_3)
-            done_2 = run(got_2, done_1[plane:])
+            done_2 = run(got_2, done_1[plane:-1])
             done_2, got_3[1], got_3[2], done_0 = join((done_2, got_3[1], got_3[2], done_0))
             back_2 = spread(done_2[:plane])
             (part_1,) = sum_rows(placed_1, back_1, wide)
             term_1 = send(part_1, along([(0, 1), (3, 2), (1, 3), (2, 0)]))
             got_3, part_1, back_2, done_0 = join((got_3, part_1, back_2, done_0))
-            part_2a, part_2b, tag_2 = sum_rows(placed_2, back_2, width, (tok * 5 // 8, tok * 3 // 8))
+            part_2a, part_2b, tag_2 = sum_rows(placed_2, back_2, width, (tok // 2, tok // 2))
             tag_2 = send(tag_2, across(3 * plane))
             term_2a = send(part_2a, across(3 * plane))
             back_0 = spread(done_0[:plane])
-            done_3 = run(got_3, done_2[plane:])
+            done_3 = run(got_3, done_2[plane:-1])
             done_3, term_1, term_2a, part_2b, back_0 = join(
                 (done_3, term_1, term_2a, part_2b, back_0)
             )
+            pieces = spread([done_3[-1][p * cap : (p + 1) * cap] for p in range(plane)])
+            done_3, pieces, tag_2 = join((done_3, pieces, tag_2))
+            swap_3 = along([(1, 0), (2, 3), (3, 1), (0, 2)])
+            tag_3 = dot_tn(placed_3, jnp.concatenate(pieces, axis=0)).astype(bf16)
+            tag_3 = send(tag_3, swap_3)
             back_3 = spread(done_3[:plane])
             term_2b = send(part_2b, across(3 * plane))
-            back_3, back_0, term_2b = join((back_3, back_0, term_2b))
             part_0, tag_0 = sum_rows(placed_0, back_0, width)
-            part_3, tag_3 = sum_rows(placed_3, back_3, width)
-            swap_3 = along([(1, 0), (2, 3), (3, 1), (0, 2)])
-            tag_3 = send(tag_3, swap_3)
+            back_3, term_2b = join((back_3, term_2b))
+            part_3, _ = sum_rows(placed_3, back_3, width)
             term_3 = send(part_3, swap_3)
             tags = [tag_0, term_1[:, width:], tag_2, tag_3]
             terms = [[part_0], [term_1], [term_2a, term_2b], [term_3]]
@@ -406,7 +413,7 @@
             for g in range(layers):
                 block = own if g == 0 else send(own, across(g * plane))
                 sel, placed = take(flag, [block])
-                result = run(spread(sel), done[-1][plane:] if done else ())
+                result = run(spread(sel), done[-1][plane:-1] if done else ())
                 (part,) = sum_rows(placed, spread(result[:plane]), wide)
                 terms.append([part if g == 0 else send(part, across(g * plane))])
                 done.append(result)
@@ -425,7 +432,7 @@
 
         in_grad = final_sum(d_logit, router_matrix.T, terms)
 
-        grad_gate_a, grad_up_a, grad_gate_b, grad_up_b = done[-1][plane:]
+        grad_gate_a, grad_up_a, grad_gate_b, grad_up_b = done[-1][plane:-1]
         return (
             in_grad,
             router_grad,

time: 289 us -> 291 us (level)
  waiting for transfers between devices: 104 us -> 96.2 us
  starting transfers between devices: 32.8 us -> 38.8 us
  blocking collectives: 22.3 us -> 25.8 us
    ppermute x34 -> x37, waiting for transfers between devices: 104 us -> 96.2 us  [send(): return lax.ppermute(array, 'expert', pairs)]
    ppermute x34 -> x37, starting transfers between devices: 32.8 us -> 38.8 us  [send(): return lax.ppermute(array, 'expert', pairs)]
    all_to_all x1, blocking collectives: 22.3 us -> 25.8 us  [shards(): lax.all_to_all(router_part, 'expert', split_axis=0, concat_axis=0, tiled=...]
  transfers between devices with their start and end apart: 34 -> 37, of which waited for: 13 -> 15; matrix products, arithmetic and copies ran while one was open for 2% -> 2% of each run, Pallas kernels for 36% -> 34%
where the time goes in v9:
time: 291 us; the launch traced here: 289 us
  Pallas kernels  110 us (38%)
  waiting for transfers between devices  96.2 us (33%)
  starting transfers between devices  38.8 us (13%)
  blocking collectives  25.8 us (9%)
  local copies, waits for them, and re-layouts  9.12 us (3%)
  other arithmetic  4.83 us (2%)
    ppermute x37, waiting for transfers between devices, send(): return lax.ppermute(array, 'expert', pairs)  96.2 us
    pallas_call x4, Pallas kernels, expert_rows(): pl.pallas_call(functools.partial(expert_kernel, len(carry), cap, width, r...  78.7 us
    ppermute x37, starting transfers between devices, send(): return lax.ppermute(array, 'expert', pairs)  38.8 us
    all_to_all x1, blocking collectives, shards(): lax.all_to_all(router_part, 'expert', split_axis=0, concat_axis=0, tiled=...  25.8 us
    pallas_call x4, Pallas kernels, select_rows(): pl.pallas_call(functools.partial(select_kernel, parts, meta_at, slots_hel...  16.9 us
    pallas_call x4, Pallas kernels, sum_rows(): pl.pallas_call(functools.partial(sum_kernel, apart), out_shape=shapes, in...  11 us
  transfers between devices with their start and end apart: 37, of which 15 were waited for; matrix products, arithmetic and copies ran while one was open for 2% of the time, Pallas kernels for 34%

profile of v9, /device:TPU:15, one launch (start us, length us, event | category | flops | bytes accessed | tf_op | source)
XLA Modules:
  0.0 288.8 jit_solution(932852413864620442)
XLA Ops:
  1.7 2.2 fusion.14
  4.5 2.2 concatenate.8.refs_0_
  8.0 4.1 %shard_map.154 = (bf16[48,7296]{1,0:T(8,128)(2,1)}, bf16[48,7296]{1,0:T(8,128)(2,1)}, bf16[48,7296]{1,0:T(8,128)(2,1)}, bf16[48,7296]{1,0:T(8,128)(2,1)}, bf16[192,128]{1,0:T(8,128)(2,1)}) custom-call(s32[1]{0:T(128)} %bitcast.flag_ref, bf16[16,128]{1,0:T(8,128)(2,1)} %pad_convert_fusion.guide_ref, bf16[128,7296]{1,0:T(8,128)(2,1)} %copy-done), custom_call_target="tpu_custom_call" | custom-call | flops 1024 | bytes 1024 | tf_op jit(solution)/shard_map/pallas_call | solution.py:87
  13.0 1.4 collective-permute-start.3
  14.8 15.6 %collective-permute-done.2.refs_2_ = bf16[48,7296]{1,0:T(8,128)(2,1)S(1)} collective-permute-done((bf16[48,7296]{1,0:T(8,128)(2,1)}, bf16[48,7296]{1,0:T(8,128)(2,1)S(1)}, u32[]{:S(2)}, u32[]{:S(2)}) %collective-permute-start.2) | collective-permute-done | bytes 700448 | tf_op jit(solution)/shard_map/ppermute | solution.py:286
  30.4 15.4 %collective-permute-done.3.refs_3_ = bf16[48,7296]{1,0:T(8,128)(2,1)S(1)} collective-permute-done((bf16[48,7296]{1,0:T(8,128)(2,1)}, bf16[48,7296]{1,0:T(8,128)(2,1)S(1)}, u32[]{:S(2)}, u32[]{:S(2)}) %collective-permute-start.3) | collective-permute-done | bytes 700448 | tf_op jit(solution)/shard_map/ppermute | solution.py:286
  45.8 3.5 %collective-permute-done.refs_0_ = bf16[128,7296]{1,0:T(8,128)(2,1)} collective-permute-done((bf16[128,7296]{1,0:T(8,128)(2,1)S(1)}, bf16[128,7296]{1,0:T(8,128)(2,1)}, u32[]{:S(2)}, u32[]{:S(2)}) %collective-permute-start) | collective-permute-done | bytes 1867808 | tf_op jit(solution)/shard_map/ppermute | solution.py:286
  49.4 3.2 %collective-permute-start.4 = (bf16[128,7296]{1,0:T(8,128)(2,1)}, bf16[128,7296]{1,0:T(8,128)(2,1)S(1)}, u32[]{:S(2)}, u32[]{:S(2)}) collective-permute-start(bf16[128,7296]{1,0:T(8,128)(2,1)} %copy-done), channel_id=1, source_target_pairs={{4,8},{5,9},{6,10},{7,11},{8,4},{9,5},{10,6},{11,7},{20,24},{21,25... | collective-permute-start | bytes 5603336 | tf_op jit(solution)/shard_map/ppermute | solution.py:286
  52.6 2.5 collective-permute-start.5
  55.1 4.1 %shard_map.156 = (bf16[48,7296]{1,0:T(8,128)(2,1)}, bf16[48,7296]{1,0:T(8,128)(2,1)}, bf16[48,7296]{1,0:T(8,128)(2,1)}, bf16[48,7296]{1,0:T(8,128)(2,1)}, bf16[192,128]{1,0:T(8,128)(2,1)}) custom-call(s32[1]{0:T(128)} %bitcast.flag_ref, bf16[16,128]{1,0:T(8,128)(2,1)} %pad_convert_fusion.guide_ref, bf16[128,7296]{1,0:T(8,128)(2,1)} %collective-permute-done.refs_0_), custom_call_target="tpu_custom_call" | custom-call | flops 1024 | bytes 1024 | tf_op jit(solution)/shard_map/pallas_call | solution.py:87
  59.2 1.8 collective-permute-start.6
  61.3 1.4 collective-permute-start.8
  63.2 19.4 %shard_map.157 = (bf16[48,3712]{1,0:T(8,128)(2,1)}, bf16[48,3712]{1,0:T(8,128)(2,1)}, bf16[48,3712]{1,0:T(8,128)(2,1)}, bf16[48,3712]{1,0:T(8,128)(2,1)}, f32[32...) custom-call(f32[1,128]{1,0:T(1,128)} %compare_convert_fusion.mine_re, ...), custom_call_target="tpu_custom_call" | custom-call | flops 1024 | bytes 1024 | tf_op jit(solution)/shard_map/pallas_call | solution.py:234
  82.6 11.3 %collective-permute-done.8.refs_3_ = bf16[48,7296]{1,0:T(8,128)(2,1)} collective-permute-done((bf16[48,7296]{1,0:T(8,128)(2,1)}, bf16[48,7296]{1,0:T(8,128)(2,1)}, u32[]{:S(2)}, u32[]{:S(2)}) %collective-permute-start.8) | collective-permute-done | bytes 700448 | tf_op jit(solution)/shard_map/ppermute | solution.py:286
  94.0 1.2 copy-done.3
  95.2 4.6 %shard_map.155 = (bf16[48,7296]{1,0:T(8,128)(2,1)}, bf16[48,7296]{1,0:T(8,128)(2,1)}, bf16[48,7296]{1,0:T(8,128)(2,1)}, bf16[48,7296]{1,0:T(8,128)(2,1)}, bf16[192,128]{1,0:T(8,128)(2,1)}) custom-call(s32[1]{0:T(128)} %bitcast.flag_ref, bf16[16,128]{1,0:T(8,128)(2,1)} %pad_convert_fusion.guide_ref, bf16[128,7296]{1,0:T(8,128)(2,1)} %copy-done.3, ...), custom_call_target="tpu_custom_call" | custom-call | flops 1024 | bytes 1024 | tf_op jit(solution)/shard_map/pallas_call | solution.py:87
  99.9 2.3 collective-permute-start.10
  102.4 1.4 collective-permute-start.15
  103.8 19.8 %shard_map.159 = (bf16[48,3712]{1,0:T(8,128)(2,1)}, bf16[48,3712]{1,0:T(8,128)(2,1)}, bf16[48,3712]{1,0:T(8,128)(2,1)}, bf16[48,3712]{1,0:T(8,128)(2,1)}, f32[32...) custom-call(f32[1,128]{1,0:T(1,128)} %compare_convert_fusion.mine_re, ...), custom_call_target="tpu_custom_call" | custom-call | flops 1024 | bytes 1024 | tf_op jit(solution)/shard_map/pallas_call | solution.py:234
  124.1 1.7 collective-permute-start.14
  125.8 15.7 %collective-permute-done.9.refs_0_ = bf16[128,7296]{1,0:T(8,128)(2,1)S(1)} collective-permute-done((bf16[128,7296]{1,0:T(8,128)(2,1)S(1)}, bf16[128,7296]{1,0:T(8,128)(2,1)S(1)}, u32[]{:S(2)}, u32[]{:S(2)}) %collective-permute-start.9) | collective-permute-done | bytes 1867808 | tf_op jit(solution)/shard_map/ppermute | solution.py:286
  141.5 1.3 copy-done.4
  142.8 4.1 %shard_map.158 = (bf16[48,7296]{1,0:T(8,128)(2,1)}, bf16[48,7296]{1,0:T(8,128)(2,1)}, bf16[48,7296]{1,0:T(8,128)(2,1)}, bf16[48,7296]{1,0:T(8,128)(2,1)}, bf16[192,128]{1,0:T(8,128)(2,1)}) custom-call(s32[1]{0:T(128)} %bitcast.flag_ref, bf16[16,128]{1,0:T(8,128)(2,1)} %pad_convert_fusion.guide_ref, bf16[128,7296]{1,0:T(8,128)(2,1)} %copy-done.4), custom_call_target="tpu_custom_call" | custom-call | flops 1024 | bytes 1024 | tf_op jit(solution)/shard_map/pallas_call | solution.py:87
  146.9 3.2 %collective-permute-done.14.refs_3_ = bf16[48,3712]{1,0:T(8,128)(2,1)S(1)} collective-permute-done((bf16[48,3712]{1,0:T(8,128)(2,1)}, bf16[48,3712]{1,0:T(8,128)(2,1)S(1)}, u32[]{:S(2)}, u32[]{:S(2)}) %collective-permute-start.14) | collective-permute-done | bytes 356384 | tf_op jit(solution)/shard_map/ppermute | solution.py:286
  150.6 1.6 collective-permute-start.18
  152.2 2.7 shard_map.161
  154.9 1.1 collective-permute-start.22
  156.1 19.8 %shard_map.160 = (bf16[48,3712]{1,0:T(8,128)(2,1)}, bf16[48,3712]{1,0:T(8,128)(2,1)}, bf16[48,3712]{1,0:T(8,128)(2,1)}, bf16[48,3712]{1,0:T(8,128)(2,1)}, f32[32...) custom-call(f32[1,128]{1,0:T(1,128)} %compare_convert_fusion.mine_re, ...), custom_call_target="tpu_custom_call" | custom-call | flops 1024 | bytes 1024 | tf_op jit(solution)/shard_map/pallas_call | solution.py:234
  176.5 1.6 collective-permute-start.21
  178.1 5.5 %collective-permute-done.18.refs_3_ = bf16[48,7296]{1,0:T(8,128)(2,1)S(1)} collective-permute-done((bf16[48,7296]{1,0:T(8,128)(2,1)}, bf16[48,7296]{1,0:T(8,128)(2,1)S(1)}, u32[]{:S(2)}, u32[]{:S(2)}) %collective-permute-start.18) | collective-permute-done | bytes 700448 | tf_op jit(solution)/shard_map/ppermute | solution.py:286
  183.6 6.7 %collective-permute-done.20.refs_2_ = bf16[48,3712]{1,0:T(8,128)(2,1)S(1)} collective-permute-done((bf16[48,3712]{1,0:T(8,128)(2,1)}, bf16[48,3712]{1,0:T(8,128)(2,1)S(1)}, u32[]{:S(2)}, u32[]{:S(2)}) %collective-permute-start.20) | collective-permute-done | bytes 356384 | tf_op jit(solution)/shard_map/ppermute | solution.py:286
  190.3 8.0 %collective-permute-done.21.refs_3_ = bf16[48,3712]{1,0:T(8,128)(2,1)S(1)} collective-permute-done((bf16[48,3712]{1,0:T(8,128)(2,1)}, bf16[48,3712]{1,0:T(8,128)(2,1)S(1)}, u32[]{:S(2)}, u32[]{:S(2)}) %collective-permute-start.21) | collective-permute-done | bytes 356384 | tf_op jit(solution)/shard_map/ppermute | solution.py:286
  199.0 2.7 shard_map.163
  201.7 1.4 collective-permute-start.23
  203.6 1.6 collective-permute-start.26
  205.2 19.8 %shard_map.162 = (bf16[48,3712]{1,0:T(8,128)(2,1)}, bf16[48,3712]{1,0:T(8,128)(2,1)}, bf16[48,3712]{1,0:T(8,128)(2,1)}, bf16[48,3712]{1,0:T(8,128)(2,1)}, f32[32...) custom-call(f32[1,128]{1,0:T(1,128)} %compare_convert_fusion.mine_re, ...), custom_call_target="tpu_custom_call" | custom-call | flops 1024 | bytes 1024 | tf_op jit(solution)/shard_map/pallas_call | solution.py:234
  225.3 1.4 collective-permute-start.35
  228.3 1.5 collective-permute-start.29
  229.8 1.1 collective-permute-done.28
  231.9 1.1 collective-permute-start.33
  234.1 3.1 %collective-permute-start.31 = (bf16[128,128]{1,0:T(8,128)(2,1)S(1)}, bf16[128,128]{1,0:T(8,128)(2,1)S(1)}, u32[]{:S(2)}, u32[]{:S(2)}) collective-permute-start(bf16[128,128]{1,0:T(8,128)(2,1)S(1)} %convolution_convert_fusion), channel_id=1, source_target_pairs={{4,0},{5,1},{6,2},{7,3},{8,12},{9,13},{10,14},{11,15},{12,4},{13,5... | collective-permute-start | bytes 98312 | tf_op jit(solution)/shard_map/ppermute | solution.py:286
  237.2 2.7 shard_map.164
  240.1 0.9 multiply_reduce_fusion
  241.7 8.1 %collective-permute-done.34.refs_3_ = bf16[48,3712]{1,0:T(8,128)(2,1)S(1)} collective-permute-done((bf16[48,3712]{1,0:T(8,128)(2,1)}, bf16[48,3712]{1,0:T(8,128)(2,1)S(1)}, u32[]{:S(2)}, u32[]{:S(2)}) %collective-permute-start.34) | collective-permute-done | bytes 356384 | tf_op jit(solution)/shard_map/ppermute | solution.py:286
  250.5 2.9 shard_map.165
  253.4 2.8 collective-permute-start.36
  257.8 25.8 %all_to_all.5 = f32[16,16,224]{2,1,0:T(8,128)S(1)} all-to-all(f32[16,16,224]{2,1,0:T(8,128)S(1)} %bitcast.58), channel_id=1, replica_groups=mesh['groups'=2,'expert'=16] {'expert'}, dimensions={0} | all-to-all | bytes 458752 | tf_op jit(solution)/shard_map/all_to_all | solution.py:430
  285.1 3.7 %shard_map.166 = bf16[128,3584]{1,0:T(8,128)(2,1)} custom-call(bf16[128,16]{1,0:T(8,128)(2,1)} %copy-done.31, bf16[16,3584]{1,0:T(8,128)(2,1)} %bitcast.59, bf16[128,3584]{1,0:T(8,128)(2,1)} %get-tuple-element.339.refs_0_, bf16[128,3712]{1,0:T(8,128)(2,1)} %copy-done.5, bf16[64,3584]{1,0:T(8,128)(2,1)} %copy-done.17, bf16[64,3584]{1,0:T(8,128)(2,1)} %copy-done.18, ...), custom_call_target="tpu_custom_call" | custom-call | flops 1024 | bytes 1024 | tf_op jit(solution)/shard_map/pallas_call | solution.py:146
  (138 shorter events, 16.8 us)
Async XLA Ops:
  6.7 42.6 %collective-permute-start = (bf16[128,7296]{1,0:T(8,128)(2,1)S(1)}, bf16[128,7296]{1,0:T(8,128)(2,1)}, u32[]{:S(2)}, u32[]{:S(2)}) collective-permute-start(bf16[128,7296]{1,0:T(8,128)(2,1)S(1)} %concatenate.8.refs_0_), channel_id=1, source_target_pairs={{0,8},{1,9},{2,10},{3,11},{12,4},{13,5},{14,6},{15,7},{4,0},{5,1},... | collective-permute-start | bytes 5603336 | tf_op jit(solution)/shard_map/ppermute | solution.py:286
  12.1 2.7 collective-permute-start.1
  12.8 17.6 %collective-permute-start.2 = (bf16[48,7296]{1,0:T(8,128)(2,1)}, bf16[48,7296]{1,0:T(8,128)(2,1)S(1)}, u32[]{:S(2)}, u32[]{:S(2)}) collective-permute-start(bf16[48,7296]{1,0:T(8,128)(2,1)} %get-tuple-element.190), channel_id=1, source_target_pairs={{0,2},{1,3},{2,0},{3,1},{4,6},{5,7},{6,4},{7,5},{8,10},{9,11},{10,... | collective-permute-start | bytes 2101256 | tf_op jit(solution)/shard_map/ppermute | solution.py:286
  13.0 32.8 %collective-permute-start.3 = (bf16[48,7296]{1,0:T(8,128)(2,1)}, bf16[48,7296]{1,0:T(8,128)(2,1)S(1)}, u32[]{:S(2)}, u32[]{:S(2)}) collective-permute-start(bf16[48,7296]{1,0:T(8,128)(2,1)} %get-tuple-element.191), channel_id=1, source_target_pairs={{0,3},{1,2},{2,1},{3,0},{4,7},{5,6},{6,5},{7,4},{8,11},{9,10},{10,... | collective-permute-start | bytes 2101256 | tf_op jit(solution)/shard_map/ppermute | solution.py:286
  14.8 34.6 %copy-start.14 = (bf16[48,7296]{1,0:T(8,128)(2,1)}, bf16[48,7296]{1,0:T(8,128)(2,1)S(1)}, u32[]{:S(2)}) copy-start(bf16[48,7296]{1,0:T(8,128)(2,1)S(1)} %collective-permute-done.1.refs_1_) | copy-start | bytes 2101252
  49.4 44.6 %collective-permute-start.4 = (bf16[128,7296]{1,0:T(8,128)(2,1)}, bf16[128,7296]{1,0:T(8,128)(2,1)S(1)}, u32[]{:S(2)}, u32[]{:S(2)}) collective-permute-start(bf16[128,7296]{1,0:T(8,128)(2,1)} %copy-done), channel_id=1, source_target_pairs={{4,8},{5,9},{6,10},{7,11},{8,4},{9,5},{10,6},{11,7},{20,24},{21,25... | collective-permute-start | bytes 5603336 | tf_op jit(solution)/shard_map/ppermute | solution.py:286
  52.6 41.4 %collective-permute-start.5 = (bf16[128,7296]{1,0:T(8,128)(2,1)}, bf16[128,7296]{1,0:T(8,128)(2,1)}, u32[]{:S(2)}, u32[]{:S(2)}) collective-permute-start(bf16[128,7296]{1,0:T(8,128)(2,1)} %collective-permute-done.refs_0_), channel_id=1, source_target_pairs={{4,0},{5,1},{6,2},{7,3},{8,12},{9,13},{10,14},{11,15},{20,16},{21,... | collective-permute-start | bytes 5603336 | tf_op jit(solution)/shard_map/ppermute | solution.py:286
  59.2 23.4 %collective-permute-start.6 = (bf16[48,7296]{1,0:T(8,128)(2,1)}, bf16[48,7296]{1,0:T(8,128)(2,1)S(1)}, u32[]{:S(2)}, u32[]{:S(2)}) collective-permute-start(bf16[48,7296]{1,0:T(8,128)(2,1)} %get-tuple-element.199), channel_id=1, source_target_pairs={{0,1},{1,0},{2,3},{3,2},{4,5},{5,4},{6,7},{7,6},{8,9},{9,8},{10,11... | collective-permute-start | bytes 2101256 | tf_op jit(solution)/shard_map/ppermute | solution.py:286
  61.0 21.6 %collective-permute-start.7 = (bf16[48,7296]{1,0:T(8,128)(2,1)}, bf16[48,7296]{1,0:T(8,128)(2,1)}, u32[]{:S(2)}, u32[]{:S(2)}) collective-permute-start(bf16[48,7296]{1,0:T(8,128)(2,1)} %get-tuple-element.200), channel_id=1, source_target_pairs={{0,2},{1,3},{2,0},{3,1},{4,6},{5,7},{6,4},{7,5},{8,10},{9,11},{10,... | collective-permute-start | bytes 2101256 | tf_op jit(solution)/shard_map/ppermute | solution.py:286
  61.3 32.7 %collective-permute-start.8 = (bf16[48,7296]{1,0:T(8,128)(2,1)}, bf16[48,7296]{1,0:T(8,128)(2,1)}, u32[]{:S(2)}, u32[]{:S(2)}) collective-permute-start(bf16[48,7296]{1,0:T(8,128)(2,1)} %get-tuple-element.201), channel_id=1, source_target_pairs={{0,3},{1,2},{2,1},{3,0},{4,7},{5,6},{6,5},{7,4},{8,11},{9,10},{10,... | collective-permute-start | bytes 2101256 | tf_op jit(solution)/shard_map/ppermute | solution.py:286
  99.8 41.6 %collective-permute-start.9 = (bf16[128,7296]{1,0:T(8,128)(2,1)S(1)}, bf16[128,7296]{1,0:T(8,128)(2,1)S(1)}, u32[]{:S(2)}, u32[]{:S(2)}) collective-permute-start(bf16[128,7296]{1,0:T(8,128)(2,1)S(1)} %copy-done.1), channel_id=1, source_target_pairs={{0,4},{1,5},{2,6},{3,7},{12,8},{13,9},{14,10},{15,11},{4,12},{5,13... | collective-permute-start | bytes 5603336 | tf_op jit(solution)/shard_map/ppermute | solution.py:286
  99.9 23.7 %collective-permute-start.10 = (bf16[48,7296]{1,0:T(8,128)(2,1)}, bf16[48,7296]{1,0:T(8,128)(2,1)S(1)}, u32[]{:S(2)}, u32[]{:S(2)}) collective-permute-start(bf16[48,7296]{1,0:T(8,128)(2,1)} %get-tuple-element.240), channel_id=1, source_target_pairs={{0,1},{1,0},{2,3},{3,2},{4,5},{5,4},{6,7},{7,6},{8,9},{9,8},{10,11... | collective-permute-start | bytes 2101256 | tf_op jit(solution)/shard_map/ppermute | solution.py:286
  102.1 21.4 %collective-permute-start.11 = (bf16[48,7296]{1,0:T(8,128)(2,1)}, bf16[48,7296]{1,0:T(8,128)(2,1)S(1)}, u32[]{:S(2)}, u32[]{:S(2)}) collective-permute-start(bf16[48,7296]{1,0:T(8,128)(2,1)} %get-tuple-element.241), channel_id=1, source_target_pairs={{0,2},{1,3},{2,0},{3,1},{4,6},{5,7},{6,4},{7,5},{8,10},{9,11},{10,... | collective-permute-start | bytes 2101256 | tf_op jit(solution)/shard_map/ppermute | solution.py:286
  102.4 44.5 %collective-permute-start.15 = (bf16[48,7296]{1,0:T(8,128)(2,1)}, bf16[48,7296]{1,0:T(8,128)(2,1)S(1)}, u32[]{:S(2)}, u32[]{:S(2)}) collective-permute-start(bf16[48,7296]{1,0:T(8,128)(2,1)} %get-tuple-element.249), channel_id=1, source_target_pairs={{0,3},{1,2},{2,1},{3,0},{4,7},{5,6},{6,5},{7,4},{8,11},{9,10},{10,... | collective-permute-start | bytes 2101256 | tf_op jit(solution)/shard_map/ppermute | solution.py:286
  123.5 32.5 %copy-start.8 = (bf16[48,7296]{1,0:T(8,128)(2,1)}, bf16[48,7296]{1,0:T(8,128)(2,1)S(1)}, u32[]{:S(2)}) copy-start(bf16[48,7296]{1,0:T(8,128)(2,1)S(1)} %collective-permute-done.10.refs_1_) | copy-start | bytes 2101252
  123.6 32.5 %copy-start.10 = (bf16[48,7296]{1,0:T(8,128)(2,1)}, bf16[48,7296]{1,0:T(8,128)(2,1)S(1)}, u32[]{:S(2)}) copy-start(bf16[48,7296]{1,0:T(8,128)(2,1)S(1)} %collective-permute-done.11.refs_2_) | copy-start | bytes 2101252
  123.6 23.3 %collective-permute-start.12 = (bf16[48,3712]{1,0:T(8,128)(2,1)}, bf16[48,3712]{1,0:T(8,128)(2,1)S(1)}, u32[]{:S(2)}, u32[]{:S(2)}) collective-permute-start(bf16[48,3712]{1,0:T(8,128)(2,1)} %get-tuple-element.243), channel_id=1, source_target_pairs={{0,1},{1,0},{2,3},{3,2},{4,5},{5,4},{6,7},{7,6},{8,9},{9,8},{10,11... | collective-permute-start | bytes 1069064 | tf_op jit(solution)/shard_map/ppermute | solution.py:286
  123.9 23.0 %collective-permute-start.13 = (bf16[48,3712]{1,0:T(8,128)(2,1)}, bf16[48,3712]{1,0:T(8,128)(2,1)S(1)}, u32[]{:S(2)}, u32[]{:S(2)}) collective-permute-start(bf16[48,3712]{1,0:T(8,128)(2,1)} %get-tuple-element.244), channel_id=1, source_target_pairs={{0,2},{1,3},{2,0},{3,1},{4,6},{5,7},{6,4},{7,5},{8,10},{9,11},{10,... | collective-permute-start | bytes 1069064 | tf_op jit(solution)/shard_map/ppermute | solution.py:286
  124.1 25.9 %collective-permute-start.14 = (bf16[48,3712]{1,0:T(8,128)(2,1)}, bf16[48,3712]{1,0:T(8,128)(2,1)S(1)}, u32[]{:S(2)}, u32[]{:S(2)}) collective-permute-start(bf16[48,3712]{1,0:T(8,128)(2,1)} %get-tuple-element.245), channel_id=1, source_target_pairs={{0,3},{1,2},{2,1},{3,0},{4,7},{5,6},{6,5},{7,4},{8,11},{9,10},{10,... | collective-permute-start | bytes 1069064 | tf_op jit(solution)/shard_map/ppermute | solution.py:286
  150.0 25.8 %collective-permute-start.16 = (bf16[48,7296]{1,0:T(8,128)(2,1)}, bf16[48,7296]{1,0:T(8,128)(2,1)S(1)}, u32[]{:S(2)}, u32[]{:S(2)}) collective-permute-start(bf16[48,7296]{1,0:T(8,128)(2,1)} %get-tuple-element.267), channel_id=1, source_target_pairs={{0,1},{1,0},{2,3},{3,2},{4,5},{5,4},{6,7},{7,6},{8,9},{9,8},{10,11... | collective-permute-start | bytes 2101256 | tf_op jit(solution)/shard_map/ppermute | solution.py:286
  150.3 25.5 %collective-permute-start.17 = (bf16[48,7296]{1,0:T(8,128)(2,1)}, bf16[48,7296]{1,0:T(8,128)(2,1)S(1)}, u32[]{:S(2)}, u32[]{:S(2)}) collective-permute-start(bf16[48,7296]{1,0:T(8,128)(2,1)} %get-tuple-element.268), channel_id=1, source_target_pairs={{0,2},{1,3},{2,0},{3,1},{4,6},{5,7},{6,4},{7,5},{8,10},{9,11},{10,... | collective-permute-start | bytes 2101256 | tf_op jit(solution)/shard_map/ppermute | solution.py:286
  150.6 33.0 %collective-permute-start.18 = (bf16[48,7296]{1,0:T(8,128)(2,1)}, bf16[48,7296]{1,0:T(8,128)(2,1)S(1)}, u32[]{:S(2)}, u32[]{:S(2)}) collective-permute-start(bf16[48,7296]{1,0:T(8,128)(2,1)} %get-tuple-element.275), channel_id=1, source_target_pairs={{0,3},{1,2},{2,1},{3,0},{4,7},{5,6},{6,5},{7,4},{8,11},{9,10},{10,... | collective-permute-start | bytes 2101256 | tf_op jit(solution)/shard_map/ppermute | solution.py:286
  154.9 48.7 %copy-start.37 = (bf16[48,3712]{1,0:T(8,128)(2,1)S(1)}, bf16[48,3712]{1,0:T(8,128)(2,1)}, u32[]{:S(2)}) copy-start(bf16[48,3712]{1,0:T(8,128)(2,1)} %get-tuple-element.316) | copy-start | bytes 1069060
  154.9 70.1 %collective-permute-start.22 = (bf16[128,3712]{1,0:T(8,128)(2,1)}, bf16[128,3712]{1,0:T(8,128)(2,1)S(1)}, u32[]{:S(2)}, u32[]{:S(2)}) collective-permute-start(bf16[128,3712]{1,0:T(8,128)(2,1)} %shard_map.161), channel_id=1, source_target_pairs={{0,4},{1,5},{2,6},{3,7},{12,8},{13,9},{14,10},{15,11},{4,12},{5,13... | collective-permute-start | bytes 2850824 | tf_op jit(solution)/shard_map/ppermute | solution.py:286
  175.8 29.4 %copy-start.7 = (bf16[48,7296]{1,0:T(8,128)(2,1)}, bf16[48,7296]{1,0:T(8,128)(2,1)S(1)}, u32[]{:S(2)}) copy-start(bf16[48,7296]{1,0:T(8,128)(2,1)S(1)} %collective-permute-done.16.refs_1_) | copy-start | bytes 2101252
  175.9 29.4 %copy-start.9 = (bf16[48,7296]{1,0:T(8,128)(2,1)}, bf16[48,7296]{1,0:T(8,128)(2,1)S(1)}, u32[]{:S(2)}) copy-start(bf16[48,7296]{1,0:T(8,128)(2,1)S(1)} %collective-permute-done.17.refs_2_) | copy-start | bytes 2101252
  175.9 7.7 %collective-permute-start.19 = (bf16[48,3712]{1,0:T(8,128)(2,1)}, bf16[48,3712]{1,0:T(8,128)(2,1)S(1)}, u32[]{:S(2)}, u32[]{:S(2)}) collective-permute-start(bf16[48,3712]{1,0:T(8,128)(2,1)} %get-tuple-element.282), channel_id=1, source_target_pairs={{0,1},{1,0},{2,3},{3,2},{4,5},{5,4},{6,7},{7,6},{8,9},{9,8},{10,11... | collective-permute-start | bytes 1069064 | tf_op jit(solution)/shard_map/ppermute | solution.py:286
  176.2 14.1 %collective-permute-start.20 = (bf16[48,3712]{1,0:T(8,128)(2,1)}, bf16[48,3712]{1,0:T(8,128)(2,1)S(1)}, u32[]{:S(2)}, u32[]{:S(2)}) collective-permute-start(bf16[48,3712]{1,0:T(8,128)(2,1)} %get-tuple-element.283), channel_id=1, source_target_pairs={{0,2},{1,3},{2,0},{3,1},{4,6},{5,7},{6,4},{7,5},{8,10},{9,11},{10,... | collective-permute-start | bytes 1069064 | tf_op jit(solution)/shard_map/ppermute | solution.py:286
  176.5 21.8 %collective-permute-start.21 = (bf16[48,3712]{1,0:T(8,128)(2,1)}, bf16[48,3712]{1,0:T(8,128)(2,1)S(1)}, u32[]{:S(2)}, u32[]{:S(2)}) collective-permute-start(bf16[48,3712]{1,0:T(8,128)(2,1)} %get-tuple-element.284), channel_id=1, source_target_pairs={{0,3},{1,2},{2,1},{3,0},{4,7},{5,6},{6,5},{7,4},{8,11},{9,10},{10,... | collective-permute-start | bytes 1069064 | tf_op jit(solution)/shard_map/ppermute | solution.py:286
  201.7 32.2 %copy-start.35 = (bf16[192,128]{1,0:T(8,128)(2,1)S(1)}, bf16[192,128]{1,0:T(8,128)(2,1)}, u32[]{:S(2)}) copy-start(bf16[192,128]{1,0:T(8,128)(2,1)} %get-tuple-element.334.placed_ref) | copy-start | bytes 147460
  201.7 23.6 %collective-permute-start.23 = (bf16[64,3584]{1,0:T(8,128)(2,1)}, bf16[64,3584]{1,0:T(8,128)(2,1)S(1)}, u32[]{:S(2)}, u32[]{:S(2)}) collective-permute-start(bf16[64,3584]{1,0:T(8,128)(2,1)} %get-tuple-element.311), channel_id=1, source_target_pairs={{0,12},{1,13},{2,14},{3,15},{4,8},{5,9},{6,10},{7,11},{8,4},{9,5},... | collective-permute-start | bytes 1376264 | tf_op jit(solution)/shard_map/ppermute | solution.py:286
  203.1 22.2 %collective-permute-start.24 = (bf16[48,3712]{1,0:T(8,128)(2,1)}, bf16[48,3712]{1,0:T(8,128)(2,1)S(1)}, u32[]{:S(2)}, u32[]{:S(2)}) collective-permute-start(bf16[48,3712]{1,0:T(8,128)(2,1)} %get-tuple-element.314), channel_id=1, source_target_pairs={{0,1},{1,0},{2,3},{3,2},{4,5},{5,4},{6,7},{7,6},{8,9},{9,8},{10,11... | collective-permute-start | bytes 1069064 | tf_op jit(solution)/shard_map/ppermute | solution.py:286
  203.4 21.8 %collective-permute-start.25 = (bf16[48,3712]{1,0:T(8,128)(2,1)}, bf16[48,3712]{1,0:T(8,128)(2,1)S(1)}, u32[]{:S(2)}, u32[]{:S(2)}) collective-permute-start(bf16[48,3712]{1,0:T(8,128)(2,1)} %get-tuple-element.315), channel_id=1, source_target_pairs={{0,2},{1,3},{2,0},{3,1},{4,6},{5,7},{6,4},{7,5},{8,10},{9,11},{10,... | collective-permute-start | bytes 1069064 | tf_op jit(solution)/shard_map/ppermute | solution.py:286
  203.6 21.6 %collective-permute-start.26 = (bf16[48,3712]{1,0:T(8,128)(2,1)S(1)}, bf16[48,3712]{1,0:T(8,128)(2,1)S(1)}, u32[]{:S(2)}, u32[]{:S(2)}) collective-permute-start(bf16[48,3712]{1,0:T(8,128)(2,1)S(1)} %copy-done.37), channel_id=1, source_target_pairs={{0,3},{1,2},{2,1},{3,0},{4,7},{5,6},{6,5},{7,4},{8,11},{9,10},{10,... | collective-permute-start | bytes 1069064 | tf_op jit(solution)/shard_map/ppermute | solution.py:286
  225.0 31.2 %copy-start.34 = (f32[128,16]{1,0:T(8,128)S(1)}, f32[128,16]{1,0:T(8,128)}, u32[]{:S(2)}) copy-start(f32[128,16]{1,0:T(8,128)} %get-tuple-element.362) | copy-start | bytes 24580
  225.0 32.1 %copy-start.5 = (bf16[128,3712]{1,0:T(8,128)(2,1)}, bf16[128,3712]{1,0:T(8,128)(2,1)S(1)}, u32[]{:S(2)}) copy-start(bf16[128,3712]{1,0:T(8,128)(2,1)S(1)} %collective-permute-done.22.refs_1_) | copy-start | bytes 2850820
  225.0 4.8 %collective-permute-start.30 = (bf16[128,128]{1,0:T(8,128)(2,1)S(1)}, bf16[128,128]{1,0:T(8,128)(2,1)S(1)}, u32[]{:S(2)}, u32[]{:S(2)}) collective-permute-start(bf16[128,128]{1,0:T(8,128)(2,1)S(1)} %copy-done.38), channel_id=1, source_target_pairs={{0,12},{1,13},{2,14},{3,15},{4,8},{5,9},{6,10},{7,11},{8,4},{9,5},... | collective-permute-start | bytes 98312 | tf_op jit(solution)/shard_map/ppermute | solution.py:286
  225.3 31.8 %copy-start.17 = (bf16[64,3584]{1,0:T(8,128)(2,1)}, bf16[64,3584]{1,0:T(8,128)(2,1)S(1)}, u32[]{:S(2)}) copy-start(bf16[64,3584]{1,0:T(8,128)(2,1)S(1)} %collective-permute-done.23.refs_2_) | copy-start | bytes 1376260
  225.3 24.5 %collective-permute-start.35 = (bf16[64,3584]{1,0:T(8,128)(2,1)S(1)}, bf16[64,3584]{1,0:T(8,128)(2,1)S(1)}, u32[]{:S(2)}, u32[]{:S(2)}) collective-permute-start(bf16[64,3584]{1,0:T(8,128)(2,1)S(1)} %copy-done.36), channel_id=1, source_target_pairs={{0,12},{1,13},{2,14},{3,15},{4,8},{5,9},{6,10},{7,11},{8,4},{9,5},... | collective-permute-start | bytes 1376264 | tf_op jit(solution)/shard_map/ppermute | solution.py:286
  227.5 2.3 collective-permute-start.27
  228.1 2.8 collective-permute-start.28
  228.3 3.4 %collective-permute-start.29 = (bf16[48,128]{1,0:T(8,128)(2,1)S(1)}, bf16[48,128]{1,0:T(8,128)(2,1)S(1)}, u32[]{:S(2)}, u32[]{:S(2)}) collective-permute-start(bf16[48,128]{1,0:T(8,128)(2,1)S(1)} %get-tuple-element.358), channel_id=1, source_target_pairs={{0,3},{1,2},{2,1},{3,0},{4,7},{5,6},{6,5},{7,4},{8,11},{9,10},{10,... | collective-permute-start | bytes 36872 | tf_op jit(solution)/shard_map/ppermute | solution.py:286
  231.7 9.3 %collective-permute-start.32 = (bf16[48,3712]{1,0:T(8,128)(2,1)}, bf16[48,3712]{1,0:T(8,128)(2,1)S(1)}, u32[]{:S(2)}, u32[]{:S(2)}) collective-permute-start(bf16[48,3712]{1,0:T(8,128)(2,1)} %get-tuple-element.342), channel_id=1, source_target_pairs={{0,1},{1,0},{2,3},{3,2},{4,5},{5,4},{6,7},{7,6},{8,9},{9,8},{10,11... | collective-permute-start | bytes 1069064 | tf_op jit(solution)/shard_map/ppermute | solution.py:286
  231.9 9.8 %collective-permute-start.33 = (bf16[48,3712]{1,0:T(8,128)(2,1)}, bf16[48,3712]{1,0:T(8,128)(2,1)S(1)}, u32[]{:S(2)}, u32[]{:S(2)}) collective-permute-start(bf16[48,3712]{1,0:T(8,128)(2,1)} %get-tuple-element.343), channel_id=1, source_target_pairs={{0,2},{1,3},{2,0},{3,1},{4,6},{5,7},{6,4},{7,5},{8,10},{9,11},{10,... | collective-permute-start | bytes 1069064 | tf_op jit(solution)/shard_map/ppermute | solution.py:286
  233.0 16.8 %collective-permute-start.34 = (bf16[48,3712]{1,0:T(8,128)(2,1)}, bf16[48,3712]{1,0:T(8,128)(2,1)S(1)}, u32[]{:S(2)}, u32[]{:S(2)}) collective-permute-start(bf16[48,3712]{1,0:T(8,128)(2,1)} %get-tuple-element.344), channel_id=1, source_target_pairs={{0,3},{1,2},{2,1},{3,0},{4,7},{5,6},{6,5},{7,4},{8,11},{9,10},{10,... | collective-permute-start | bytes 1069064 | tf_op jit(solution)/shard_map/ppermute | solution.py:286
  234.1 6.0 %collective-permute-start.31 = (bf16[128,128]{1,0:T(8,128)(2,1)S(1)}, bf16[128,128]{1,0:T(8,128)(2,1)S(1)}, u32[]{:S(2)}, u32[]{:S(2)}) collective-permute-start(bf16[128,128]{1,0:T(8,128)(2,1)S(1)} %convolution_convert_fusion), channel_id=1, source_target_pairs={{4,0},{5,1},{6,2},{7,3},{8,12},{9,13},{10,14},{11,15},{12,4},{13,5... | collective-permute-start | bytes 98312 | tf_op jit(solution)/shard_map/ppermute | solution.py:286
  253.4 30.8 %collective-permute-start.36 = (bf16[128,3584]{1,0:T(8,128)(2,1)}, bf16[128,3584]{1,0:T(8,128)(2,1)S(1)}, u32[]{:S(2)}, u32[]{:S(2)}) collective-permute-start(bf16[128,3584]{1,0:T(8,128)(2,1)} %get-tuple-element.351), channel_id=1, source_target_pairs={{4,0},{5,1},{6,2},{7,3},{8,12},{9,13},{10,14},{11,15},{12,4},{13,5... | collective-permute-start | bytes 2752520 | tf_op jit(solution)/shard_map/ppermute | solution.py:286
  257.1 27.0 %copy-start.31 = (bf16[128,16]{1,0:T(8,128)(2,1)}, bf16[128,16]{1,0:T(8,128)(2,1)S(1)}, u32[]{:S(2)}) copy-start(bf16[128,16]{1,0:T(8,128)(2,1)S(1)} %multiply_convert_fusion.logit_ref) | copy-start | bytes 12292
  (28 other events, 251.6 us)

commit v10 on v9

--- a/solution.py
+++ b/solution.py
@@ -401,11 +401,8 @@
             back_3 = spread(done_3[:plane])
             term_2b = send(part_2b, across(3 * plane))
             part_0, tag_0 = sum_rows(placed_0, back_0, width)
-            back_3, term_2b = join((back_3, term_2b))
-            part_3, _ = sum_rows(placed_3, back_3, width)
-            term_3 = send(part_3, swap_3)
+            tag_3, back_3[1], back_3[2] = join((tag_3, back_3[1], back_3[2]))
             tags = [tag_0, term_1[:, width:], tag_2, tag_3]
-            terms = [[part_0], [term_1], [term_2a, term_2b], [term_3]]
             done = [done_3]
         else:
             flag = jnp.zeros((1,), jnp.int32)
@@ -428,6 +425,10 @@
         share = width // devices
         router_part = router_part.reshape(experts, devices, share).transpose(1, 0, 2)
         router_got = lax.all_to_all(router_part, "expert", split_axis=0, concat_axis=0, tiled=True)
+        if layers == 4:
+            back_3, router_got, term_2b = join((back_3, router_got, term_2b))
+            part_3, _ = sum_rows(placed_3, back_3, width)
+            terms = [[part_0], [term_1], [term_2a, term_2b], [send(part_3, swap_3)]]
         router_grad = jnp.sum(router_got, axis=0).T
 
         in_grad = final_sum(d_logit, router_matrix.T, terms)

time: 291 us -> 297 us (1.021)
  waiting for transfers between devices: 96.2 us -> 123 us
  blocking collectives: 25.8 us -> 0 us
  starting transfers between devices: 38.8 us -> 42.6 us
    ppermute x37, waiting for transfers between devices: 96.2 us -> 123 us  [send(): return lax.ppermute(array, 'expert', pairs)]
    all_to_all x1 -> x0, blocking collectives: 25.8 us -> none  [shards(): lax.all_to_all(router_part, 'expert', split_axis=0, concat_axis=0, tiled=...]
    all_to_all x0 -> x1, starting transfers between devices: none -> 7.41 us  [shards(): lax.all_to_all(router_part, 'expert', split_axis=0, concat_axis=0, tiled=...]
    ppermute x37, starting transfers between devices: 38.8 us -> 35.2 us  [send(): return lax.ppermute(array, 'expert', pairs)]
  transfers between devices with their start and end apart: 37 -> 38, of which waited for: 15 -> 15; matrix products, arithmetic and copies ran while one was open for 2% -> 2% of each run, Pallas kernels for 34% -> 34%
where the time goes in v10:
time: 297 us; the launch traced here: 294 us
  waiting for transfers between devices  123 us (41%)
  Pallas kernels  110 us (37%)
  starting transfers between devices  42.6 us (14%)
  local copies, waits for them, and re-layouts  10 us (3%)
  other arithmetic  4.81 us (2%)
    ppermute x37, waiting for transfers between devices, send(): return lax.ppermute(array, 'expert', pairs)  123 us
    pallas_call x4, Pallas kernels, expert_rows(): pl.pallas_call(functools.partial(expert_kernel, len(carry), cap, width, r...  78.7 us
    ppermute x37, starting transfers between devices, send(): return lax.ppermute(array, 'expert', pairs)  35.2 us
    pallas_call x4, Pallas kernels, select_rows(): pl.pallas_call(functools.partial(select_kernel, parts, meta_at, slots_hel...  16.9 us
    pallas_call x4, Pallas kernels, sum_rows(): pl.pallas_call(functools.partial(sum_kernel, apart), out_shape=shapes, in...  10.9 us
    all_to_all x1, starting transfers between devices, shards(): lax.all_to_all(router_part, 'expert', split_axis=0, concat_axis=0, tiled=...  7.41 us
  transfers between devices with their start and end apart: 38, of which 15 were waited for; matrix products, arithmetic and copies ran while one was open for 2% of the time, Pallas kernels for 34%

profile of v10, /device:TPU:15, one launch (start us, length us, event | category | flops | bytes accessed | tf_op | source)
XLA Modules:
  0.0 294.3 jit_solution(4682281052002740721)
XLA Ops:
  1.7 2.2 fusion.14
  4.5 2.2 concatenate.8.refs_0_
  8.0 4.1 %shard_map.154 = (bf16[48,7296]{1,0:T(8,128)(2,1)}, bf16[48,7296]{1,0:T(8,128)(2,1)}, bf16[48,7296]{1,0:T(8,128)(2,1)}, bf16[48,7296]{1,0:T(8,128)(2,1)}, bf16[192,128]{1,0:T(8,128)(2,1)}) custom-call(s32[1]{0:T(128)} %bitcast.flag_ref, bf16[16,128]{1,0:T(8,128)(2,1)} %pad_convert_fusion.guide_ref, bf16[128,7296]{1,0:T(8,128)(2,1)} %copy-done), custom_call_target="tpu_custom_call" | custom-call | flops 1024 | bytes 1024 | tf_op jit(solution)/shard_map/pallas_call | solution.py:87
  13.0 1.4 collective-permute-start.3
  14.7 15.6 %collective-permute-done.2.refs_2_ = bf16[48,7296]{1,0:T(8,128)(2,1)S(1)} collective-permute-done((bf16[48,7296]{1,0:T(8,128)(2,1)}, bf16[48,7296]{1,0:T(8,128)(2,1)S(1)}, u32[]{:S(2)}, u32[]{:S(2)}) %collective-permute-start.2) | collective-permute-done | bytes 700448 | tf_op jit(solution)/shard_map/ppermute | solution.py:286
  30.4 15.4 %collective-permute-done.3.refs_3_ = bf16[48,7296]{1,0:T(8,128)(2,1)S(1)} collective-permute-done((bf16[48,7296]{1,0:T(8,128)(2,1)}, bf16[48,7296]{1,0:T(8,128)(2,1)S(1)}, u32[]{:S(2)}, u32[]{:S(2)}) %collective-permute-start.3) | collective-permute-done | bytes 700448 | tf_op jit(solution)/shard_map/ppermute | solution.py:286
  45.8 3.6 %collective-permute-done.refs_0_ = bf16[128,7296]{1,0:T(8,128)(2,1)} collective-permute-done((bf16[128,7296]{1,0:T(8,128)(2,1)S(1)}, bf16[128,7296]{1,0:T(8,128)(2,1)}, u32[]{:S(2)}, u32[]{:S(2)}) %collective-permute-start) | collective-permute-done | bytes 1867808 | tf_op jit(solution)/shard_map/ppermute | solution.py:286
  49.4 3.2 %collective-permute-start.4 = (bf16[128,7296]{1,0:T(8,128)(2,1)}, bf16[128,7296]{1,0:T(8,128)(2,1)S(1)}, u32[]{:S(2)}, u32[]{:S(2)}) collective-permute-start(bf16[128,7296]{1,0:T(8,128)(2,1)} %copy-done), channel_id=1, source_target_pairs={{4,8},{5,9},{6,10},{7,11},{8,4},{9,5},{10,6},{11,7},{20,24},{21,25... | collective-permute-start | bytes 5603336 | tf_op jit(solution)/shard_map/ppermute | solution.py:286
  52.6 2.6 collective-permute-start.5
  55.2 4.1 %shard_map.156 = (bf16[48,7296]{1,0:T(8,128)(2,1)}, bf16[48,7296]{1,0:T(8,128)(2,1)}, bf16[48,7296]{1,0:T(8,128)(2,1)}, bf16[48,7296]{1,0:T(8,128)(2,1)}, bf16[192,128]{1,0:T(8,128)(2,1)}) custom-call(s32[1]{0:T(128)} %bitcast.flag_ref, bf16[16,128]{1,0:T(8,128)(2,1)} %pad_convert_fusion.guide_ref, bf16[128,7296]{1,0:T(8,128)(2,1)} %collective-permute-done.refs_0_), custom_call_target="tpu_custom_call" | custom-call | flops 1024 | bytes 1024 | tf_op jit(solution)/shard_map/pallas_call | solution.py:87
  59.3 1.8 collective-permute-start.6
  61.4 1.4 collective-permute-start.8
  63.3 19.4 %shard_map.157 = (bf16[48,3712]{1,0:T(8,128)(2,1)}, bf16[48,3712]{1,0:T(8,128)(2,1)}, bf16[48,3712]{1,0:T(8,128)(2,1)}, bf16[48,3712]{1,0:T(8,128)(2,1)}, f32[32...) custom-call(f32[1,128]{1,0:T(1,128)} %compare_convert_fusion.mine_re, ...), custom_call_target="tpu_custom_call" | custom-call | flops 1024 | bytes 1024 | tf_op jit(solution)/shard_map/pallas_call | solution.py:234
  82.7 11.4 %collective-permute-done.8.refs_3_ = bf16[48,7296]{1,0:T(8,128)(2,1)} collective-permute-done((bf16[48,7296]{1,0:T(8,128)(2,1)}, bf16[48,7296]{1,0:T(8,128)(2,1)}, u32[]{:S(2)}, u32[]{:S(2)}) %collective-permute-start.8) | collective-permute-done | bytes 700448 | tf_op jit(solution)/shard_map/ppermute | solution.py:286
  94.1 1.3 copy-done.3
  95.4 4.7 %shard_map.155 = (bf16[48,7296]{1,0:T(8,128)(2,1)}, bf16[48,7296]{1,0:T(8,128)(2,1)}, bf16[48,7296]{1,0:T(8,128)(2,1)}, bf16[48,7296]{1,0:T(8,128)(2,1)}, bf16[192,128]{1,0:T(8,128)(2,1)}) custom-call(s32[1]{0:T(128)} %bitcast.flag_ref, bf16[16,128]{1,0:T(8,128)(2,1)} %pad_convert_fusion.guide_ref, bf16[128,7296]{1,0:T(8,128)(2,1)} %copy-done.3, ...), custom_call_target="tpu_custom_call" | custom-call | flops 1024 | bytes 1024 | tf_op jit(solution)/shard_map/pallas_call | solution.py:87
  100.1 2.1 collective-permute-start.10
  102.4 1.4 collective-permute-start.15
  103.8 19.8 %shard_map.159 = (bf16[48,3712]{1,0:T(8,128)(2,1)}, bf16[48,3712]{1,0:T(8,128)(2,1)}, bf16[48,3712]{1,0:T(8,128)(2,1)}, bf16[48,3712]{1,0:T(8,128)(2,1)}, f32[32...) custom-call(f32[1,128]{1,0:T(1,128)} %compare_convert_fusion.mine_re, ...), custom_call_target="tpu_custom_call" | custom-call | flops 1024 | bytes 1024 | tf_op jit(solution)/shard_map/pallas_call | solution.py:234
  124.2 1.7 collective-permute-start.14
  125.8 15.9 %collective-permute-done.9.refs_0_ = bf16[128,7296]{1,0:T(8,128)(2,1)S(1)} collective-permute-done((bf16[128,7296]{1,0:T(8,128)(2,1)S(1)}, bf16[128,7296]{1,0:T(8,128)(2,1)S(1)}, u32[]{:S(2)}, u32[]{:S(2)}) %collective-permute-start.9) | collective-permute-done | bytes 1867808 | tf_op jit(solution)/shard_map/ppermute | solution.py:286
  141.8 1.3 copy-done.4
  143.0 4.1 %shard_map.158 = (bf16[48,7296]{1,0:T(8,128)(2,1)}, bf16[48,7296]{1,0:T(8,128)(2,1)}, bf16[48,7296]{1,0:T(8,128)(2,1)}, bf16[48,7296]{1,0:T(8,128)(2,1)}, bf16[192,128]{1,0:T(8,128)(2,1)}) custom-call(s32[1]{0:T(128)} %bitcast.flag_ref, bf16[16,128]{1,0:T(8,128)(2,1)} %pad_convert_fusion.guide_ref, bf16[128,7296]{1,0:T(8,128)(2,1)} %copy-done.4), custom_call_target="tpu_custom_call" | custom-call | flops 1024 | bytes 1024 | tf_op jit(solution)/shard_map/pallas_call | solution.py:87
  147.2 2.9 collective-permute-done.14.refs_3_
  150.6 1.6 collective-permute-start.18
  152.2 2.8 shard_map.161
  155.0 1.2 collective-permute-start.22
  156.2 19.8 %shard_map.160 = (bf16[48,3712]{1,0:T(8,128)(2,1)}, bf16[48,3712]{1,0:T(8,128)(2,1)}, bf16[48,3712]{1,0:T(8,128)(2,1)}, bf16[48,3712]{1,0:T(8,128)(2,1)}, f32[32...) custom-call(f32[1,128]{1,0:T(1,128)} %compare_convert_fusion.mine_re, ...), custom_call_target="tpu_custom_call" | custom-call | flops 1024 | bytes 1024 | tf_op jit(solution)/shard_map/pallas_call | solution.py:234
  176.6 1.6 collective-permute-start.21
  178.2 5.4 %collective-permute-done.18.refs_3_ = bf16[48,7296]{1,0:T(8,128)(2,1)S(1)} collective-permute-done((bf16[48,7296]{1,0:T(8,128)(2,1)}, bf16[48,7296]{1,0:T(8,128)(2,1)S(1)}, u32[]{:S(2)}, u32[]{:S(2)}) %collective-permute-start.18) | collective-permute-done | bytes 700448 | tf_op jit(solution)/shard_map/ppermute | solution.py:286
  183.7 6.7 %collective-permute-done.20.refs_2_ = bf16[48,3712]{1,0:T(8,128)(2,1)S(1)} collective-permute-done((bf16[48,3712]{1,0:T(8,128)(2,1)}, bf16[48,3712]{1,0:T(8,128)(2,1)S(1)}, u32[]{:S(2)}, u32[]{:S(2)}) %collective-permute-start.20) | collective-permute-done | bytes 356384 | tf_op jit(solution)/shard_map/ppermute | solution.py:286
  190.3 8.0 %collective-permute-done.21.refs_3_ = bf16[48,3712]{1,0:T(8,128)(2,1)S(1)} collective-permute-done((bf16[48,3712]{1,0:T(8,128)(2,1)}, bf16[48,3712]{1,0:T(8,128)(2,1)S(1)}, u32[]{:S(2)}, u32[]{:S(2)}) %collective-permute-start.21) | collective-permute-done | bytes 356384 | tf_op jit(solution)/shard_map/ppermute | solution.py:286
  199.0 2.7 shard_map.163
  201.8 1.3 collective-permute-start.23
  203.6 1.6 collective-permute-start.26
  205.2 19.8 %shard_map.162 = (bf16[48,3712]{1,0:T(8,128)(2,1)}, bf16[48,3712]{1,0:T(8,128)(2,1)}, bf16[48,3712]{1,0:T(8,128)(2,1)}, bf16[48,3712]{1,0:T(8,128)(2,1)}, f32[32...) custom-call(f32[1,128]{1,0:T(1,128)} %compare_convert_fusion.mine_re, ...), custom_call_target="tpu_custom_call" | custom-call | flops 1024 | bytes 1024 | tf_op jit(solution)/shard_map/pallas_call | solution.py:234
  226.8 1.6 collective-permute-start.29
  229.1 1.0 collective-permute-done.29
  230.5 1.1 collective-permute-start.33
  231.8 2.3 collective-permute-start.31
  234.1 1.3 collective-permute-start.35
  235.4 2.7 shard_map.164
  238.1 2.5 collective-permute-done.33.refs_2_
  243.9 7.4 %all-to-all-start = ((f32[16,16,224]{2,1,0:T(8,128)}), f32[16,16,224]{2,1,0:T(8,128)S(1)}, u32[]{:S(2)}, u32[]{:S(2)}) async-start(f32[16,16,224]{2,1,0:T(8,128)} %bitcast.29), calls=%async_computation | async-start | bytes 524288 | tf_op jit(solution)/shard_map/all_to_all | solution.py:427
  251.9 11.7 %collective-permute-done.34.refs_3_ = bf16[48,3712]{1,0:T(8,128)(2,1)S(1)} collective-permute-done((bf16[48,3712]{1,0:T(8,128)(2,1)}, bf16[48,3712]{1,0:T(8,128)(2,1)S(1)}, u32[]{:S(2)}, u32[]{:S(2)}) %collective-permute-start.34) | collective-permute-done | bytes 356384 | tf_op jit(solution)/shard_map/ppermute | solution.py:286
  264.3 2.7 shard_map.165
  268.2 21.5 %collective-permute-done.36.refs_4_ = bf16[128,3584]{1,0:T(8,128)(2,1)S(1)} collective-permute-done((bf16[128,3584]{1,0:T(8,128)(2,1)}, bf16[128,3584]{1,0:T(8,128)(2,1)S(1)}, u32[]{:S(2)}, u32[]{:S(2)}) %collective-permute-start.36) | collective-permute-done | bytes 917536 | tf_op jit(solution)/shard_map/ppermute | solution.py:286
  290.6 3.7 %shard_map.166 = bf16[128,3584]{1,0:T(8,128)(2,1)} custom-call(bf16[128,16]{1,0:T(8,128)(2,1)} %copy-done.31, bf16[16,3584]{1,0:T(8,128)(2,1)} %bitcast.58, bf16[128,3584]{1,0:T(8,128)(2,1)} %get-tuple-element.346.refs_0_, bf16[128,3712]{1,0:T(8,128)(2,1)} %copy-done.5, bf16[64,3584]{1,0:T(8,128)(2,1)} %copy-done.17, bf16[64,3584]{1,0:T(8,128)(2,1)} %copy-done.18, ...), custom_call_target="tpu_custom_call" | custom-call | flops 1024 | bytes 1024 | tf_op jit(solution)/shard_map/pallas_call | solution.py:146
  (139 shorter events, 17.8 us)
Async XLA Ops:
  6.7 42.6 %collective-permute-start = (bf16[128,7296]{1,0:T(8,128)(2,1)S(1)}, bf16[128,7296]{1,0:T(8,128)(2,1)}, u32[]{:S(2)}, u32[]{:S(2)}) collective-permute-start(bf16[128,7296]{1,0:T(8,128)(2,1)S(1)} %concatenate.8.refs_0_), channel_id=1, source_target_pairs={{0,8},{1,9},{2,10},{3,11},{12,4},{13,5},{14,6},{15,7},{4,0},{5,1},... | collective-permute-start | bytes 5603336 | tf_op jit(solution)/shard_map/ppermute | solution.py:286
  12.1 2.7 collective-permute-start.1
  12.7 17.6 %collective-permute-start.2 = (bf16[48,7296]{1,0:T(8,128)(2,1)}, bf16[48,7296]{1,0:T(8,128)(2,1)S(1)}, u32[]{:S(2)}, u32[]{:S(2)}) collective-permute-start(bf16[48,7296]{1,0:T(8,128)(2,1)} %get-tuple-element.194), channel_id=1, source_target_pairs={{0,2},{1,3},{2,0},{3,1},{4,6},{5,7},{6,4},{7,5},{8,10},{9,11},{10,... | collective-permute-start | bytes 2101256 | tf_op jit(solution)/shard_map/ppermute | solution.py:286
  13.0 32.8 %collective-permute-start.3 = (bf16[48,7296]{1,0:T(8,128)(2,1)}, bf16[48,7296]{1,0:T(8,128)(2,1)S(1)}, u32[]{:S(2)}, u32[]{:S(2)}) collective-permute-start(bf16[48,7296]{1,0:T(8,128)(2,1)} %get-tuple-element.195), channel_id=1, source_target_pairs={{0,3},{1,2},{2,1},{3,0},{4,7},{5,6},{6,5},{7,4},{8,11},{9,10},{10,... | collective-permute-start | bytes 2101256 | tf_op jit(solution)/shard_map/ppermute | solution.py:286
  14.7 34.6 %copy-start.14 = (bf16[48,7296]{1,0:T(8,128)(2,1)}, bf16[48,7296]{1,0:T(8,128)(2,1)S(1)}, u32[]{:S(2)}) copy-start(bf16[48,7296]{1,0:T(8,128)(2,1)S(1)} %collective-permute-done.1.refs_1_) | copy-start | bytes 2101252
  49.4 44.7 %collective-permute-start.4 = (bf16[128,7296]{1,0:T(8,128)(2,1)}, bf16[128,7296]{1,0:T(8,128)(2,1)S(1)}, u32[]{:S(2)}, u32[]{:S(2)}) collective-permute-start(bf16[128,7296]{1,0:T(8,128)(2,1)} %copy-done), channel_id=1, source_target_pairs={{4,8},{5,9},{6,10},{7,11},{8,4},{9,5},{10,6},{11,7},{20,24},{21,25... | collective-permute-start | bytes 5603336 | tf_op jit(solution)/shard_map/ppermute | solution.py:286
  52.6 41.5 %collective-permute-start.5 = (bf16[128,7296]{1,0:T(8,128)(2,1)}, bf16[128,7296]{1,0:T(8,128)(2,1)}, u32[]{:S(2)}, u32[]{:S(2)}) collective-permute-start(bf16[128,7296]{1,0:T(8,128)(2,1)} %collective-permute-done.refs_0_), channel_id=1, source_target_pairs={{4,0},{5,1},{6,2},{7,3},{8,12},{9,13},{10,14},{11,15},{20,16},{21,... | collective-permute-start | bytes 5603336 | tf_op jit(solution)/shard_map/ppermute | solution.py:286
  59.3 23.4 %collective-permute-start.6 = (bf16[48,7296]{1,0:T(8,128)(2,1)}, bf16[48,7296]{1,0:T(8,128)(2,1)S(1)}, u32[]{:S(2)}, u32[]{:S(2)}) collective-permute-start(bf16[48,7296]{1,0:T(8,128)(2,1)} %get-tuple-element.203), channel_id=1, source_target_pairs={{0,1},{1,0},{2,3},{3,2},{4,5},{5,4},{6,7},{7,6},{8,9},{9,8},{10,11... | collective-permute-start | bytes 2101256 | tf_op jit(solution)/shard_map/ppermute | solution.py:286
  61.1 21.6 %collective-permute-start.7 = (bf16[48,7296]{1,0:T(8,128)(2,1)}, bf16[48,7296]{1,0:T(8,128)(2,1)}, u32[]{:S(2)}, u32[]{:S(2)}) collective-permute-start(bf16[48,7296]{1,0:T(8,128)(2,1)} %get-tuple-element.204), channel_id=1, source_target_pairs={{0,2},{1,3},{2,0},{3,1},{4,6},{5,7},{6,4},{7,5},{8,10},{9,11},{10,... | collective-permute-start | bytes 2101256 | tf_op jit(solution)/shard_map/ppermute | solution.py:286
  61.4 32.7 %collective-permute-start.8 = (bf16[48,7296]{1,0:T(8,128)(2,1)}, bf16[48,7296]{1,0:T(8,128)(2,1)}, u32[]{:S(2)}, u32[]{:S(2)}) collective-permute-start(bf16[48,7296]{1,0:T(8,128)(2,1)} %get-tuple-element.205), channel_id=1, source_target_pairs={{0,3},{1,2},{2,1},{3,0},{4,7},{5,6},{6,5},{7,4},{8,11},{9,10},{10,... | collective-permute-start | bytes 2101256 | tf_op jit(solution)/shard_map/ppermute | solution.py:286
  100.0 41.7 %collective-permute-start.9 = (bf16[128,7296]{1,0:T(8,128)(2,1)S(1)}, bf16[128,7296]{1,0:T(8,128)(2,1)S(1)}, u32[]{:S(2)}, u32[]{:S(2)}) collective-permute-start(bf16[128,7296]{1,0:T(8,128)(2,1)S(1)} %copy-done.1), channel_id=1, source_target_pairs={{0,4},{1,5},{2,6},{3,7},{12,8},{13,9},{14,10},{15,11},{4,12},{5,13... | collective-permute-start | bytes 5603336 | tf_op jit(solution)/shard_map/ppermute | solution.py:286
  100.1 23.6 %collective-permute-start.10 = (bf16[48,7296]{1,0:T(8,128)(2,1)}, bf16[48,7296]{1,0:T(8,128)(2,1)S(1)}, u32[]{:S(2)}, u32[]{:S(2)}) collective-permute-start(bf16[48,7296]{1,0:T(8,128)(2,1)} %get-tuple-element.244), channel_id=1, source_target_pairs={{0,1},{1,0},{2,3},{3,2},{4,5},{5,4},{6,7},{7,6},{8,9},{9,8},{10,11... | collective-permute-start | bytes 2101256 | tf_op jit(solution)/shard_map/ppermute | solution.py:286
  102.2 21.5 %collective-permute-start.11 = (bf16[48,7296]{1,0:T(8,128)(2,1)}, bf16[48,7296]{1,0:T(8,128)(2,1)S(1)}, u32[]{:S(2)}, u32[]{:S(2)}) collective-permute-start(bf16[48,7296]{1,0:T(8,128)(2,1)} %get-tuple-element.245), channel_id=1, source_target_pairs={{0,2},{1,3},{2,0},{3,1},{4,6},{5,7},{6,4},{7,5},{8,10},{9,11},{10,... | collective-permute-start | bytes 2101256 | tf_op jit(solution)/shard_map/ppermute | solution.py:286
  102.4 44.7 %collective-permute-start.15 = (bf16[48,7296]{1,0:T(8,128)(2,1)}, bf16[48,7296]{1,0:T(8,128)(2,1)S(1)}, u32[]{:S(2)}, u32[]{:S(2)}) collective-permute-start(bf16[48,7296]{1,0:T(8,128)(2,1)} %get-tuple-element.253), channel_id=1, source_target_pairs={{0,3},{1,2},{2,1},{3,0},{4,7},{5,6},{6,5},{7,4},{8,11},{9,10},{10,... | collective-permute-start | bytes 2101256 | tf_op jit(solution)/shard_map/ppermute | solution.py:286
  123.6 32.6 %copy-start.8 = (bf16[48,7296]{1,0:T(8,128)(2,1)}, bf16[48,7296]{1,0:T(8,128)(2,1)S(1)}, u32[]{:S(2)}) copy-start(bf16[48,7296]{1,0:T(8,128)(2,1)S(1)} %collective-permute-done.10.refs_1_) | copy-start | bytes 2101252
  123.6 32.6 %copy-start.10 = (bf16[48,7296]{1,0:T(8,128)(2,1)}, bf16[48,7296]{1,0:T(8,128)(2,1)S(1)}, u32[]{:S(2)}) copy-start(bf16[48,7296]{1,0:T(8,128)(2,1)S(1)} %collective-permute-done.11.refs_2_) | copy-start | bytes 2101252
  123.6 23.5 %collective-permute-start.12 = (bf16[48,3712]{1,0:T(8,128)(2,1)}, bf16[48,3712]{1,0:T(8,128)(2,1)S(1)}, u32[]{:S(2)}, u32[]{:S(2)}) collective-permute-start(bf16[48,3712]{1,0:T(8,128)(2,1)} %get-tuple-element.247), channel_id=1, source_target_pairs={{0,1},{1,0},{2,3},{3,2},{4,5},{5,4},{6,7},{7,6},{8,9},{9,8},{10,11... | collective-permute-start | bytes 1069064 | tf_op jit(solution)/shard_map/ppermute | solution.py:286
  123.9 23.2 %collective-permute-start.13 = (bf16[48,3712]{1,0:T(8,128)(2,1)}, bf16[48,3712]{1,0:T(8,128)(2,1)S(1)}, u32[]{:S(2)}, u32[]{:S(2)}) collective-permute-start(bf16[48,3712]{1,0:T(8,128)(2,1)} %get-tuple-element.248), channel_id=1, source_target_pairs={{0,2},{1,3},{2,0},{3,1},{4,6},{5,7},{6,4},{7,5},{8,10},{9,11},{10,... | collective-permute-start | bytes 1069064 | tf_op jit(solution)/shard_map/ppermute | solution.py:286
  124.2 25.9 %collective-permute-start.14 = (bf16[48,3712]{1,0:T(8,128)(2,1)}, bf16[48,3712]{1,0:T(8,128)(2,1)S(1)}, u32[]{:S(2)}, u32[]{:S(2)}) collective-permute-start(bf16[48,3712]{1,0:T(8,128)(2,1)} %get-tuple-element.249), channel_id=1, source_target_pairs={{0,3},{1,2},{2,1},{3,0},{4,7},{5,6},{6,5},{7,4},{8,11},{9,10},{10,... | collective-permute-start | bytes 1069064 | tf_op jit(solution)/shard_map/ppermute | solution.py:286
  150.1 25.9 %collective-permute-start.16 = (bf16[48,7296]{1,0:T(8,128)(2,1)}, bf16[48,7296]{1,0:T(8,128)(2,1)S(1)}, u32[]{:S(2)}, u32[]{:S(2)}) collective-permute-start(bf16[48,7296]{1,0:T(8,128)(2,1)} %get-tuple-element.271), channel_id=1, source_target_pairs={{0,1},{1,0},{2,3},{3,2},{4,5},{5,4},{6,7},{7,6},{8,9},{9,8},{10,11... | collective-permute-start | bytes 2101256 | tf_op jit(solution)/shard_map/ppermute | solution.py:286
  150.4 25.6 %collective-permute-start.17 = (bf16[48,7296]{1,0:T(8,128)(2,1)}, bf16[48,7296]{1,0:T(8,128)(2,1)S(1)}, u32[]{:S(2)}, u32[]{:S(2)}) collective-permute-start(bf16[48,7296]{1,0:T(8,128)(2,1)} %get-tuple-element.272), channel_id=1, source_target_pairs={{0,2},{1,3},{2,0},{3,1},{4,6},{5,7},{6,4},{7,5},{8,10},{9,11},{10,... | collective-permute-start | bytes 2101256 | tf_op jit(solution)/shard_map/ppermute | solution.py:286
  150.6 33.0 %collective-permute-start.18 = (bf16[48,7296]{1,0:T(8,128)(2,1)}, bf16[48,7296]{1,0:T(8,128)(2,1)S(1)}, u32[]{:S(2)}, u32[]{:S(2)}) collective-permute-start(bf16[48,7296]{1,0:T(8,128)(2,1)} %get-tuple-element.279), channel_id=1, source_target_pairs={{0,3},{1,2},{2,1},{3,0},{4,7},{5,6},{6,5},{7,4},{8,11},{9,10},{10,... | collective-permute-start | bytes 2101256 | tf_op jit(solution)/shard_map/ppermute | solution.py:286
  155.0 48.4 %copy-start.37 = (bf16[48,3712]{1,0:T(8,128)(2,1)S(1)}, bf16[48,3712]{1,0:T(8,128)(2,1)}, u32[]{:S(2)}) copy-start(bf16[48,3712]{1,0:T(8,128)(2,1)} %get-tuple-element.319) | copy-start | bytes 1069060
  155.0 48.7 %copy-start.36 = (bf16[48,3712]{1,0:T(8,128)(2,1)S(1)}, bf16[48,3712]{1,0:T(8,128)(2,1)}, u32[]{:S(2)}) copy-start(bf16[48,3712]{1,0:T(8,128)(2,1)} %get-tuple-element.320) | copy-start | bytes 1069060
  155.0 70.0 %collective-permute-start.22 = (bf16[128,3712]{1,0:T(8,128)(2,1)}, bf16[128,3712]{1,0:T(8,128)(2,1)S(1)}, u32[]{:S(2)}, u32[]{:S(2)}) collective-permute-start(bf16[128,3712]{1,0:T(8,128)(2,1)} %shard_map.161), channel_id=1, source_target_pairs={{0,4},{1,5},{2,6},{3,7},{12,8},{13,9},{14,10},{15,11},{4,12},{5,13... | collective-permute-start | bytes 2850824 | tf_op jit(solution)/shard_map/ppermute | solution.py:286
  176.0 29.2 %copy-start.7 = (bf16[48,7296]{1,0:T(8,128)(2,1)}, bf16[48,7296]{1,0:T(8,128)(2,1)S(1)}, u32[]{:S(2)}) copy-start(bf16[48,7296]{1,0:T(8,128)(2,1)S(1)} %collective-permute-done.16.refs_1_) | copy-start | bytes 2101252
  176.0 29.2 %copy-start.9 = (bf16[48,7296]{1,0:T(8,128)(2,1)}, bf16[48,7296]{1,0:T(8,128)(2,1)S(1)}, u32[]{:S(2)}) copy-start(bf16[48,7296]{1,0:T(8,128)(2,1)S(1)} %collective-permute-done.17.refs_2_) | copy-start | bytes 2101252
  176.0 7.6 %collective-permute-start.19 = (bf16[48,3712]{1,0:T(8,128)(2,1)}, bf16[48,3712]{1,0:T(8,128)(2,1)S(1)}, u32[]{:S(2)}, u32[]{:S(2)}) collective-permute-start(bf16[48,3712]{1,0:T(8,128)(2,1)} %get-tuple-element.286), channel_id=1, source_target_pairs={{0,1},{1,0},{2,3},{3,2},{4,5},{5,4},{6,7},{7,6},{8,9},{9,8},{10,11... | collective-permute-start | bytes 1069064 | tf_op jit(solution)/shard_map/ppermute | solution.py:286
  176.4 14.0 %collective-permute-start.20 = (bf16[48,3712]{1,0:T(8,128)(2,1)}, bf16[48,3712]{1,0:T(8,128)(2,1)S(1)}, u32[]{:S(2)}, u32[]{:S(2)}) collective-permute-start(bf16[48,3712]{1,0:T(8,128)(2,1)} %get-tuple-element.287), channel_id=1, source_target_pairs={{0,2},{1,3},{2,0},{3,1},{4,6},{5,7},{6,4},{7,5},{8,10},{9,11},{10,... | collective-permute-start | bytes 1069064 | tf_op jit(solution)/shard_map/ppermute | solution.py:286
  176.6 21.7 %collective-permute-start.21 = (bf16[48,3712]{1,0:T(8,128)(2,1)}, bf16[48,3712]{1,0:T(8,128)(2,1)S(1)}, u32[]{:S(2)}, u32[]{:S(2)}) collective-permute-start(bf16[48,3712]{1,0:T(8,128)(2,1)} %get-tuple-element.288), channel_id=1, source_target_pairs={{0,3},{1,2},{2,1},{3,0},{4,7},{5,6},{6,5},{7,4},{8,11},{9,10},{10,... | collective-permute-start | bytes 1069064 | tf_op jit(solution)/shard_map/ppermute | solution.py:286
  201.8 29.9 %copy-start.35 = (bf16[192,128]{1,0:T(8,128)(2,1)S(1)}, bf16[192,128]{1,0:T(8,128)(2,1)}, u32[]{:S(2)}) copy-start(bf16[192,128]{1,0:T(8,128)(2,1)} %get-tuple-element.338.placed_ref) | copy-start | bytes 147460
  201.8 23.5 %collective-permute-start.23 = (bf16[64,3584]{1,0:T(8,128)(2,1)}, bf16[64,3584]{1,0:T(8,128)(2,1)S(1)}, u32[]{:S(2)}, u32[]{:S(2)}) collective-permute-start(bf16[64,3584]{1,0:T(8,128)(2,1)} %get-tuple-element.315), channel_id=1, source_target_pairs={{0,12},{1,13},{2,14},{3,15},{4,8},{5,9},{6,10},{7,11},{8,4},{9,5},... | collective-permute-start | bytes 1376264 | tf_op jit(solution)/shard_map/ppermute | solution.py:286
  203.1 22.2 %collective-permute-start.24 = (bf16[48,3712]{1,0:T(8,128)(2,1)}, bf16[48,3712]{1,0:T(8,128)(2,1)S(1)}, u32[]{:S(2)}, u32[]{:S(2)}) collective-permute-start(bf16[48,3712]{1,0:T(8,128)(2,1)} %get-tuple-element.318), channel_id=1, source_target_pairs={{0,1},{1,0},{2,3},{3,2},{4,5},{5,4},{6,7},{7,6},{8,9},{9,8},{10,11... | collective-permute-start | bytes 1069064 | tf_op jit(solution)/shard_map/ppermute | solution.py:286
  203.4 21.9 %collective-permute-start.25 = (bf16[48,3712]{1,0:T(8,128)(2,1)S(1)}, bf16[48,3712]{1,0:T(8,128)(2,1)S(1)}, u32[]{:S(2)}, u32[]{:S(2)}) collective-permute-start(bf16[48,3712]{1,0:T(8,128)(2,1)S(1)} %copy-done.37), channel_id=1, source_target_pairs={{0,2},{1,3},{2,0},{3,1},{4,6},{5,7},{6,4},{7,5},{8,10},{9,11},{10,... | collective-permute-start | bytes 1069064 | tf_op jit(solution)/shard_map/ppermute | solution.py:286
  203.6 21.6 %collective-permute-start.26 = (bf16[48,3712]{1,0:T(8,128)(2,1)S(1)}, bf16[48,3712]{1,0:T(8,128)(2,1)S(1)}, u32[]{:S(2)}, u32[]{:S(2)}) collective-permute-start(bf16[48,3712]{1,0:T(8,128)(2,1)S(1)} %copy-done.36), channel_id=1, source_target_pairs={{0,3},{1,2},{2,1},{3,0},{4,7},{5,6},{6,5},{7,4},{8,11},{9,10},{10,... | collective-permute-start | bytes 1069064 | tf_op jit(solution)/shard_map/ppermute | solution.py:286
  225.0 3.3 %collective-permute-start.30 = (bf16[128,128]{1,0:T(8,128)(2,1)S(1)}, bf16[128,128]{1,0:T(8,128)(2,1)S(1)}, u32[]{:S(2)}, u32[]{:S(2)}) collective-permute-start(bf16[128,128]{1,0:T(8,128)(2,1)S(1)} %copy-done.38), channel_id=1, source_target_pairs={{0,12},{1,13},{2,14},{3,15},{4,8},{5,9},{6,10},{7,11},{8,4},{9,5},... | collective-permute-start | bytes 98312 | tf_op jit(solution)/shard_map/ppermute | solution.py:286
  226.2 2.1 collective-permute-start.27
  226.6 2.5 collective-permute-start.28
  226.8 3.3 %collective-permute-start.29 = (bf16[48,128]{1,0:T(8,128)(2,1)S(1)}, bf16[48,128]{1,0:T(8,128)(2,1)S(1)}, u32[]{:S(2)}, u32[]{:S(2)}) collective-permute-start(bf16[48,128]{1,0:T(8,128)(2,1)S(1)} %get-tuple-element.366), channel_id=1, source_target_pairs={{0,3},{1,2},{2,1},{3,0},{4,7},{5,6},{6,5},{7,4},{8,11},{9,10},{10,... | collective-permute-start | bytes 36872 | tf_op jit(solution)/shard_map/ppermute | solution.py:286
  230.1 8.0 %collective-permute-start.32 = (bf16[48,3712]{1,0:T(8,128)(2,1)}, bf16[48,3712]{1,0:T(8,128)(2,1)S(1)}, u32[]{:S(2)}, u32[]{:S(2)}) collective-permute-start(bf16[48,3712]{1,0:T(8,128)(2,1)} %get-tuple-element.343), channel_id=1, source_target_pairs={{0,1},{1,0},{2,3},{3,2},{4,5},{5,4},{6,7},{7,6},{8,9},{9,8},{10,11... | collective-permute-start | bytes 1069064 | tf_op jit(solution)/shard_map/ppermute | solution.py:286
  230.5 10.1 %collective-permute-start.33 = (bf16[48,3712]{1,0:T(8,128)(2,1)}, bf16[48,3712]{1,0:T(8,128)(2,1)S(1)}, u32[]{:S(2)}, u32[]{:S(2)}) collective-permute-start(bf16[48,3712]{1,0:T(8,128)(2,1)} %get-tuple-element.344), channel_id=1, source_target_pairs={{0,2},{1,3},{2,0},{3,1},{4,6},{5,7},{6,4},{7,5},{8,10},{9,11},{10,... | collective-permute-start | bytes 1069064 | tf_op jit(solution)/shard_map/ppermute | solution.py:286
  231.8 6.3 %collective-permute-start.31 = (bf16[128,128]{1,0:T(8,128)(2,1)S(1)}, bf16[128,128]{1,0:T(8,128)(2,1)S(1)}, u32[]{:S(2)}, u32[]{:S(2)}) collective-permute-start(bf16[128,128]{1,0:T(8,128)(2,1)S(1)} %convolution_convert_fusion), channel_id=1, source_target_pairs={{4,0},{5,1},{6,2},{7,3},{8,12},{9,13},{10,14},{11,15},{12,4},{13,5... | collective-permute-start | bytes 98312 | tf_op jit(solution)/shard_map/ppermute | solution.py:286
  234.1 29.5 %collective-permute-start.35 = (bf16[64,3584]{1,0:T(8,128)(2,1)}, bf16[64,3584]{1,0:T(8,128)(2,1)S(1)}, u32[]{:S(2)}, u32[]{:S(2)}) collective-permute-start(bf16[64,3584]{1,0:T(8,128)(2,1)} %get-tuple-element.352), channel_id=1, source_target_pairs={{0,12},{1,13},{2,14},{3,15},{4,8},{5,9},{6,10},{7,11},{8,4},{9,5},... | collective-permute-start | bytes 1376264 | tf_op jit(solution)/shard_map/ppermute | solution.py:286
  242.6 24.5 %copy-start.31 = (bf16[128,16]{1,0:T(8,128)(2,1)}, bf16[128,16]{1,0:T(8,128)(2,1)S(1)}, u32[]{:S(2)}) copy-start(bf16[128,16]{1,0:T(8,128)(2,1)S(1)} %multiply_convert_fusion.logit_ref) | copy-start | bytes 12292
  243.9 19.7 %all-to-all-start = ((f32[16,16,224]{2,1,0:T(8,128)}), f32[16,16,224]{2,1,0:T(8,128)S(1)}, u32[]{:S(2)}, u32[]{:S(2)}) async-start(f32[16,16,224]{2,1,0:T(8,128)} %bitcast.29), calls=%async_computation | async-start | bytes 524288 | tf_op jit(solution)/shard_map/all_to_all | solution.py:427
  251.3 12.3 %collective-permute-start.34 = (bf16[48,3712]{1,0:T(8,128)(2,1)}, bf16[48,3712]{1,0:T(8,128)(2,1)S(1)}, u32[]{:S(2)}, u32[]{:S(2)}) collective-permute-start(bf16[48,3712]{1,0:T(8,128)(2,1)} %get-tuple-element.351), channel_id=1, source_target_pairs={{0,3},{1,2},{2,1},{3,0},{4,7},{5,6},{6,5},{7,4},{8,11},{9,10},{10,... | collective-permute-start | bytes 1069064 | tf_op jit(solution)/shard_map/ppermute | solution.py:286
  263.6 26.1 %copy-start.18 = (bf16[64,3584]{1,0:T(8,128)(2,1)}, bf16[64,3584]{1,0:T(8,128)(2,1)S(1)}, u32[]{:S(2)}) copy-start(bf16[64,3584]{1,0:T(8,128)(2,1)S(1)} %collective-permute-done.35.refs_3_) | copy-start | bytes 1376260
  267.0 22.7 %collective-permute-start.36 = (bf16[128,3584]{1,0:T(8,128)(2,1)}, bf16[128,3584]{1,0:T(8,128)(2,1)S(1)}, u32[]{:S(2)}, u32[]{:S(2)}) collective-permute-start(bf16[128,3584]{1,0:T(8,128)(2,1)} %get-tuple-element.358), channel_id=1, source_target_pairs={{4,0},{5,1},{6,2},{7,3},{8,12},{9,13},{10,14},{11,15},{12,4},{13,5... | collective-permute-start | bytes 2752520 | tf_op jit(solution)/shard_map/ppermute | solution.py:286
  (29 other events, 255.6 us)

commit v11 on v8

--- a/solution.py
+++ b/solution.py
@@ -381,7 +381,7 @@
             (part_1,) = sum_rows(placed_1, back_1, wide)
             term_1 = send(part_1, along([(0, 1), (3, 2), (1, 3), (2, 0)]))
             got_3, part_1, back_2, done_0 = join((got_3, part_1, back_2, done_0))
-            part_2a, part_2b, tag_2 = sum_rows(placed_2, back_2, width, (tok * 5 // 8, tok * 3 // 8))
+            part_2a, part_2b, tag_2 = sum_rows(placed_2, back_2, width, (tok // 2, tok // 2))
             tag_2 = send(tag_2, across(3 * plane))
             term_2a = send(part_2a, across(3 * plane))
             back_0 = spread(done_0[:plane])

time: 289 us -> 288 us (level)
  transfers between devices with their start and end apart: 34 -> 34, of which waited for: 13 -> 14; matrix products, arithmetic and copies ran while one was open for 2% -> 2% of each run, Pallas kernels for 36% -> 36%
where the time goes in v11:
time: 288 us; the launch traced here: 286 us
  Pallas kernels  110 us (38%)
  waiting for transfers between devices  105 us (36%)
  starting transfers between devices  31 us (11%)
  blocking collectives  22.8 us (8%)
  local copies, waits for them, and re-layouts  8.27 us (3%)
  other arithmetic  4.88 us (2%)
    ppermute x34, waiting for transfers between devices, send(): return lax.ppermute(array, 'expert', pairs)  105 us
    pallas_call x4, Pallas kernels, expert_rows(): pl.pallas_call(functools.partial(expert_kernel, len(carry), cap, width, r...  78.7 us
    ppermute x34, starting transfers between devices, send(): return lax.ppermute(array, 'expert', pairs)  31 us
    all_to_all x1, blocking collectives, shards(): lax.all_to_all(router_part, 'expert', split_axis=0, concat_axis=0, tiled=...  22.8 us
    pallas_call x4, Pallas kernels, select_rows(): pl.pallas_call(functools.partial(select_kernel, parts, meta_at, slots_hel...  17 us
    pallas_call x4, Pallas kernels, sum_rows(): pl.pallas_call(functools.partial(sum_kernel, apart), out_shape=shapes, in...  11 us
  transfers between devices with their start and end apart: 34, of which 14 were waited for; matrix products, arithmetic and copies ran while one was open for 2% of the time, Pallas kernels for 36%

profile of v11, /device:TPU:15, one launch (start us, length us, event | category | flops | bytes accessed | tf_op | source)
XLA Modules:
  0.0 285.6 jit_solution(10883774685713266601)
XLA Ops:
  1.7 2.2 fusion.6
  4.5 2.2 concatenate.5.refs_0_
  8.0 4.1 %shard_map.154 = (bf16[48,7296]{1,0:T(8,128)(2,1)}, bf16[48,7296]{1,0:T(8,128)(2,1)}, bf16[48,7296]{1,0:T(8,128)(2,1)}, bf16[48,7296]{1,0:T(8,128)(2,1)}, bf16[192,128]{1,0:T(8,128)(2,1)}) custom-call(s32[1]{0:T(128)} %bitcast.flag_ref, bf16[16,128]{1,0:T(8,128)(2,1)} %pad_convert_fusion.guide_ref, bf16[128,7296]{1,0:T(8,128)(2,1)} %copy-done), custom_call_target="tpu_custom_call" | custom-call | flops 1024 | bytes 1024 | tf_op jit(solution)/shard_map/pallas_call | solution.py:87
  13.0 1.4 collective-permute-start.3
  14.8 15.6 %collective-permute-done.2.refs_2_ = bf16[48,7296]{1,0:T(8,128)(2,1)S(1)} collective-permute-done((bf16[48,7296]{1,0:T(8,128)(2,1)}, bf16[48,7296]{1,0:T(8,128)(2,1)S(1)}, u32[]{:S(2)}, u32[]{:S(2)}) %collective-permute-start.2) | collective-permute-done | bytes 700448 | tf_op jit(solution)/shard_map/ppermute | solution.py:282
  30.4 15.4 %collective-permute-done.3.refs_3_ = bf16[48,7296]{1,0:T(8,128)(2,1)S(1)} collective-permute-done((bf16[48,7296]{1,0:T(8,128)(2,1)}, bf16[48,7296]{1,0:T(8,128)(2,1)S(1)}, u32[]{:S(2)}, u32[]{:S(2)}) %collective-permute-start.3) | collective-permute-done | bytes 700448 | tf_op jit(solution)/shard_map/ppermute | solution.py:282
  45.8 3.6 %collective-permute-done.refs_0_ = bf16[128,7296]{1,0:T(8,128)(2,1)} collective-permute-done((bf16[128,7296]{1,0:T(8,128)(2,1)S(1)}, bf16[128,7296]{1,0:T(8,128)(2,1)}, u32[]{:S(2)}, u32[]{:S(2)}) %collective-permute-start) | collective-permute-done | bytes 1867808 | tf_op jit(solution)/shard_map/ppermute | solution.py:282
  49.4 3.2 %collective-permute-start.4 = (bf16[128,7296]{1,0:T(8,128)(2,1)}, bf16[128,7296]{1,0:T(8,128)(2,1)S(1)}, u32[]{:S(2)}, u32[]{:S(2)}) collective-permute-start(bf16[128,7296]{1,0:T(8,128)(2,1)} %copy-done), channel_id=1, source_target_pairs={{4,8},{5,9},{6,10},{7,11},{8,4},{9,5},{10,6},{11,7},{20,24},{21,25... | collective-permute-start | bytes 5603336 | tf_op jit(solution)/shard_map/ppermute | solution.py:282
  52.6 2.6 collective-permute-start.5
  55.2 4.1 %shard_map.156 = (bf16[48,7296]{1,0:T(8,128)(2,1)}, bf16[48,7296]{1,0:T(8,128)(2,1)}, bf16[48,7296]{1,0:T(8,128)(2,1)}, bf16[48,7296]{1,0:T(8,128)(2,1)}, bf16[192,128]{1,0:T(8,128)(2,1)}) custom-call(s32[1]{0:T(128)} %bitcast.flag_ref, bf16[16,128]{1,0:T(8,128)(2,1)} %pad_convert_fusion.guide_ref, bf16[128,7296]{1,0:T(8,128)(2,1)} %collective-permute-done.refs_0_), custom_call_target="tpu_custom_call" | custom-call | flops 1024 | bytes 1024 | tf_op jit(solution)/shard_map/pallas_call | solution.py:87
  59.3 1.8 collective-permute-start.6
  61.4 1.4 collective-permute-start.8
  63.4 19.4 %shard_map.157 = (bf16[48,3712]{1,0:T(8,128)(2,1)}, bf16[48,3712]{1,0:T(8,128)(2,1)}, bf16[48,3712]{1,0:T(8,128)(2,1)}, bf16[48,3712]{1,0:T(8,128)(2,1)}, f32[32...) custom-call(f32[1,128]{1,0:T(1,128)} %compare_convert_fusion.mine_ref, ...), custom_call_target="tpu_custom_call" | custom-call | flops 1024 | bytes 1024 | tf_op jit(solution)/shard_map/pallas_call | solution.py:233
  82.8 11.3 %collective-permute-done.8.refs_3_ = bf16[48,7296]{1,0:T(8,128)(2,1)} collective-permute-done((bf16[48,7296]{1,0:T(8,128)(2,1)}, bf16[48,7296]{1,0:T(8,128)(2,1)}, u32[]{:S(2)}, u32[]{:S(2)}) %collective-permute-start.8) | collective-permute-done | bytes 700448 | tf_op jit(solution)/shard_map/ppermute | solution.py:282
  94.1 1.3 copy-done.3
  95.4 4.7 %shard_map.155 = (bf16[48,7296]{1,0:T(8,128)(2,1)}, bf16[48,7296]{1,0:T(8,128)(2,1)}, bf16[48,7296]{1,0:T(8,128)(2,1)}, bf16[48,7296]{1,0:T(8,128)(2,1)}, bf16[192,128]{1,0:T(8,128)(2,1)}) custom-call(s32[1]{0:T(128)} %bitcast.flag_ref, bf16[16,128]{1,0:T(8,128)(2,1)} %pad_convert_fusion.guide_ref, bf16[128,7296]{1,0:T(8,128)(2,1)} %copy-done.3, ...), custom_call_target="tpu_custom_call" | custom-call | flops 1024 | bytes 1024 | tf_op jit(solution)/shard_map/pallas_call | solution.py:87
  100.1 2.1 collective-permute-start.10
  102.4 1.4 collective-permute-start.15
  103.8 19.8 %shard_map.159 = (bf16[48,3712]{1,0:T(8,128)(2,1)}, bf16[48,3712]{1,0:T(8,128)(2,1)}, bf16[48,3712]{1,0:T(8,128)(2,1)}, bf16[48,3712]{1,0:T(8,128)(2,1)}, f32[32...) custom-call(f32[1,128]{1,0:T(1,128)} %compare_convert_fusion.mine_ref, ...), custom_call_target="tpu_custom_call" | custom-call | flops 1024 | bytes 1024 | tf_op jit(solution)/shard_map/pallas_call | solution.py:233
  124.2 1.7 collective-permute-start.14
  125.8 16.0 %collective-permute-done.9.refs_0_ = bf16[128,7296]{1,0:T(8,128)(2,1)S(1)} collective-permute-done((bf16[128,7296]{1,0:T(8,128)(2,1)S(1)}, bf16[128,7296]{1,0:T(8,128)(2,1)S(1)}, u32[]{:S(2)}, u32[]{:S(2)}) %collective-permute-start.9) | collective-permute-done | bytes 1867808 | tf_op jit(solution)/shard_map/ppermute | solution.py:282
  141.9 1.3 copy-done.4
  143.1 4.1 %shard_map.158 = (bf16[48,7296]{1,0:T(8,128)(2,1)}, bf16[48,7296]{1,0:T(8,128)(2,1)}, bf16[48,7296]{1,0:T(8,128)(2,1)}, bf16[48,7296]{1,0:T(8,128)(2,1)}, bf16[192,128]{1,0:T(8,128)(2,1)}) custom-call(s32[1]{0:T(128)} %bitcast.flag_ref, bf16[16,128]{1,0:T(8,128)(2,1)} %pad_convert_fusion.guide_ref, bf16[128,7296]{1,0:T(8,128)(2,1)} %copy-done.4), custom_call_target="tpu_custom_call" | custom-call | flops 1024 | bytes 1024 | tf_op jit(solution)/shard_map/pallas_call | solution.py:87
  147.2 2.8 collective-permute-done.14.refs_3_
  150.6 1.6 collective-permute-start.18
  152.2 2.8 shard_map.161
  155.0 1.2 collective-permute-start.22
  156.2 19.8 %shard_map.160 = (bf16[48,3712]{1,0:T(8,128)(2,1)}, bf16[48,3712]{1,0:T(8,128)(2,1)}, bf16[48,3712]{1,0:T(8,128)(2,1)}, bf16[48,3712]{1,0:T(8,128)(2,1)}, f32[32...) custom-call(f32[1,128]{1,0:T(1,128)} %compare_convert_fusion.mine_ref, ...), custom_call_target="tpu_custom_call" | custom-call | flops 1024 | bytes 1024 | tf_op jit(solution)/shard_map/pallas_call | solution.py:233
  176.6 1.6 collective-permute-start.21
  178.2 5.4 %collective-permute-done.18.refs_3_ = bf16[48,7296]{1,0:T(8,128)(2,1)S(1)} collective-permute-done((bf16[48,7296]{1,0:T(8,128)(2,1)}, bf16[48,7296]{1,0:T(8,128)(2,1)S(1)}, u32[]{:S(2)}, u32[]{:S(2)}) %collective-permute-start.18) | collective-permute-done | bytes 700448 | tf_op jit(solution)/shard_map/ppermute | solution.py:282
  183.6 6.7 %collective-permute-done.20.refs_2_ = bf16[48,3712]{1,0:T(8,128)(2,1)S(1)} collective-permute-done((bf16[48,3712]{1,0:T(8,128)(2,1)}, bf16[48,3712]{1,0:T(8,128)(2,1)S(1)}, u32[]{:S(2)}, u32[]{:S(2)}) %collective-permute-start.20) | collective-permute-done | bytes 356384 | tf_op jit(solution)/shard_map/ppermute | solution.py:282
  190.3 8.0 %collective-permute-done.21.refs_3_ = bf16[48,3712]{1,0:T(8,128)(2,1)S(1)} collective-permute-done((bf16[48,3712]{1,0:T(8,128)(2,1)}, bf16[48,3712]{1,0:T(8,128)(2,1)S(1)}, u32[]{:S(2)}, u32[]{:S(2)}) %collective-permute-start.21) | collective-permute-done | bytes 356384 | tf_op jit(solution)/shard_map/ppermute | solution.py:282
  199.0 2.7 shard_map.163
  201.7 1.3 collective-permute-start.23
  203.6 1.6 collective-permute-start.26
  205.2 19.8 %shard_map.162 = (bf16[48,3712]{1,0:T(8,128)(2,1)}, bf16[48,3712]{1,0:T(8,128)(2,1)}, bf16[48,3712]{1,0:T(8,128)(2,1)}, bf16[48,3712]{1,0:T(8,128)(2,1)}, f32[32...) custom-call(f32[1,128]{1,0:T(1,128)} %compare_convert_fusion.mine_ref, ...), custom_call_target="tpu_custom_call" | custom-call | flops 1024 | bytes 1024 | tf_op jit(solution)/shard_map/pallas_call | solution.py:233
  225.3 1.0 collective-permute-start.27
  226.5 1.4 collective-permute-start.29
  228.8 7.7 %collective-permute-done.28.refs_2_ = bf16[48,3712]{1,0:T(8,128)(2,1)S(1)} collective-permute-done((bf16[48,3712]{1,0:T(8,128)(2,1)}, bf16[48,3712]{1,0:T(8,128)(2,1)S(1)}, u32[]{:S(2)}, u32[]{:S(2)}) %collective-permute-start.28) | collective-permute-done | bytes 356384 | tf_op jit(solution)/shard_map/ppermute | solution.py:282
  236.5 8.0 %collective-permute-done.29.refs_3_ = bf16[48,3712]{1,0:T(8,128)(2,1)S(1)} collective-permute-done((bf16[48,3712]{1,0:T(8,128)(2,1)}, bf16[48,3712]{1,0:T(8,128)(2,1)S(1)}, u32[]{:S(2)}, u32[]{:S(2)}) %collective-permute-start.29) | collective-permute-done | bytes 356384 | tf_op jit(solution)/shard_map/ppermute | solution.py:282
  244.5 3.3 %collective-permute-done.30.refs_3_ = bf16[64,3584]{1,0:T(8,128)(2,1)S(1)} collective-permute-done((bf16[64,3584]{1,0:T(8,128)(2,1)S(1)}, bf16[64,3584]{1,0:T(8,128)(2,1)S(1)}, u32[]{:S(2)}, u32[]{:S(2)}) %collective-permute-start.30) | collective-permute-done | bytes 458784 | tf_op jit(solution)/shard_map/ppermute | solution.py:282
  247.8 2.9 shard_map.165
  251.3 2.7 shard_map.164
  254.5 0.9 multiply_reduce_fusion
  255.5 0.9 multiply_convert_fusion.logit_ref
  257.6 22.8 %all_to_all.5 = f32[16,16,224]{2,1,0:T(8,128)S(1)} all-to-all(f32[16,16,224]{2,1,0:T(8,128)S(1)} %bitcast.57), channel_id=1, replica_groups=mesh['groups'=2,'expert'=16] {'expert'}, dimensions={0} | all-to-all | bytes 458752 | tf_op jit(solution)/shard_map/all_to_all | solution.py:423
  281.0 0.9 copy-done.6
  281.9 3.7 %shard_map.166 = bf16[128,3584]{1,0:T(8,128)(2,1)} custom-call(bf16[128,16]{1,0:T(8,128)(2,1)} %copy-done.31, bf16[16,3584]{1,0:T(8,128)(2,1)} %bitcast.58, bf16[128,3584]{1,0:T(8,128)(2,1)} %get-tuple-element.328.refs_0_, bf16[128,3712]{1,0:T(8,128)(2,1)} %copy-done.5, bf16[64,3584]{1,0:T(8,128)(2,1)} %copy-done.17, bf16[64,3584]{1,0:T(8,128)(2,1)} %copy-done.18, ...), custom_call_target="tpu_custom_call" | custom-call | flops 1024 | bytes 1024 | tf_op jit(solution)/shard_map/pallas_call | solution.py:146
  (128 shorter events, 12.7 us)
Async XLA Ops:
  6.7 42.6 %collective-permute-start = (bf16[128,7296]{1,0:T(8,128)(2,1)S(1)}, bf16[128,7296]{1,0:T(8,128)(2,1)}, u32[]{:S(2)}, u32[]{:S(2)}) collective-permute-start(bf16[128,7296]{1,0:T(8,128)(2,1)S(1)} %concatenate.5.refs_0_), channel_id=1, source_target_pairs={{0,8},{1,9},{2,10},{3,11},{12,4},{13,5},{14,6},{15,7},{4,0},{5,1},... | collective-permute-start | bytes 5603336 | tf_op jit(solution)/shard_map/ppermute | solution.py:282
  12.1 2.7 collective-permute-start.1
  12.8 17.6 %collective-permute-start.2 = (bf16[48,7296]{1,0:T(8,128)(2,1)}, bf16[48,7296]{1,0:T(8,128)(2,1)S(1)}, u32[]{:S(2)}, u32[]{:S(2)}) collective-permute-start(bf16[48,7296]{1,0:T(8,128)(2,1)} %get-tuple-element.180), channel_id=1, source_target_pairs={{0,2},{1,3},{2,0},{3,1},{4,6},{5,7},{6,4},{7,5},{8,10},{9,11},{10,... | collective-permute-start | bytes 2101256 | tf_op jit(solution)/shard_map/ppermute | solution.py:282
  13.0 32.8 %collective-permute-start.3 = (bf16[48,7296]{1,0:T(8,128)(2,1)}, bf16[48,7296]{1,0:T(8,128)(2,1)S(1)}, u32[]{:S(2)}, u32[]{:S(2)}) collective-permute-start(bf16[48,7296]{1,0:T(8,128)(2,1)} %get-tuple-element.181), channel_id=1, source_target_pairs={{0,3},{1,2},{2,1},{3,0},{4,7},{5,6},{6,5},{7,4},{8,11},{9,10},{10,... | collective-permute-start | bytes 2101256 | tf_op jit(solution)/shard_map/ppermute | solution.py:282
  14.8 34.6 %copy-start.14 = (bf16[48,7296]{1,0:T(8,128)(2,1)}, bf16[48,7296]{1,0:T(8,128)(2,1)S(1)}, u32[]{:S(2)}) copy-start(bf16[48,7296]{1,0:T(8,128)(2,1)S(1)} %collective-permute-done.1.refs_1_) | copy-start | bytes 2101252
  49.4 44.7 %collective-permute-start.4 = (bf16[128,7296]{1,0:T(8,128)(2,1)}, bf16[128,7296]{1,0:T(8,128)(2,1)S(1)}, u32[]{:S(2)}, u32[]{:S(2)}) collective-permute-start(bf16[128,7296]{1,0:T(8,128)(2,1)} %copy-done), channel_id=1, source_target_pairs={{4,8},{5,9},{6,10},{7,11},{8,4},{9,5},{10,6},{11,7},{20,24},{21,25... | collective-permute-start | bytes 5603336 | tf_op jit(solution)/shard_map/ppermute | solution.py:282
  52.6 41.5 %collective-permute-start.5 = (bf16[128,7296]{1,0:T(8,128)(2,1)}, bf16[128,7296]{1,0:T(8,128)(2,1)}, u32[]{:S(2)}, u32[]{:S(2)}) collective-permute-start(bf16[128,7296]{1,0:T(8,128)(2,1)} %collective-permute-done.refs_0_), channel_id=1, source_target_pairs={{4,0},{5,1},{6,2},{7,3},{8,12},{9,13},{10,14},{11,15},{20,16},{21,... | collective-permute-start | bytes 5603336 | tf_op jit(solution)/shard_map/ppermute | solution.py:282
  59.3 23.4 %collective-permute-start.6 = (bf16[48,7296]{1,0:T(8,128)(2,1)}, bf16[48,7296]{1,0:T(8,128)(2,1)S(1)}, u32[]{:S(2)}, u32[]{:S(2)}) collective-permute-start(bf16[48,7296]{1,0:T(8,128)(2,1)} %get-tuple-element.189), channel_id=1, source_target_pairs={{0,1},{1,0},{2,3},{3,2},{4,5},{5,4},{6,7},{7,6},{8,9},{9,8},{10,11... | collective-permute-start | bytes 2101256 | tf_op jit(solution)/shard_map/ppermute | solution.py:282
  61.2 21.6 %collective-permute-start.7 = (bf16[48,7296]{1,0:T(8,128)(2,1)}, bf16[48,7296]{1,0:T(8,128)(2,1)}, u32[]{:S(2)}, u32[]{:S(2)}) collective-permute-start(bf16[48,7296]{1,0:T(8,128)(2,1)} %get-tuple-element.190), channel_id=1, source_target_pairs={{0,2},{1,3},{2,0},{3,1},{4,6},{5,7},{6,4},{7,5},{8,10},{9,11},{10,... | collective-permute-start | bytes 2101256 | tf_op jit(solution)/shard_map/ppermute | solution.py:282
  61.4 32.7 %collective-permute-start.8 = (bf16[48,7296]{1,0:T(8,128)(2,1)}, bf16[48,7296]{1,0:T(8,128)(2,1)}, u32[]{:S(2)}, u32[]{:S(2)}) collective-permute-start(bf16[48,7296]{1,0:T(8,128)(2,1)} %get-tuple-element.191), channel_id=1, source_target_pairs={{0,3},{1,2},{2,1},{3,0},{4,7},{5,6},{6,5},{7,4},{8,11},{9,10},{10,... | collective-permute-start | bytes 2101256 | tf_op jit(solution)/shard_map/ppermute | solution.py:282
  100.1 41.8 %collective-permute-start.9 = (bf16[128,7296]{1,0:T(8,128)(2,1)S(1)}, bf16[128,7296]{1,0:T(8,128)(2,1)S(1)}, u32[]{:S(2)}, u32[]{:S(2)}) collective-permute-start(bf16[128,7296]{1,0:T(8,128)(2,1)S(1)} %copy-done.1), channel_id=1, source_target_pairs={{0,4},{1,5},{2,6},{3,7},{12,8},{13,9},{14,10},{15,11},{4,12},{5,13... | collective-permute-start | bytes 5603336 | tf_op jit(solution)/shard_map/ppermute | solution.py:282
  100.1 23.5 %collective-permute-start.10 = (bf16[48,7296]{1,0:T(8,128)(2,1)}, bf16[48,7296]{1,0:T(8,128)(2,1)S(1)}, u32[]{:S(2)}, u32[]{:S(2)}) collective-permute-start(bf16[48,7296]{1,0:T(8,128)(2,1)} %get-tuple-element.230), channel_id=1, source_target_pairs={{0,1},{1,0},{2,3},{3,2},{4,5},{5,4},{6,7},{7,6},{8,9},{9,8},{10,11... | collective-permute-start | bytes 2101256 | tf_op jit(solution)/shard_map/ppermute | solution.py:282
  102.1 21.5 %collective-permute-start.11 = (bf16[48,7296]{1,0:T(8,128)(2,1)}, bf16[48,7296]{1,0:T(8,128)(2,1)S(1)}, u32[]{:S(2)}, u32[]{:S(2)}) collective-permute-start(bf16[48,7296]{1,0:T(8,128)(2,1)} %get-tuple-element.231), channel_id=1, source_target_pairs={{0,2},{1,3},{2,0},{3,1},{4,6},{5,7},{6,4},{7,5},{8,10},{9,11},{10,... | collective-permute-start | bytes 2101256 | tf_op jit(solution)/shard_map/ppermute | solution.py:282
  102.4 44.8 %collective-permute-start.15 = (bf16[48,7296]{1,0:T(8,128)(2,1)}, bf16[48,7296]{1,0:T(8,128)(2,1)S(1)}, u32[]{:S(2)}, u32[]{:S(2)}) collective-permute-start(bf16[48,7296]{1,0:T(8,128)(2,1)} %get-tuple-element.239), channel_id=1, source_target_pairs={{0,3},{1,2},{2,1},{3,0},{4,7},{5,6},{6,5},{7,4},{8,11},{9,10},{10,... | collective-permute-start | bytes 2101256 | tf_op jit(solution)/shard_map/ppermute | solution.py:282
  123.6 32.6 %copy-start.8 = (bf16[48,7296]{1,0:T(8,128)(2,1)}, bf16[48,7296]{1,0:T(8,128)(2,1)S(1)}, u32[]{:S(2)}) copy-start(bf16[48,7296]{1,0:T(8,128)(2,1)S(1)} %collective-permute-done.10.refs_1_) | copy-start | bytes 2101252
  123.6 32.6 %copy-start.10 = (bf16[48,7296]{1,0:T(8,128)(2,1)}, bf16[48,7296]{1,0:T(8,128)(2,1)S(1)}, u32[]{:S(2)}) copy-start(bf16[48,7296]{1,0:T(8,128)(2,1)S(1)} %collective-permute-done.11.refs_2_) | copy-start | bytes 2101252
  123.6 23.6 %collective-permute-start.12 = (bf16[48,3712]{1,0:T(8,128)(2,1)}, bf16[48,3712]{1,0:T(8,128)(2,1)S(1)}, u32[]{:S(2)}, u32[]{:S(2)}) collective-permute-start(bf16[48,3712]{1,0:T(8,128)(2,1)} %get-tuple-element.233), channel_id=1, source_target_pairs={{0,1},{1,0},{2,3},{3,2},{4,5},{5,4},{6,7},{7,6},{8,9},{9,8},{10,11... | collective-permute-start | bytes 1069064 | tf_op jit(solution)/shard_map/ppermute | solution.py:282
  123.9 23.3 %collective-permute-start.13 = (bf16[48,3712]{1,0:T(8,128)(2,1)}, bf16[48,3712]{1,0:T(8,128)(2,1)S(1)}, u32[]{:S(2)}, u32[]{:S(2)}) collective-permute-start(bf16[48,3712]{1,0:T(8,128)(2,1)} %get-tuple-element.234), channel_id=1, source_target_pairs={{0,2},{1,3},{2,0},{3,1},{4,6},{5,7},{6,4},{7,5},{8,10},{9,11},{10,... | collective-permute-start | bytes 1069064 | tf_op jit(solution)/shard_map/ppermute | solution.py:282
  124.2 25.9 %collective-permute-start.14 = (bf16[48,3712]{1,0:T(8,128)(2,1)}, bf16[48,3712]{1,0:T(8,128)(2,1)S(1)}, u32[]{:S(2)}, u32[]{:S(2)}) collective-permute-start(bf16[48,3712]{1,0:T(8,128)(2,1)} %get-tuple-element.235), channel_id=1, source_target_pairs={{0,3},{1,2},{2,1},{3,0},{4,7},{5,6},{6,5},{7,4},{8,11},{9,10},{10,... | collective-permute-start | bytes 1069064 | tf_op jit(solution)/shard_map/ppermute | solution.py:282
  150.1 25.9 %collective-permute-start.16 = (bf16[48,7296]{1,0:T(8,128)(2,1)}, bf16[48,7296]{1,0:T(8,128)(2,1)S(1)}, u32[]{:S(2)}, u32[]{:S(2)}) collective-permute-start(bf16[48,7296]{1,0:T(8,128)(2,1)} %get-tuple-element.257), channel_id=1, source_target_pairs={{0,1},{1,0},{2,3},{3,2},{4,5},{5,4},{6,7},{7,6},{8,9},{9,8},{10,11... | collective-permute-start | bytes 2101256 | tf_op jit(solution)/shard_map/ppermute | solution.py:282
  150.4 25.6 %collective-permute-start.17 = (bf16[48,7296]{1,0:T(8,128)(2,1)}, bf16[48,7296]{1,0:T(8,128)(2,1)S(1)}, u32[]{:S(2)}, u32[]{:S(2)}) collective-permute-start(bf16[48,7296]{1,0:T(8,128)(2,1)} %get-tuple-element.258), channel_id=1, source_target_pairs={{0,2},{1,3},{2,0},{3,1},{4,6},{5,7},{6,4},{7,5},{8,10},{9,11},{10,... | collective-permute-start | bytes 2101256 | tf_op jit(solution)/shard_map/ppermute | solution.py:282
  150.6 33.0 %collective-permute-start.18 = (bf16[48,7296]{1,0:T(8,128)(2,1)}, bf16[48,7296]{1,0:T(8,128)(2,1)S(1)}, u32[]{:S(2)}, u32[]{:S(2)}) collective-permute-start(bf16[48,7296]{1,0:T(8,128)(2,1)} %get-tuple-element.265), channel_id=1, source_target_pairs={{0,3},{1,2},{2,1},{3,0},{4,7},{5,6},{6,5},{7,4},{8,11},{9,10},{10,... | collective-permute-start | bytes 2101256 | tf_op jit(solution)/shard_map/ppermute | solution.py:282
  155.0 48.6 %copy-start.36 = (bf16[48,3712]{1,0:T(8,128)(2,1)S(1)}, bf16[48,3712]{1,0:T(8,128)(2,1)}, u32[]{:S(2)}) copy-start(bf16[48,3712]{1,0:T(8,128)(2,1)} %get-tuple-element.305) | copy-start | bytes 1069060
  155.0 70.0 %collective-permute-start.22 = (bf16[128,3712]{1,0:T(8,128)(2,1)}, bf16[128,3712]{1,0:T(8,128)(2,1)S(1)}, u32[]{:S(2)}, u32[]{:S(2)}) collective-permute-start(bf16[128,3712]{1,0:T(8,128)(2,1)} %shard_map.161), channel_id=1, source_target_pairs={{0,4},{1,5},{2,6},{3,7},{12,8},{13,9},{14,10},{15,11},{4,12},{5,13... | collective-permute-start | bytes 2850824 | tf_op jit(solution)/shard_map/ppermute | solution.py:282
  176.0 29.2 %copy-start.7 = (bf16[48,7296]{1,0:T(8,128)(2,1)}, bf16[48,7296]{1,0:T(8,128)(2,1)S(1)}, u32[]{:S(2)}) copy-start(bf16[48,7296]{1,0:T(8,128)(2,1)S(1)} %collective-permute-done.16.refs_1_) | copy-start | bytes 2101252
  176.0 29.2 %copy-start.9 = (bf16[48,7296]{1,0:T(8,128)(2,1)}, bf16[48,7296]{1,0:T(8,128)(2,1)S(1)}, u32[]{:S(2)}) copy-start(bf16[48,7296]{1,0:T(8,128)(2,1)S(1)} %collective-permute-done.17.refs_2_) | copy-start | bytes 2101252
  176.0 7.6 %collective-permute-start.19 = (bf16[48,3712]{1,0:T(8,128)(2,1)}, bf16[48,3712]{1,0:T(8,128)(2,1)S(1)}, u32[]{:S(2)}, u32[]{:S(2)}) collective-permute-start(bf16[48,3712]{1,0:T(8,128)(2,1)} %get-tuple-element.272), channel_id=1, source_target_pairs={{0,1},{1,0},{2,3},{3,2},{4,5},{5,4},{6,7},{7,6},{8,9},{9,8},{10,11... | collective-permute-start | bytes 1069064 | tf_op jit(solution)/shard_map/ppermute | solution.py:282
  176.3 14.0 %collective-permute-start.20 = (bf16[48,3712]{1,0:T(8,128)(2,1)}, bf16[48,3712]{1,0:T(8,128)(2,1)S(1)}, u32[]{:S(2)}, u32[]{:S(2)}) collective-permute-start(bf16[48,3712]{1,0:T(8,128)(2,1)} %get-tuple-element.273), channel_id=1, source_target_pairs={{0,2},{1,3},{2,0},{3,1},{4,6},{5,7},{6,4},{7,5},{8,10},{9,11},{10,... | collective-permute-start | bytes 1069064 | tf_op jit(solution)/shard_map/ppermute | solution.py:282
  176.6 21.7 %collective-permute-start.21 = (bf16[48,3712]{1,0:T(8,128)(2,1)}, bf16[48,3712]{1,0:T(8,128)(2,1)S(1)}, u32[]{:S(2)}, u32[]{:S(2)}) collective-permute-start(bf16[48,3712]{1,0:T(8,128)(2,1)} %get-tuple-element.274), channel_id=1, source_target_pairs={{0,3},{1,2},{2,1},{3,0},{4,7},{5,6},{6,5},{7,4},{8,11},{9,10},{10,... | collective-permute-start | bytes 1069064 | tf_op jit(solution)/shard_map/ppermute | solution.py:282
  201.7 26.2 %copy-start.37 = (bf16[128,128]{1,0:T(8,128)(2,1)S(1)}, bf16[128,128]{1,0:T(8,128)(2,1)}, u32[]{:S(2)}) copy-start(bf16[128,128]{1,0:T(8,128)(2,1)} %get-tuple-element.321) | copy-start | bytes 98308
  201.7 23.3 %collective-permute-start.23 = (bf16[64,3584]{1,0:T(8,128)(2,1)}, bf16[64,3584]{1,0:T(8,128)(2,1)S(1)}, u32[]{:S(2)}, u32[]{:S(2)}) collective-permute-start(bf16[64,3584]{1,0:T(8,128)(2,1)} %get-tuple-element.300), channel_id=1, source_target_pairs={{0,12},{1,13},{2,14},{3,15},{4,8},{5,9},{6,10},{7,11},{8,4},{9,5},... | collective-permute-start | bytes 1376264 | tf_op jit(solution)/shard_map/ppermute | solution.py:282
  203.0 22.0 %collective-permute-start.24 = (bf16[48,3712]{1,0:T(8,128)(2,1)}, bf16[48,3712]{1,0:T(8,128)(2,1)S(1)}, u32[]{:S(2)}, u32[]{:S(2)}) collective-permute-start(bf16[48,3712]{1,0:T(8,128)(2,1)} %get-tuple-element.303), channel_id=1, source_target_pairs={{0,1},{1,0},{2,3},{3,2},{4,5},{5,4},{6,7},{7,6},{8,9},{9,8},{10,11... | collective-permute-start | bytes 1069064 | tf_op jit(solution)/shard_map/ppermute | solution.py:282
  203.4 21.6 %collective-permute-start.25 = (bf16[48,3712]{1,0:T(8,128)(2,1)}, bf16[48,3712]{1,0:T(8,128)(2,1)S(1)}, u32[]{:S(2)}, u32[]{:S(2)}) collective-permute-start(bf16[48,3712]{1,0:T(8,128)(2,1)} %get-tuple-element.304), channel_id=1, source_target_pairs={{0,2},{1,3},{2,0},{3,1},{4,6},{5,7},{6,4},{7,5},{8,10},{9,11},{10,... | collective-permute-start | bytes 1069064 | tf_op jit(solution)/shard_map/ppermute | solution.py:282
  203.6 21.4 %collective-permute-start.26 = (bf16[48,3712]{1,0:T(8,128)(2,1)S(1)}, bf16[48,3712]{1,0:T(8,128)(2,1)S(1)}, u32[]{:S(2)}, u32[]{:S(2)}) collective-permute-start(bf16[48,3712]{1,0:T(8,128)(2,1)S(1)} %copy-done.36), channel_id=1, source_target_pairs={{0,3},{1,2},{2,1},{3,0},{4,7},{5,6},{6,5},{7,4},{8,11},{9,10},{10,... | collective-permute-start | bytes 1069064 | tf_op jit(solution)/shard_map/ppermute | solution.py:282
  225.0 29.6 %copy-start.33 = (f32[128,16]{1,0:T(8,128)S(1)}, f32[128,16]{1,0:T(8,128)}, u32[]{:S(2)}) copy-start(f32[128,16]{1,0:T(8,128)} %copy-done.32) | copy-start | bytes 24580
  225.0 30.5 %copy-start.34 = (f32[128,16]{1,0:T(8,128)S(1)}, f32[128,16]{1,0:T(8,128)}, u32[]{:S(2)}) copy-start(f32[128,16]{1,0:T(8,128)} %get-tuple-element.338) | copy-start | bytes 24580
  225.0 32.3 %copy-start.5 = (bf16[128,3712]{1,0:T(8,128)(2,1)}, bf16[128,3712]{1,0:T(8,128)(2,1)S(1)}, u32[]{:S(2)}) copy-start(bf16[128,3712]{1,0:T(8,128)(2,1)S(1)} %collective-permute-done.22.refs_1_) | copy-start | bytes 2850820
  225.0 26.2 %copy-start.22 = (bf16[48,3712]{1,0:T(8,128)(2,1)}, bf16[48,3712]{1,0:T(8,128)(2,1)S(1)}, u32[]{:S(2)}) copy-start(bf16[48,3712]{1,0:T(8,128)(2,1)S(1)} %collective-permute-done.24.refs_1_) | copy-start | bytes 1069060
  225.0 26.2 %copy-start.23 = (bf16[48,3712]{1,0:T(8,128)(2,1)}, bf16[48,3712]{1,0:T(8,128)(2,1)S(1)}, u32[]{:S(2)}) copy-start(bf16[48,3712]{1,0:T(8,128)(2,1)S(1)} %collective-permute-done.25.refs_2_) | copy-start | bytes 1069060
  225.1 26.2 %copy-start.24 = (bf16[48,3712]{1,0:T(8,128)(2,1)}, bf16[48,3712]{1,0:T(8,128)(2,1)S(1)}, u32[]{:S(2)}) copy-start(bf16[48,3712]{1,0:T(8,128)(2,1)S(1)} %collective-permute-done.26.refs_3_) | copy-start | bytes 1069060
  225.1 32.2 %copy-start.17 = (bf16[64,3584]{1,0:T(8,128)(2,1)}, bf16[64,3584]{1,0:T(8,128)(2,1)S(1)}, u32[]{:S(2)}) copy-start(bf16[64,3584]{1,0:T(8,128)(2,1)S(1)} %collective-permute-done.23.refs_2_) | copy-start | bytes 1376260
  225.1 22.7 %collective-permute-start.30 = (bf16[64,3584]{1,0:T(8,128)(2,1)S(1)}, bf16[64,3584]{1,0:T(8,128)(2,1)S(1)}, u32[]{:S(2)}, u32[]{:S(2)}) collective-permute-start(bf16[64,3584]{1,0:T(8,128)(2,1)S(1)} %copy-done.35), channel_id=1, source_target_pairs={{0,12},{1,13},{2,14},{3,15},{4,8},{5,9},{6,10},{7,11},{8,4},{9,5},... | collective-permute-start | bytes 1376264 | tf_op jit(solution)/shard_map/ppermute | solution.py:282
  225.3 3.5 %collective-permute-start.27 = (bf16[48,3712]{1,0:T(8,128)(2,1)}, bf16[48,3712]{1,0:T(8,128)(2,1)S(1)}, u32[]{:S(2)}, u32[]{:S(2)}) collective-permute-start(bf16[48,3712]{1,0:T(8,128)(2,1)} %get-tuple-element.307), channel_id=1, source_target_pairs={{0,1},{1,0},{2,3},{3,2},{4,5},{5,4},{6,7},{7,6},{8,9},{9,8},{10,11... | collective-permute-start | bytes 1069064 | tf_op jit(solution)/shard_map/ppermute | solution.py:282
  226.3 10.2 %collective-permute-start.28 = (bf16[48,3712]{1,0:T(8,128)(2,1)}, bf16[48,3712]{1,0:T(8,128)(2,1)S(1)}, u32[]{:S(2)}, u32[]{:S(2)}) collective-permute-start(bf16[48,3712]{1,0:T(8,128)(2,1)} %get-tuple-element.308), channel_id=1, source_target_pairs={{0,2},{1,3},{2,0},{3,1},{4,6},{5,7},{6,4},{7,5},{8,10},{9,11},{10,... | collective-permute-start | bytes 1069064 | tf_op jit(solution)/shard_map/ppermute | solution.py:282
  226.5 18.0 %collective-permute-start.29 = (bf16[48,3712]{1,0:T(8,128)(2,1)}, bf16[48,3712]{1,0:T(8,128)(2,1)S(1)}, u32[]{:S(2)}, u32[]{:S(2)}) collective-permute-start(bf16[48,3712]{1,0:T(8,128)(2,1)} %get-tuple-element.309), channel_id=1, source_target_pairs={{0,3},{1,2},{2,1},{3,0},{4,7},{5,6},{6,5},{7,4},{8,11},{9,10},{10,... | collective-permute-start | bytes 1069064 | tf_op jit(solution)/shard_map/ppermute | solution.py:282
  227.9 26.0 %collective-permute-start.31 = (bf16[128,128]{1,0:T(8,128)(2,1)S(1)}, bf16[128,128]{1,0:T(8,128)(2,1)S(1)}, u32[]{:S(2)}, u32[]{:S(2)}) collective-permute-start(bf16[128,128]{1,0:T(8,128)(2,1)S(1)} %copy-done.37), channel_id=1, source_target_pairs={{0,12},{1,13},{2,14},{3,15},{4,8},{5,9},{6,10},{7,11},{8,4},{9,5},... | collective-permute-start | bytes 98312 | tf_op jit(solution)/shard_map/ppermute | solution.py:282
  250.6 3.9 %collective-permute-start.32 = (bf16[128,128]{1,0:T(8,128)(2,1)}, bf16[128,128]{1,0:T(8,128)(2,1)S(1)}, u32[]{:S(2)}, u32[]{:S(2)}) collective-permute-start(bf16[128,128]{1,0:T(8,128)(2,1)} %get-tuple-element.327), channel_id=1, source_target_pairs={{4,0},{5,1},{6,2},{7,3},{8,12},{9,13},{10,14},{11,15},{12,4},{13,5... | collective-permute-start | bytes 98312 | tf_op jit(solution)/shard_map/ppermute | solution.py:282
  250.6 30.4 %collective-permute-start.33 = (bf16[128,3584]{1,0:T(8,128)(2,1)}, bf16[128,3584]{1,0:T(8,128)(2,1)S(1)}, u32[]{:S(2)}, u32[]{:S(2)}) collective-permute-start(bf16[128,3584]{1,0:T(8,128)(2,1)} %get-tuple-element.331), channel_id=1, source_target_pairs={{4,0},{5,1},{6,2},{7,3},{8,12},{9,13},{10,14},{11,15},{12,4},{13,5... | collective-permute-start | bytes 2752520 | tf_op jit(solution)/shard_map/ppermute | solution.py:282
  (24 other events, 186.8 us)
